TPU v7x, 32 devices: a whole 2x2x4 slice. The times are simulated.
32 devices in a mesh: rep: 2 (over y), grid: 16 (over z, x, core).
Axes of the slice: x: 2, y: 2, z: 4, core: 2. Of those that a mesh axis runs over, the one named last changes fastest.
Arguments:
- pair_density: float32 [4, 2, 32, 32, 256], P('rep', None, 'grid'), parts along dimension 0, may hold values from -6 to 6
- moments: float32 [384, 2, 2, 25], P(('rep', 'grid')), parts along dimension 0, may hold values from -6 to 6
- shapes: float32 [2048, 25, 256], P(('rep', 'grid')), parts along dimension 0, may hold values from -2 to 2
- slot_atom: int32 [2048], P(('rep', 'grid')), parts along dimension 0, may hold values from 0 to 11
- slot_tile: int32 [2048, 1], P(('rep', 'grid')), parts along dimension 0, may hold values from 0 to 15; in each aligned block of 64 rows (0 to 63, 64 to 127, ...) at most 8 rows name the same one
- slot_row: int32 [2048], P(('rep', 'grid')), parts along dimension 0, may hold values from 0 to 63
- pair_table: int32 [2, 2], replicated, may hold values from 0 to 7
- k_fraction: float32 [8], replicated, may hold values from 0 to 1
Outputs:
- potential: float32 [4, 2, 32, 32, 256], P('rep', None, 'grid'), parts along dimension 0
There are 2 independent parts, one for each index of `rep`. A program takes and returns all parts, laid end to end along the dimension named above; an argument that names none is the same for every part. Nothing has to cross between parts.
Inputs may be any that keep to these rules, and one draw needn't show every extreme that they name: `slot_tile`: among the slots of one device at most 8 name the same tile, and in every draw some device names some tile exactly 8 times.
All inputs are finite; a program needn't handle non-finite values.
Results may differ from a plain program's by a relative error of at most 0.0001.
Values sent between devices are 32-bit elements; how exact they have to be, the bound alone decides.
No kernel may reach another device: no remote copies, remote signals or barrier semaphores. Data moves between devices by JAX's collectives and lax.ppermute only.
A program may use at most 128 MiB of HBM per device.

v0:
```python
from functools import partial

import jax
import jax.numpy as jnp
from jax import lax
from jax.sharding import PartitionSpec as P

LEVELS = 3
SWEEPS = 2
COARSE_SWEEPS = 6


omega = 0.8
screen = 0.05
highest = lax.Precision.HIGHEST


def from_behind(block, axis, distance):
    devices = range(lax.axis_size(axis))
    route = [((i - distance) % len(devices), i) for i in devices]
    return lax.ppermute(block, axis, route)


def from_partner(value, axis, distance):
    mask = 2**distance
    pairs = [(source, source ^ mask) for source in range(lax.axis_size(axis))]
    return lax.ppermute(value, axis, pairs)


def with_halo(block, sides, width):
    for axis, dim in sides:
        count = lax.axis_size(axis)
        forward = [(i, i + 1) for i in range(count - 1)]
        forward.append((count - 1, 0))
        backward = [(target, source) for source, target in forward]
        low = lax.ppermute(
            lax.slice_in_dim(block, block.shape[dim] - width, None, axis=dim), axis, forward
        )
        high = lax.ppermute(lax.slice_in_dim(block, 0, width, axis=dim), axis, backward)
        block = jnp.concatenate([low, block, high], axis=dim)
    return block


def pair_phases(pair_table, k_fraction):
    kcount = k_fraction.shape[0]
    picks = (pair_table[:, :, None] == jnp.arange(kcount, dtype=jnp.int32)[None, None, :]).astype(
        jnp.float32
    )
    chosen = jnp.sum(picks * k_fraction[None, None, :], axis=2)
    angle = 6.283185307179586 * (chosen[:, 0] - chosen[:, 1])
    return (jnp.cos(angle).reshape(-1, 1, 1, 1), jnp.sin(angle).reshape(-1, 1, 1, 1))


def rotate(values, cosine, sine):
    real_part = values[:, 0]
    imag_part = values[:, 1]
    return jnp.stack(
        [cosine * real_part - sine * imag_part, sine * real_part + cosine * imag_part], axis=1
    )


def fix_rims(padded, width, cosine, sine, at_start, at_end):
    before = padded[:, :, :width]
    after = padded[:, :, -width:]
    before = jnp.where(at_start, rotate(before, cosine, -sine), before)
    after = jnp.where(at_end, rotate(after, cosine, sine), after)
    return jnp.concatenate([before, padded[:, :, width:-width], after], axis=2)


def fine_apply(values, padded):
    planes = values.shape[2]
    nearest = padded[:, :, 1 : planes + 1] + padded[:, :, 3 : planes + 3]
    farther = padded[:, :, 0:planes] + padded[:, :, 4 : planes + 4]
    for axis_id in (3, 4):
        nearest = nearest + jnp.roll(values, 1, axis_id) + jnp.roll(values, -1, axis_id)
        farther = farther + jnp.roll(values, 2, axis_id) + jnp.roll(values, -2, axis_id)
    return (7.5 + screen) * values - 4.0 / 3.0 * nearest + 1.0 / 12.0 * farther


def coarse_apply(values, padded, depth):
    scale_value = 1.0 / 4**depth
    planes = values.shape[2]
    nearest = padded[:, :, 0:planes] + padded[:, :, 2 : planes + 2]
    for axis_id in (3, 4):
        nearest = nearest + jnp.roll(values, 1, axis_id) + jnp.roll(values, -1, axis_id)
    return (6.0 * scale_value + screen) * values - scale_value * nearest


def restrict_yz(values):
    sizes = values.shape
    blocks = values.reshape(sizes[0], sizes[1], sizes[2], sizes[3] // 2, 2, sizes[4] // 2, 2)
    return blocks.mean(axis=(4, 6))


def restrict_x(values):
    sizes = values.shape
    blocks = values.reshape(sizes[0], sizes[1], sizes[2] // 2, 2, sizes[3], sizes[4])
    return (blocks[:, :, :, 0] + blocks[:, :, :, 1]) * 0.5


def restrict(values):
    return restrict_x(restrict_yz(values))


def prolong_yz(values):
    return jnp.repeat(jnp.repeat(values, 2, axis=3), 2, axis=4)


def prolong(values):
    return jnp.repeat(prolong_yz(values), 2, axis=2)


def relax(iterate, source, depth, padder, sweeps):
    diagonal_value = 6.0 / 4**depth + screen
    remaining = sweeps
    if iterate is None:
        iterate = omega * source / diagonal_value
        remaining = sweeps - 1
    for sweep_index in range(remaining):
        iterate = (
            iterate
            + omega * (source - coarse_apply(iterate, padder(iterate), depth)) / diagonal_value
        )
    return iterate


def from_group(values, offset):
    return from_behind(values, "grid", offset)


def group_pad(values, group, cosine, sine, position, tile_count):
    before = from_group(values, group)
    after = from_group(values, tile_count - group)
    before = jnp.where(position < group, rotate(before, cosine, -sine), before)
    after = jnp.where(position >= tile_count - group, rotate(after, cosine, sine), after)
    return jnp.concatenate([before, values, after], axis=2)


def group_cycle(residual, cosine, sine, position, tile_count):
    sources = []
    iterates = []
    padders = []
    current = residual
    iterate = residual
    for depth in range(2, LEVELS + 1):
        half = restrict_yz(current)
        partner = from_partner(half, "grid", depth - 2)
        source = (half + partner) * 0.5
        group = 2 ** (depth - 1)
        padder = partial(
            group_pad,
            group=group,
            cosine=cosine,
            sine=sine,
            position=position,
            tile_count=tile_count,
        )
        if depth < LEVELS:
            iterate = relax(None, source, depth, padder, SWEEPS)
            current = source - coarse_apply(iterate, padder(iterate), depth)
            sources.append(source)
            iterates.append(iterate)
            padders.append(padder)
        else:
            iterate = relax(None, source, depth, padder, COARSE_SWEEPS)
    depth = 2
    place = depth - 2
    iterate = iterates[place] + prolong_yz(iterate)
    iterate = relax(iterate, sources[place], depth, padders[place], SWEEPS)
    return iterate


def compensation(field_shape, moments, shapes, slot_atom, slot_tile, slot_row, tile_count):
    slot_count = shapes.shape[0]
    atom_count = moments.shape[0]
    capacity = max(2, 2 * slot_count // tile_count)
    atom_pick = (slot_atom[:, None] == jnp.arange(atom_count, dtype=jnp.int32)[None, :]).astype(
        jnp.float32
    )
    chosen = jnp.dot(atom_pick, moments.reshape(atom_count, -1), precision=highest)
    chosen = chosen.reshape(slot_count, moments.shape[1] * moments.shape[2], moments.shape[3])
    row_values = jnp.einsum("sfl,slz->sfz", chosen, shapes, precision=highest)
    tiles = slot_tile[:, 0]
    slot_ids = jnp.arange(slot_count, dtype=jnp.int32)
    before = (tiles[:, None] == tiles[None, :]) & (slot_ids[None, :] < slot_ids[:, None])
    ranks = jnp.sum(before.astype(jnp.int32), axis=1)
    places = tiles * capacity + ranks
    buckets = jnp.arange(tile_count * capacity, dtype=jnp.int32)
    pick = buckets[:, None] == places[None, :]
    packed = jnp.dot(
        pick.astype(jnp.float32), row_values.reshape(slot_count, -1), precision=highest
    )
    packed = packed.reshape(tile_count, capacity, row_values.shape[1], row_values.shape[2])
    targets = (
        jnp.sum(jnp.where(pick, slot_row[None, :] + 1, 0), axis=1).reshape(tile_count, capacity) - 1
    )
    received, destinations = (
        lax.all_to_all(packed, "grid", split_axis=0, concat_axis=0, tiled=True),
        lax.all_to_all(targets, "grid", split_axis=0, concat_axis=0, tiled=True),
    )
    row_total = field_shape[2] * field_shape[3]
    spread = (
        jnp.arange(row_total, dtype=jnp.int32)[:, None] == destinations.reshape(1, -1)
    ).astype(jnp.float32)
    incoming = received.reshape(tile_count * capacity, row_values.shape[1], row_values.shape[2])
    added = jnp.einsum("rk,kfz->frz", spread, incoming, precision=highest)
    return added.reshape(field_shape)


def per_device(
    pair_density, moments, shapes, slot_atom, slot_tile, slot_row, pair_table, k_fraction
):
    tile_count = lax.axis_size("grid")
    position = lax.axis_index("grid")
    cosine, sine = pair_phases(pair_table, k_fraction)
    density = pair_density + compensation(
        pair_density.shape, moments, shapes, slot_atom, slot_tile, slot_row, tile_count
    )
    at_start = position == 0
    at_end = position == tile_count - 1

    def fine_pad(values):
        padded = with_halo(values, (("grid", 2),), 2)
        return fix_rims(padded, 2, cosine, sine, at_start, at_end)

    def plane_pad(values):
        padded = with_halo(values, (("grid", 2),), 1)
        return fix_rims(padded, 1, cosine, sine, at_start, at_end)

    fine_diagonal = 7.5 + screen
    iterate = omega * density / fine_diagonal
    iterate = iterate + omega * (density - fine_apply(iterate, fine_pad(iterate))) / fine_diagonal
    kept_pad = fine_pad(iterate)
    residual = density - fine_apply(iterate, kept_pad)
    first_source = restrict(residual)
    correction = relax(None, first_source, 1, plane_pad, SWEEPS)
    first_residual = first_source - coarse_apply(correction, plane_pad(correction), 1)
    deeper = group_cycle(first_residual, cosine, sine, position, tile_count)
    correction = correction + prolong_yz(deeper)
    correction = relax(correction, first_source, 1, plane_pad, SWEEPS)
    iterate = iterate + prolong(correction)
    remaining = SWEEPS
    for sweep_index in range(remaining):
        iterate = (
            iterate + omega * (density - fine_apply(iterate, fine_pad(iterate))) / fine_diagonal
        )
    return iterate


def solution(mesh):
    return jax.shard_map(
        per_device,
        mesh=mesh,
        in_specs=(
            P("rep", None, "grid", None, None),
            P(("rep", "grid"), None, None, None),
            P(("rep", "grid"), None, None),
            P(("rep", "grid")),
            P(("rep", "grid"), None),
            P(("rep", "grid")),
            P(),
            P(),
        ),
        out_specs=P("rep", None, "grid", None, None),
        check_vma=False,
    )
```

profile of v0, /device:TPU:0, one launch (start us, length us, event | category | flops | bytes accessed | tf_op | source)
XLA Modules:
  0.0 197.5 jit_solution(12631715992843563386)
XLA Ops:
  2.5 7.4 %all-to-all-start.1 = ((s32[16,1,8]{2,1,0:T(1,128)}), s32[16,1,8]{2,1,0:T(1,128)S(1)}, u32[]{:S(2)}, u32[]{:S(2)}) async-start(s32[16,1,8]{2,1,0:T(1,128)} %bitcast.8), calls=%async_computation.1 | async-start | bytes 16384 | tf_op jit(solution)/shard_map/all_to_all | solution.py:199
  11.8 2.0 %fusion = f32[64,4,256]{2,1,0:T(4,128)S(1)} fusion(f32[64,4,25]{2,1,0:T(4,128)S(1)} %copy.214, f32[64,25,256]{2,0,1:T(8,128)S(1)} %copy-done), kind=kOutput, calls=%fused_computation | convolution fusion | flops 19660800 | bytes 1926144 | tf_op jit(solution)/shard_map/sfl,slz->sfz/dot_general | solution.py:182
  13.8 1.2 fusion.5
  16.2 4.9 %all-to-all-start = ((f32[16,8,4,256]{3,1,2,0:T(8,128)}), f32[16,8,4,256]{3,1,2,0:T(8,128)S(1)}, u32[]{:S(2)}, u32[]{:S(2)}) async-start(f32[16,8,4,256]{3,1,2,0:T(8,128)} %fusion.5), calls=%async_computation | async-start | bytes 1048576 | tf_op jit(solution)/shard_map/all_to_all | solution.py:198
  22.8 12.8 %all-to-all-done = f32[16,8,4,256]{3,1,2,0:T(8,128)S(1)} async-done(((f32[16,8,4,256]{3,1,2,0:T(8,128)}), f32[16,8,4,256]{3,1,2,0:T(8,128)S(1)}, u32[]{:S(2)}, u32[]{:S(2)}) %all-to-all-start) | async-done | bytes 524320 | tf_op jit(solution)/shard_map/all_to_all | solution.py:198
  36.0 4.4 %collective-permute-start.1 = (f32[2,2,2,32,256]{4,3,2,1,0:T(8,128)S(1)}, f32[2,2,2,32,256]{4,3,2,1,0:T(8,128)S(1)}, u32[]{:S(2)}, u32[]{:S(2)}) collective-permute-start(f32[2,2,2,32,256]{4,3,2,1,0:T(8,128)S(1)} %get-tuple-element.13), channel_id=1, source_target_pairs={{1,0},{2,1},{3,2},{4,3},{5,4},{6,5},{7,6},{8,7},{9,8},{10,9},{11,1... | collective-permute-start | bytes 786440 | tf_op jit(solution)/shard_map/ppermute | solution.py:39
  41.0 3.5 %collective-permute-done = f32[2,2,2,32,256]{4,3,2,1,0:T(8,128)S(1)} collective-permute-done((f32[2,2,2,32,256]{4,3,2,1,0:T(8,128)S(1)}, f32[2,2,2,32,256]{4,3,2,1,0:T(8,128)S(1)}, u32[]{:S(2)}, u32[]{:S(2)}) %collective-permute-start) | collective-permute-done | bytes 262176 | tf_op jit(solution)/shard_map/ppermute | solution.py:36
  45.8 3.9 %collective-permute-start.3 = (f32[2,2,2,32,256]{4,3,2,1,0:T(8,128)S(1)}, f32[2,2,2,32,256]{4,3,2,1,0:T(8,128)S(1)}, u32[]{:S(2)}, u32[]{:S(2)}) collective-permute-start(f32[2,2,2,32,256]{4,3,2,1,0:T(8,128)S(1)} %fusion.48), channel_id=1, source_target_pairs={{1,0},{2,1},{3,2},{4,3},{5,4},{6,5},{7,6},{8,7},{9,8},{10,9},{11,1... | collective-permute-start | bytes 786440 | tf_op jit(solution)/shard_map/ppermute | solution.py:39
  50.4 3.5 %collective-permute-done.2 = f32[2,2,2,32,256]{4,3,2,1,0:T(8,128)S(1)} collective-permute-done((f32[2,2,2,32,256]{4,3,2,1,0:T(8,128)S(1)}, f32[2,2,2,32,256]{4,3,2,1,0:T(8,128)S(1)}, u32[]{:S(2)}, u32[]{:S(2)}) %collective-permute-start.2) | collective-permute-done | bytes 262176 | tf_op jit(solution)/shard_map/ppermute | solution.py:36
  54.6 18.1 %reshape.595 = f32[2,2,2,16,2,128,2]{6,5,4,3,2,1,0:T(8,128)} reshape(f32[2,2,2,32,256]{4,3,2,1,0:T(8,128)S(1)} %fusion.37) | data formatting | bytes 524288 | tf_op jit(solution)/shard_map/reshape | solution.py:91
  72.7 8.0 %reduce_sum.57 = f32[2,2,2,16,128]{4,3,2,1,0:T(8,128)S(1)} reduce(f32[2,2,2,16,2,128,2]{6,5,4,3,2,1,0:T(8,128)} %reshape.595, f32[]{:T(128)} %constant.90.clone.1), dimensions={4,6}, to_apply=%region_3.4 | reduce | flops 49152 | bytes 327684 | tf_op jit(solution)/shard_map/reduce_sum | solution.py:92
  81.4 3.9 %collective-permute-start.5 = (f32[2,2,1,16,128]{4,3,1,0,2:T(8,128)S(1)}, f32[2,2,1,16,128]{4,3,1,0,2:T(8,128)S(1)}, u32[]{:S(2)}, u32[]{:S(2)}) collective-permute-start(f32[2,2,1,16,128]{4,3,1,0,2:T(8,128)S(1)} %get-tuple-element.11), channel_id=1, source_target_pairs={{1,0},{2,1},{3,2},{4,3},{5,4},{6,5},{7,6},{8,7},{9,8},{10,9},{11,1... | collective-permute-start | bytes 98312 | tf_op jit(solution)/shard_map/ppermute | solution.py:39
  85.4 1.4 collective-permute-done.4
  87.1 4.7 %collective-permute-start.7 = (f32[2,2,1,16,128]{4,3,1,0,2:T(8,128)S(1)}, f32[2,2,1,16,128]{4,3,1,0,2:T(8,128)S(1)}, u32[]{:S(2)}, u32[]{:S(2)}) collective-permute-start(f32[2,2,1,16,128]{4,3,1,0,2:T(8,128)S(1)} %fusion.76), channel_id=1, source_target_pairs={{1,0},{2,1},{3,2},{4,3},{5,4},{6,5},{7,6},{8,7},{9,8},{10,9},{11,1... | collective-permute-start | bytes 98312 | tf_op jit(solution)/shard_map/ppermute | solution.py:39
  91.9 1.2 collective-permute-done.6
  93.5 3.4 %reshape.596 = f32[2,2,8,2,64,2]{5,4,3,2,1,0:T(8,128)} reshape(f32[2,2,1,16,128]{4,3,1,0,2:T(8,128)S(1)} %fusion.84) | data formatting | bytes 65536 | tf_op jit(solution)/shard_map/reshape | solution.py:91
  96.9 1.9 reduce_sum.58
  100.1 4.5 %collective-permute-start.10 = (f32[2,2,1,8,64]{4,3,1,0,2:T(8,128)S(1)}, f32[2,2,1,8,64]{4,3,1,0,2:T(8,128)S(1)}, u32[]{:S(2)}, u32[]{:S(2)}) collective-permute-start(f32[2,2,1,8,64]{4,3,1,0,2:T(8,128)S(1)} %get-tuple-element.9), channel_id=1, source_target_pairs={{2,0},{3,1},{4,2},{5,3},{6,4},{7,5},{8,6},{9,7},{10,8},{11,9},{12,... | collective-permute-start | bytes 24584 | tf_op jit(solution)/shard_map/ppermute | solution.py:21
  104.8 1.3 collective-permute-done.10
  106.0 5.0 %collective-permute-done.9 = f32[2,2,1,8,64]{4,3,1,0,2:T(8,128)S(1)} collective-permute-done((f32[2,2,1,8,64]{4,3,1,0,2:T(8,128)S(1)}, f32[2,2,1,8,64]{4,3,1,0,2:T(8,128)S(1)}, u32[]{:S(2)}, u32[]{:S(2)}) %collective-permute-start.9) | collective-permute-done | bytes 8224 | tf_op jit(solution)/shard_map/ppermute | solution.py:21
  111.2 4.7 %collective-permute-start.12 = (f32[2,2,1,8,64]{4,3,1,0,2:T(8,128)S(1)}, f32[2,2,1,8,64]{4,3,1,0,2:T(8,128)S(1)}, u32[]{:S(2)}, u32[]{:S(2)}) collective-permute-start(f32[2,2,1,8,64]{4,3,1,0,2:T(8,128)S(1)} %fusion.123), channel_id=1, source_target_pairs={{2,0},{3,1},{4,2},{5,3},{6,4},{7,5},{8,6},{9,7},{10,8},{11,9},{12,... | collective-permute-start | bytes 24584 | tf_op jit(solution)/shard_map/ppermute | solution.py:21
  116.1 1.6 collective-permute-done.11
  118.6 3.6 %collective-permute-done.13 = f32[2,2,1,4,32]{4,3,1,0,2:T(4,128)S(1)} collective-permute-done((f32[2,2,1,4,32]{4,3,1,0,2:T(4,128)S(1)}, f32[2,2,1,4,32]{4,3,1,0,2:T(4,128)S(1)}, u32[]{:S(2)}, u32[]{:S(2)}) %collective-permute-start.13) | collective-permute-done | bytes 2080 | tf_op jit(solution)/shard_map/ppermute | solution.py:27
  122.3 3.8 %collective-permute-start.15 = (f32[2,2,1,4,32]{4,3,1,0,2:T(4,128)S(1)}, f32[2,2,1,4,32]{4,3,1,0,2:T(4,128)S(1)}, u32[]{:S(2)}, u32[]{:S(2)}) collective-permute-start(f32[2,2,1,4,32]{4,3,1,0,2:T(4,128)S(1)} %get-tuple-element.7), channel_id=1, source_target_pairs={{4,0},{5,1},{6,2},{7,3},{8,4},{9,5},{10,6},{11,7},{12,8},{13,9},{1... | collective-permute-start | bytes 6152 | tf_op jit(solution)/shard_map/ppermute | solution.py:21
  126.2 1.5 collective-permute-done.14
  128.6 3.3 %collective-permute-start.17 = (f32[2,2,1,4,32]{4,3,1,0,2:T(4,128)S(1)}, f32[2,2,1,4,32]{4,3,1,0,2:T(4,128)S(1)}, u32[]{:S(2)}, u32[]{:S(2)}) collective-permute-start(f32[2,2,1,4,32]{4,3,1,0,2:T(4,128)S(1)} %multiply_add_fusion.23), channel_id=1, source_target_pairs={{4,0},{5,1},{6,2},{7,3},{8,4},{9,5},{10,6},{11,7},{12,8},{13,9},{1... | collective-permute-start | bytes 6152 | tf_op jit(solution)/shard_map/ppermute | solution.py:21
  132.0 1.4 collective-permute-done.16
  134.8 2.8 %collective-permute-start.19 = (f32[2,2,1,4,32]{4,3,1,0,2:T(4,128)S(1)}, f32[2,2,1,4,32]{4,3,1,0,2:T(4,128)S(1)}, u32[]{:S(2)}, u32[]{:S(2)}) collective-permute-start(f32[2,2,1,4,32]{4,3,1,0,2:T(4,128)S(1)} %multiply_add_fusion.22), channel_id=1, source_target_pairs={{4,0},{5,1},{6,2},{7,3},{8,4},{9,5},{10,6},{11,7},{12,8},{13,9},{1... | collective-permute-start | bytes 6152 | tf_op jit(solution)/shard_map/ppermute | solution.py:21
  137.7 1.4 collective-permute-done.18
  139.3 1.3 collective-permute-start.20
  140.7 2.7 %collective-permute-start.21 = (f32[2,2,1,4,32]{4,3,1,0,2:T(4,128)S(1)}, f32[2,2,1,4,32]{4,3,1,0,2:T(4,128)S(1)}, u32[]{:S(2)}, u32[]{:S(2)}) collective-permute-start(f32[2,2,1,4,32]{4,3,1,0,2:T(4,128)S(1)} %multiply_add_fusion.21), channel_id=1, source_target_pairs={{4,0},{5,1},{6,2},{7,3},{8,4},{9,5},{10,6},{11,7},{12,8},{13,9},{1... | collective-permute-start | bytes 6152 | tf_op jit(solution)/shard_map/ppermute | solution.py:21
  143.5 1.4 collective-permute-done.20
  145.1 1.3 collective-permute-start.22
  146.4 2.7 %collective-permute-start.23 = (f32[2,2,1,4,32]{4,3,1,0,2:T(4,128)S(1)}, f32[2,2,1,4,32]{4,3,1,0,2:T(4,128)S(1)}, u32[]{:S(2)}, u32[]{:S(2)}) collective-permute-start(f32[2,2,1,4,32]{4,3,1,0,2:T(4,128)S(1)} %multiply_add_fusion.20), channel_id=1, source_target_pairs={{4,0},{5,1},{6,2},{7,3},{8,4},{9,5},{10,6},{11,7},{12,8},{13,9},{1... | collective-permute-start | bytes 6152 | tf_op jit(solution)/shard_map/ppermute | solution.py:21
  149.3 1.4 collective-permute-done.22
  151.1 1.5 collective-permute-start.24
  152.6 3.4 %collective-permute-start.25 = (f32[2,2,1,8,64]{4,3,1,0,2:T(8,128)S(1)}, f32[2,2,1,8,64]{4,3,1,0,2:T(8,128)S(1)}, u32[]{:S(2)}, u32[]{:S(2)}) collective-permute-start(f32[2,2,1,8,64]{4,3,1,0,2:T(8,128)S(1)} %add.733), channel_id=1, source_target_pairs={{2,0},{3,1},{4,2},{5,3},{6,4},{7,5},{8,6},{9,7},{10,8},{11,9},{12,... | collective-permute-start | bytes 24584 | tf_op jit(solution)/shard_map/ppermute | solution.py:21
  156.2 1.5 collective-permute-done.24
  158.7 4.0 %collective-permute-start.27 = (f32[2,2,1,8,64]{4,3,1,0,2:T(8,128)S(1)}, f32[2,2,1,8,64]{4,3,1,0,2:T(8,128)S(1)}, u32[]{:S(2)}, u32[]{:S(2)}) collective-permute-start(f32[2,2,1,8,64]{4,3,1,0,2:T(8,128)S(1)} %fusion.141), channel_id=1, source_target_pairs={{2,0},{3,1},{4,2},{5,3},{6,4},{7,5},{8,6},{9,7},{10,8},{11,9},{12,... | collective-permute-start | bytes 24584 | tf_op jit(solution)/shard_map/ppermute | solution.py:21
  162.9 1.5 collective-permute-done.26
  164.9 4.4 %collective-permute-start.29 = (f32[2,2,1,16,128]{4,3,1,0,2:T(8,128)S(1)}, f32[2,2,1,16,128]{4,3,1,0,2:T(8,128)S(1)}, u32[]{:S(2)}, u32[]{:S(2)}) collective-permute-start(f32[2,2,1,16,128]{4,3,1,0,2:T(8,128)S(1)} %add.751), channel_id=1, source_target_pairs={{1,0},{2,1},{3,2},{4,3},{5,4},{6,5},{7,6},{8,7},{9,8},{10,9},{11,1... | collective-permute-start | bytes 98312 | tf_op jit(solution)/shard_map/ppermute | solution.py:39
  169.5 1.4 collective-permute-done.28
  171.2 4.5 %collective-permute-start.31 = (f32[2,2,1,16,128]{4,3,1,0,2:T(8,128)S(1)}, f32[2,2,1,16,128]{4,3,1,0,2:T(8,128)S(1)}, u32[]{:S(2)}, u32[]{:S(2)}) collective-permute-start(f32[2,2,1,16,128]{4,3,1,0,2:T(8,128)S(1)} %fusion.94), channel_id=1, source_target_pairs={{1,0},{2,1},{3,2},{4,3},{5,4},{6,5},{7,6},{8,7},{9,8},{10,9},{11,1... | collective-permute-start | bytes 98312 | tf_op jit(solution)/shard_map/ppermute | solution.py:39
  175.9 1.4 collective-permute-done.30
  178.1 4.6 %collective-permute-start.33 = (f32[2,2,2,32,256]{4,3,2,1,0:T(8,128)S(1)}, f32[2,2,2,32,256]{4,3,2,1,0:T(8,128)S(1)}, u32[]{:S(2)}, u32[]{:S(2)}) collective-permute-start(f32[2,2,2,32,256]{4,3,2,1,0:T(8,128)S(1)} %broadcast_add_fusion), channel_id=1, source_target_pairs={{1,0},{2,1},{3,2},{4,3},{5,4},{6,5},{7,6},{8,7},{9,8},{10,9},{11,1... | collective-permute-start | bytes 786440 | tf_op jit(solution)/shard_map/ppermute | solution.py:39
  183.3 3.5 %collective-permute-done.32 = f32[2,2,2,32,256]{4,3,2,1,0:T(8,128)S(1)} collective-permute-done((f32[2,2,2,32,256]{4,3,2,1,0:T(8,128)S(1)}, f32[2,2,2,32,256]{4,3,2,1,0:T(8,128)S(1)}, u32[]{:S(2)}, u32[]{:S(2)}) %collective-permute-start.32) | collective-permute-done | bytes 262176 | tf_op jit(solution)/shard_map/ppermute | solution.py:36
  187.5 4.6 %collective-permute-start.35 = (f32[2,2,2,32,256]{4,3,2,1,0:T(8,128)S(1)}, f32[2,2,2,32,256]{4,3,2,1,0:T(8,128)S(1)}, u32[]{:S(2)}, u32[]{:S(2)}) collective-permute-start(f32[2,2,2,32,256]{4,3,2,1,0:T(8,128)S(1)} %fusion.28), channel_id=1, source_target_pairs={{1,0},{2,1},{3,2},{4,3},{5,4},{6,5},{7,6},{8,7},{9,8},{10,9},{11,1... | collective-permute-start | bytes 786440 | tf_op jit(solution)/shard_map/ppermute | solution.py:39
  192.7 3.4 %collective-permute-done.34 = f32[2,2,2,32,256]{4,3,2,1,0:T(8,128)S(1)} collective-permute-done((f32[2,2,2,32,256]{4,3,2,1,0:T(8,128)S(1)}, f32[2,2,2,32,256]{4,3,2,1,0:T(8,128)S(1)}, u32[]{:S(2)}, u32[]{:S(2)}) %collective-permute-start.34) | collective-permute-done | bytes 262176 | tf_op jit(solution)/shard_map/ppermute | solution.py:36
  (209 shorter events, 25.1 us)
Async XLA Ops:
  0.0 11.8 %copy-start = (f32[64,25,256]{2,0,1:T(8,128)S(1)}, f32[64,25,256]{2,0,1:T(8,128)}, u32[]{:S(2)}) copy-start(f32[64,25,256]{2,0,1:T(8,128)} %param.10) | copy-start | bytes 4915204
  2.5 13.7 %all-to-all-start.1 = ((s32[16,1,8]{2,1,0:T(1,128)}), s32[16,1,8]{2,1,0:T(1,128)S(1)}, u32[]{:S(2)}, u32[]{:S(2)}) async-start(s32[16,1,8]{2,1,0:T(1,128)} %bitcast.8), calls=%async_computation.1 | async-start | bytes 16384 | tf_op jit(solution)/shard_map/all_to_all | solution.py:199
  11.8 9.3 %copy-start.2 = (s32[2,2]{1,0:T(2,128)S(1)}, s32[2,2]{1,0:T(2,128)}, u32[]{:S(2)}) copy-start(s32[2,2]{1,0:T(2,128)} %param.14) | copy-start | bytes 52
  11.8 9.3 %copy-start.3 = (f32[8]{0:T(128)S(1)}, f32[8]{0:T(128)}, u32[]{:S(2)}) copy-start(f32[8]{0:T(128)} %param.15) | copy-start | bytes 100
  11.8 24.0 %copy-start.1 = (f32[2,2,2,32,256]{4,3,2,1,0:T(8,128)S(1)}, f32[2,2,2,32,256]{4,3,2,1,0:T(8,128)}, u32[]{:S(2)}) copy-start(f32[2,2,2,32,256]{4,3,2,1,0:T(8,128)} %param.8) | copy-start | bytes 786436
  16.2 19.4 %all-to-all-start = ((f32[16,8,4,256]{3,1,2,0:T(8,128)}), f32[16,8,4,256]{3,1,2,0:T(8,128)S(1)}, u32[]{:S(2)}, u32[]{:S(2)}) async-start(f32[16,8,4,256]{3,1,2,0:T(8,128)} %fusion.5), calls=%async_computation | async-start | bytes 1048576 | tf_op jit(solution)/shard_map/all_to_all | solution.py:198
  35.9 8.7 %collective-permute-start = (f32[2,2,2,32,256]{4,3,2,1,0:T(8,128)S(1)}, f32[2,2,2,32,256]{4,3,2,1,0:T(8,128)S(1)}, u32[]{:S(2)}, u32[]{:S(2)}) collective-permute-start(f32[2,2,2,32,256]{4,3,2,1,0:T(8,128)S(1)} %get-tuple-element.13), channel_id=1, source_target_pairs={{0,1},{1,2},{2,3},{3,4},{4,5},{5,6},{6,7},{7,8},{8,9},{9,10},{10,1... | collective-permute-start | bytes 786440 | tf_op jit(solution)/shard_map/ppermute | solution.py:36
  36.0 8.6 %collective-permute-start.1 = (f32[2,2,2,32,256]{4,3,2,1,0:T(8,128)S(1)}, f32[2,2,2,32,256]{4,3,2,1,0:T(8,128)S(1)}, u32[]{:S(2)}, u32[]{:S(2)}) collective-permute-start(f32[2,2,2,32,256]{4,3,2,1,0:T(8,128)S(1)} %get-tuple-element.13), channel_id=1, source_target_pairs={{1,0},{2,1},{3,2},{4,3},{5,4},{6,5},{7,6},{8,7},{9,8},{10,9},{11,1... | collective-permute-start | bytes 786440 | tf_op jit(solution)/shard_map/ppermute | solution.py:39
  45.2 8.7 %collective-permute-start.2 = (f32[2,2,2,32,256]{4,3,2,1,0:T(8,128)S(1)}, f32[2,2,2,32,256]{4,3,2,1,0:T(8,128)S(1)}, u32[]{:S(2)}, u32[]{:S(2)}) collective-permute-start(f32[2,2,2,32,256]{4,3,2,1,0:T(8,128)S(1)} %fusion.48), channel_id=1, source_target_pairs={{0,1},{1,2},{2,3},{3,4},{4,5},{5,6},{6,7},{7,8},{8,9},{9,10},{10,1... | collective-permute-start | bytes 786440 | tf_op jit(solution)/shard_map/ppermute | solution.py:36
  45.8 8.1 %collective-permute-start.3 = (f32[2,2,2,32,256]{4,3,2,1,0:T(8,128)S(1)}, f32[2,2,2,32,256]{4,3,2,1,0:T(8,128)S(1)}, u32[]{:S(2)}, u32[]{:S(2)}) collective-permute-start(f32[2,2,2,32,256]{4,3,2,1,0:T(8,128)S(1)} %fusion.48), channel_id=1, source_target_pairs={{1,0},{2,1},{3,2},{4,3},{5,4},{6,5},{7,6},{8,7},{9,8},{10,9},{11,1... | collective-permute-start | bytes 786440 | tf_op jit(solution)/shard_map/ppermute | solution.py:39
  80.7 6.1 %collective-permute-start.4 = (f32[2,2,1,16,128]{4,3,1,0,2:T(8,128)S(1)}, f32[2,2,1,16,128]{4,3,1,0,2:T(8,128)S(1)}, u32[]{:S(2)}, u32[]{:S(2)}) collective-permute-start(f32[2,2,1,16,128]{4,3,1,0,2:T(8,128)S(1)} %get-tuple-element.11), channel_id=1, source_target_pairs={{0,1},{1,2},{2,3},{3,4},{4,5},{5,6},{6,7},{7,8},{8,9},{9,10},{10,1... | collective-permute-start | bytes 98312 | tf_op jit(solution)/shard_map/ppermute | solution.py:36
  81.4 5.5 %collective-permute-start.5 = (f32[2,2,1,16,128]{4,3,1,0,2:T(8,128)S(1)}, f32[2,2,1,16,128]{4,3,1,0,2:T(8,128)S(1)}, u32[]{:S(2)}, u32[]{:S(2)}) collective-permute-start(f32[2,2,1,16,128]{4,3,1,0,2:T(8,128)S(1)} %get-tuple-element.11), channel_id=1, source_target_pairs={{1,0},{2,1},{3,2},{4,3},{5,4},{6,5},{7,6},{8,7},{9,8},{10,9},{11,1... | collective-permute-start | bytes 98312 | tf_op jit(solution)/shard_map/ppermute | solution.py:39
  87.0 6.1 %collective-permute-start.6 = (f32[2,2,1,16,128]{4,3,1,0,2:T(8,128)S(1)}, f32[2,2,1,16,128]{4,3,1,0,2:T(8,128)S(1)}, u32[]{:S(2)}, u32[]{:S(2)}) collective-permute-start(f32[2,2,1,16,128]{4,3,1,0,2:T(8,128)S(1)} %fusion.76), channel_id=1, source_target_pairs={{0,1},{1,2},{2,3},{3,4},{4,5},{5,6},{6,7},{7,8},{8,9},{9,10},{10,1... | collective-permute-start | bytes 98312 | tf_op jit(solution)/shard_map/ppermute | solution.py:36
  87.1 6.3 %collective-permute-start.7 = (f32[2,2,1,16,128]{4,3,1,0,2:T(8,128)S(1)}, f32[2,2,1,16,128]{4,3,1,0,2:T(8,128)S(1)}, u32[]{:S(2)}, u32[]{:S(2)}) collective-permute-start(f32[2,2,1,16,128]{4,3,1,0,2:T(8,128)S(1)} %fusion.76), channel_id=1, source_target_pairs={{1,0},{2,1},{3,2},{4,3},{5,4},{6,5},{7,6},{8,7},{9,8},{10,9},{11,1... | collective-permute-start | bytes 98312 | tf_op jit(solution)/shard_map/ppermute | solution.py:39
  98.8 1.2 collective-permute-start.8
  100.1 5.9 %collective-permute-start.10 = (f32[2,2,1,8,64]{4,3,1,0,2:T(8,128)S(1)}, f32[2,2,1,8,64]{4,3,1,0,2:T(8,128)S(1)}, u32[]{:S(2)}, u32[]{:S(2)}) collective-permute-start(f32[2,2,1,8,64]{4,3,1,0,2:T(8,128)S(1)} %get-tuple-element.9), channel_id=1, source_target_pairs={{2,0},{3,1},{4,2},{5,3},{6,4},{7,5},{8,6},{9,7},{10,8},{11,9},{12,... | collective-permute-start | bytes 24584 | tf_op jit(solution)/shard_map/ppermute | solution.py:21
  104.6 6.4 %collective-permute-start.9 = (f32[2,2,1,8,64]{4,3,1,0,2:T(8,128)S(1)}, f32[2,2,1,8,64]{4,3,1,0,2:T(8,128)S(1)}, u32[]{:S(2)}, u32[]{:S(2)}) collective-permute-start(f32[2,2,1,8,64]{4,3,1,0,2:T(8,128)S(1)} %get-tuple-element.9), channel_id=1, source_target_pairs={{14,0},{15,1},{0,2},{1,3},{2,4},{3,5},{4,6},{5,7},{6,8},{7,9},{8,1... | collective-permute-start | bytes 24584 | tf_op jit(solution)/shard_map/ppermute | solution.py:21
  111.2 6.5 %collective-permute-start.11 = (f32[2,2,1,8,64]{4,3,1,0,2:T(8,128)S(1)}, f32[2,2,1,8,64]{4,3,1,0,2:T(8,128)S(1)}, u32[]{:S(2)}, u32[]{:S(2)}) collective-permute-start(f32[2,2,1,8,64]{4,3,1,0,2:T(8,128)S(1)} %fusion.123), channel_id=1, source_target_pairs={{14,0},{15,1},{0,2},{1,3},{2,4},{3,5},{4,6},{5,7},{6,8},{7,9},{8,1... | collective-permute-start | bytes 24584 | tf_op jit(solution)/shard_map/ppermute | solution.py:21
  111.2 6.4 %collective-permute-start.12 = (f32[2,2,1,8,64]{4,3,1,0,2:T(8,128)S(1)}, f32[2,2,1,8,64]{4,3,1,0,2:T(8,128)S(1)}, u32[]{:S(2)}, u32[]{:S(2)}) collective-permute-start(f32[2,2,1,8,64]{4,3,1,0,2:T(8,128)S(1)} %fusion.123), channel_id=1, source_target_pairs={{2,0},{3,1},{4,2},{5,3},{6,4},{7,5},{8,6},{9,7},{10,8},{11,9},{12,... | collective-permute-start | bytes 24584 | tf_op jit(solution)/shard_map/ppermute | solution.py:21
  118.5 3.7 %collective-permute-start.13 = (f32[2,2,1,4,32]{4,3,1,0,2:T(4,128)S(1)}, f32[2,2,1,4,32]{4,3,1,0,2:T(4,128)S(1)}, u32[]{:S(2)}, u32[]{:S(2)}) collective-permute-start(f32[2,2,1,4,32]{4,3,1,0,2:T(4,128)S(1)} %multiply_bitcast_fusion.2), channel_id=1, source_target_pairs={{0,2},{1,3},{2,0},{3,1},{4,6},{5,7},{6,4},{7,5},{8,10},{9,11},{10,... | collective-permute-start | bytes 6152 | tf_op jit(solution)/shard_map/ppermute | solution.py:27
  122.3 5.5 %collective-permute-start.14 = (f32[2,2,1,4,32]{4,3,1,0,2:T(4,128)S(1)}, f32[2,2,1,4,32]{4,3,1,0,2:T(4,128)S(1)}, u32[]{:S(2)}, u32[]{:S(2)}) collective-permute-start(f32[2,2,1,4,32]{4,3,1,0,2:T(4,128)S(1)} %get-tuple-element.7), channel_id=1, source_target_pairs={{12,0},{13,1},{14,2},{15,3},{0,4},{1,5},{2,6},{3,7},{4,8},{5,9},{6... | collective-permute-start | bytes 6152 | tf_op jit(solution)/shard_map/ppermute | solution.py:21
  122.3 5.4 %collective-permute-start.15 = (f32[2,2,1,4,32]{4,3,1,0,2:T(4,128)S(1)}, f32[2,2,1,4,32]{4,3,1,0,2:T(4,128)S(1)}, u32[]{:S(2)}, u32[]{:S(2)}) collective-permute-start(f32[2,2,1,4,32]{4,3,1,0,2:T(4,128)S(1)} %get-tuple-element.7), channel_id=1, source_target_pairs={{4,0},{5,1},{6,2},{7,3},{8,4},{9,5},{10,6},{11,7},{12,8},{13,9},{1... | collective-permute-start | bytes 6152 | tf_op jit(solution)/shard_map/ppermute | solution.py:21
  127.9 5.5 %collective-permute-start.16 = (f32[2,2,1,4,32]{4,3,1,0,2:T(4,128)S(1)}, f32[2,2,1,4,32]{4,3,1,0,2:T(4,128)S(1)}, u32[]{:S(2)}, u32[]{:S(2)}) collective-permute-start(f32[2,2,1,4,32]{4,3,1,0,2:T(4,128)S(1)} %multiply_add_fusion.23), channel_id=1, source_target_pairs={{12,0},{13,1},{14,2},{15,3},{0,4},{1,5},{2,6},{3,7},{4,8},{5,9},{6... | collective-permute-start | bytes 6152 | tf_op jit(solution)/shard_map/ppermute | solution.py:21
  128.6 4.8 %collective-permute-start.17 = (f32[2,2,1,4,32]{4,3,1,0,2:T(4,128)S(1)}, f32[2,2,1,4,32]{4,3,1,0,2:T(4,128)S(1)}, u32[]{:S(2)}, u32[]{:S(2)}) collective-permute-start(f32[2,2,1,4,32]{4,3,1,0,2:T(4,128)S(1)} %multiply_add_fusion.23), channel_id=1, source_target_pairs={{4,0},{5,1},{6,2},{7,3},{8,4},{9,5},{10,6},{11,7},{12,8},{13,9},{1... | collective-permute-start | bytes 6152 | tf_op jit(solution)/shard_map/ppermute | solution.py:21
  133.6 5.6 %collective-permute-start.18 = (f32[2,2,1,4,32]{4,3,1,0,2:T(4,128)S(1)}, f32[2,2,1,4,32]{4,3,1,0,2:T(4,128)S(1)}, u32[]{:S(2)}, u32[]{:S(2)}) collective-permute-start(f32[2,2,1,4,32]{4,3,1,0,2:T(4,128)S(1)} %multiply_add_fusion.22), channel_id=1, source_target_pairs={{12,0},{13,1},{14,2},{15,3},{0,4},{1,5},{2,6},{3,7},{4,8},{5,9},{6... | collective-permute-start | bytes 6152 | tf_op jit(solution)/shard_map/ppermute | solution.py:21
  134.8 4.4 %collective-permute-start.19 = (f32[2,2,1,4,32]{4,3,1,0,2:T(4,128)S(1)}, f32[2,2,1,4,32]{4,3,1,0,2:T(4,128)S(1)}, u32[]{:S(2)}, u32[]{:S(2)}) collective-permute-start(f32[2,2,1,4,32]{4,3,1,0,2:T(4,128)S(1)} %multiply_add_fusion.22), channel_id=1, source_target_pairs={{4,0},{5,1},{6,2},{7,3},{8,4},{9,5},{10,6},{11,7},{12,8},{13,9},{1... | collective-permute-start | bytes 6152 | tf_op jit(solution)/shard_map/ppermute | solution.py:21
  139.3 5.6 %collective-permute-start.20 = (f32[2,2,1,4,32]{4,3,1,0,2:T(4,128)S(1)}, f32[2,2,1,4,32]{4,3,1,0,2:T(4,128)S(1)}, u32[]{:S(2)}, u32[]{:S(2)}) collective-permute-start(f32[2,2,1,4,32]{4,3,1,0,2:T(4,128)S(1)} %multiply_add_fusion.21), channel_id=1, source_target_pairs={{12,0},{13,1},{14,2},{15,3},{0,4},{1,5},{2,6},{3,7},{4,8},{5,9},{6... | collective-permute-start | bytes 6152 | tf_op jit(solution)/shard_map/ppermute | solution.py:21
  140.7 4.3 %collective-permute-start.21 = (f32[2,2,1,4,32]{4,3,1,0,2:T(4,128)S(1)}, f32[2,2,1,4,32]{4,3,1,0,2:T(4,128)S(1)}, u32[]{:S(2)}, u32[]{:S(2)}) collective-permute-start(f32[2,2,1,4,32]{4,3,1,0,2:T(4,128)S(1)} %multiply_add_fusion.21), channel_id=1, source_target_pairs={{4,0},{5,1},{6,2},{7,3},{8,4},{9,5},{10,6},{11,7},{12,8},{13,9},{1... | collective-permute-start | bytes 6152 | tf_op jit(solution)/shard_map/ppermute | solution.py:21
  145.1 5.6 %collective-permute-start.22 = (f32[2,2,1,4,32]{4,3,1,0,2:T(4,128)S(1)}, f32[2,2,1,4,32]{4,3,1,0,2:T(4,128)S(1)}, u32[]{:S(2)}, u32[]{:S(2)}) collective-permute-start(f32[2,2,1,4,32]{4,3,1,0,2:T(4,128)S(1)} %multiply_add_fusion.20), channel_id=1, source_target_pairs={{12,0},{13,1},{14,2},{15,3},{0,4},{1,5},{2,6},{3,7},{4,8},{5,9},{6... | collective-permute-start | bytes 6152 | tf_op jit(solution)/shard_map/ppermute | solution.py:21
  146.4 4.3 %collective-permute-start.23 = (f32[2,2,1,4,32]{4,3,1,0,2:T(4,128)S(1)}, f32[2,2,1,4,32]{4,3,1,0,2:T(4,128)S(1)}, u32[]{:S(2)}, u32[]{:S(2)}) collective-permute-start(f32[2,2,1,4,32]{4,3,1,0,2:T(4,128)S(1)} %multiply_add_fusion.20), channel_id=1, source_target_pairs={{4,0},{5,1},{6,2},{7,3},{8,4},{9,5},{10,6},{11,7},{12,8},{13,9},{1... | collective-permute-start | bytes 6152 | tf_op jit(solution)/shard_map/ppermute | solution.py:21
  151.1 6.6 %collective-permute-start.24 = (f32[2,2,1,8,64]{4,3,1,0,2:T(8,128)S(1)}, f32[2,2,1,8,64]{4,3,1,0,2:T(8,128)S(1)}, u32[]{:S(2)}, u32[]{:S(2)}) collective-permute-start(f32[2,2,1,8,64]{4,3,1,0,2:T(8,128)S(1)} %add.733), channel_id=1, source_target_pairs={{14,0},{15,1},{0,2},{1,3},{2,4},{3,5},{4,6},{5,7},{6,8},{7,9},{8,1... | collective-permute-start | bytes 24584 | tf_op jit(solution)/shard_map/ppermute | solution.py:21
  152.6 5.0 %collective-permute-start.25 = (f32[2,2,1,8,64]{4,3,1,0,2:T(8,128)S(1)}, f32[2,2,1,8,64]{4,3,1,0,2:T(8,128)S(1)}, u32[]{:S(2)}, u32[]{:S(2)}) collective-permute-start(f32[2,2,1,8,64]{4,3,1,0,2:T(8,128)S(1)} %add.733), channel_id=1, source_target_pairs={{2,0},{3,1},{4,2},{5,3},{6,4},{7,5},{8,6},{9,7},{10,8},{11,9},{12,... | collective-permute-start | bytes 24584 | tf_op jit(solution)/shard_map/ppermute | solution.py:21
  157.8 6.5 %collective-permute-start.26 = (f32[2,2,1,8,64]{4,3,1,0,2:T(8,128)S(1)}, f32[2,2,1,8,64]{4,3,1,0,2:T(8,128)S(1)}, u32[]{:S(2)}, u32[]{:S(2)}) collective-permute-start(f32[2,2,1,8,64]{4,3,1,0,2:T(8,128)S(1)} %fusion.141), channel_id=1, source_target_pairs={{14,0},{15,1},{0,2},{1,3},{2,4},{3,5},{4,6},{5,7},{6,8},{7,9},{8,1... | collective-permute-start | bytes 24584 | tf_op jit(solution)/shard_map/ppermute | solution.py:21
  158.7 5.7 %collective-permute-start.27 = (f32[2,2,1,8,64]{4,3,1,0,2:T(8,128)S(1)}, f32[2,2,1,8,64]{4,3,1,0,2:T(8,128)S(1)}, u32[]{:S(2)}, u32[]{:S(2)}) collective-permute-start(f32[2,2,1,8,64]{4,3,1,0,2:T(8,128)S(1)} %fusion.141), channel_id=1, source_target_pairs={{2,0},{3,1},{4,2},{5,3},{6,4},{7,5},{8,6},{9,7},{10,8},{11,9},{12,... | collective-permute-start | bytes 24584 | tf_op jit(solution)/shard_map/ppermute | solution.py:21
  164.9 6.1 %collective-permute-start.28 = (f32[2,2,1,16,128]{4,3,1,0,2:T(8,128)S(1)}, f32[2,2,1,16,128]{4,3,1,0,2:T(8,128)S(1)}, u32[]{:S(2)}, u32[]{:S(2)}) collective-permute-start(f32[2,2,1,16,128]{4,3,1,0,2:T(8,128)S(1)} %add.751), channel_id=1, source_target_pairs={{0,1},{1,2},{2,3},{3,4},{4,5},{5,6},{6,7},{7,8},{8,9},{9,10},{10,1... | collective-permute-start | bytes 98312 | tf_op jit(solution)/shard_map/ppermute | solution.py:36
  164.9 6.0 %collective-permute-start.29 = (f32[2,2,1,16,128]{4,3,1,0,2:T(8,128)S(1)}, f32[2,2,1,16,128]{4,3,1,0,2:T(8,128)S(1)}, u32[]{:S(2)}, u32[]{:S(2)}) collective-permute-start(f32[2,2,1,16,128]{4,3,1,0,2:T(8,128)S(1)} %add.751), channel_id=1, source_target_pairs={{1,0},{2,1},{3,2},{4,3},{5,4},{6,5},{7,6},{8,7},{9,8},{10,9},{11,1... | collective-permute-start | bytes 98312 | tf_op jit(solution)/shard_map/ppermute | solution.py:39
  171.1 6.1 %collective-permute-start.30 = (f32[2,2,1,16,128]{4,3,1,0,2:T(8,128)S(1)}, f32[2,2,1,16,128]{4,3,1,0,2:T(8,128)S(1)}, u32[]{:S(2)}, u32[]{:S(2)}) collective-permute-start(f32[2,2,1,16,128]{4,3,1,0,2:T(8,128)S(1)} %fusion.94), channel_id=1, source_target_pairs={{0,1},{1,2},{2,3},{3,4},{4,5},{5,6},{6,7},{7,8},{8,9},{9,10},{10,1... | collective-permute-start | bytes 98312 | tf_op jit(solution)/shard_map/ppermute | solution.py:36
  171.2 6.1 %collective-permute-start.31 = (f32[2,2,1,16,128]{4,3,1,0,2:T(8,128)S(1)}, f32[2,2,1,16,128]{4,3,1,0,2:T(8,128)S(1)}, u32[]{:S(2)}, u32[]{:S(2)}) collective-permute-start(f32[2,2,1,16,128]{4,3,1,0,2:T(8,128)S(1)} %fusion.94), channel_id=1, source_target_pairs={{1,0},{2,1},{3,2},{4,3},{5,4},{6,5},{7,6},{8,7},{9,8},{10,9},{11,1... | collective-permute-start | bytes 98312 | tf_op jit(solution)/shard_map/ppermute | solution.py:39
  178.0 8.8 %collective-permute-start.32 = (f32[2,2,2,32,256]{4,3,2,1,0:T(8,128)S(1)}, f32[2,2,2,32,256]{4,3,2,1,0:T(8,128)S(1)}, u32[]{:S(2)}, u32[]{:S(2)}) collective-permute-start(f32[2,2,2,32,256]{4,3,2,1,0:T(8,128)S(1)} %broadcast_add_fusion), channel_id=1, source_target_pairs={{0,1},{1,2},{2,3},{3,4},{4,5},{5,6},{6,7},{7,8},{8,9},{9,10},{10,1... | collective-permute-start | bytes 786440 | tf_op jit(solution)/shard_map/ppermute | solution.py:36
  178.1 8.7 %collective-permute-start.33 = (f32[2,2,2,32,256]{4,3,2,1,0:T(8,128)S(1)}, f32[2,2,2,32,256]{4,3,2,1,0:T(8,128)S(1)}, u32[]{:S(2)}, u32[]{:S(2)}) collective-permute-start(f32[2,2,2,32,256]{4,3,2,1,0:T(8,128)S(1)} %broadcast_add_fusion), channel_id=1, source_target_pairs={{1,0},{2,1},{3,2},{4,3},{5,4},{6,5},{7,6},{8,7},{9,8},{10,9},{11,1... | collective-permute-start | bytes 786440 | tf_op jit(solution)/shard_map/ppermute | solution.py:39
  187.5 8.6 %collective-permute-start.34 = (f32[2,2,2,32,256]{4,3,2,1,0:T(8,128)S(1)}, f32[2,2,2,32,256]{4,3,2,1,0:T(8,128)S(1)}, u32[]{:S(2)}, u32[]{:S(2)}) collective-permute-start(f32[2,2,2,32,256]{4,3,2,1,0:T(8,128)S(1)} %fusion.28), channel_id=1, source_target_pairs={{0,1},{1,2},{2,3},{3,4},{4,5},{5,6},{6,7},{7,8},{8,9},{9,10},{10,1... | collective-permute-start | bytes 786440 | tf_op jit(solution)/shard_map/ppermute | solution.py:36
  187.5 8.5 %collective-permute-start.35 = (f32[2,2,2,32,256]{4,3,2,1,0:T(8,128)S(1)}, f32[2,2,2,32,256]{4,3,2,1,0:T(8,128)S(1)}, u32[]{:S(2)}, u32[]{:S(2)}) collective-permute-start(f32[2,2,2,32,256]{4,3,2,1,0:T(8,128)S(1)} %fusion.28), channel_id=1, source_target_pairs={{1,0},{2,1},{3,2},{4,3},{5,4},{6,5},{7,6},{8,7},{9,8},{10,9},{11,1... | collective-permute-start | bytes 786440 | tf_op jit(solution)/shard_map/ppermute | solution.py:39
where the time goes:
time: 198 us; the launch traced here: 197 us
  starting transfers between devices  87.8 us (44%)
  waiting for transfers between devices  56.2 us (28%)
  local copies, waits for them, and re-layouts  29.7 us (15%)
  other arithmetic  18.5 us (9%)
  matrix products  4.43 us (2%)
    ppermute x18, starting transfers between devices, from_behind(): return lax.ppermute(block, axis, route)  38.9 us
    ppermute x8, starting transfers between devices, with_halo(): lax.ppermute(lax.slice_in_dim(block, 0, width, axis=dim), axis, backward)  35 us
    reshape x3, local copies, waits for them, and re-layouts, restrict_yz(): values.reshape(sizes[0], sizes[1], sizes[2], sizes[3] // 2, 2, sizes[4] /...  22 us
    ppermute x8, waiting for transfers between devices, with_halo(): lax.ppermute(lax.slice_in_dim(block, block.shape[dim] - width, None, axis...  19.3 us
    ppermute x18, waiting for transfers between devices, from_behind(): return lax.ppermute(block, axis, route)  17.9 us
    all_to_all x1, waiting for transfers between devices, compensation(): lax.all_to_all(packed, 'grid', split_axis=0, concat_axis=0, tiled=True)  12.8 us
    reduce_sum x3, other arithmetic, restrict_yz(): return blocks.mean(axis=(4, 6))  10.1 us
    all_to_all x1, starting transfers between devices, compensation(): lax.all_to_all(targets, 'grid', split_axis=0, concat_axis=0, tiled=True)  7.36 us
  transfers between devices with their start and end apart: 38, of which 24 were waited for; matrix products, arithmetic and copies ran while one was open for 6% of the time, Pallas kernels for 0%

commit v1 on v0

v1 whole, which is shorter than its diff:
```python
import jax
import jax.numpy as jnp
from jax import lax
from jax.experimental import pallas as pl
from jax.experimental.pallas import tpu as pltpu
from jax.sharding import PartitionSpec as P

omega = 0.8
screen = 0.05
highest = lax.Precision.HIGHEST

fine_diagonal = 7.5 + screen
fine_scale = omega / fine_diagonal
fine_near = fine_scale * 4.0 / 3.0
fine_far = fine_scale / 12.0
keep = 1.0 - omega


def level_numbers(depth):
    quarter = 1.0 / 4**depth
    diagonal = 6.0 * quarter + screen
    return omega / diagonal, omega / diagonal * quarter


def each(count, body, most=16):
    if count <= most:
        for i in range(count):
            body(i)
    else:
        pl.loop(0, count, unroll=4)(body)


def dot(a, b):
    return jnp.dot(a, b, precision=highest, preferred_element_type=jnp.float32)


def pair_matrix(rows, columns, value):
    i = lax.broadcasted_iota(jnp.int32, (rows, columns), 0)
    j = lax.broadcasted_iota(jnp.int32, (rows, columns), 1)
    return jnp.where(i // 2 == j, value, 0.0)


def spread_matrix(rows, columns):
    i = lax.broadcasted_iota(jnp.int32, (rows, columns), 0)
    j = lax.broadcasted_iota(jnp.int32, (rows, columns), 1)
    return jnp.where(i == j // 2, 1.0, 0.0)


def roll(v, shift, axis):
    return pltpu.roll(v, shift % v.shape[axis], axis)


def smooth_fine(at, x, f):
    v = at(x, f)
    near = at(x - 1, f) + at(x + 1, f)
    far = at(x - 2, f) + at(x + 2, f)
    for axis in (0, 1):
        near = near + (roll(v, 1, axis) + roll(v, -1, axis))
        far = far + (roll(v, 2, axis) + roll(v, -2, axis))
    return keep * v + (fine_near * near - fine_far * far)


def rotated(real, imag, cosine, sine):
    return cosine * real - sine * imag, sine * real + cosine * imag


def place_planes(target, base, source, cosine, sine):
    for x in range(source.shape[0]):
        real, imag = rotated(source[x, 0], source[x, 1], cosine, sine)
        target[base + x, 0] = real
        target[base + x, 1] = imag


def place_halo(ext, middle, even_ref, odd_ref, cs_ref):
    position = lax.axis_index("grid")
    chips = lax.axis_size("grid") // 2
    core, chip = lax.rem(position, 2), lax.div(position, 2)
    cosine, sine = cs_ref[core], cs_ref[2 + core]
    first, last = chip == 0, chip == chips - 1
    low = (jnp.where(first, cosine, 1.0), jnp.where(first, -sine, 0.0))
    high = (jnp.where(last, cosine, 1.0), jnp.where(last, sine, 0.0))
    planes = even_ref.shape[0]
    parity = lax.rem(chip, 2)

    @pl.when(parity == 0)
    def _():
        place_planes(ext, middle - planes, odd_ref, *low)
        place_planes(ext, middle + planes, even_ref, *high)

    @pl.when(parity == 1)
    def _():
        place_planes(ext, middle - planes, even_ref, *low)
        place_planes(ext, middle + planes, odd_ref, *high)


def density_kernel(pd_ref, other_ref, received_ref, lines_ref, f_ref):
    core = lax.rem(lax.axis_index("grid"), 2)
    planes, _, lines, depth = f_ref.shape
    count = received_ref.shape[0]
    spread = (
        lax.broadcasted_iota(jnp.int32, (planes * lines, count), 0) == lines_ref[...]
    ).astype(jnp.float32)
    added = dot(spread, received_ref[...])
    for x in range(planes):
        for part in range(2):
            f_ref[x, part] = added[x * lines : (x + 1) * lines, part * depth : (part + 1) * depth]
    half = planes // 2
    for x in range(half):
        for part in range(2):
            f_ref[core * half + x, part] += pd_ref[core, part, x]
            f_ref[(1 - core) * half + x, part] += other_ref[part, x]


def source_kernel(even_ref, odd_ref, f_ref, cs_ref, s_ref, ext, b1, half):
    planes = f_ref.shape[0]
    lines, depth = f_ref.shape[2:]
    place_halo(ext, planes, even_ref, odd_ref, cs_ref)
    ext[planes : 2 * planes] = f_ref[...]
    for x in range(planes + 4):
        for part in range(2):
            b1[x, part] = smooth_fine(lambda i, p: ext[i, p], x + planes - 2, part)
    for i in range(planes // 2):
        for part in range(2):
            total = None
            for x in (2 * i, 2 * i + 1):
                value = smooth_fine(lambda i, p: b1[i, p], x + 2, part)
                total = value if total is None else total + value
            for h in range(2):
                half[(2 * i + part) * 2 + h] = total[:, h * 128 : (h + 1) * 128]
    rows = planes // 2 * 2
    left = [
        half[2 * r + h, pl.ds(0, lines // 2, 2)] + half[2 * r + h, pl.ds(1, lines // 2, 2)]
        for h in range(2)
        for r in range(rows)
    ]
    stacked = jnp.concatenate(left, axis=0)
    low, high = stacked[: rows * lines // 2], stacked[rows * lines // 2 :]
    matrix = pair_matrix(depth, depth // 2, 0.125)
    total = dot(low, matrix[:128]) + dot(high, matrix[128:])
    for r in range(rows):
        s_ref[r // 2, r % 2] = total[r * lines // 2 : (r + 1) * lines // 2]


def fine_kernel(
    even_ref, odd_ref, after_ref, before_ref, f_ref, cs_ref, own_ref, send_ref, ext, b1, b2, g
):
    position = lax.axis_index("grid")
    chips = lax.axis_size("grid") // 2
    core, chip = lax.rem(position, 2), lax.div(position, 2)
    cosine, sine = cs_ref[core], cs_ref[2 + core]
    planes = f_ref.shape[0]
    place_halo(ext, planes + 2, even_ref, odd_ref, cs_ref)
    ext[planes + 2 : 2 * planes + 2] = f_ref[...]
    first, last = chip < 2, chip >= chips - 2
    place_planes(
        ext, 0, before_ref, jnp.where(first, cosine, 1.0), jnp.where(first, -sine, 0.0)
    )
    place_planes(
        ext,
        3 * planes + 2,
        after_ref,
        jnp.where(last, cosine, 1.0),
        jnp.where(last, sine, 0.0),
    )
    for x in range(planes + 8):
        for part in range(2):
            b1[x, part] = smooth_fine(lambda i, p: ext[i, p], x + 2, part)
    for x in range(planes + 4):
        for part in range(2):
            b2[x, part] = smooth_fine(lambda i, p: b1[i, p], x + 2, part)
    for x in range(planes):
        for part in range(2):
            b3 = smooth_fine(lambda i, p: b2[i, p], x + 2, part)
            g[x, part] = fine_scale * (f_ref[x, part] + b1[x + 4, part] + b2[x + 2, part] + b3)
    half = planes // 2
    for x in range(half):
        own_ref[x] = g[core * half + x]
        send_ref[x] = g[(1 - core) * half + x]


def shift_z(v, step):
    width = v.shape[-1] // 2
    lane = lax.broadcasted_iota(jnp.int32, v.shape, len(v.shape) - 1)
    edge = 0 if step > 0 else width - 1
    inner = roll(v, step, 1)
    outer = roll(v, step + (width if step > 0 else -width), 1)
    return jnp.where(lane % width == edge, outer, inner)


def packed_sweep(values, count, depth, source, target, cosine, sine, residual=False):
    rate, near_rate = level_numbers(depth)
    real, imag = rotated(values[count, 0], values[count, 1], cosine, -sine)
    values[0, 0], values[0, 1] = real, imag
    real, imag = rotated(values[1, 0], values[1, 1], cosine, sine)
    values[count + 1, 0], values[count + 1, 1] = real, imag

    def body(x):
        for part in range(2):
            v = values[x + 1, part]
            near = values[x, part] + values[x + 2, part]
            near = near + (roll(v, 1, 0) + roll(v, -1, 0))
            near = near + (shift_z(v, 1) + shift_z(v, -1))
            if residual:
                target[x, part] = source[x, part] - omega / rate * v + near_rate / rate * near
            else:
                target[x + 1, part] = rate * source[x, part] + keep * v + near_rate * near

    each(count, body)


def first_sweep(values, count, depth, source):
    rate, _ = level_numbers(depth)

    def body(x):
        for part in range(2):
            values[x + 1, part] = rate * source[x, part]

    each(count, body)


def cycle_kernel(
    ag_ref, own_ref, other_ref, cs_ref, out_ref, u, v, r1, u2, v2, s2, r2, u3, v3, s3, w2, w1, e, b1
):
    position = lax.axis_index("grid")
    core = lax.rem(position, 2)
    count = u.shape[0] - 2
    lines, depth = u.shape[2:]
    rate, near_rate = level_numbers(1)
    cosines = [cs_ref[0], cs_ref[1]]
    sines = [cs_ref[2], cs_ref[3]]
    lane = lax.broadcasted_iota(jnp.int32, (8, 128), 1)
    lane_cosine = jnp.where(lane < 64, cosines[0], cosines[1])
    lane_sine = jnp.where(lane < 64, sines[0], sines[1])

    def source(x, f):
        return ag_ref[x // 2 * 2 + f // 2, x % 2, f % 2]

    def rims(values):
        for p in range(2):
            real, imag = rotated(
                values[count, 2 * p], values[count, 2 * p + 1], cosines[p], -sines[p]
            )
            values[0, 2 * p], values[0, 2 * p + 1] = real, imag
            real, imag = rotated(values[1, 2 * p], values[1, 2 * p + 1], cosines[p], sines[p])
            values[count + 1, 2 * p], values[count + 1, 2 * p + 1] = real, imag

    def sweep(values, target, residual=False):
        rims(values)

        def body(x):
            for f in range(4):
                a = values[x + 1, f]
                near = values[x, f] + values[x + 2, f]
                near = near + (roll(a, 1, 0) + roll(a, -1, 0))
                near = near + (roll(a, 1, 1) + roll(a, -1, 1))
                if residual:
                    target[x, f] = source(x, f) - omega / rate * a + near_rate / rate * near
                else:
                    target[x + 1, f] = rate * source(x, f) + keep * a + near_rate * near

        each(count, body)

    def start(x):
        for f in range(4):
            u[x + 1, f] = rate * source(x, f)

    each(count, start)
    sweep(u, v)
    sweep(v, r1, residual=True)

    count2 = count // 2
    i = lax.broadcasted_iota(jnp.int32, (128, 128), 0)
    j = lax.broadcasted_iota(jnp.int32, (128, 128), 1)
    down = [jnp.where(i // 2 + 64 * p == j, 0.125, 0.0) for p in range(2)]

    def lower(x):
        for f in range(4):
            r1[2 * x, f] = r1[2 * x, f] + r1[2 * x + 1, f]
        for part in range(2):
            total = None
            for p in range(2):
                f = 2 * p + part
                rows = r1[2 * x, f, pl.ds(0, 8, 2)] + r1[2 * x, f, pl.ds(1, 8, 2)]
                value = dot(rows, down[p])
                total = value if total is None else total + value
            s2[x, part] = total

    each(count2, lower)
    first_sweep(u2, count2, 2, s2)
    packed_sweep(u2, count2, 2, s2, v2, lane_cosine, lane_sine)

    packed_sweep(v2, count2, 2, s2, w2, lane_cosine, lane_sine, residual=True)

    count3 = count2 // 2
    down3 = jnp.where(i // 64 == j // 64, jnp.where(i % 64 // 2 == j % 32, 0.125, 0.0), 0.0)

    def lower3(x):
        for part in range(2):
            total = w2[2 * x, part] + w2[2 * x + 1, part]
            r2[x, part, 0:8] = total
            r2[x, part, 8:16] = total
            rows = r2[x, part, pl.ds(0, 8, 2)] + r2[x, part, pl.ds(1, 8, 2)]
            s3[x, part] = dot(rows, down3)

    each(count3, lower3)
    first_sweep(u3, count3, 3, s3)
    a, b = u3, v3
    for _ in range(5):
        packed_sweep(a, count3, 3, s3, b, lane_cosine, lane_sine)
        a, b = b, a

    up3 = jnp.where(i // 64 == j // 64, jnp.where(i % 64 == j % 64 // 2, 1.0, 0.0), 0.0)

    def raise3(x):
        for part in range(2):
            value = dot(a[x + 1, part], up3)
            r2[x, part, pl.ds(0, 8, 2)] = value
            r2[x, part, pl.ds(1, 8, 2)] = value
            value = r2[x, part, 0:8]
            for k in range(2):
                v2[2 * x + k + 1, part] = v2[2 * x + k + 1, part] + value

    each(count3, raise3)
    packed_sweep(v2, count2, 2, s2, u2, lane_cosine, lane_sine)
    packed_sweep(u2, count2, 2, s2, v2, lane_cosine, lane_sine)

    up = [jnp.where(i == j // 2 + 64 * p, 1.0, 0.0) for p in range(2)]

    def raise2(x):
        for part in range(2):
            for p in range(2):
                f = 2 * p + part
                value = dot(v2[x + 1, part], up[p])
                w1[x, f, pl.ds(0, 8, 2)] = value
                w1[x, f, pl.ds(1, 8, 2)] = value
                value = w1[x, f]
                for k in range(2):
                    v[2 * x + k + 1, f] = v[2 * x + k + 1, f] + value

    each(count2, raise2)
    sweep(v, u)
    sweep(u, v)

    matrix = spread_matrix(128, 256)
    planes = []
    for k in range(-2, 3):
        q = position + k
        low, high = q < 0, q >= count
        q = jnp.where(low, q + count, jnp.where(high, q - count, q))
        for p in range(2):
            cosine = jnp.where(low | high, cosines[p], 1.0)
            sine = jnp.where(low, -sines[p], jnp.where(high, sines[p], 0.0))
            planes.extend(rotated(v[q + 1, 2 * p], v[q + 1, 2 * p + 1], cosine, sine))
    wide = dot(jnp.concatenate(planes, axis=0), matrix)
    for k in range(5):
        for f in range(4):
            row = (4 * k + f) * lines
            for h in range(2):
                value = wide[row : row + lines, 128 * h : 128 * (h + 1)]
                e[(4 * k + f) * 2 + h, pl.ds(0, lines, 2)] = value
                e[(4 * k + f) * 2 + h, pl.ds(1, lines, 2)] = value

    def expanded(x, f):
        place = (4 * (x // 2) + f) * 2
        return jnp.concatenate([e[place], e[place + 1]], axis=1)

    for x in range(6):
        for f in range(4):
            b1[x, f] = smooth_fine(expanded, x + 2, f)
    half = own_ref.shape[0]
    for x in range(half):
        for part in range(2):
            out_ref[core, part, x] = own_ref[x, part]
            out_ref[1 - core, part, x] = other_ref[x, part]
    for x in range(half):
        for f in range(4):
            out_ref[f // 2, f % 2, x] += smooth_fine(lambda i, g: b1[i, g], x + 2, f)


def pair_phases(pair_table, k_fraction):
    kcount = k_fraction.shape[0]
    picks = pair_table[:, :, None] == jnp.arange(kcount, dtype=jnp.int32)[None, None, :]
    chosen = jnp.sum(jnp.where(picks, k_fraction[None, None, :], 0.0), axis=2)
    angle = 6.283185307179586 * (chosen[:, 0] - chosen[:, 1])
    return jnp.concatenate([jnp.cos(angle), jnp.sin(angle)])


def make_rows(moments, shapes, slot_atom, slot_tile, slot_row, tile_count):
    slot_count = shapes.shape[0]
    atom_count = moments.shape[0]
    capacity = max(2, 2 * slot_count // tile_count)
    atom_pick = (slot_atom[:, None] == jnp.arange(atom_count, dtype=jnp.int32)[None, :]).astype(
        jnp.float32
    )
    chosen = jnp.dot(atom_pick, moments.reshape(atom_count, -1), precision=highest)
    chosen = chosen.reshape(slot_count, moments.shape[1] * moments.shape[2], moments.shape[3])
    row_values = jnp.einsum("sfl,slz->sfz", chosen, shapes, precision=highest)
    tiles = slot_tile[:, 0]
    slot_ids = jnp.arange(slot_count, dtype=jnp.int32)
    before = (tiles[:, None] == tiles[None, :]) & (slot_ids[None, :] < slot_ids[:, None])
    ranks = jnp.sum(before.astype(jnp.int32), axis=1)
    places = tiles * capacity + ranks
    buckets = jnp.arange(tile_count * capacity, dtype=jnp.int32)
    pick = buckets[:, None] == places[None, :]
    targets = jnp.sum(jnp.where(pick, slot_row[None, :] + 1, 0), axis=1) - 1
    packed = jnp.dot(
        pick.astype(jnp.float32), row_values.reshape(slot_count, -1), precision=highest
    )
    packed = packed.reshape(tile_count // 2, 2 * capacity, 2, -1).transpose(0, 2, 1, 3)
    return packed.reshape(tile_count, 2 * capacity, -1), targets.reshape(tile_count, capacity)


def vmem(count):
    return [pl.BlockSpec(memory_space=pltpu.VMEM)] * count


smem = [pl.BlockSpec(memory_space=pltpu.SMEM)]


def call(kernel, out_shape, in_specs, scratch, flops):
    single = not isinstance(out_shape, (list, tuple))
    return pl.pallas_call(
        kernel,
        out_shape=out_shape,
        in_specs=in_specs,
        out_specs=vmem(1)[0] if single else vmem(len(out_shape)),
        scratch_shapes=[pltpu.VMEM(shape, jnp.float32) for shape in scratch],
        compiler_params=pltpu.CompilerParams(vmem_limit_bytes=48 * 2**20),
        cost_estimate=pl.CostEstimate(flops=flops, bytes_accessed=2**20, transcendentals=0),
    )


def shaped(*shape):
    return jax.ShapeDtypeStruct(shape, jnp.float32)


def per_device(
    pair_density, moments, shapes, slot_atom, slot_tile, slot_row, pair_table, k_fraction
):
    tile_count = lax.axis_size("grid")
    chips = tile_count // 2
    position = lax.axis_index("grid")
    core = position % 2
    chip = position // 2
    _, _, thick, lines, depth = pair_density.shape
    planes = 2 * thick
    devices = range(tile_count)

    def permute(value, target):
        return lax.ppermute(value, "grid", [(i, target(i)) for i in devices])

    def partner(i):
        return i ^ 1

    def even_side(i):
        return i ^ 2

    def odd_side(i):
        return (i // 2 + (1 if i // 2 % 2 else -1)) % chips * 2 + i % 2

    cs = pair_phases(pair_table, k_fraction)

    other = permute(lax.dynamic_index_in_dim(pair_density, 1 - core, 0, False), partner)
    packed, targets = make_rows(moments, shapes, slot_atom, slot_tile, slot_row, tile_count)
    every = lax.all_gather(targets, "grid", axis=0)
    mine = lax.dynamic_slice_in_dim(every, 2 * chip, 2, axis=1)
    tile_base = jnp.arange(2, dtype=jnp.int32)[None, :, None] * (thick * lines)
    line_ids = jnp.where(mine >= 0, mine + tile_base, -1).reshape(1, -1)
    received = lax.all_to_all(packed, "grid", split_axis=0, concat_axis=0, tiled=True)
    received = received.reshape(-1, received.shape[-1])

    block = (planes, 2, lines, depth)
    f = call(density_kernel, shaped(*block), vmem(4), [], 10**8)(
        pair_density, other, received, line_ids
    )
    even = permute(f, even_side)
    odd = permute(f, odd_side)
    after = permute(f[:thick], lambda i: (i - 4) % tile_count)
    before = permute(f[thick:], lambda i: (i + 4) % tile_count)
    source = call(
        source_kernel,
        shaped(planes // 2, 2, lines // 2, depth // 2),
        vmem(3) + smem,
        [
            (3 * planes, 2, lines, depth),
            (planes + 4, 2, lines, depth),
            (2 * planes, lines, 128),
        ],
        10**7,
    )(even, odd, f, cs)
    gathered = lax.all_gather(source, "grid", axis=0)
    own, send = call(
        fine_kernel,
        [shaped(thick, 2, lines, depth)] * 2,
        vmem(5) + smem,
        [
            (3 * planes + 4, 2, lines, depth),
            (planes + 8, 2, lines, depth),
            (planes + 4, 2, lines, depth),
            block,
        ],
        10**7,
    )(even, odd, after, before, f, cs)
    got = permute(send, partner)
    n1, n2, n3 = tile_count, tile_count // 2, tile_count // 4
    return call(
        cycle_kernel,
        shaped(*pair_density.shape),
        vmem(3) + smem,
        [
            (n1 + 2, 4, 16, 128),
            (n1 + 2, 4, 16, 128),
            (n1, 4, 16, 128),
            (n2 + 2, 2, 8, 128),
            (n2 + 2, 2, 8, 128),
            (n2, 2, 8, 128),
            (n2, 2, 16, 128),
            (n3 + 2, 2, 8, 128),
            (n3 + 2, 2, 8, 128),
            (n3, 2, 8, 128),
            (n2, 2, 8, 128),
            (n2, 4, 16, 128),
            (40, 32, 128),
            (6, 4, 32, 256),
        ],
        10**8,
    )(gathered, own, got, cs)


def solution(mesh):
    return jax.shard_map(
        per_device,
        mesh=mesh,
        in_specs=(
            P("rep", None, "grid", None, None),
            P(("rep", "grid"), None, None, None),
            P(("rep", "grid"), None, None),
            P(("rep", "grid")),
            P(("rep", "grid"), None),
            P(("rep", "grid")),
            P(),
            P(),
        ),
        out_specs=P("rep", None, "grid", None, None),
        check_vma=False,
    )
```

time: 198 us -> 90.2 us (0.46)
  starting transfers between devices: 87.8 us -> 14 us
  waiting for transfers between devices: 56.2 us -> 9.22 us
  blocking collectives: 0 us -> 46.1 us
  local copies, waits for them, and re-layouts: 29.7 us -> 1.57 us
  other arithmetic: 18.5 us -> 1.62 us
  Pallas kernels: 0 us -> 13.1 us
    ppermute x36 -> x6, starting transfers between devices: 75.6 us -> 6.69 us  [permute(): return lax.ppermute(value, 'grid', [(i, target(i)) for i in devices])]
    all_gather x0 -> x2, blocking collectives: none -> 46.1 us  [the longest x1 24.4 us: per_device(): every = lax.all_gather(targets, 'grid', axis=0)]
    ppermute x36 -> x6, waiting for transfers between devices: 42.3 us -> 9.22 us  [permute(): return lax.ppermute(value, 'grid', [(i, target(i)) for i in devices])]
    reshape x4 -> x2, local copies, waits for them, and re-layouts: 22.9 us -> 0.94 us  [the longest x1 0.83 us: make_rows(): moments.reshape(atom_count, -1)]
    all_to_all x2 -> x1, waiting for transfers between devices: 13.9 us -> 0.01 us  [per_device(): lax.all_to_all(packed, 'grid', split_axis=0, concat_axis=0, tiled=True)]
    pallas_call x0 -> x4, Pallas kernels: none -> 13.1 us  [the longest x1 8.21 us: per_device(): call(cycle_kernel, shaped(*pair_density.shape), vmem(3) + smem, [(n1 + 2,...]
    reduce_sum x6 -> x3, other arithmetic: 11.3 us -> 1.22 us  [the longest x1 0.97 us: make_rows(): ranks = jnp.sum(before.astype(jnp.int32), axis=1)]
    all_to_all x2 -> x1, starting transfers between devices: 12.2 us -> 7.36 us  [per_device(): lax.all_to_all(packed, 'grid', split_axis=0, concat_axis=0, tiled=True)]
  transfers between devices with their start and end apart: 38 -> 7, of which waited for: 24 -> 3; matrix products, arithmetic and copies ran while one was open for 6% -> 1% of each run, Pallas kernels for 0% -> 2%
where the time goes in v1:
time: 90.2 us; the launch traced here: 89.9 us
  blocking collectives  46.1 us (51%)
  starting transfers between devices  14 us (16%)
  Pallas kernels  13.1 us (15%)
  waiting for transfers between devices  9.22 us (10%)
  matrix products  4.12 us (5%)
  other arithmetic  1.62 us (2%)
  local copies, waits for them, and re-layouts  1.57 us (2%)
    all_gather x1, blocking collectives, per_device(): every = lax.all_gather(targets, 'grid', axis=0)  24.4 us
    all_gather x1, blocking collectives, per_device(): gathered = lax.all_gather(source, 'grid', axis=0)  21.7 us
    ppermute x6, waiting for transfers between devices, permute(): return lax.ppermute(value, 'grid', [(i, target(i)) for i in devices])  9.22 us
    pallas_call x1, Pallas kernels, per_device(): call(cycle_kernel, shaped(*pair_density.shape), vmem(3) + smem, [(n1 + 2,...  8.21 us
    all_to_all x1, starting transfers between devices, per_device(): lax.all_to_all(packed, 'grid', split_axis=0, concat_axis=0, tiled=True)  7.36 us
    ppermute x6, starting transfers between devices, permute(): return lax.ppermute(value, 'grid', [(i, target(i)) for i in devices])  6.69 us
    pallas_call x1, Pallas kernels, per_device(): call(fine_kernel, [shaped(thick, 2, lines, depth)] * 2, vmem(5) + smem, [...  2.51 us
    dot_general x1, matrix products, make_rows(): row_values = jnp.einsum('sfl,slz->sfz', chosen, shapes, precision=highest)  2.01 us
  transfers between devices with their start and end apart: 7, of which 3 were waited for; matrix products, arithmetic and copies ran while one was open for 1% of the time, Pallas kernels for 2%

profile of v1, /device:TPU:0, one launch (start us, length us, event | category | flops | bytes accessed | tf_op | source)
XLA Modules:
  0.0 89.9 jit_solution(14379400054263660630)
XLA Ops:
  0.0 0.0 copy-start
  0.0 1.0 %convert_reduce_fusion = s32[64]{0:T(128)S(1)} fusion(s32[64]{0:T(128)} %bitcast.37), kind=kLoop, calls=%fused_computation.14 | loop fusion | flops 20416 | bytes 512 | tf_op jit(solution)/shard_map/reduce_sum | solution.py:401
  1.0 0.8 reshape.73
  1.8 0.1 dot_general.18
  1.9 0.0 copy-start.3
  1.9 0.0 copy-start.4
  1.9 0.9 %fusion.6 = f32[64,4,25]{0,2,1:T(8,128)S(1)} fusion(f32[4,25,12]{1,0,2:T(4,128)S(1)} %dot_general.18, s32[64]{0:T(128)} %param.11), kind=kOutput, calls=%fused_computation.9 | convolution fusion | flops 922368 | bytes 30656 | tf_op jit(solution)/shard_map/dot_general | solution.py:395
  2.8 0.1 copy.30
  3.0 0.0 copy-done
  3.0 2.0 %fusion = f32[64,4,256]{2,1,0:T(4,128)S(1)} fusion(f32[64,4,25]{2,1,0:T(4,128)S(1)} %copy.30, f32[64,25,256]{2,0,1:T(8,128)S(1)} %copy-done), kind=kOutput, calls=%fused_computation | convolution fusion | flops 19660800 | bytes 1926144 | tf_op jit(solution)/shard_map/sfl,slz->sfz/dot_general | solution.py:397
  5.0 0.0 copy-start.1
  5.0 0.0 copy-start.2
  5.0 0.0 copy-start.5
  5.1 0.0 copy-done.3
  5.1 0.0 copy-done.4
  5.1 1.2 %fusion.2 = f32[8,16,2,512]{3,1,2,0:T(8,128)} fusion(f32[8,2,8,512]{3,2,1,0:T(8,128)S(1)} %bitcast.35, s32[64]{0:T(128)S(1)} %get-tuple-element.13, s32[8,16]{1,0:T(8,128)S(1)} %multiply_add_fusion), kind=kOutput, calls=%fused_computation.3 | convolution fusion | flops 100671488 | bytes 787200 | tf_op jit(solution)/shard_map/dot_general | solution.py:406
  6.3 7.4 %all-to-all-start = ((f32[16,16,512]{2,1,0:T(8,128)}), f32[16,16,512]{2,1,0:T(8,128)S(1)}, u32[]{:S(2)}, u32[]{:S(2)}) async-start(f32[16,16,512]{2,1,0:T(8,128)} %bitcast.9), calls=%async_computation | async-start | bytes 1048576 | tf_op jit(solution)/shard_map/all_to_all | solution.py:469
  13.7 0.0 copy-done.1
  13.7 0.5 collective-permute-start
  14.2 0.1 select_reduce_fusion
  14.3 0.1 sub.19
  14.4 0.1 copy.33
  14.4 24.4 %all_gather.9 = s32[16,16,8]{1,2,0:T(8,128)S(1)} all-gather(s32[1,16,8]{1,2,0:T(8,128)S(1)} %copy.33), channel_id=1, replica_groups=mesh['rep'=2,'grid'=16] {'grid'}, dimensions={0}, use_global_device_ids=true | all-gather | bytes 8704 | tf_op jit(solution)/shard_map/all_gather | solution.py:465
  38.8 0.1 add_select_fusion
  38.9 0.2 copy.34
  39.1 0.1 reshape.77.lines_ref
  39.2 0.0 copy-done.2
  39.2 0.0 copy-done.5
  39.2 0.2 fusion.14
  39.4 0.0 collective-permute-done.other_ref
  39.4 0.0 all-to-all-done
  39.4 0.5 shard_map.82.f_ref
  39.9 1.8 %collective-permute-start.2 = (f32[4,2,32,256]{3,2,1,0:T(8,128)S(1)}, f32[4,2,32,256]{3,2,1,0:T(8,128)S(1)}, u32[]{:S(2)}, u32[]{:S(2)}) collective-permute-start(f32[4,2,32,256]{3,2,1,0:T(8,128)S(1)} %shard_map.82.f_ref), channel_id=1, source_target_pairs={{0,14},{1,15},{2,4},{3,5},{4,2},{5,3},{6,8},{7,9},{8,6},{9,7},{10,... | collective-permute-start | bytes 786440 | tf_op jit(solution)/shard_map/ppermute | solution.py:450
  41.7 0.5 collective-permute-start.1
  42.2 1.5 %collective-permute-start.4 = (f32[2,2,32,256]{3,2,1,0:T(8,128)S(1)}, f32[2,2,32,256]{3,2,1,0:T(8,128)S(1)}, u32[]{:S(2)}, u32[]{:S(2)}) collective-permute-start(f32[2,2,32,256]{3,2,1,0:T(8,128)S(1)} %get-tuple-element.11), channel_id=1, source_target_pairs={{0,4},{1,5},{2,6},{3,7},{4,8},{5,9},{6,10},{7,11},{8,12},{9,13},{1... | collective-permute-start | bytes 393224 | tf_op jit(solution)/shard_map/ppermute | solution.py:450
  43.7 2.4 %collective-permute-start.3 = (f32[2,2,32,256]{3,2,1,0:T(8,128)S(1)}, f32[2,2,32,256]{3,2,1,0:T(8,128)S(1)}, u32[]{:S(2)}, u32[]{:S(2)}) collective-permute-start(f32[2,2,32,256]{3,2,1,0:T(8,128)S(1)} %get-tuple-element.12), channel_id=1, source_target_pairs={{0,12},{1,13},{2,14},{3,15},{4,0},{5,1},{6,2},{7,3},{8,4},{9,5},{1... | collective-permute-start | bytes 393224 | tf_op jit(solution)/shard_map/ppermute | solution.py:450
  46.1 0.2 cosine_reduce_fusion
  46.3 0.1 pad_maximum_fusion.cs_ref
  46.4 6.7 %collective-permute-done.4.before_ref = f32[2,2,32,256]{3,2,1,0:T(8,128)S(1)} collective-permute-done((f32[2,2,32,256]{3,2,1,0:T(8,128)S(1)}, f32[2,2,32,256]{3,2,1,0:T(8,128)S(1)}, u32[]{:S(2)}, u32[]{:S(2)}) %collective-permute-start.4) | collective-permute-done | bytes 131104 | tf_op jit(solution)/shard_map/ppermute | solution.py:450
  53.0 2.3 %collective-permute-done.3.after_ref = f32[2,2,32,256]{3,2,1,0:T(8,128)S(1)} collective-permute-done((f32[2,2,32,256]{3,2,1,0:T(8,128)S(1)}, f32[2,2,32,256]{3,2,1,0:T(8,128)S(1)}, u32[]{:S(2)}, u32[]{:S(2)}) %collective-permute-start.3) | collective-permute-done | bytes 131104 | tf_op jit(solution)/shard_map/ppermute | solution.py:450
  55.3 0.0 collective-permute-done.2.odd_ref
  55.3 0.2 collective-permute-done.1.even_ref
  55.6 2.5 %shard_map.84 = (f32[2,2,32,256]{3,2,1,0:T(8,128)S(1)}, f32[2,2,32,256]{3,2,1,0:T(8,128)S(1)}) custom-call(f32[4,2,32,256]{3,2,1,0:T(8,128)S(1)} %collective-permute-done.1.even_ref, f32[4,2,32,256]{3,2,1,0:T(8,128)S(1)} %collective-permute-done.2.odd_ref, f32[2,2,32,256]{3,2,1,0:T(8,128)S(1)} %collective-permute-done.3.after_ref, ...), custom_call_target="tpu_custom_call" | custom-call | flops 10000000 | bytes 1048576 | tf_op jit(solution)/shard_map/pallas_call | solution.py:492
  58.1 0.1 collective-permute-start.5
  58.2 1.8 %shard_map.83 = f32[2,2,16,128]{3,2,1,0:T(8,128)S(1)} custom-call(f32[4,2,32,256]{3,2,1,0:T(8,128)S(1)} %collective-permute-done.1.even_ref, f32[4,2,32,256]{3,2,1,0:T(8,128)S(1)} %collective-permute-done.2.odd_ref, f32[4,2,32,256]{3,2,1,0:T(8,128)S(1)} %shard_map.82.f_ref, f32[4]{0:T(128)S(1)} %pad_maximum_fusion.cs_ref), custom_call_target="tpu_custom_call" | custom-call | flops 10000000 | bytes 1048576 | tf_op jit(solution)/shard_map/pallas_call | solution.py:480
  60.0 21.7 %all-gather = f32[32,2,16,128]{3,2,1,0:T(8,128)S(1)} all-gather(f32[2,2,16,128]{3,2,1,0:T(8,128)S(1)} %shard_map.83), channel_id=2, replica_groups=mesh['rep'=2,'grid'=16] {'grid'}, dimensions={0}, use_global_device_ids=true | all-gather | bytes 557056 | tf_op jit(solution)/shard_map/all_gather | solution.py:491
  81.7 0.0 collective-permute-done.5.other_ref
  81.7 8.2 %shard_map.85 = f32[2,2,2,32,256]{4,3,2,1,0:T(8,128)} custom-call(f32[16,2,2,16,128]{4,3,2,1,0:T(8,128)S(1)} %bitcast.33, f32[2,2,32,256]{3,2,1,0:T(8,128)S(1)} %get-tuple-element.7.own_ref, f32[2,2,32,256]{3,2,1,0:T(8,128)S(1)} %collective-permute-done.5.other_ref, f32[4]{0:T(128)S(1)} %pad_maximum_fusion.cs_ref), custom_call_target="tpu_custom_call" | custom-call | flops 100000000 | bytes 1048576 | tf_op jit(solution)/shard_map/pallas_call | solution.py:506
  (7 shorter events, 0.1 us)
Async XLA Ops:
  0.0 3.0 %copy-start = (f32[64,25,256]{2,0,1:T(8,128)S(1)}, f32[64,25,256]{2,0,1:T(8,128)}, u32[]{:S(2)}) copy-start(f32[64,25,256]{2,0,1:T(8,128)} %param.10) | copy-start | bytes 4915204
  1.9 3.2 %copy-start.3 = (s32[64,1]{0,1:T(1,128)S(1)}, s32[64,1]{0,1:T(1,128)}, u32[]{:S(2)}) copy-start(s32[64,1]{0,1:T(1,128)} %param.12) | copy-start | bytes 772
  1.9 3.2 %copy-start.4 = (s32[64]{0:T(128)S(1)}, s32[64]{0:T(128)}, u32[]{:S(2)}) copy-start(s32[64]{0:T(128)} %param.13) | copy-start | bytes 772
  5.0 8.7 %copy-start.1 = (f32[2,2,2,32,256]{4,3,2,1,0:T(8,128)S(1)}, f32[2,2,2,32,256]{4,3,2,1,0:T(8,128)}, u32[]{:S(2)}) copy-start(f32[2,2,2,32,256]{4,3,2,1,0:T(8,128)} %pd_ref.1) | copy-start | bytes 786436
  5.0 34.2 %copy-start.2 = (s32[2,2]{1,0:T(2,128)S(1)}, s32[2,2]{1,0:T(2,128)}, u32[]{:S(2)}) copy-start(s32[2,2]{1,0:T(2,128)} %param.14) | copy-start | bytes 52
  5.0 34.2 %copy-start.5 = (f32[8]{0:T(128)S(1)}, f32[8]{0:T(128)}, u32[]{:S(2)}) copy-start(f32[8]{0:T(128)} %param.15) | copy-start | bytes 100
  6.3 33.1 %all-to-all-start = ((f32[16,16,512]{2,1,0:T(8,128)}), f32[16,16,512]{2,1,0:T(8,128)S(1)}, u32[]{:S(2)}, u32[]{:S(2)}) async-start(f32[16,16,512]{2,1,0:T(8,128)} %bitcast.9), calls=%async_computation | async-start | bytes 1048576 | tf_op jit(solution)/shard_map/all_to_all | solution.py:469
  13.7 25.6 %collective-permute-start = (f32[2,2,32,256]{3,2,1,0:T(8,128)S(1)}, f32[2,2,32,256]{3,2,1,0:T(8,128)S(1)}, u32[]{:S(2)}, u32[]{:S(2)}) collective-permute-start(f32[2,2,32,256]{3,2,1,0:T(8,128)S(1)} %dynamic-slice_bitcast_fusion), channel_id=1, source_target_pairs={{0,1},{1,0},{2,3},{3,2},{4,5},{5,4},{6,7},{7,6},{8,9},{9,8},{10,11... | collective-permute-start | bytes 393224 | tf_op jit(solution)/shard_map/ppermute | solution.py:450
  39.9 15.5 %collective-permute-start.2 = (f32[4,2,32,256]{3,2,1,0:T(8,128)S(1)}, f32[4,2,32,256]{3,2,1,0:T(8,128)S(1)}, u32[]{:S(2)}, u32[]{:S(2)}) collective-permute-start(f32[4,2,32,256]{3,2,1,0:T(8,128)S(1)} %shard_map.82.f_ref), channel_id=1, source_target_pairs={{0,14},{1,15},{2,4},{3,5},{4,2},{5,3},{6,8},{7,9},{8,6},{9,7},{10,... | collective-permute-start | bytes 786440 | tf_op jit(solution)/shard_map/ppermute | solution.py:450
  41.7 13.9 %collective-permute-start.1 = (f32[4,2,32,256]{3,2,1,0:T(8,128)S(1)}, f32[4,2,32,256]{3,2,1,0:T(8,128)S(1)}, u32[]{:S(2)}, u32[]{:S(2)}) collective-permute-start(f32[4,2,32,256]{3,2,1,0:T(8,128)S(1)} %shard_map.82.f_ref), channel_id=1, source_target_pairs={{0,2},{1,3},{2,0},{3,1},{4,6},{5,7},{6,4},{7,5},{8,10},{9,11},{10,... | collective-permute-start | bytes 786440 | tf_op jit(solution)/shard_map/ppermute | solution.py:450
  42.2 10.9 %collective-permute-start.4 = (f32[2,2,32,256]{3,2,1,0:T(8,128)S(1)}, f32[2,2,32,256]{3,2,1,0:T(8,128)S(1)}, u32[]{:S(2)}, u32[]{:S(2)}) collective-permute-start(f32[2,2,32,256]{3,2,1,0:T(8,128)S(1)} %get-tuple-element.11), channel_id=1, source_target_pairs={{0,4},{1,5},{2,6},{3,7},{4,8},{5,9},{6,10},{7,11},{8,12},{9,13},{1... | collective-permute-start | bytes 393224 | tf_op jit(solution)/shard_map/ppermute | solution.py:450
  43.7 11.6 %collective-permute-start.3 = (f32[2,2,32,256]{3,2,1,0:T(8,128)S(1)}, f32[2,2,32,256]{3,2,1,0:T(8,128)S(1)}, u32[]{:S(2)}, u32[]{:S(2)}) collective-permute-start(f32[2,2,32,256]{3,2,1,0:T(8,128)S(1)} %get-tuple-element.12), channel_id=1, source_target_pairs={{0,12},{1,13},{2,14},{3,15},{4,0},{5,1},{6,2},{7,3},{8,4},{9,5},{1... | collective-permute-start | bytes 393224 | tf_op jit(solution)/shard_map/ppermute | solution.py:450
  58.1 23.6 %collective-permute-start.5 = (f32[2,2,32,256]{3,2,1,0:T(8,128)S(1)}, f32[2,2,32,256]{3,2,1,0:T(8,128)S(1)}, u32[]{:S(2)}, u32[]{:S(2)}) collective-permute-start(f32[2,2,32,256]{3,2,1,0:T(8,128)S(1)} %get-tuple-element.8), channel_id=1, source_target_pairs={{0,1},{1,0},{2,3},{3,2},{4,5},{5,4},{6,7},{7,6},{8,9},{9,8},{10,11... | collective-permute-start | bytes 393224 | tf_op jit(solution)/shard_map/ppermute | solution.py:450

commit v2 on v1

v2 whole, which is shorter than its diff:
```python
import jax
import jax.numpy as jnp
from jax import lax
from jax.experimental import pallas as pl
from jax.experimental.pallas import tpu as pltpu
from jax.sharding import PartitionSpec as P

omega = 0.8
screen = 0.05
highest = lax.Precision.HIGHEST

fine_diagonal = 7.5 + screen
fine_scale = omega / fine_diagonal
fine_near = fine_scale * 4.0 / 3.0
fine_far = fine_scale / 12.0
keep = 1.0 - omega


def level_numbers(depth):
    quarter = 1.0 / 4**depth
    diagonal = 6.0 * quarter + screen
    return omega / diagonal, omega / diagonal * quarter


def each(count, body, most=16):
    if count <= most:
        for i in range(count):
            body(i)
    else:
        pl.loop(0, count, unroll=4)(body)


def dot(a, b):
    return jnp.dot(a, b, precision=highest, preferred_element_type=jnp.float32)


def pair_matrix(rows, columns, value):
    i = lax.broadcasted_iota(jnp.int32, (rows, columns), 0)
    j = lax.broadcasted_iota(jnp.int32, (rows, columns), 1)
    return jnp.where(i // 2 == j, value, 0.0)


def spread_matrix(rows, columns):
    i = lax.broadcasted_iota(jnp.int32, (rows, columns), 0)
    j = lax.broadcasted_iota(jnp.int32, (rows, columns), 1)
    return jnp.where(i == j // 2, 1.0, 0.0)


def roll(v, shift, axis):
    return pltpu.roll(v, shift % v.shape[axis], axis)


def smooth_fine(at, x, f):
    total = None
    for step, weight in ((1, fine_near), (2, -fine_far)):
        sides = [p for p in (at(x - step, f), at(x + step, f)) if p is not None]
        v = at(x, f)
        if v is not None:
            for axis in (0, 1):
                sides.append(roll(v, step, axis) + roll(v, -step, axis))
            if step == 1:
                total = keep * v
        if sides:
            part = weight * sum(sides[1:], sides[0])
            total = part if total is None else total + part
    return total


def rotated(real, imag, cosine, sine):
    return cosine * real - sine * imag, sine * real + cosine * imag


def place_planes(target, base, source, cosine, sine):
    for x in range(source.shape[0]):
        real, imag = rotated(source[x, 0], source[x, 1], cosine, sine)
        target[base + x, 0] = real
        target[base + x, 1] = imag


def place_halo(ext, middle, even_ref, odd_ref, cs_ref):
    position = lax.axis_index("grid")
    chips = lax.axis_size("grid") // 2
    core, chip = lax.rem(position, 2), lax.div(position, 2)
    cosine, sine = cs_ref[core], cs_ref[2 + core]
    first, last = chip == 0, chip == chips - 1
    low = (jnp.where(first, cosine, 1.0), jnp.where(first, -sine, 0.0))
    high = (jnp.where(last, cosine, 1.0), jnp.where(last, sine, 0.0))
    planes = even_ref.shape[0]
    parity = lax.rem(chip, 2)

    @pl.when(parity == 0)
    def _():
        place_planes(ext, middle - planes, odd_ref, *low)
        place_planes(ext, middle + planes, even_ref, *high)

    @pl.when(parity == 1)
    def _():
        place_planes(ext, middle - planes, even_ref, *low)
        place_planes(ext, middle + planes, odd_ref, *high)


def pack_kernel(rows_ref, column_ref, row_ref, line_ref, out_ref):
    slots = rows_ref.shape[0]
    tiles, height, _ = out_ref.shape
    ranks = (height - 8) // 4
    capacity = ranks // 2
    buckets = tiles * capacity
    chips = tiles // 2
    position = lax.axis_index("grid")
    i = lax.broadcasted_iota(jnp.int32, (slots, slots), 0)
    j = lax.broadcasted_iota(jnp.int32, (slots, slots), 1)
    ahead = jnp.where((column_ref[...] == row_ref[...]) & (i < j), 1.0, 0.0)
    rank = jnp.sum(ahead, axis=0, keepdims=True).astype(jnp.int32)
    place = row_ref[...] * capacity + rank
    bucket = lax.broadcasted_iota(jnp.int32, (buckets, slots), 0)
    pick = bucket == place
    packed = dot(pick.astype(jnp.float32), rows_ref[...])
    for chip in range(chips):
        for p in range(2):
            for q in range(4):
                out_ref[2 * chip + p, q * ranks : (q + 1) * ranks] = packed[
                    chip * ranks : (chip + 1) * ranks, (4 * p + q) * 128 : (4 * p + q + 1) * 128
                ]
    thick_lines = 64
    line = jnp.sum(jnp.where(pick, line_ref[...] + 1, 0).astype(jnp.float32), axis=1, keepdims=True)
    own = lax.broadcasted_iota(jnp.int32, (buckets, 1), 0) // capacity % 2
    line = jnp.where(line > 0, line + (own * thick_lines).astype(jnp.float32), 0.0)
    bucket = lax.broadcasted_iota(jnp.int32, (buckets, 128), 0)
    lane = lax.broadcasted_iota(jnp.int32, (buckets, 128), 1)
    start = lax.rem(position, 128 // ranks) * ranks
    spots = jnp.where(lane - start == bucket % ranks, line, 0.0)
    i = lax.broadcasted_iota(jnp.int32, (chips, buckets), 0)
    j = lax.broadcasted_iota(jnp.int32, (chips, buckets), 1)
    numbers = dot(jnp.where(i == j // ranks, 1.0, 0.0), spots)
    for chip in range(chips):
        value = jnp.broadcast_to(numbers[chip : chip + 1], (8, 128))
        for p in range(2):
            out_ref[2 * chip + p, 4 * ranks :] = value


def density_kernel(pd_ref, other_ref, received_ref, f_ref, inner_ref, outer_ref, b1, half):
    position = lax.axis_index("grid")
    core, side = lax.rem(position, 2), lax.rem(lax.div(position, 2), 2)
    planes, _, lines, depth = f_ref.shape
    sources, height, _ = received_ref.shape
    ranks = (height - 8) // 4
    group = 128 // ranks
    added = [None, None]
    for first in range(0, sources, group):
        count = min(group, sources - first)
        numbers = received_ref[first, 4 * ranks : 4 * ranks + 1]
        for k in range(1, count):
            numbers = numbers + received_ref[first + k, 4 * ranks : 4 * ranks + 1]
        line = lax.broadcasted_iota(jnp.int32, (planes * lines, 128), 0)
        spread = jnp.where(line == numbers.astype(jnp.int32) - 1, 1.0, 0.0)
        for part in range(2):
            values = jnp.concatenate(
                [
                    received_ref[first : first + count, q * ranks : (q + 1) * ranks].reshape(
                        count * ranks, 128
                    )
                    for q in (2 * part, 2 * part + 1)
                ],
                axis=1,
            )
            value = dot(spread[:, : count * ranks], values)
            added[part] = value if added[part] is None else added[part] + value
    for x in range(planes):
        for part in range(2):
            f_ref[x, part] = added[part][x * lines : (x + 1) * lines]
    thick = planes // 2
    for x in range(thick):
        for part in range(2):
            f_ref[core * thick + x, part] += pd_ref[core, part, x]
            f_ref[(1 - core) * thick + x, part] += other_ref[part, x]

    def density(x, part):
        return f_ref[x, part] if 0 <= x < planes else None

    def once(x, part):
        return b1[x + 2, part] if -2 <= x < planes + 2 else None

    for x in range(-2, planes + 2):
        for part in range(2):
            b1[x + 2, part] = smooth_fine(density, x, part)
    rows = (planes + 8) // 2 * 2
    for i in range(rows // 2):
        for part in range(2):
            total = smooth_fine(once, 2 * i - 4, part) + smooth_fine(once, 2 * i - 3, part)
            for h in range(2):
                half[(2 * i + part) * 2 + h] = total[:, h * 128 : (h + 1) * 128]
    matrix = pair_matrix(depth, depth // 2, 0.125)
    total = None
    for h in range(2):
        stacked = jnp.concatenate(
            [
                half[2 * r + h, pl.ds(0, lines // 2, 2)] + half[2 * r + h, pl.ds(1, lines // 2, 2)]
                for r in range(rows)
            ],
            axis=0,
        )
        value = dot(stacked, matrix[h * 128 : (h + 1) * 128])
        total = value if total is None else total + value

    def coarse(r):
        return total[r * lines // 2 : (r + 1) * lines // 2]

    @pl.when(side == 0)
    def _():
        for r in range(8):
            inner_ref[r // 2, r % 2] = coarse(4 + r)
        for r in range(4):
            outer_ref[r // 2, r % 2] = coarse(r)

    @pl.when(side == 1)
    def _():
        for r in range(8):
            inner_ref[r // 2, r % 2] = coarse(r)
        for r in range(4):
            outer_ref[r // 2, r % 2] = coarse(8 + r)


def source_kernel(own_ref, partner_ref, straight_ref, across_ref, cs_ref, s_ref):
    position = lax.axis_index("grid")
    blocks = lax.axis_size("grid") // 4
    core, side, block = lax.rem(position, 2), lax.rem(lax.div(position, 2), 2), lax.div(position, 4)
    cosine, sine = cs_ref[core], cs_ref[2 + core]
    first, last = block == 0, block == blocks - 1
    low = (jnp.where(first, cosine, 1.0), jnp.where(first, -sine, 0.0))
    high = (jnp.where(last, cosine, 1.0), jnp.where(last, sine, 0.0))

    def total(low_ref, high_ref):
        for x in range(4):
            source, (c, s) = (low_ref, low) if x < 2 else (high_ref, high)
            real, imag = rotated(source[x % 2, 0], source[x % 2, 1], c, s)
            s_ref[x, 0] = own_ref[x, 0] + partner_ref[x, 0] + real
            s_ref[x, 1] = own_ref[x, 1] + partner_ref[x, 1] + imag

    @pl.when(side == 0)
    def _():
        total(across_ref, straight_ref)

    @pl.when(side == 1)
    def _():
        total(straight_ref, across_ref)


def fine_kernel(
    even_ref, odd_ref, after_ref, before_ref, f_ref, cs_ref, own_ref, send_ref, ext, b1, b2, g
):
    position = lax.axis_index("grid")
    chips = lax.axis_size("grid") // 2
    core, chip = lax.rem(position, 2), lax.div(position, 2)
    cosine, sine = cs_ref[core], cs_ref[2 + core]
    planes = f_ref.shape[0]
    place_halo(ext, planes + 2, even_ref, odd_ref, cs_ref)
    ext[planes + 2 : 2 * planes + 2] = f_ref[...]
    first, last = chip < 2, chip >= chips - 2
    place_planes(
        ext, 0, before_ref, jnp.where(first, cosine, 1.0), jnp.where(first, -sine, 0.0)
    )
    place_planes(
        ext,
        3 * planes + 2,
        after_ref,
        jnp.where(last, cosine, 1.0),
        jnp.where(last, sine, 0.0),
    )
    for x in range(planes + 8):
        for part in range(2):
            b1[x, part] = smooth_fine(lambda i, p: ext[i, p], x + 2, part)
    for x in range(planes + 4):
        for part in range(2):
            b2[x, part] = smooth_fine(lambda i, p: b1[i, p], x + 2, part)
    for x in range(planes):
        for part in range(2):
            b3 = smooth_fine(lambda i, p: b2[i, p], x + 2, part)
            g[x, part] = fine_scale * (f_ref[x, part] + b1[x + 4, part] + b2[x + 2, part] + b3)
    half = planes // 2
    for x in range(half):
        own_ref[x] = g[core * half + x]
        send_ref[x] = g[(1 - core) * half + x]


def shift_z(v, step):
    width = v.shape[-1] // 2
    lane = lax.broadcasted_iota(jnp.int32, v.shape, len(v.shape) - 1)
    edge = 0 if step > 0 else width - 1
    inner = roll(v, step, 1)
    outer = roll(v, step + (width if step > 0 else -width), 1)
    return jnp.where(lane % width == edge, outer, inner)


def packed_sweep(values, count, depth, source, target, cosine, sine, residual=False):
    rate, near_rate = level_numbers(depth)
    values[0] = cosine * values[count] - sine * roll(values[count], 64, 1)
    values[count + 1] = cosine * values[1] + sine * roll(values[1], 64, 1)

    def body(x):
        v = values[x + 1]
        near = values[x] + values[x + 2]
        near = near + (roll(v, 1, 0) + roll(v, -1, 0))
        near = near + (shift_z(v, 1) + shift_z(v, -1))
        if residual:
            target[x] = source[x] - omega / rate * v + near_rate / rate * near
        else:
            target[x + 1] = rate * source[x] + keep * v + near_rate * near

    each(count, body)


def first_sweep(values, count, depth, source):
    rate, _ = level_numbers(depth)

    def body(x):
        values[x + 1] = rate * source[x]

    each(count, body)


def cycle_kernel(*refs):
    radix = len(refs) - 14
    pieces, refs = refs[:radix], refs[radix:]
    cs_ref, own_ref, send_ref, s, u, v, r1, s2, u2, v2, r2, s3, u3, v3 = refs
    position = lax.axis_index("grid")
    core, block = lax.rem(position, 2), lax.div(position, 4)
    count = s.shape[0]
    rate, near_rate = level_numbers(1)
    cosine, sine = cs_ref[core], cs_ref[2 + core]
    lane = lax.broadcasted_iota(jnp.int32, (8, 128), 1)
    lane_sine = jnp.where(lane < 64, -sine, sine)

    length = count // radix
    digit = lax.div(block, length // 4)
    for k, piece in enumerate(pieces):
        s[pl.ds(lax.rem(digit + k, radix) * length, length)] = piece[...]

    def sweep(values, target, residual=False):
        values[0, 0], values[0, 1] = rotated(values[count, 0], values[count, 1], cosine, -sine)
        values[count + 1, 0], values[count + 1, 1] = rotated(
            values[1, 0], values[1, 1], cosine, sine
        )

        def body(x):
            for f in range(2):
                a = values[x + 1, f]
                near = values[x, f] + values[x + 2, f]
                near = near + (roll(a, 1, 0) + roll(a, -1, 0))
                near = near + (roll(a, 1, 1) + roll(a, -1, 1))
                if residual:
                    target[x, f] = s[x, f] - omega / rate * a + near_rate / rate * near
                else:
                    target[x + 1, f] = rate * s[x, f] + keep * a + near_rate * near

        each(count, body)

    def start(x):
        for f in range(2):
            u[x + 1, f] = rate * s[x, f]

    each(count, start)
    sweep(u, v)
    sweep(v, r1, residual=True)

    count2 = count // 2
    i = lax.broadcasted_iota(jnp.int32, (128, 128), 0)
    j = lax.broadcasted_iota(jnp.int32, (128, 128), 1)
    rows = []
    for f in range(2):

        def lower(x):
            r1[2 * x, f] = r1[2 * x, f] + r1[2 * x + 1, f]
            r2[x, 8 * f : 8 * f + 8] = r1[2 * x, f, pl.ds(0, 8, 2)] + r1[2 * x, f, pl.ds(1, 8, 2)]

        each(count2, lower)
        rows.append(r2[:, 8 * f : 8 * f + 8].reshape(count2 * 8, 128))
    lowered = sum(
        dot(rows[f], jnp.where(i // 2 + 64 * f == j, 0.125, 0.0)) for f in range(2)
    )
    s2[...] = lowered.reshape(count2, 8, 128)
    first_sweep(u2, count2, 2, s2)
    packed_sweep(u2, count2, 2, s2, v2, cosine, lane_sine)
    packed_sweep(v2, count2, 2, s2, u2, cosine, lane_sine, residual=True)

    count3 = count2 // 2

    def lower3(x):
        total = u2[2 * x] + u2[2 * x + 1]
        r2[x, 0:8] = total
        r2[x, 8:16] = total
        s3[x] = r2[x, pl.ds(0, 8, 2)] + r2[x, pl.ds(1, 8, 2)]

    each(count3, lower3)
    same = i // 64 == j // 64
    lowered = dot(
        s3[...].reshape(count3 * 8, 128), jnp.where(same & (i % 64 // 2 == j % 32), 0.125, 0.0)
    )
    s3[...] = lowered.reshape(count3, 8, 128)
    first_sweep(u3, count3, 3, s3)
    a, b = u3, v3
    for _ in range(5):
        packed_sweep(a, count3, 3, s3, b, cosine, lane_sine)
        a, b = b, a

    raised = dot(
        a[1 : count3 + 1].reshape(count3 * 8, 128),
        jnp.where(same & (i % 64 == j % 64 // 2), 1.0, 0.0),
    )
    s3[...] = raised.reshape(count3, 8, 128)

    def raise3(x):
        r2[x, pl.ds(0, 8, 2)] = s3[x]
        r2[x, pl.ds(1, 8, 2)] = s3[x]
        for k in range(2):
            v2[2 * x + k + 1] = v2[2 * x + k + 1] + r2[x, 0:8]

    each(count3, raise3)
    packed_sweep(v2, count2, 2, s2, u2, cosine, lane_sine)
    packed_sweep(u2, count2, 2, s2, v2, cosine, lane_sine)

    rows = v2[1 : count2 + 1].reshape(count2 * 8, 128)
    for f in range(2):
        raised = dot(rows, jnp.where(i == j // 2 + 64 * f, 1.0, 0.0))
        s2[...] = raised.reshape(count2, 8, 128)

        def raise2(x):
            r1[x, f, pl.ds(0, 8, 2)] = s2[x]
            r1[x, f, pl.ds(1, 8, 2)] = s2[x]
            for k in range(2):
                v[2 * x + k + 1, f] = v[2 * x + k + 1, f] + r1[x, f]

        each(count2, raise2)
    sweep(v, u)
    sweep(u, v)

    for target, tile in ((own_ref, position), (send_ref, position + 1 - 2 * core)):
        for k in range(5):
            q = tile + k - 2
            low, high = q < 0, q >= count
            q = jnp.where(low, q + count, jnp.where(high, q - count, q))
            c = jnp.where(low | high, cosine, 1.0)
            t = jnp.where(low, -sine, jnp.where(high, sine, 0.0))
            target[k, 0], target[k, 1] = rotated(v[q + 1, 0], v[q + 1, 1], c, t)


def correct(w_ref, g_ref, e, b1, store):
    lines = w_ref.shape[2]
    wide = dot(w_ref[...].reshape(10 * lines, 128), spread_matrix(128, 256))
    for r in range(10):
        for h in range(2):
            value = wide[r * lines : (r + 1) * lines, 128 * h : 128 * (h + 1)]
            e[2 * r + h, pl.ds(0, lines, 2)] = value
            e[2 * r + h, pl.ds(1, lines, 2)] = value

    def expanded(x, f):
        place = (2 * (x // 2) + f) * 2
        return jnp.concatenate([e[place], e[place + 1]], axis=1)

    for x in range(6):
        for f in range(2):
            b1[x, f] = smooth_fine(expanded, x + 2, f)
    for x in range(2):
        for f in range(2):
            store(f, x, g_ref[x, f] + smooth_fine(lambda i, g: b1[i, g], x + 2, f))


def own_kernel(w_ref, g_ref, out_ref, e, b1):
    def store(part, x, value):
        out_ref[part, x] = value

    correct(w_ref, g_ref, e, b1, store)


def output_kernel(own_ref, w_ref, g_ref, out_ref, e, b1):
    core = lax.rem(lax.axis_index("grid"), 2)
    out_ref[core] = own_ref[...]

    def store(part, x, value):
        out_ref[1 - core, part, x] = value

    correct(w_ref, g_ref, e, b1, store)


def pair_phases(pair_table, k_fraction):
    kcount = k_fraction.shape[0]
    picks = pair_table[:, :, None] == jnp.arange(kcount, dtype=jnp.int32)[None, None, :]
    chosen = jnp.sum(jnp.where(picks, k_fraction[None, None, :], 0.0), axis=2)
    angle = 6.283185307179586 * (chosen[:, 0] - chosen[:, 1])
    return jnp.concatenate([jnp.cos(angle), jnp.sin(angle)])


def make_rows(moments, shapes, slot_atom):
    slot_count = shapes.shape[0]
    atom_count = moments.shape[0]
    atom_pick = (slot_atom[:, None] == jnp.arange(atom_count, dtype=jnp.int32)[None, :]).astype(
        jnp.float32
    )
    chosen = jnp.dot(atom_pick, moments.reshape(atom_count, -1), precision=highest)
    chosen = chosen.reshape(slot_count, moments.shape[1] * moments.shape[2], moments.shape[3])
    return jnp.einsum("sfl,slz->sfz", chosen, shapes, precision=highest).reshape(slot_count, -1)


def gather_blocks(value, blocks, block, permute_block):
    stride = 1
    while True:
        radix = min(4, blocks // stride)
        digit = block // stride % radix

        def towards(k):
            def target(b):
                own = b // stride % radix
                return b + ((own - k) % radix - own) * stride

            return target

        pieces = [value] + [permute_block(value, towards(k)) for k in range(1, radix)]
        stride *= radix
        if stride == blocks:
            return pieces
        stacked = jnp.roll(jnp.stack(pieces), digit, axis=0)
        value = stacked.reshape(-1, *value.shape[1:])


def vmem(count):
    return [pl.BlockSpec(memory_space=pltpu.VMEM)] * count


smem = [pl.BlockSpec(memory_space=pltpu.SMEM)]


def call(kernel, out_shape, in_specs, scratch, flops):
    single = not isinstance(out_shape, (list, tuple))
    return pl.pallas_call(
        kernel,
        out_shape=out_shape,
        in_specs=in_specs,
        out_specs=vmem(1)[0] if single else vmem(len(out_shape)),
        scratch_shapes=[pltpu.VMEM(shape, jnp.float32) for shape in scratch],
        compiler_params=pltpu.CompilerParams(vmem_limit_bytes=48 * 2**20),
        cost_estimate=pl.CostEstimate(flops=flops, bytes_accessed=2**20, transcendentals=0),
    )


def shaped(*shape):
    return jax.ShapeDtypeStruct(shape, jnp.float32)


def per_device(
    pair_density, moments, shapes, slot_atom, slot_tile, slot_row, pair_table, k_fraction
):
    tile_count = lax.axis_size("grid")
    chips, blocks = tile_count // 2, tile_count // 4
    position = lax.axis_index("grid")
    core, block = position % 2, position // 4
    _, _, thick, lines, depth = pair_density.shape
    planes = 2 * thick
    slot_count = shapes.shape[0]
    capacity = max(2, 2 * slot_count // tile_count)
    devices = range(tile_count)

    def permute(value, target):
        return lax.ppermute(value, "grid", [(i, target(i)) for i in devices])

    def permute_block(value, target):
        return permute(value, lambda i: target(i // 4) * 4 + i % 4)

    def partner(i):
        return i ^ 1

    def even_side(i):
        return i ^ 2

    def odd_side(i):
        return (i // 2 + (1 if i // 2 % 2 else -1)) % chips * 2 + i % 2

    def next_block(i):
        return (i + (4 if i // 2 % 2 else -4)) % tile_count

    cs = pair_phases(pair_table, k_fraction)

    other = permute(lax.dynamic_index_in_dim(pair_density, 1 - core, 0, False), partner)
    rows = make_rows(moments, shapes, slot_atom)
    packed = call(pack_kernel, shaped(tile_count, 8 * capacity + 8, 128), vmem(4), [], 10**8)(
        rows, slot_tile, slot_tile.reshape(1, -1), slot_row.reshape(1, -1)
    )
    received = lax.all_to_all(packed, "grid", split_axis=0, concat_axis=0, tiled=True)

    full = (2, lines, depth)
    small = (2, lines // 2, depth // 2)
    f, inner, outer = call(
        density_kernel,
        [shaped(planes, *full), shaped(4, *small), shaped(2, *small)],
        vmem(3),
        [(planes + 4, *full), (2 * (planes + 8), lines, 128)],
        10**8,
    )(pair_density, other, received)
    source = call(source_kernel, shaped(4, *small), vmem(4) + smem, [], 10**6)(
        inner, permute(inner, even_side), permute(outer, next_block), permute(outer, odd_side), cs
    )
    pieces = gather_blocks(source, blocks, block, permute_block)

    even = permute(f, even_side)
    odd = permute(f, odd_side)
    after = permute(f[:thick], lambda i: (i - 4) % tile_count)
    before = permute(f[thick:], lambda i: (i + 4) % tile_count)
    own, send = call(
        fine_kernel,
        [shaped(thick, *full)] * 2,
        vmem(5) + smem,
        [(3 * planes + 4, *full), (planes + 8, *full), (planes + 4, *full), (planes, *full)],
        10**7,
    )(even, odd, after, before, f, cs)
    got = permute(send, partner)

    n1, n2, n3 = tile_count, tile_count // 2, tile_count // 4
    tile = (8, 128)
    w_own, w_send = call(
        cycle_kernel,
        [shaped(5, *small)] * 2,
        vmem(len(pieces)) + smem,
        [
            (n1, *small),
            (n1 + 2, *small),
            (n1 + 2, *small),
            (n1, *small),
            (n2, *tile),
            (n2 + 2, *tile),
            (n2 + 2, *tile),
            (n2, 16, 128),
            (n3, *tile),
            (n3 + 2, *tile),
            (n3 + 2, *tile),
        ],
        10**8,
    )(*pieces, cs)
    w_got = permute(w_send, partner)
    scratch = [(20, lines, 128), (6, *full)]
    result = call(own_kernel, shaped(2, thick, lines, depth), vmem(2), scratch, 10**7)(w_own, own)
    return call(output_kernel, shaped(*pair_density.shape), vmem(3), scratch, 10**7)(
        result, w_got, got
    )


def solution(mesh):
    return jax.shard_map(
        per_device,
        mesh=mesh,
        in_specs=(
            P("rep", None, "grid", None, None),
            P(("rep", "grid"), None, None, None),
            P(("rep", "grid"), None, None),
            P(("rep", "grid")),
            P(("rep", "grid"), None),
            P(("rep", "grid")),
            P(),
            P(),
        ),
        out_specs=P("rep", None, "grid", None, None),
        check_vma=False,
    )
```

time: 90.2 us -> 64.3 us (0.71)
  blocking collectives: 46.1 us -> 0 us
  waiting for transfers between devices: 9.22 us -> 24.9 us
  starting transfers between devices: 14 us -> 22.2 us
  matrix products: 4.12 us -> 2.92 us
  other arithmetic: 1.62 us -> 0.45 us
  Pallas kernels: 13.1 us -> 12 us
    all_gather x2 -> x0, blocking collectives: 46.1 us -> none  [the longest x1 24.4 us: per_device(): every = lax.all_gather(targets, 'grid', axis=0)]
    all_to_all x1, waiting for transfers between devices: 0.01 us -> 14.1 us  [per_device(): lax.all_to_all(packed, 'grid', split_axis=0, concat_axis=0, tiled=True)]
    ppermute x6 -> x13, starting transfers between devices: 6.69 us -> 14.8 us  [permute(): return lax.ppermute(value, 'grid', [(i, target(i)) for i in devices])]
    ppermute x6 -> x13, waiting for transfers between devices: 9.22 us -> 10.8 us  [permute(): return lax.ppermute(value, 'grid', [(i, target(i)) for i in devices])]
    dot_general x2 -> x1, matrix products: 3.21 us -> 2.01 us  [make_rows(): jnp.einsum('sfl,slz->sfz', chosen, shapes, precision=highest)]
    reduce_sum x2 -> x0, other arithmetic: 1.06 us -> none  [the longest x1 0.97 us: make_rows(): ranks = jnp.sum(before.astype(jnp.int32), axis=1)]
    pallas_call x4 -> x7, Pallas kernels: 13.1 us -> 12 us  [the longest x1 2.92 us: per_device(): call(cycle_kernel, [shaped(5, *small)] * 2, vmem(len(pieces)) + smem, [(n...]
  transfers between devices with their start and end apart: 7 -> 14, of which waited for: 3 -> 7; matrix products, arithmetic and copies ran while one was open for 1% -> 1% of each run, Pallas kernels for 2% -> 11%
where the time goes in v2:
time: 64.3 us; the launch traced here: 64 us
  waiting for transfers between devices  24.9 us (39%)
  starting transfers between devices  22.2 us (35%)
  Pallas kernels  12 us (19%)
  matrix products  2.92 us (5%)
  local copies, waits for them, and re-layouts  1.36 us (2%)
    ppermute x13, starting transfers between devices, permute(): return lax.ppermute(value, 'grid', [(i, target(i)) for i in devices])  14.8 us
    all_to_all x1, waiting for transfers between devices, per_device(): lax.all_to_all(packed, 'grid', split_axis=0, concat_axis=0, tiled=True)  14.1 us
    ppermute x13, waiting for transfers between devices, permute(): return lax.ppermute(value, 'grid', [(i, target(i)) for i in devices])  10.8 us
    all_to_all x1, starting transfers between devices, per_device(): lax.all_to_all(packed, 'grid', split_axis=0, concat_axis=0, tiled=True)  7.35 us
    pallas_call x1, Pallas kernels, per_device(): call(cycle_kernel, [shaped(5, *small)] * 2, vmem(len(pieces)) + smem, [(n...  2.92 us
    pallas_call x1, Pallas kernels, per_device(): call(fine_kernel, [shaped(thick, *full)] * 2, vmem(5) + smem, [(3 * plane...  2.51 us
    dot_general x1, matrix products, make_rows(): jnp.einsum('sfl,slz->sfz', chosen, shapes, precision=highest)  2.01 us
    pallas_call x1, Pallas kernels, per_device(): call(density_kernel, [shaped(planes, *full), shaped(4, *small), shaped(2,...  2 us
  transfers between devices with their start and end apart: 14, of which 7 were waited for; matrix products, arithmetic and copies ran while one was open for 1% of the time, Pallas kernels for 11%

profile of v2, /device:TPU:0, one launch (start us, length us, event | category | flops | bytes accessed | tf_op | source)
XLA Modules:
  0.0 64.0 jit_solution(9413349194482235236)
XLA Ops:
  0.0 0.9 %reshape.22 = f32[12,100]{1,0:T(8,128)S(1)} reshape(f32[12,2,2,25]{3,2,1,0:T(2,128)} %param.9) | data formatting | bytes 9600 | tf_op jit(solution)/shard_map/reshape | solution.py:498
  0.9 0.1 dot_general.11
  1.0 0.9 %fusion.2 = f32[64,4,25]{0,2,1:T(8,128)S(1)} fusion(f32[4,25,12]{1,0,2:T(4,128)S(1)} %dot_general.11, s32[64]{0:T(128)} %param.11), kind=kOutput, calls=%fused_computation.3 | convolution fusion | flops 922368 | bytes 30656 | tf_op jit(solution)/shard_map/dot_general | solution.py:498
  2.0 0.0 copy-start.3
  2.0 0.1 copy.17
  2.1 2.0 %fusion = f32[64,4,256]{2,1,0:T(4,128)S(1)} fusion(f32[64,4,25]{2,1,0:T(4,128)S(1)} %copy.17, f32[64,25,256]{2,0,1:T(8,128)S(1)} %copy-done), kind=kOutput, calls=%fused_computation | convolution fusion | flops 19660800 | bytes 1926144 | tf_op jit(solution)/shard_map/sfl,slz->sfz/dot_general | solution.py:500
  4.1 0.0 copy-start.1
  4.1 0.0 copy-start.4
  4.1 0.0 copy-start.5
  4.2 0.1 copy.19.column_ref
  4.3 1.5 %shard_map.82 = f32[16,72,128]{2,1,0:T(8,128)} custom-call(f32[64,1024]{1,0:T(8,128)S(1)} %bitcast.13, s32[64,1]{1,0:T(8,128)S(1)} %copy.19.column_ref, s32[1,64]{1,0:T(1,128)S(1)} %bitcast.14, s32[1,64]{1,0:T(1,128)S(1)} %bitcast.15), custom_call_target="tpu_custom_call" | custom-call | flops 100000000 | bytes 1048576 | tf_op jit(solution)/shard_map/pallas_call | solution.py:583
  5.8 7.4 %all-to-all-start = ((f32[16,72,128]{2,1,0:T(8,128)}), f32[16,72,128]{2,1,0:T(8,128)S(1)}, u32[]{:S(2)}, u32[]{:S(2)}) async-start(f32[16,72,128]{2,1,0:T(8,128)} %shard_map.82), calls=%async_computation | async-start | bytes 1179648 | tf_op jit(solution)/shard_map/all_to_all | solution.py:586
  13.2 0.5 collective-permute-start
  13.7 0.2 fusion.7
  13.8 0.8 %collective-permute-done.other_ref = f32[2,2,32,256]{3,2,1,0:T(8,128)S(1)} collective-permute-done((f32[2,2,32,256]{3,2,1,0:T(8,128)S(1)}, f32[2,2,32,256]{3,2,1,0:T(8,128)S(1)}, u32[]{:S(2)}, u32[]{:S(2)}) %collective-permute-start) | collective-permute-done | bytes 131104 | tf_op jit(solution)/shard_map/ppermute | solution.py:562
  14.7 14.1 %all-to-all-done.received_ref = f32[16,72,128]{2,1,0:T(8,128)S(1)} async-done(((f32[16,72,128]{2,1,0:T(8,128)}), f32[16,72,128]{2,1,0:T(8,128)S(1)}, u32[]{:S(2)}, u32[]{:S(2)}) %all-to-all-start) | async-done | bytes 589856 | tf_op jit(solution)/shard_map/all_to_all | solution.py:586
  28.7 2.0 %shard_map.83 = (f32[4,2,32,256]{3,2,1,0:T(8,128)S(1)}, f32[4,2,16,128]{3,2,1,0:T(8,128)S(1)}, f32[2,2,16,128]{3,2,1,0:T(8,128)S(1)}) custom-call(f32[2,2,2,32,256]{4,3,2,1,0:T(8,128)S(1)} %copy-done.1, f32[2,2,32,256]{3,2,1,0:T(8,128)S(1)} %collective-permute-done.other_ref, f32[16,72,128]{2,1,0:T(8,128)S(1)} %all-to-all-done.received_ref), custom_call_target="tpu_custom_call" | custom-call | flops 100000000 | bytes 1048576 | tf_op jit(solution)/shard_map/pallas_call | solution.py:590
  30.7 0.6 %collective-permute-start.7 = (f32[4,2,32,256]{3,2,1,0:T(8,128)S(1)}, f32[4,2,32,256]{3,2,1,0:T(8,128)S(1)}, u32[]{:S(2)}, u32[]{:S(2)}) collective-permute-start(f32[4,2,32,256]{3,2,1,0:T(8,128)S(1)} %get-tuple-element.15.f_ref), channel_id=1, source_target_pairs={{0,2},{1,3},{2,0},{3,1},{4,6},{5,7},{6,4},{7,5},{8,10},{9,11},{10,... | collective-permute-start | bytes 786440 | tf_op jit(solution)/shard_map/ppermute | solution.py:562
  31.4 2.5 %collective-permute-start.8 = (f32[4,2,32,256]{3,2,1,0:T(8,128)S(1)}, f32[4,2,32,256]{3,2,1,0:T(8,128)S(1)}, u32[]{:S(2)}, u32[]{:S(2)}) collective-permute-start(f32[4,2,32,256]{3,2,1,0:T(8,128)S(1)} %get-tuple-element.15.f_ref), channel_id=1, source_target_pairs={{0,14},{1,15},{2,4},{3,5},{4,2},{5,3},{6,8},{7,9},{8,6},{9,7},{10,... | collective-permute-start | bytes 786440 | tf_op jit(solution)/shard_map/ppermute | solution.py:562
  33.9 2.4 %collective-permute-start.2 = (f32[2,2,16,128]{3,2,1,0:T(8,128)S(1)}, f32[2,2,16,128]{3,2,1,0:T(8,128)S(1)}, u32[]{:S(2)}, u32[]{:S(2)}) collective-permute-start(f32[2,2,16,128]{3,2,1,0:T(8,128)S(1)} %get-tuple-element.13), channel_id=1, source_target_pairs={{0,12},{1,13},{2,6},{3,7},{4,0},{5,1},{6,10},{7,11},{8,4},{9,5},{1... | collective-permute-start | bytes 98312 | tf_op jit(solution)/shard_map/ppermute | solution.py:562
  36.3 2.0 %collective-permute-start.3 = (f32[2,2,16,128]{3,2,1,0:T(8,128)S(1)}, f32[2,2,16,128]{3,2,1,0:T(8,128)S(1)}, u32[]{:S(2)}, u32[]{:S(2)}) collective-permute-start(f32[2,2,16,128]{3,2,1,0:T(8,128)S(1)} %get-tuple-element.13), channel_id=1, source_target_pairs={{0,14},{1,15},{2,4},{3,5},{4,2},{5,3},{6,8},{7,9},{8,6},{9,7},{10,... | collective-permute-start | bytes 98312 | tf_op jit(solution)/shard_map/ppermute | solution.py:562
  38.3 0.0 collective-permute-start.10
  38.3 3.0 %collective-permute-done.2.straight_ref = f32[2,2,16,128]{3,2,1,0:T(8,128)S(1)} collective-permute-done((f32[2,2,16,128]{3,2,1,0:T(8,128)S(1)}, f32[2,2,16,128]{3,2,1,0:T(8,128)S(1)}, u32[]{:S(2)}, u32[]{:S(2)}) %collective-permute-start.2) | collective-permute-done | bytes 32800 | tf_op jit(solution)/shard_map/ppermute | solution.py:562
  41.3 4.3 %collective-permute-start.9 = (f32[2,2,32,256]{3,2,1,0:T(8,128)S(1)}, f32[2,2,32,256]{3,2,1,0:T(8,128)S(1)}, u32[]{:S(2)}, u32[]{:S(2)}) collective-permute-start(f32[2,2,32,256]{3,2,1,0:T(8,128)S(1)} %get-tuple-element.22), channel_id=1, source_target_pairs={{0,12},{1,13},{2,14},{3,15},{4,0},{5,1},{6,2},{7,3},{8,4},{9,5},{1... | collective-permute-start | bytes 393224 | tf_op jit(solution)/shard_map/ppermute | solution.py:562
  45.6 0.2 cosine_reduce_fusion
  45.8 0.0 collective-permute-done.3.across_ref
  45.8 0.3 collective-permute-start.1
  46.1 0.1 pad_maximum_fusion.cs_ref.refs_4_
  46.2 4.0 %collective-permute-done.1.partner_ref = f32[4,2,16,128]{3,2,1,0:T(8,128)S(1)} collective-permute-done((f32[4,2,16,128]{3,2,1,0:T(8,128)S(1)}, f32[4,2,16,128]{3,2,1,0:T(8,128)S(1)}, u32[]{:S(2)}, u32[]{:S(2)}) %collective-permute-start.1) | collective-permute-done | bytes 65568 | tf_op jit(solution)/shard_map/ppermute | solution.py:562
  50.2 0.6 shard_map.84.refs_0_
  50.7 0.1 collective-permute-start.4
  50.8 0.0 collective-permute-done.10.before_ref
  50.8 0.6 collective-permute-start.5
  51.4 0.0 collective-permute-done.9.after_ref
  51.4 1.5 %collective-permute-start.6 = (f32[4,2,16,128]{3,2,1,0:T(8,128)S(1)}, f32[4,2,16,128]{3,2,1,0:T(8,128)S(1)}, u32[]{:S(2)}, u32[]{:S(2)}) collective-permute-start(f32[4,2,16,128]{3,2,1,0:T(8,128)S(1)} %shard_map.84.refs_0_), channel_id=1, source_target_pairs={{0,4},{1,5},{2,6},{3,7},{4,8},{5,9},{6,10},{7,11},{8,12},{9,13},{1... | collective-permute-start | bytes 196616 | tf_op jit(solution)/shard_map/ppermute | solution.py:562
  52.9 0.0 collective-permute-done.7.even_ref
  52.9 0.0 collective-permute-done.8.odd_ref
  52.9 2.5 %shard_map.86 = (f32[2,2,32,256]{3,2,1,0:T(8,128)S(1)}, f32[2,2,32,256]{3,2,1,0:T(8,128)S(1)}) custom-call(f32[4,2,32,256]{3,2,1,0:T(8,128)S(1)} %collective-permute-done.7.even_ref, f32[4,2,32,256]{3,2,1,0:T(8,128)S(1)} %collective-permute-done.8.odd_ref, f32[2,2,32,256]{3,2,1,0:T(8,128)S(1)} %collective-permute-done.9.after_ref, ...), custom_call_target="tpu_custom_call" | custom-call | flops 10000000 | bytes 1048576 | tf_op jit(solution)/shard_map/pallas_call | solution.py:606
  55.4 0.1 collective-permute-start.12
  55.5 0.9 %collective-permute-done.4.refs_1_ = f32[4,2,16,128]{3,2,1,0:T(8,128)S(1)} collective-permute-done((f32[4,2,16,128]{3,2,1,0:T(8,128)S(1)}, f32[4,2,16,128]{3,2,1,0:T(8,128)S(1)}, u32[]{:S(2)}, u32[]{:S(2)}) %collective-permute-start.4) | collective-permute-done | bytes 65568 | tf_op jit(solution)/shard_map/ppermute | solution.py:562
  56.4 0.0 collective-permute-done.5.refs_2_
  56.4 1.8 %collective-permute-done.6.refs_3_ = f32[4,2,16,128]{3,2,1,0:T(8,128)S(1)} collective-permute-done((f32[4,2,16,128]{3,2,1,0:T(8,128)S(1)}, f32[4,2,16,128]{3,2,1,0:T(8,128)S(1)}, u32[]{:S(2)}, u32[]{:S(2)}) %collective-permute-start.6) | collective-permute-done | bytes 65568 | tf_op jit(solution)/shard_map/ppermute | solution.py:562
  58.1 2.9 %shard_map.85 = (f32[5,2,16,128]{3,2,1,0:T(8,128)S(1)}, f32[5,2,16,128]{3,2,1,0:T(8,128)S(1)}) custom-call(f32[4,2,16,128]{3,2,1,0:T(8,128)S(1)} %shard_map.84.refs_0_, f32[4,2,16,128]{3,2,1,0:T(8,128)S(1)} %collective-permute-done.4.refs_1_, f32[4,2,16,128]{3,2,1,0:T(8,128)S(1)} %collective-permute-done.5.refs_2_, ...), custom_call_target="tpu_custom_call" | custom-call | flops 100000000 | bytes 1048576 | tf_op jit(solution)/shard_map/pallas_call | solution.py:617
  61.1 0.1 collective-permute-start.11
  61.1 0.9 %shard_map.87.own_ref = f32[2,2,32,256]{3,2,1,0:T(8,128)S(1)} custom-call(f32[5,2,16,128]{3,2,1,0:T(8,128)S(1)} %get-tuple-element.14.w_ref, f32[2,2,32,256]{3,2,1,0:T(8,128)S(1)} %get-tuple-element.16.g_ref), custom_call_target="tpu_custom_call" | custom-call | flops 10000000 | bytes 1048576 | tf_op jit(solution)/shard_map/pallas_call | solution.py:638
  62.0 0.4 collective-permute-done.11.w_ref
  62.4 0.0 collective-permute-done.12.g_ref
  62.4 1.6 %shard_map.88 = f32[2,2,2,32,256]{4,3,2,1,0:T(8,128)} custom-call(f32[2,2,32,256]{3,2,1,0:T(8,128)S(1)} %shard_map.87.own_ref, f32[5,2,16,128]{3,2,1,0:T(8,128)S(1)} %collective-permute-done.11.w_ref, f32[2,2,32,256]{3,2,1,0:T(8,128)S(1)} %collective-permute-done.12.g_ref), custom_call_target="tpu_custom_call" | custom-call | flops 10000000 | bytes 1048576 | tf_op jit(solution)/shard_map/pallas_call | solution.py:639
  (11 shorter events, 0.1 us)
Async XLA Ops:
  0.0 2.1 %copy-start = (f32[64,25,256]{2,0,1:T(8,128)S(1)}, f32[64,25,256]{2,0,1:T(8,128)}, u32[]{:S(2)}) copy-start(f32[64,25,256]{2,0,1:T(8,128)} %param.10) | copy-start | bytes 4915204
  1.0 3.2 %copy-start.2 = (s32[64,1]{0,1:T(1,128)S(1)}, s32[64,1]{0,1:T(1,128)}, u32[]{:S(2)}) copy-start(s32[64,1]{0,1:T(1,128)} %param.12) | copy-start | bytes 772
  2.0 2.4 %copy-start.3 = (s32[64]{0:T(128)S(1)}, s32[64]{0:T(128)}, u32[]{:S(2)}) copy-start(s32[64]{0:T(128)} %param.13) | copy-start | bytes 772
  4.1 9.1 %copy-start.1 = (f32[2,2,2,32,256]{4,3,2,1,0:T(8,128)S(1)}, f32[2,2,2,32,256]{4,3,2,1,0:T(8,128)}, u32[]{:S(2)}) copy-start(f32[2,2,2,32,256]{4,3,2,1,0:T(8,128)} %pd_ref.1) | copy-start | bytes 786436
  4.1 9.6 %copy-start.4 = (s32[2,2]{1,0:T(2,128)S(1)}, s32[2,2]{1,0:T(2,128)}, u32[]{:S(2)}) copy-start(s32[2,2]{1,0:T(2,128)} %param.14) | copy-start | bytes 52
  4.1 9.6 %copy-start.5 = (f32[8]{0:T(128)S(1)}, f32[8]{0:T(128)}, u32[]{:S(2)}) copy-start(f32[8]{0:T(128)} %param.15) | copy-start | bytes 100
  5.8 22.9 %all-to-all-start = ((f32[16,72,128]{2,1,0:T(8,128)}), f32[16,72,128]{2,1,0:T(8,128)S(1)}, u32[]{:S(2)}, u32[]{:S(2)}) async-start(f32[16,72,128]{2,1,0:T(8,128)} %shard_map.82), calls=%async_computation | async-start | bytes 1179648 | tf_op jit(solution)/shard_map/all_to_all | solution.py:586
  13.2 1.4 %collective-permute-start = (f32[2,2,32,256]{3,2,1,0:T(8,128)S(1)}, f32[2,2,32,256]{3,2,1,0:T(8,128)S(1)}, u32[]{:S(2)}, u32[]{:S(2)}) collective-permute-start(f32[2,2,32,256]{3,2,1,0:T(8,128)S(1)} %dynamic-slice_bitcast_fusion), channel_id=1, source_target_pairs={{0,1},{1,0},{2,3},{3,2},{4,5},{5,4},{6,7},{7,6},{8,9},{9,8},{10,11... | collective-permute-start | bytes 393224 | tf_op jit(solution)/shard_map/ppermute | solution.py:562
  30.7 22.2 %collective-permute-start.7 = (f32[4,2,32,256]{3,2,1,0:T(8,128)S(1)}, f32[4,2,32,256]{3,2,1,0:T(8,128)S(1)}, u32[]{:S(2)}, u32[]{:S(2)}) collective-permute-start(f32[4,2,32,256]{3,2,1,0:T(8,128)S(1)} %get-tuple-element.15.f_ref), channel_id=1, source_target_pairs={{0,2},{1,3},{2,0},{3,1},{4,6},{5,7},{6,4},{7,5},{8,10},{9,11},{10,... | collective-permute-start | bytes 786440 | tf_op jit(solution)/shard_map/ppermute | solution.py:562
  31.4 21.5 %collective-permute-start.8 = (f32[4,2,32,256]{3,2,1,0:T(8,128)S(1)}, f32[4,2,32,256]{3,2,1,0:T(8,128)S(1)}, u32[]{:S(2)}, u32[]{:S(2)}) collective-permute-start(f32[4,2,32,256]{3,2,1,0:T(8,128)S(1)} %get-tuple-element.15.f_ref), channel_id=1, source_target_pairs={{0,14},{1,15},{2,4},{3,5},{4,2},{5,3},{6,8},{7,9},{8,6},{9,7},{10,... | collective-permute-start | bytes 786440 | tf_op jit(solution)/shard_map/ppermute | solution.py:562
  33.9 7.4 %collective-permute-start.2 = (f32[2,2,16,128]{3,2,1,0:T(8,128)S(1)}, f32[2,2,16,128]{3,2,1,0:T(8,128)S(1)}, u32[]{:S(2)}, u32[]{:S(2)}) collective-permute-start(f32[2,2,16,128]{3,2,1,0:T(8,128)S(1)} %get-tuple-element.13), channel_id=1, source_target_pairs={{0,12},{1,13},{2,6},{3,7},{4,0},{5,1},{6,10},{7,11},{8,4},{9,5},{1... | collective-permute-start | bytes 98312 | tf_op jit(solution)/shard_map/ppermute | solution.py:562
  36.3 9.5 %collective-permute-start.3 = (f32[2,2,16,128]{3,2,1,0:T(8,128)S(1)}, f32[2,2,16,128]{3,2,1,0:T(8,128)S(1)}, u32[]{:S(2)}, u32[]{:S(2)}) collective-permute-start(f32[2,2,16,128]{3,2,1,0:T(8,128)S(1)} %get-tuple-element.13), channel_id=1, source_target_pairs={{0,14},{1,15},{2,4},{3,5},{4,2},{5,3},{6,8},{7,9},{8,6},{9,7},{10,... | collective-permute-start | bytes 98312 | tf_op jit(solution)/shard_map/ppermute | solution.py:562
  38.3 12.5 %collective-permute-start.10 = (f32[2,2,32,256]{3,2,1,0:T(8,128)S(1)}, f32[2,2,32,256]{3,2,1,0:T(8,128)S(1)}, u32[]{:S(2)}, u32[]{:S(2)}) collective-permute-start(f32[2,2,32,256]{3,2,1,0:T(8,128)S(1)} %get-tuple-element.21), channel_id=1, source_target_pairs={{0,4},{1,5},{2,6},{3,7},{4,8},{5,9},{6,10},{7,11},{8,12},{9,13},{1... | collective-permute-start | bytes 393224 | tf_op jit(solution)/shard_map/ppermute | solution.py:562
  41.3 10.1 %collective-permute-start.9 = (f32[2,2,32,256]{3,2,1,0:T(8,128)S(1)}, f32[2,2,32,256]{3,2,1,0:T(8,128)S(1)}, u32[]{:S(2)}, u32[]{:S(2)}) collective-permute-start(f32[2,2,32,256]{3,2,1,0:T(8,128)S(1)} %get-tuple-element.22), channel_id=1, source_target_pairs={{0,12},{1,13},{2,14},{3,15},{4,0},{5,1},{6,2},{7,3},{8,4},{9,5},{1... | collective-permute-start | bytes 393224 | tf_op jit(solution)/shard_map/ppermute | solution.py:562
  45.8 4.3 %collective-permute-start.1 = (f32[4,2,16,128]{3,2,1,0:T(8,128)S(1)}, f32[4,2,16,128]{3,2,1,0:T(8,128)S(1)}, u32[]{:S(2)}, u32[]{:S(2)}) collective-permute-start(f32[4,2,16,128]{3,2,1,0:T(8,128)S(1)} %get-tuple-element.12.own_ref), channel_id=1, source_target_pairs={{0,2},{1,3},{2,0},{3,1},{4,6},{5,7},{6,4},{7,5},{8,10},{9,11},{10,... | collective-permute-start | bytes 196616 | tf_op jit(solution)/shard_map/ppermute | solution.py:562
  50.7 5.6 %collective-permute-start.4 = (f32[4,2,16,128]{3,2,1,0:T(8,128)S(1)}, f32[4,2,16,128]{3,2,1,0:T(8,128)S(1)}, u32[]{:S(2)}, u32[]{:S(2)}) collective-permute-start(f32[4,2,16,128]{3,2,1,0:T(8,128)S(1)} %shard_map.84.refs_0_), channel_id=1, source_target_pairs={{0,12},{1,13},{2,14},{3,15},{4,0},{5,1},{6,2},{7,3},{8,4},{9,5},{1... | collective-permute-start | bytes 196616 | tf_op jit(solution)/shard_map/ppermute | solution.py:562
  50.8 5.5 %collective-permute-start.5 = (f32[4,2,16,128]{3,2,1,0:T(8,128)S(1)}, f32[4,2,16,128]{3,2,1,0:T(8,128)S(1)}, u32[]{:S(2)}, u32[]{:S(2)}) collective-permute-start(f32[4,2,16,128]{3,2,1,0:T(8,128)S(1)} %shard_map.84.refs_0_), channel_id=1, source_target_pairs={{0,8},{1,9},{2,10},{3,11},{4,12},{5,13},{6,14},{7,15},{8,0},{9,1},... | collective-permute-start | bytes 196616 | tf_op jit(solution)/shard_map/ppermute | solution.py:562
  51.4 6.7 %collective-permute-start.6 = (f32[4,2,16,128]{3,2,1,0:T(8,128)S(1)}, f32[4,2,16,128]{3,2,1,0:T(8,128)S(1)}, u32[]{:S(2)}, u32[]{:S(2)}) collective-permute-start(f32[4,2,16,128]{3,2,1,0:T(8,128)S(1)} %shard_map.84.refs_0_), channel_id=1, source_target_pairs={{0,4},{1,5},{2,6},{3,7},{4,8},{5,9},{6,10},{7,11},{8,12},{9,13},{1... | collective-permute-start | bytes 196616 | tf_op jit(solution)/shard_map/ppermute | solution.py:562
  55.4 7.0 %collective-permute-start.12 = (f32[2,2,32,256]{3,2,1,0:T(8,128)S(1)}, f32[2,2,32,256]{3,2,1,0:T(8,128)S(1)}, u32[]{:S(2)}, u32[]{:S(2)}) collective-permute-start(f32[2,2,32,256]{3,2,1,0:T(8,128)S(1)} %get-tuple-element.18), channel_id=1, source_target_pairs={{0,1},{1,0},{2,3},{3,2},{4,5},{5,4},{6,7},{7,6},{8,9},{9,8},{10,11... | collective-permute-start | bytes 393224 | tf_op jit(solution)/shard_map/ppermute | solution.py:562
  61.1 1.3 %collective-permute-start.11 = (f32[5,2,16,128]{3,2,1,0:T(8,128)S(1)}, f32[5,2,16,128]{3,2,1,0:T(8,128)S(1)}, u32[]{:S(2)}, u32[]{:S(2)}) collective-permute-start(f32[5,2,16,128]{3,2,1,0:T(8,128)S(1)} %get-tuple-element.17), channel_id=1, source_target_pairs={{0,1},{1,0},{2,3},{3,2},{4,5},{5,4},{6,7},{7,6},{8,9},{9,8},{10,11... | collective-permute-start | bytes 245768 | tf_op jit(solution)/shard_map/ppermute | solution.py:562

commit v3 on v2

--- a/solution.py
+++ b/solution.py
@@ -138,7 +138,7 @@
             out_ref[2 * chip + p, 4 * ranks :] = value
 
 
-def density_kernel(pd_ref, other_ref, received_ref, f_ref, inner_ref, outer_ref, b1, half):
+def density_kernel(pd_ref, other_ref, received_ref, f_ref, straight_ref, across_ref, b1, half):
     position = lax.axis_index("grid")
     core, side = lax.rem(position, 2), lax.rem(lax.div(position, 2), 2)
     planes, _, lines, depth = f_ref.shape
@@ -180,15 +180,38 @@
     def once(x, part):
         return b1[x + 2, part] if -2 <= x < planes + 2 else None
 
-    for x in range(-2, planes + 2):
-        for part in range(2):
-            b1[x + 2, part] = smooth_fine(density, x, part)
-    rows = (planes + 8) // 2 * 2
-    for i in range(rows // 2):
-        for part in range(2):
-            total = smooth_fine(once, 2 * i - 4, part) + smooth_fine(once, 2 * i - 3, part)
-            for h in range(2):
-                half[(2 * i + part) * 2 + h] = total[:, h * 128 : (h + 1) * 128]
+    def outer(base, first_plane, one):
+        for x in range(one, one + 4):
+            for part in range(2):
+                b1[x + 2, part] = smooth_fine(density, x, part)
+        for i in range(2):
+            for part in range(2):
+                x = base + 2 * i
+                total = smooth_fine(once, x, part) + smooth_fine(once, x + 1, part)
+                for h in range(2):
+                    half[(2 * i + part) * 2 + h] = total[:, h * 128 : (h + 1) * 128]
+        for r, value in enumerate(lowered(half, 4, lines, depth)):
+            straight_ref[8 + r // 2, r % 2 * 16 : r % 2 * 16 + 16] = value
+        for x in range(2):
+            for part in range(2):
+                for h in range(2):
+                    straight_ref[(2 * x + part) * 2 + h] = f_ref[
+                        first_plane + x, part, :, h * 128 : (h + 1) * 128
+                    ]
+        other = planes - 2 - first_plane
+        for x in range(2):
+            across_ref[x] = f_ref[other + x]
+
+    @pl.when(side == 0)
+    def _():
+        outer(-4, 0, -2)
+
+    @pl.when(side == 1)
+    def _():
+        outer(planes, planes - 2, planes - 2)
+
+
+def lowered(half, rows, lines, depth):
     matrix = pair_matrix(depth, depth // 2, 0.125)
     total = None
     for h in range(2):
@@ -201,52 +224,64 @@
         )
         value = dot(stacked, matrix[h * 128 : (h + 1) * 128])
         total = value if total is None else total + value
-
-    def coarse(r):
-        return total[r * lines // 2 : (r + 1) * lines // 2]
-
-    @pl.when(side == 0)
-    def _():
-        for r in range(8):
-            inner_ref[r // 2, r % 2] = coarse(4 + r)
-        for r in range(4):
-            outer_ref[r // 2, r % 2] = coarse(r)
-
-    @pl.when(side == 1)
-    def _():
-        for r in range(8):
-            inner_ref[r // 2, r % 2] = coarse(r)
-        for r in range(4):
-            outer_ref[r // 2, r % 2] = coarse(8 + r)
-
-
-def source_kernel(own_ref, partner_ref, straight_ref, across_ref, cs_ref, s_ref):
+    return [total[r * lines // 2 : (r + 1) * lines // 2] for r in range(rows)]
+
+
+def source_kernel(even_ref, odd_ref, straight_ref, f_ref, cs_ref, s_ref, ext, b1, half):
     position = lax.axis_index("grid")
     blocks = lax.axis_size("grid") // 4
     core, side, block = lax.rem(position, 2), lax.rem(lax.div(position, 2), 2), lax.div(position, 4)
     cosine, sine = cs_ref[core], cs_ref[2 + core]
+    planes = f_ref.shape[0]
+    lines, depth = f_ref.shape[2:]
     first, last = block == 0, block == blocks - 1
     low = (jnp.where(first, cosine, 1.0), jnp.where(first, -sine, 0.0))
     high = (jnp.where(last, cosine, 1.0), jnp.where(last, sine, 0.0))
 
-    def total(low_ref, high_ref):
-        for x in range(4):
-            source, (c, s) = (low_ref, low) if x < 2 else (high_ref, high)
-            real, imag = rotated(source[x % 2, 0], source[x % 2, 1], c, s)
-            s_ref[x, 0] = own_ref[x, 0] + partner_ref[x, 0] + real
-            s_ref[x, 1] = own_ref[x, 1] + partner_ref[x, 1] + imag
-
     @pl.when(side == 0)
     def _():
-        total(across_ref, straight_ref)
+        place_planes(ext, 0, odd_ref, *low)
+        ext[planes : 2 * planes] = f_ref[...]
+        ext[2 * planes : 3 * planes] = even_ref[...]
+        ext[3 * planes :] = jnp.zeros((planes, 2, lines, depth), jnp.float32)
 
     @pl.when(side == 1)
     def _():
-        total(straight_ref, across_ref)
+        ext[:planes] = jnp.zeros((planes, 2, lines, depth), jnp.float32)
+        ext[planes : 2 * planes] = even_ref[...]
+        ext[2 * planes : 3 * planes] = f_ref[...]
+        place_planes(ext, 3 * planes, odd_ref, *high)
+
+    for x in range(2 * planes + 4):
+        for part in range(2):
+            b1[x, part] = smooth_fine(lambda i, p: ext[i, p], x + planes - 2, part)
+    for i in range(planes):
+        for part in range(2):
+            total = smooth_fine(lambda i, p: b1[i, p], 2 * i + 2, part) + smooth_fine(
+                lambda i, p: b1[i, p], 2 * i + 3, part
+            )
+            for h in range(2):
+                half[(2 * i + part) * 2 + h] = total[:, h * 128 : (h + 1) * 128]
+    for r, value in enumerate(lowered(half, 2 * planes, lines, depth)):
+        s_ref[r // 2, r % 2] = value
+
+    def add(base, c, t):
+        for x in range(2):
+            real, imag = rotated(straight_ref[8 + x, 0:16], straight_ref[8 + x, 16:32], c, t)
+            s_ref[base + x, 0] += real
+            s_ref[base + x, 1] += imag
+
+    @pl.when(side == 0)
+    def _():
+        add(2, *high)
+
+    @pl.when(side == 1)
+    def _():
+        add(0, *low)
 
 
 def fine_kernel(
-    even_ref, odd_ref, after_ref, before_ref, f_ref, cs_ref, own_ref, send_ref, ext, b1, b2, g
+    even_ref, odd_ref, straight_ref, across_ref, f_ref, cs_ref, own_ref, send_ref, ext, b1, b2, g
 ):
     position = lax.axis_index("grid")
     chips = lax.axis_size("grid") // 2
@@ -256,16 +291,27 @@
     place_halo(ext, planes + 2, even_ref, odd_ref, cs_ref)
     ext[planes + 2 : 2 * planes + 2] = f_ref[...]
     first, last = chip < 2, chip >= chips - 2
-    place_planes(
-        ext, 0, before_ref, jnp.where(first, cosine, 1.0), jnp.where(first, -sine, 0.0)
-    )
-    place_planes(
-        ext,
-        3 * planes + 2,
-        after_ref,
-        jnp.where(last, cosine, 1.0),
-        jnp.where(last, sine, 0.0),
-    )
+    low = (jnp.where(first, cosine, 1.0), jnp.where(first, -sine, 0.0))
+    high = (jnp.where(last, cosine, 1.0), jnp.where(last, sine, 0.0))
+
+    def place_straight(base, c, t):
+        for x in range(2):
+            real, imag = [
+                jnp.concatenate([straight_ref[4 * x + 2 * p], straight_ref[4 * x + 2 * p + 1]], axis=1)
+                for p in range(2)
+            ]
+            ext[base + x, 0], ext[base + x, 1] = rotated(real, imag, c, t)
+
+    @pl.when(lax.rem(chip, 2) == 0)
+    def _():
+        place_planes(ext, 0, across_ref, *low)
+        place_straight(3 * planes + 2, *high)
+
+    @pl.when(lax.rem(chip, 2) == 1)
+    def _():
+        place_straight(0, *low)
+        place_planes(ext, 3 * planes + 2, across_ref, *high)
+
     for x in range(planes + 8):
         for part in range(2):
             b1[x, part] = smooth_fine(lambda i, p: ext[i, p], x + 2, part)
@@ -587,29 +633,32 @@
 
     full = (2, lines, depth)
     small = (2, lines // 2, depth // 2)
-    f, inner, outer = call(
+    f, straight, across = call(
         density_kernel,
-        [shaped(planes, *full), shaped(4, *small), shaped(2, *small)],
+        [shaped(planes, *full), shaped(10, lines, 128), shaped(2, *full)],
         vmem(3),
-        [(planes + 4, *full), (2 * (planes + 8), lines, 128)],
+        [(planes + 4, *full), (8, lines, 128)],
         10**8,
     )(pair_density, other, received)
-    source = call(source_kernel, shaped(4, *small), vmem(4) + smem, [], 10**6)(
-        inner, permute(inner, even_side), permute(outer, next_block), permute(outer, odd_side), cs
-    )
-    pieces = gather_blocks(source, blocks, block, permute_block)
-
     even = permute(f, even_side)
     odd = permute(f, odd_side)
-    after = permute(f[:thick], lambda i: (i - 4) % tile_count)
-    before = permute(f[thick:], lambda i: (i + 4) % tile_count)
+    straight = permute(straight, next_block)
+    across = permute(across, lambda i: (i + (-4 if i // 2 % 2 else 4)) % tile_count)
+    source = call(
+        source_kernel,
+        shaped(planes, *small),
+        vmem(4) + smem,
+        [(4 * planes, *full), (2 * planes + 4, *full), (4 * planes, lines, 128)],
+        10**7,
+    )(even, odd, straight, f, cs)
+    pieces = gather_blocks(source, blocks, block, permute_block)
     own, send = call(
         fine_kernel,
         [shaped(thick, *full)] * 2,
         vmem(5) + smem,
         [(3 * planes + 4, *full), (planes + 8, *full), (planes + 4, *full), (planes, *full)],
         10**7,
-    )(even, odd, after, before, f, cs)
+    )(even, odd, straight, across, f, cs)
     got = permute(send, partner)
 
     n1, n2, n3 = tile_count, tile_count // 2, tile_count // 4

time: 64.3 us -> 64.1 us (level)
  starting transfers between devices: 22.2 us -> 19.1 us
  waiting for transfers between devices: 24.9 us -> 26.4 us
  Pallas kernels: 12 us -> 13.4 us
    ppermute x13 -> x10, starting transfers between devices: 14.8 us -> 11.7 us  [permute(): return lax.ppermute(value, 'grid', [(i, target(i)) for i in devices])]
    ppermute x13 -> x10, waiting for transfers between devices: 10.8 us -> 12.4 us  [permute(): return lax.ppermute(value, 'grid', [(i, target(i)) for i in devices])]
    pallas_call x2, Pallas kernels: 2.57 us -> 3.74 us  [the longest x1 2.51 us: per_device(): call(source_kernel, shaped(planes, *small), vmem(4) + smem, [(4 * planes,...]
  transfers between devices with their start and end apart: 14 -> 11, of which waited for: 7 -> 7; matrix products, arithmetic and copies ran while one was open for 1% -> 1% of each run, Pallas kernels for 11% -> 14%
where the time goes in v3:
time: 64.1 us; the launch traced here: 63.8 us
  waiting for transfers between devices  26.4 us (41%)
  starting transfers between devices  19.1 us (30%)
  Pallas kernels  13.4 us (21%)
  matrix products  2.92 us (5%)
  local copies, waits for them, and re-layouts  1.34 us (2%)
    all_to_all x1, waiting for transfers between devices, per_device(): lax.all_to_all(packed, 'grid', split_axis=0, concat_axis=0, tiled=True)  14.1 us
    ppermute x10, waiting for transfers between devices, permute(): return lax.ppermute(value, 'grid', [(i, target(i)) for i in devices])  12.4 us
    ppermute x10, starting transfers between devices, permute(): return lax.ppermute(value, 'grid', [(i, target(i)) for i in devices])  11.7 us
    all_to_all x1, starting transfers between devices, per_device(): lax.all_to_all(packed, 'grid', split_axis=0, concat_axis=0, tiled=True)  7.35 us
    pallas_call x1, Pallas kernels, per_device(): call(cycle_kernel, [shaped(5, *small)] * 2, vmem(len(pieces)) + smem, [(n...  2.92 us
    pallas_call x1, Pallas kernels, per_device(): call(fine_kernel, [shaped(thick, *full)] * 2, vmem(5) + smem, [(3 * plane...  2.73 us
    pallas_call x1, Pallas kernels, per_device(): call(source_kernel, shaped(planes, *small), vmem(4) + smem, [(4 * planes,...  2.51 us
    dot_general x1, matrix products, make_rows(): jnp.einsum('sfl,slz->sfz', chosen, shapes, precision=highest)  2.01 us
  transfers between devices with their start and end apart: 11, of which 7 were waited for; matrix products, arithmetic and copies ran while one was open for 1% of the time, Pallas kernels for 14%

profile of v3, /device:TPU:0, one launch (start us, length us, event | category | flops | bytes accessed | tf_op | source)
XLA Modules:
  0.0 63.8 jit_solution(7239714854281450401)
XLA Ops:
  0.0 0.0 copy-start
  0.0 0.9 %reshape.22 = f32[12,100]{1,0:T(8,128)S(1)} reshape(f32[12,2,2,25]{3,2,1,0:T(2,128)} %param.9) | data formatting | bytes 9600 | tf_op jit(solution)/shard_map/reshape | solution.py:544
  0.9 0.1 dot_general.11
  1.0 0.9 %fusion.2 = f32[64,4,25]{0,2,1:T(8,128)S(1)} fusion(f32[4,25,12]{1,0,2:T(4,128)S(1)} %dot_general.11, s32[64]{0:T(128)} %param.11), kind=kOutput, calls=%fused_computation.3 | convolution fusion | flops 922368 | bytes 30656 | tf_op jit(solution)/shard_map/dot_general | solution.py:544
  2.0 0.0 copy-start.3
  2.0 0.1 copy.17
  2.1 0.0 copy-done
  2.1 2.0 %fusion = f32[64,4,256]{2,1,0:T(4,128)S(1)} fusion(f32[64,4,25]{2,1,0:T(4,128)S(1)} %copy.17, f32[64,25,256]{2,0,1:T(8,128)S(1)} %copy-done), kind=kOutput, calls=%fused_computation | convolution fusion | flops 19660800 | bytes 1926144 | tf_op jit(solution)/shard_map/sfl,slz->sfz/dot_general | solution.py:546
  4.1 0.0 copy-start.1
  4.2 0.0 copy-done.2
  4.2 0.1 copy.19.column_ref
  4.3 0.0 copy-done.3
  4.3 0.0 copy-start.5
  4.3 1.5 %shard_map.82 = f32[16,72,128]{2,1,0:T(8,128)} custom-call(f32[64,1024]{1,0:T(8,128)S(1)} %bitcast.13, s32[64,1]{1,0:T(8,128)S(1)} %copy.19.column_ref, s32[1,64]{1,0:T(1,128)S(1)} %bitcast.14, s32[1,64]{1,0:T(1,128)S(1)} %bitcast.15), custom_call_target="tpu_custom_call" | custom-call | flops 100000000 | bytes 1048576 | tf_op jit(solution)/shard_map/pallas_call | solution.py:629
  5.8 7.4 %all-to-all-start = ((f32[16,72,128]{2,1,0:T(8,128)}), f32[16,72,128]{2,1,0:T(8,128)S(1)}, u32[]{:S(2)}, u32[]{:S(2)}) async-start(f32[16,72,128]{2,1,0:T(8,128)} %shard_map.82), calls=%async_computation | async-start | bytes 1179648 | tf_op jit(solution)/shard_map/all_to_all | solution.py:632
  13.2 0.0 copy-done.1
  13.2 0.5 collective-permute-start
  13.7 1.0 %collective-permute-done.other_ref = f32[2,2,32,256]{3,2,1,0:T(8,128)S(1)} collective-permute-done((f32[2,2,32,256]{3,2,1,0:T(8,128)S(1)}, f32[2,2,32,256]{3,2,1,0:T(8,128)S(1)}, u32[]{:S(2)}, u32[]{:S(2)}) %collective-permute-start) | collective-permute-done | bytes 131104 | tf_op jit(solution)/shard_map/ppermute | solution.py:608
  14.7 14.1 %all-to-all-done.received_ref = f32[16,72,128]{2,1,0:T(8,128)S(1)} async-done(((f32[16,72,128]{2,1,0:T(8,128)}), f32[16,72,128]{2,1,0:T(8,128)S(1)}, u32[]{:S(2)}, u32[]{:S(2)}) %all-to-all-start) | async-done | bytes 589856 | tf_op jit(solution)/shard_map/all_to_all | solution.py:632
  28.7 1.2 %shard_map.83 = (f32[4,2,32,256]{3,2,1,0:T(8,128)S(1)}, f32[10,32,128]{2,1,0:T(8,128)S(1)}, f32[2,2,32,256]{3,2,1,0:T(8,128)S(1)}) custom-call(f32[2,2,2,32,256]{4,3,2,1,0:T(8,128)S(1)} %copy-done.1, f32[2,2,32,256]{3,2,1,0:T(8,128)S(1)} %collective-permute-done.other_ref, f32[16,72,128]{2,1,0:T(8,128)S(1)} %all-to-all-done.received_ref), custom_call_target="tpu_custom_call" | custom-call | flops 100000000 | bytes 1048576 | tf_op jit(solution)/shard_map/pallas_call | solution.py:636
  29.9 0.7 %collective-permute-start.1 = (f32[4,2,32,256]{3,2,1,0:T(8,128)S(1)}, f32[4,2,32,256]{3,2,1,0:T(8,128)S(1)}, u32[]{:S(2)}, u32[]{:S(2)}) collective-permute-start(f32[4,2,32,256]{3,2,1,0:T(8,128)S(1)} %get-tuple-element.12.f_ref), channel_id=1, source_target_pairs={{0,2},{1,3},{2,0},{3,1},{4,6},{5,7},{6,4},{7,5},{8,10},{9,11},{10,... | collective-permute-start | bytes 786440 | tf_op jit(solution)/shard_map/ppermute | solution.py:608
  30.6 2.5 %collective-permute-start.2 = (f32[4,2,32,256]{3,2,1,0:T(8,128)S(1)}, f32[4,2,32,256]{3,2,1,0:T(8,128)S(1)}, u32[]{:S(2)}, u32[]{:S(2)}) collective-permute-start(f32[4,2,32,256]{3,2,1,0:T(8,128)S(1)} %get-tuple-element.12.f_ref), channel_id=1, source_target_pairs={{0,14},{1,15},{2,4},{3,5},{4,2},{5,3},{6,8},{7,9},{8,6},{9,7},{10,... | collective-permute-start | bytes 786440 | tf_op jit(solution)/shard_map/ppermute | solution.py:608
  33.1 0.0 copy-done.4
  33.1 0.0 copy-done.5
  33.2 0.2 fusion.7
  33.3 2.4 %collective-permute-start.3 = (f32[10,32,128]{2,1,0:T(8,128)S(1)}, f32[10,32,128]{2,1,0:T(8,128)S(1)}, u32[]{:S(2)}, u32[]{:S(2)}) collective-permute-start(f32[10,32,128]{2,1,0:T(8,128)S(1)} %get-tuple-element.13), channel_id=1, source_target_pairs={{0,12},{1,13},{2,6},{3,7},{4,0},{5,1},{6,10},{7,11},{8,4},{9,5},{1... | collective-permute-start | bytes 491528 | tf_op jit(solution)/shard_map/ppermute | solution.py:608
  35.7 0.2 cosine_reduce_fusion
  35.9 0.1 collective-permute-start.7
  36.0 0.1 pad_maximum_fusion.cs_ref.refs_4_
  36.0 7.4 %collective-permute-done.3.straight_ref = f32[10,32,128]{2,1,0:T(8,128)S(1)} collective-permute-done((f32[10,32,128]{2,1,0:T(8,128)S(1)}, f32[10,32,128]{2,1,0:T(8,128)S(1)}, u32[]{:S(2)}, u32[]{:S(2)}) %collective-permute-start.3) | collective-permute-done | bytes 163872 | tf_op jit(solution)/shard_map/ppermute | solution.py:608
  43.5 0.4 collective-permute-done.1.even_ref
  43.9 0.0 collective-permute-done.2.odd_ref
  43.9 2.5 %shard_map.84.refs_0_ = f32[4,2,16,128]{3,2,1,0:T(8,128)S(1)} custom-call(f32[4,2,32,256]{3,2,1,0:T(8,128)S(1)} %collective-permute-done.1.even_ref, f32[4,2,32,256]{3,2,1,0:T(8,128)S(1)} %collective-permute-done.2.odd_ref, f32[10,32,128]{2,1,0:T(8,128)S(1)} %collective-permute-done.3.straight_ref, f32[4,2,32,256]{3,2,1,0:T(8,128)S(1)} %get-tuple-element.12.f_ref, ...), custom_call_target="tpu_custom_call" | custom-call | flops 10000000 | bytes 1048576 | tf_op jit(solution)/shard_map/pallas_call | solution.py:647
  46.4 3.8 %collective-permute-start.4 = (f32[4,2,16,128]{3,2,1,0:T(8,128)S(1)}, f32[4,2,16,128]{3,2,1,0:T(8,128)S(1)}, u32[]{:S(2)}, u32[]{:S(2)}) collective-permute-start(f32[4,2,16,128]{3,2,1,0:T(8,128)S(1)} %shard_map.84.refs_0_), channel_id=1, source_target_pairs={{0,12},{1,13},{2,14},{3,15},{4,0},{5,1},{6,2},{7,3},{8,4},{9,5},{1... | collective-permute-start | bytes 196616 | tf_op jit(solution)/shard_map/ppermute | solution.py:608
  50.2 1.7 %collective-permute-start.5 = (f32[4,2,16,128]{3,2,1,0:T(8,128)S(1)}, f32[4,2,16,128]{3,2,1,0:T(8,128)S(1)}, u32[]{:S(2)}, u32[]{:S(2)}) collective-permute-start(f32[4,2,16,128]{3,2,1,0:T(8,128)S(1)} %shard_map.84.refs_0_), channel_id=1, source_target_pairs={{0,8},{1,9},{2,10},{3,11},{4,12},{5,13},{6,14},{7,15},{8,0},{9,1},... | collective-permute-start | bytes 196616 | tf_op jit(solution)/shard_map/ppermute | solution.py:608
  51.9 0.0 collective-permute-start.6
  51.9 0.0 collective-permute-done.7.across_ref
  51.9 2.7 %shard_map.86 = (f32[2,2,32,256]{3,2,1,0:T(8,128)S(1)}, f32[2,2,32,256]{3,2,1,0:T(8,128)S(1)}) custom-call(f32[4,2,32,256]{3,2,1,0:T(8,128)S(1)} %collective-permute-done.1.even_ref, f32[4,2,32,256]{3,2,1,0:T(8,128)S(1)} %collective-permute-done.2.odd_ref, f32[10,32,128]{2,1,0:T(8,128)S(1)} %collective-permute-done.3.straight_ref, ...), custom_call_target="tpu_custom_call" | custom-call | flops 10000000 | bytes 1048576 | tf_op jit(solution)/shard_map/pallas_call | solution.py:655
  54.6 0.1 collective-permute-start.9
  54.7 0.0 collective-permute-done.4.refs_1_
  54.7 1.5 %collective-permute-done.5.refs_2_ = f32[4,2,16,128]{3,2,1,0:T(8,128)S(1)} collective-permute-done((f32[4,2,16,128]{3,2,1,0:T(8,128)S(1)}, f32[4,2,16,128]{3,2,1,0:T(8,128)S(1)}, u32[]{:S(2)}, u32[]{:S(2)}) %collective-permute-start.5) | collective-permute-done | bytes 65568 | tf_op jit(solution)/shard_map/ppermute | solution.py:608
  56.2 1.7 %collective-permute-done.6.refs_3_ = f32[4,2,16,128]{3,2,1,0:T(8,128)S(1)} collective-permute-done((f32[4,2,16,128]{3,2,1,0:T(8,128)S(1)}, f32[4,2,16,128]{3,2,1,0:T(8,128)S(1)}, u32[]{:S(2)}, u32[]{:S(2)}) %collective-permute-start.6) | collective-permute-done | bytes 65568 | tf_op jit(solution)/shard_map/ppermute | solution.py:608
  58.0 2.9 %shard_map.85 = (f32[5,2,16,128]{3,2,1,0:T(8,128)S(1)}, f32[5,2,16,128]{3,2,1,0:T(8,128)S(1)}) custom-call(f32[4,2,16,128]{3,2,1,0:T(8,128)S(1)} %shard_map.84.refs_0_, f32[4,2,16,128]{3,2,1,0:T(8,128)S(1)} %collective-permute-done.4.refs_1_, f32[4,2,16,128]{3,2,1,0:T(8,128)S(1)} %collective-permute-done.5.refs_2_, ...), custom_call_target="tpu_custom_call" | custom-call | flops 100000000 | bytes 1048576 | tf_op jit(solution)/shard_map/pallas_call | solution.py:666
  60.9 0.1 collective-permute-start.8
  61.0 0.9 %shard_map.87.own_ref = f32[2,2,32,256]{3,2,1,0:T(8,128)S(1)} custom-call(f32[5,2,16,128]{3,2,1,0:T(8,128)S(1)} %get-tuple-element.14.w_ref, f32[2,2,32,256]{3,2,1,0:T(8,128)S(1)} %get-tuple-element.16.g_ref), custom_call_target="tpu_custom_call" | custom-call | flops 10000000 | bytes 1048576 | tf_op jit(solution)/shard_map/pallas_call | solution.py:687
  61.9 0.0 collective-permute-done.9.g_ref
  61.9 0.3 collective-permute-done.8.w_ref
  62.2 1.6 %shard_map.88 = f32[2,2,2,32,256]{4,3,2,1,0:T(8,128)} custom-call(f32[2,2,32,256]{3,2,1,0:T(8,128)S(1)} %shard_map.87.own_ref, f32[5,2,16,128]{3,2,1,0:T(8,128)S(1)} %collective-permute-done.8.w_ref, f32[2,2,32,256]{3,2,1,0:T(8,128)S(1)} %collective-permute-done.9.g_ref), custom_call_target="tpu_custom_call" | custom-call | flops 10000000 | bytes 1048576 | tf_op jit(solution)/shard_map/pallas_call | solution.py:688
  (4 shorter events, 0.1 us)
Async XLA Ops:
  0.0 2.1 %copy-start = (f32[64,25,256]{2,0,1:T(8,128)S(1)}, f32[64,25,256]{2,0,1:T(8,128)}, u32[]{:S(2)}) copy-start(f32[64,25,256]{2,0,1:T(8,128)} %param.10) | copy-start | bytes 4915204
  1.0 3.1 %copy-start.2 = (s32[64,1]{0,1:T(1,128)S(1)}, s32[64,1]{0,1:T(1,128)}, u32[]{:S(2)}) copy-start(s32[64,1]{0,1:T(1,128)} %param.12) | copy-start | bytes 772
  2.0 2.3 %copy-start.3 = (s32[64]{0:T(128)S(1)}, s32[64]{0:T(128)}, u32[]{:S(2)}) copy-start(s32[64]{0:T(128)} %param.13) | copy-start | bytes 772
  4.1 9.1 %copy-start.1 = (f32[2,2,2,32,256]{4,3,2,1,0:T(8,128)S(1)}, f32[2,2,2,32,256]{4,3,2,1,0:T(8,128)}, u32[]{:S(2)}) copy-start(f32[2,2,2,32,256]{4,3,2,1,0:T(8,128)} %pd_ref.1) | copy-start | bytes 786436
  4.3 28.9 %copy-start.4 = (s32[2,2]{1,0:T(2,128)S(1)}, s32[2,2]{1,0:T(2,128)}, u32[]{:S(2)}) copy-start(s32[2,2]{1,0:T(2,128)} %param.14) | copy-start | bytes 52
  4.3 28.9 %copy-start.5 = (f32[8]{0:T(128)S(1)}, f32[8]{0:T(128)}, u32[]{:S(2)}) copy-start(f32[8]{0:T(128)} %param.15) | copy-start | bytes 100
  5.8 22.9 %all-to-all-start = ((f32[16,72,128]{2,1,0:T(8,128)}), f32[16,72,128]{2,1,0:T(8,128)S(1)}, u32[]{:S(2)}, u32[]{:S(2)}) async-start(f32[16,72,128]{2,1,0:T(8,128)} %shard_map.82), calls=%async_computation | async-start | bytes 1179648 | tf_op jit(solution)/shard_map/all_to_all | solution.py:632
  13.2 1.4 %collective-permute-start = (f32[2,2,32,256]{3,2,1,0:T(8,128)S(1)}, f32[2,2,32,256]{3,2,1,0:T(8,128)S(1)}, u32[]{:S(2)}, u32[]{:S(2)}) collective-permute-start(f32[2,2,32,256]{3,2,1,0:T(8,128)S(1)} %dynamic-slice_bitcast_fusion), channel_id=1, source_target_pairs={{0,1},{1,0},{2,3},{3,2},{4,5},{5,4},{6,7},{7,6},{8,9},{9,8},{10,11... | collective-permute-start | bytes 393224 | tf_op jit(solution)/shard_map/ppermute | solution.py:608
  29.9 13.9 %collective-permute-start.1 = (f32[4,2,32,256]{3,2,1,0:T(8,128)S(1)}, f32[4,2,32,256]{3,2,1,0:T(8,128)S(1)}, u32[]{:S(2)}, u32[]{:S(2)}) collective-permute-start(f32[4,2,32,256]{3,2,1,0:T(8,128)S(1)} %get-tuple-element.12.f_ref), channel_id=1, source_target_pairs={{0,2},{1,3},{2,0},{3,1},{4,6},{5,7},{6,4},{7,5},{8,10},{9,11},{10,... | collective-permute-start | bytes 786440 | tf_op jit(solution)/shard_map/ppermute | solution.py:608
  30.6 13.3 %collective-permute-start.2 = (f32[4,2,32,256]{3,2,1,0:T(8,128)S(1)}, f32[4,2,32,256]{3,2,1,0:T(8,128)S(1)}, u32[]{:S(2)}, u32[]{:S(2)}) collective-permute-start(f32[4,2,32,256]{3,2,1,0:T(8,128)S(1)} %get-tuple-element.12.f_ref), channel_id=1, source_target_pairs={{0,14},{1,15},{2,4},{3,5},{4,2},{5,3},{6,8},{7,9},{8,6},{9,7},{10,... | collective-permute-start | bytes 786440 | tf_op jit(solution)/shard_map/ppermute | solution.py:608
  33.3 10.2 %collective-permute-start.3 = (f32[10,32,128]{2,1,0:T(8,128)S(1)}, f32[10,32,128]{2,1,0:T(8,128)S(1)}, u32[]{:S(2)}, u32[]{:S(2)}) collective-permute-start(f32[10,32,128]{2,1,0:T(8,128)S(1)} %get-tuple-element.13), channel_id=1, source_target_pairs={{0,12},{1,13},{2,6},{3,7},{4,0},{5,1},{6,10},{7,11},{8,4},{9,5},{1... | collective-permute-start | bytes 491528 | tf_op jit(solution)/shard_map/ppermute | solution.py:608
  35.9 16.0 %collective-permute-start.7 = (f32[2,2,32,256]{3,2,1,0:T(8,128)S(1)}, f32[2,2,32,256]{3,2,1,0:T(8,128)S(1)}, u32[]{:S(2)}, u32[]{:S(2)}) collective-permute-start(f32[2,2,32,256]{3,2,1,0:T(8,128)S(1)} %get-tuple-element.15), channel_id=1, source_target_pairs={{0,4},{1,5},{2,14},{3,15},{4,8},{5,9},{6,2},{7,3},{8,12},{9,13},{1... | collective-permute-start | bytes 393224 | tf_op jit(solution)/shard_map/ppermute | solution.py:608
  46.4 8.3 %collective-permute-start.4 = (f32[4,2,16,128]{3,2,1,0:T(8,128)S(1)}, f32[4,2,16,128]{3,2,1,0:T(8,128)S(1)}, u32[]{:S(2)}, u32[]{:S(2)}) collective-permute-start(f32[4,2,16,128]{3,2,1,0:T(8,128)S(1)} %shard_map.84.refs_0_), channel_id=1, source_target_pairs={{0,12},{1,13},{2,14},{3,15},{4,0},{5,1},{6,2},{7,3},{8,4},{9,5},{1... | collective-permute-start | bytes 196616 | tf_op jit(solution)/shard_map/ppermute | solution.py:608
  50.2 6.0 %collective-permute-start.5 = (f32[4,2,16,128]{3,2,1,0:T(8,128)S(1)}, f32[4,2,16,128]{3,2,1,0:T(8,128)S(1)}, u32[]{:S(2)}, u32[]{:S(2)}) collective-permute-start(f32[4,2,16,128]{3,2,1,0:T(8,128)S(1)} %shard_map.84.refs_0_), channel_id=1, source_target_pairs={{0,8},{1,9},{2,10},{3,11},{4,12},{5,13},{6,14},{7,15},{8,0},{9,1},... | collective-permute-start | bytes 196616 | tf_op jit(solution)/shard_map/ppermute | solution.py:608
  51.9 6.1 %collective-permute-start.6 = (f32[4,2,16,128]{3,2,1,0:T(8,128)S(1)}, f32[4,2,16,128]{3,2,1,0:T(8,128)S(1)}, u32[]{:S(2)}, u32[]{:S(2)}) collective-permute-start(f32[4,2,16,128]{3,2,1,0:T(8,128)S(1)} %shard_map.84.refs_0_), channel_id=1, source_target_pairs={{0,4},{1,5},{2,6},{3,7},{4,8},{5,9},{6,10},{7,11},{8,12},{9,13},{1... | collective-permute-start | bytes 196616 | tf_op jit(solution)/shard_map/ppermute | solution.py:608
  54.6 7.2 %collective-permute-start.9 = (f32[2,2,32,256]{3,2,1,0:T(8,128)S(1)}, f32[2,2,32,256]{3,2,1,0:T(8,128)S(1)}, u32[]{:S(2)}, u32[]{:S(2)}) collective-permute-start(f32[2,2,32,256]{3,2,1,0:T(8,128)S(1)} %get-tuple-element.18), channel_id=1, source_target_pairs={{0,1},{1,0},{2,3},{3,2},{4,5},{5,4},{6,7},{7,6},{8,9},{9,8},{10,11... | collective-permute-start | bytes 393224 | tf_op jit(solution)/shard_map/ppermute | solution.py:608
  60.9 1.3 %collective-permute-start.8 = (f32[5,2,16,128]{3,2,1,0:T(8,128)S(1)}, f32[5,2,16,128]{3,2,1,0:T(8,128)S(1)}, u32[]{:S(2)}, u32[]{:S(2)}) collective-permute-start(f32[5,2,16,128]{3,2,1,0:T(8,128)S(1)} %get-tuple-element.17), channel_id=1, source_target_pairs={{0,1},{1,0},{2,3},{3,2},{4,5},{5,4},{6,7},{7,6},{8,9},{9,8},{10,11... | collective-permute-start | bytes 245768 | tf_op jit(solution)/shard_map/ppermute | solution.py:608

commit v4 on v2

--- a/solution.py
+++ b/solution.py
@@ -138,9 +138,8 @@
             out_ref[2 * chip + p, 4 * ranks :] = value
 
 
-def density_kernel(pd_ref, other_ref, received_ref, f_ref, inner_ref, outer_ref, b1, half):
-    position = lax.axis_index("grid")
-    core, side = lax.rem(position, 2), lax.rem(lax.div(position, 2), 2)
+def density_kernel(pd_ref, other_ref, received_ref, f_ref):
+    core = lax.rem(lax.axis_index("grid"), 2)
     planes, _, lines, depth = f_ref.shape
     sources, height, _ = received_ref.shape
     ranks = (height - 8) // 4
@@ -174,21 +173,8 @@
             f_ref[core * thick + x, part] += pd_ref[core, part, x]
             f_ref[(1 - core) * thick + x, part] += other_ref[part, x]
 
-    def density(x, part):
-        return f_ref[x, part] if 0 <= x < planes else None
-
-    def once(x, part):
-        return b1[x + 2, part] if -2 <= x < planes + 2 else None
-
-    for x in range(-2, planes + 2):
-        for part in range(2):
-            b1[x + 2, part] = smooth_fine(density, x, part)
-    rows = (planes + 8) // 2 * 2
-    for i in range(rows // 2):
-        for part in range(2):
-            total = smooth_fine(once, 2 * i - 4, part) + smooth_fine(once, 2 * i - 3, part)
-            for h in range(2):
-                half[(2 * i + part) * 2 + h] = total[:, h * 128 : (h + 1) * 128]
+
+def lowered(half, rows, lines, depth):
     matrix = pair_matrix(depth, depth // 2, 0.125)
     total = None
     for h in range(2):
@@ -201,48 +187,118 @@
         )
         value = dot(stacked, matrix[h * 128 : (h + 1) * 128])
         total = value if total is None else total + value
-
-    def coarse(r):
-        return total[r * lines // 2 : (r + 1) * lines // 2]
-
-    @pl.when(side == 0)
-    def _():
-        for r in range(8):
-            inner_ref[r // 2, r % 2] = coarse(4 + r)
-        for r in range(4):
-            outer_ref[r // 2, r % 2] = coarse(r)
-
-    @pl.when(side == 1)
-    def _():
-        for r in range(8):
-            inner_ref[r // 2, r % 2] = coarse(r)
-        for r in range(4):
-            outer_ref[r // 2, r % 2] = coarse(8 + r)
-
-
-def source_kernel(own_ref, partner_ref, straight_ref, across_ref, cs_ref, s_ref):
+    return [total[r * lines // 2 : (r + 1) * lines // 2] for r in range(rows)]
+
+
+def convolve(a, b):
+    out = {}
+    for i, x in a.items():
+        for j, y in b.items():
+            out[i + j] = out.get(i + j, 0.0) + x * y
+    return out
+
+
+along = {-2: -fine_far, -1: fine_near, 1: fine_near, 2: -fine_far}
+powers = [{0: 1.0}, along, convolve(along, along)]
+averaged = [convolve(power, {0: 0.5, 1: 0.5}) for power in powers]
+
+
+def taps(distance, power):
+    total = jnp.zeros(distance.shape, jnp.float32)
+    for offset, value in averaged[power].items():
+        total = jnp.where(distance == offset, value, total)
+    return total
+
+
+def coarse_kernel(
+    rows_ref, tile_ref, line_ref, pd_ref, cs_ref, keep_ref, send_ref, ext, weights, b1, half
+):
     position = lax.axis_index("grid")
-    blocks = lax.axis_size("grid") // 4
-    core, side, block = lax.rem(position, 2), lax.rem(lax.div(position, 2), 2), lax.div(position, 4)
-    cosine, sine = cs_ref[core], cs_ref[2 + core]
-    first, last = block == 0, block == blocks - 1
-    low = (jnp.where(first, cosine, 1.0), jnp.where(first, -sine, 0.0))
-    high = (jnp.where(last, cosine, 1.0), jnp.where(last, sine, 0.0))
-
-    def total(low_ref, high_ref):
-        for x in range(4):
-            source, (c, s) = (low_ref, low) if x < 2 else (high_ref, high)
-            real, imag = rotated(source[x % 2, 0], source[x % 2, 1], c, s)
-            s_ref[x, 0] = own_ref[x, 0] + partner_ref[x, 0] + real
-            s_ref[x, 1] = own_ref[x, 1] + partner_ref[x, 1] + imag
-
-    @pl.when(side == 0)
-    def _():
-        total(across_ref, straight_ref)
-
-    @pl.when(side == 1)
-    def _():
-        total(straight_ref, across_ref)
+    core = lax.rem(position, 2)
+    slots = rows_ref.shape[0]
+    count = keep_ref.shape[0]
+    thick, lines, depth = pd_ref.shape[2:]
+    small_lines, small_depth = lines // 2, depth // 2
+    total = count + 4
+
+    i = lax.broadcasted_iota(jnp.int32, (depth, small_depth), 0)
+    j = lax.broadcasted_iota(jnp.int32, (depth, small_depth), 1)
+    distance = lax.rem(i - 2 * j + depth + depth // 2, depth) - depth // 2
+    matrix = jnp.concatenate([taps(distance, power) for power in range(3)], axis=1)
+    stacked = jnp.concatenate(
+        [rows_ref[:, f * depth : (f + 1) * depth] for f in range(4)], axis=0
+    )
+    cells = dot(stacked, matrix)
+    values = [
+        jnp.concatenate(
+            [
+                cells[f * slots : (f + 1) * slots, k * small_depth : (k + 1) * small_depth]
+                for f in range(4)
+            ],
+            axis=1,
+        )
+        for k in range(3)
+    ]
+
+    plane = tile_ref[...] * thick + line_ref[...] // lines
+    line = line_ref[...] % lines
+    i = lax.broadcasted_iota(jnp.int32, (weights.shape[1], slots), 0)
+    for power in range(3):
+        weights[power] = taps(plane - 2 * (i - 2), power)
+    j = lax.broadcasted_iota(jnp.int32, (small_lines, slots), 0)
+    distance = lax.rem(line - 2 * j + lines + lines // 2, lines) - lines // 2
+    q = [taps(distance, power) for power in range(3)]
+    mixed = [keep * keep * q[0] + 2.0 * keep * q[1] + q[2], 2.0 * keep * q[0] + 2.0 * q[1], q[0]]
+    chunk = total if total <= 20 else 12
+
+    def body(first):
+        parts = [[], [], []]
+        for k in range(chunk):
+            p = [weights[power, pl.ds(first * chunk + k, 1)] for power in range(3)]
+            parts[0].append(p[0] * mixed[0] + p[1] * mixed[1] + p[2] * mixed[2])
+            parts[1].append(p[0] * mixed[1] + 2.0 * p[1] * mixed[2])
+            parts[2].append(p[0] * mixed[2])
+        out = sum(dot(jnp.concatenate(parts[k], axis=0), values[k]) for k in range(3))
+        for k in range(chunk):
+            for f in range(4):
+                ext[first * chunk + k, f] = out[
+                    k * small_lines : (k + 1) * small_lines,
+                    f * small_depth : (f + 1) * small_depth,
+                ]
+
+    each(total // chunk, body, 1)
+
+    def tile(x, f):
+        return pd_ref[f // 2, f % 2, x] if 0 <= x < thick else None
+
+    def once(x, f):
+        return b1[x + 2, f] if -2 <= x < thick + 2 else None
+
+    for x in range(-2, thick + 2):
+        for f in range(4):
+            b1[x + 2, f] = smooth_fine(tile, x, f)
+    for i in range(5):
+        for f in range(4):
+            both = smooth_fine(once, 2 * i - 4, f) + smooth_fine(once, 2 * i - 3, f)
+            for h in range(2):
+                half[(4 * i + f) * 2 + h] = both[:, h * 128 : (h + 1) * 128]
+    for r, value in enumerate(lowered(half, 20, lines, depth)):
+        ext[position + r // 4, r % 4] += value
+
+    for p in range(2):
+        cosine, sine = cs_ref[p], cs_ref[2 + p]
+        for k in range(2):
+            for source, target, sign in ((k, count + k, sine), (count + 2 + k, 2 + k, -sine)):
+                real, imag = rotated(ext[source, 2 * p], ext[source, 2 * p + 1], cosine, sign)
+                ext[target, 2 * p] += real
+                ext[target, 2 * p + 1] += imag
+
+    def deliver(x):
+        for part in range(2):
+            keep_ref[x, part] = ext[x + 2, 2 * core + part]
+            send_ref[x, part] = ext[x + 2, 2 * (1 - core) + part]
+
+    each(count, deliver)
 
 
 def fine_kernel(
@@ -500,24 +556,45 @@
     return jnp.einsum("sfl,slz->sfz", chosen, shapes, precision=highest).reshape(slot_count, -1)
 
 
+def block_steps(blocks):
+    steps, stride = [], 1
+    while stride < blocks:
+        steps.append((stride, min(4, blocks // stride)))
+        stride *= steps[-1][1]
+    return steps
+
+
+def further(k, stride, radix):
+    def target(b):
+        digit = b // stride % radix
+        return b + ((digit + k) % radix - digit) * stride
+
+    return target
+
+
+def scatter_blocks(value, blocks, block, permute_block):
+    for stride, radix in reversed(block_steps(blocks)):
+        parts = value.reshape(radix, -1, *value.shape[1:])
+        digit = block // stride % radix
+        pieces = [
+            lax.dynamic_index_in_dim(parts, (digit + k) % radix, 0, False) for k in range(radix)
+        ]
+        value = sum(
+            [permute_block(pieces[k], further(k, stride, radix)) for k in range(1, radix)],
+            pieces[0],
+        )
+    return value
+
+
 def gather_blocks(value, blocks, block, permute_block):
-    stride = 1
-    while True:
-        radix = min(4, blocks // stride)
-        digit = block // stride % radix
-
-        def towards(k):
-            def target(b):
-                own = b // stride % radix
-                return b + ((own - k) % radix - own) * stride
-
-            return target
-
-        pieces = [value] + [permute_block(value, towards(k)) for k in range(1, radix)]
-        stride *= radix
-        if stride == blocks:
+    steps = block_steps(blocks)
+    for stride, radix in steps:
+        pieces = [value] + [
+            permute_block(value, further(-k, stride, radix)) for k in range(1, radix)
+        ]
+        if (stride, radix) == steps[-1]:
             return pieces
-        stacked = jnp.roll(jnp.stack(pieces), digit, axis=0)
+        stacked = jnp.roll(jnp.stack(pieces), block // stride % radix, axis=0)
         value = stacked.reshape(-1, *value.shape[1:])
 
 
@@ -573,32 +650,38 @@
     def odd_side(i):
         return (i // 2 + (1 if i // 2 % 2 else -1)) % chips * 2 + i % 2
 
-    def next_block(i):
-        return (i + (4 if i // 2 % 2 else -4)) % tile_count
-
     cs = pair_phases(pair_table, k_fraction)
 
     other = permute(lax.dynamic_index_in_dim(pair_density, 1 - core, 0, False), partner)
     rows = make_rows(moments, shapes, slot_atom)
+    tile_row, line_row = slot_tile.reshape(1, -1), slot_row.reshape(1, -1)
     packed = call(pack_kernel, shaped(tile_count, 8 * capacity + 8, 128), vmem(4), [], 10**8)(
-        rows, slot_tile, slot_tile.reshape(1, -1), slot_row.reshape(1, -1)
+        rows, slot_tile, tile_row, line_row
     )
     received = lax.all_to_all(packed, "grid", split_axis=0, concat_axis=0, tiled=True)
 
     full = (2, lines, depth)
     small = (2, lines // 2, depth // 2)
-    f, inner, outer = call(
-        density_kernel,
-        [shaped(planes, *full), shaped(4, *small), shaped(2, *small)],
-        vmem(3),
-        [(planes + 4, *full), (2 * (planes + 8), lines, 128)],
+    kept, sent = call(
+        coarse_kernel,
+        [shaped(tile_count, *small)] * 2,
+        vmem(4) + smem,
+        [
+            (tile_count + 4, 4, lines // 2, depth // 2),
+            (3, (tile_count + 11) // 8 * 8, slot_count),
+            (thick + 4, 4, lines, depth),
+            (40, lines, 128),
+        ],
         10**8,
-    )(pair_density, other, received)
-    source = call(source_kernel, shaped(4, *small), vmem(4) + smem, [], 10**6)(
-        inner, permute(inner, even_side), permute(outer, next_block), permute(outer, odd_side), cs
-    )
+    )(rows, tile_row, line_row, pair_density, cs)
+    kept = kept + permute(sent, partner)
+    kept = kept + permute(kept, even_side)
+    source = scatter_blocks(kept, blocks, block, permute_block)
     pieces = gather_blocks(source, blocks, block, permute_block)
 
+    f = call(density_kernel, shaped(planes, *full), vmem(3), [], 10**7)(
+        pair_density, other, received
+    )
     even = permute(f, even_side)
     odd = permute(f, odd_side)
     after = permute(f[:thick], lambda i: (i - 4) % tile_count)

time: 64.3 us -> 65.1 us (1.012)
  waiting for transfers between devices: 24.9 us -> 14.6 us
  starting transfers between devices: 22.2 us -> 29.8 us
  Pallas kernels: 12 us -> 14 us
  local copies, waits for them, and re-layouts: 1.36 us -> 2.68 us
    all_to_all x1, waiting for transfers between devices: 14.1 us -> 0.01 us  [per_device(): lax.all_to_all(packed, 'grid', split_axis=0, concat_axis=0, tiled=True)]
    ppermute x13 -> x15, starting transfers between devices: 14.8 us -> 22.5 us  [permute(): return lax.ppermute(value, 'grid', [(i, target(i)) for i in devices])]
    ppermute x13 -> x15, waiting for transfers between devices: 10.8 us -> 14.6 us  [permute(): return lax.ppermute(value, 'grid', [(i, target(i)) for i in devices])]
    pallas_call x2, Pallas kernels: 2.57 us -> 4.32 us  [the longest x1 3.7 us: per_device(): call(coarse_kernel, [shaped(tile_count, *small)] * 2, vmem(4) + smem, [(t...]
    squeeze x0 -> x1, local copies, waits for them, and re-layouts: none -> 0.67 us  [scatter_blocks(): lax.dynamic_index_in_dim(parts, (digit + k) % radix, 0, False)]
    unnamed x14, local copies, waits for them, and re-layouts: 0.18 us -> 0.83 us
  transfers between devices with their start and end apart: 14 -> 16, of which waited for: 7 -> 5; matrix products, arithmetic and copies ran while one was open for 1% -> 2% of each run, Pallas kernels for 11% -> 17%
where the time goes in v4:
time: 65.1 us; the launch traced here: 64.8 us
  starting transfers between devices  29.8 us (46%)
  waiting for transfers between devices  14.6 us (22%)
  Pallas kernels  14 us (22%)
  matrix products  2.92 us (4%)
  local copies, waits for them, and re-layouts  2.68 us (4%)
    ppermute x15, starting transfers between devices, permute(): return lax.ppermute(value, 'grid', [(i, target(i)) for i in devices])  22.5 us
    ppermute x15, waiting for transfers between devices, permute(): return lax.ppermute(value, 'grid', [(i, target(i)) for i in devices])  14.6 us
    all_to_all x1, starting transfers between devices, per_device(): lax.all_to_all(packed, 'grid', split_axis=0, concat_axis=0, tiled=True)  7.36 us
    pallas_call x1, Pallas kernels, per_device(): call(coarse_kernel, [shaped(tile_count, *small)] * 2, vmem(4) + smem, [(t...  3.7 us
    pallas_call x1, Pallas kernels, per_device(): call(cycle_kernel, [shaped(5, *small)] * 2, vmem(len(pieces)) + smem, [(n...  2.92 us
    pallas_call x1, Pallas kernels, per_device(): call(fine_kernel, [shaped(thick, *full)] * 2, vmem(5) + smem, [(3 * plane...  2.7 us
    dot_general x1, matrix products, make_rows(): jnp.einsum('sfl,slz->sfz', chosen, shapes, precision=highest)  2.01 us
    pallas_call x1, Pallas kernels, per_device(): call(output_kernel, shaped(*pair_density.shape), vmem(3), scratch, 10 ** 7)  1.61 us
  transfers between devices with their start and end apart: 16, of which 5 were waited for; matrix products, arithmetic and copies ran while one was open for 2% of the time, Pallas kernels for 17%

profile of v4, /device:TPU:0, one launch (start us, length us, event | category | flops | bytes accessed | tf_op | source)
XLA Modules:
  0.0 64.8 jit_solution(7928951676139619285)
XLA Ops:
  0.0 0.9 %reshape.25 = f32[12,100]{1,0:T(8,128)S(1)} reshape(f32[12,2,2,25]{3,2,1,0:T(2,128)} %param.9) | data formatting | bytes 9600 | tf_op jit(solution)/shard_map/reshape | solution.py:554
  0.9 0.1 dot_general.11
  1.0 0.7 %copy.19.column_ref = s32[64,1]{1,0:T(8,128)S(1)} copy(s32[64,1]{0,1:T(1,128)} %param.12) | data formatting | bytes 512 | tf_op args[4]
  1.8 0.9 %fusion.4 = f32[64,4,25]{0,2,1:T(8,128)S(1)} fusion(f32[4,25,12]{1,0,2:T(4,128)S(1)} %dot_general.11, s32[64]{0:T(128)} %param.11), kind=kOutput, calls=%fused_computation.9 | convolution fusion | flops 922368 | bytes 30656 | tf_op jit(solution)/shard_map/dot_general | solution.py:554
  2.7 0.1 copy.17
  2.8 2.0 %fusion = f32[64,4,256]{2,1,0:T(4,128)S(1)} fusion(f32[64,4,25]{2,1,0:T(4,128)S(1)} %copy.17, f32[64,25,256]{2,0,1:T(8,128)S(1)} %copy-done), kind=kOutput, calls=%fused_computation | convolution fusion | flops 19660800 | bytes 1926144 | tf_op jit(solution)/shard_map/sfl,slz->sfz/dot_general | solution.py:556
  4.9 0.0 copy-start.4
  4.9 0.0 copy-start.5
  4.9 0.0 copy-start.1
  5.0 1.5 %shard_map.84 = f32[16,72,128]{2,1,0:T(8,128)} custom-call(f32[64,1024]{1,0:T(8,128)S(1)} %bitcast.26, s32[64,1]{1,0:T(8,128)S(1)} %copy.19.column_ref, s32[1,64]{1,0:T(1,128)S(1)} %bitcast.28, s32[1,64]{1,0:T(1,128)S(1)} %bitcast.30), custom_call_target="tpu_custom_call" | custom-call | flops 100000000 | bytes 1048576 | tf_op jit(solution)/shard_map/pallas_call | solution.py:658
  6.5 7.4 %all-to-all-start = ((f32[16,72,128]{2,1,0:T(8,128)}), f32[16,72,128]{2,1,0:T(8,128)S(1)}, u32[]{:S(2)}, u32[]{:S(2)}) async-start(f32[16,72,128]{2,1,0:T(8,128)} %shard_map.84), calls=%async_computation | async-start | bytes 1179648 | tf_op jit(solution)/shard_map/all_to_all | solution.py:661
  13.9 0.2 fusion.9
  14.0 0.2 cosine_reduce_fusion
  14.2 0.1 pad_maximum_fusion.cs_ref.refs_4_
  14.3 3.7 %shard_map.82 = (f32[16,2,16,128]{3,2,1,0:T(8,128)S(1)}, f32[16,2,16,128]{3,2,1,0:T(8,128)S(1)}) custom-call(f32[64,1024]{1,0:T(8,128)S(1)} %bitcast.27, s32[1,64]{1,0:T(1,128)S(1)} %bitcast.29, s32[1,64]{1,0:T(1,128)S(1)} %bitcast.31, f32[2,2,2,32,256]{4,3,2,1,0:T(8,128)S(1)} %copy-done.1, f32[4]{0:T(128)S(1)} %pad_maximum_fusion.cs_ref.refs_4_), custom_call_target="tpu_custom_call" | custom-call | flops 100000000 | bytes 1048576 | tf_op jit(solution)/shard_map/pallas_call | solution.py:665
  18.0 0.5 collective-permute-start
  18.5 1.2 %collective-permute-done = f32[16,2,16,128]{3,2,1,0:T(8,128)S(1)} collective-permute-done((f32[16,2,16,128]{3,2,1,0:T(8,128)S(1)}, f32[16,2,16,128]{3,2,1,0:T(8,128)S(1)}, u32[]{:S(2)}, u32[]{:S(2)}) %collective-permute-start) | collective-permute-done | bytes 262176 | tf_op jit(solution)/shard_map/ppermute | solution.py:639
  19.7 2.0 %collective-permute-start.1 = (f32[16,2,16,128]{3,2,1,0:T(8,128)S(1)}, f32[16,2,16,128]{3,2,1,0:T(8,128)S(1)}, u32[]{:S(2)}, u32[]{:S(2)}) collective-permute-start(f32[16,2,16,128]{3,2,1,0:T(8,128)S(1)} %add.63), channel_id=1, source_target_pairs={{0,2},{1,3},{2,0},{3,1},{4,6},{5,7},{6,4},{7,5},{8,10},{9,11},{10,... | collective-permute-start | bytes 786440 | tf_op jit(solution)/shard_map/ppermute | solution.py:639
  21.7 0.1 collective-permute-start.8
  21.9 8.9 %collective-permute-done.1 = f32[16,2,16,128]{3,2,1,0:T(8,128)S(1)} collective-permute-done((f32[16,2,16,128]{3,2,1,0:T(8,128)S(1)}, f32[16,2,16,128]{3,2,1,0:T(8,128)S(1)}, u32[]{:S(2)}, u32[]{:S(2)}) %collective-permute-start.1) | collective-permute-done | bytes 262176 | tf_op jit(solution)/shard_map/ppermute | solution.py:639
  30.8 0.7 %dynamic-slice_bitcast_fusion.3 = (f32[4,2,16,128]{3,2,1,0:T(8,128)}, f32[4,2,16,128]{3,2,1,0:T(8,128)}, f32[4,2,16,128]{3,2,1,0:T(8,128)S(1)}) fusion(f32[4,4,2,16,128]{4,3,2,1,0:T(8,128)S(1)} %bitcast.32, s32[]{:T(128)S(6)} %select_n.59, s32[]{:T(128)S(6)} %select_n.63, s32[]{:T(128)S(6)} %select_n.61), kind=kLoop, calls=%fused_computation.8 | loop fusion | bytes 393228 | tf_op jit(solution)/shard_map/jit(dynamic_index_in_dim)/squeeze | solution.py:580
  31.5 1.9 %collective-permute-start.2 = (f32[4,2,16,128]{3,2,1,0:T(8,128)}, f32[4,2,16,128]{3,2,1,0:T(8,128)S(1)}, u32[]{:S(2)}, u32[]{:S(2)}) collective-permute-start(f32[4,2,16,128]{3,2,1,0:T(8,128)} %get-tuple-element.21), channel_id=1, source_target_pairs={{0,4},{1,5},{2,6},{3,7},{4,8},{5,9},{6,10},{7,11},{8,12},{9,13},{1... | collective-permute-start | bytes 196616 | tf_op jit(solution)/shard_map/ppermute | solution.py:639
  33.4 1.9 %collective-permute-start.4 = (f32[4,2,16,128]{3,2,1,0:T(8,128)}, f32[4,2,16,128]{3,2,1,0:T(8,128)S(1)}, u32[]{:S(2)}, u32[]{:S(2)}) collective-permute-start(f32[4,2,16,128]{3,2,1,0:T(8,128)} %get-tuple-element.22), channel_id=1, source_target_pairs={{0,12},{1,13},{2,14},{3,15},{4,0},{5,1},{6,2},{7,3},{8,4},{9,5},{1... | collective-permute-start | bytes 196616 | tf_op jit(solution)/shard_map/ppermute | solution.py:639
  35.3 0.9 %collective-permute-start.3 = (f32[4,2,16,128]{3,2,1,0:T(8,128)S(1)}, f32[4,2,16,128]{3,2,1,0:T(8,128)S(1)}, u32[]{:S(2)}, u32[]{:S(2)}) collective-permute-start(f32[4,2,16,128]{3,2,1,0:T(8,128)S(1)} %get-tuple-element.23), channel_id=1, source_target_pairs={{0,8},{1,9},{2,10},{3,11},{4,12},{5,13},{6,14},{7,15},{8,0},{9,1},... | collective-permute-start | bytes 196616 | tf_op jit(solution)/shard_map/ppermute | solution.py:639
  36.2 0.0 collective-permute-done.8.other_ref
  36.2 0.0 all-to-all-done.received_ref
  36.2 0.6 shard_map.85.f_ref
  36.9 2.0 %collective-permute-start.10 = (f32[4,2,32,256]{3,2,1,0:T(8,128)S(1)}, f32[4,2,32,256]{3,2,1,0:T(8,128)S(1)}, u32[]{:S(2)}, u32[]{:S(2)}) collective-permute-start(f32[4,2,32,256]{3,2,1,0:T(8,128)S(1)} %shard_map.85.f_ref), channel_id=1, source_target_pairs={{0,14},{1,15},{2,4},{3,5},{4,2},{5,3},{6,8},{7,9},{8,6},{9,7},{10,... | collective-permute-start | bytes 786440 | tf_op jit(solution)/shard_map/ppermute | solution.py:639
  38.8 0.2 collective-permute-start.9
  39.0 0.0 collective-permute-done.2
  39.0 5.3 %collective-permute-start.12 = (f32[2,2,32,256]{3,2,1,0:T(8,128)S(1)}, f32[2,2,32,256]{3,2,1,0:T(8,128)S(1)}, u32[]{:S(2)}, u32[]{:S(2)}) collective-permute-start(f32[2,2,32,256]{3,2,1,0:T(8,128)S(1)} %get-tuple-element.19), channel_id=1, source_target_pairs={{0,4},{1,5},{2,6},{3,7},{4,8},{5,9},{6,10},{7,11},{8,12},{9,13},{1... | collective-permute-start | bytes 393224 | tf_op jit(solution)/shard_map/ppermute | solution.py:639
  44.3 0.0 collective-permute-done.4
  44.3 0.0 collective-permute-start.11
  44.4 0.0 collective-permute-done.3
  44.4 3.5 %collective-permute-start.7 = (f32[4,2,16,128]{3,2,1,0:T(8,128)S(1)}, f32[4,2,16,128]{3,2,1,0:T(8,128)S(1)}, u32[]{:S(2)}, u32[]{:S(2)}) collective-permute-start(f32[4,2,16,128]{3,2,1,0:T(8,128)S(1)} %fusion.3.refs_0_), channel_id=1, source_target_pairs={{0,4},{1,5},{2,6},{3,7},{4,8},{5,9},{6,10},{7,11},{8,12},{9,13},{1... | collective-permute-start | bytes 196616 | tf_op jit(solution)/shard_map/ppermute | solution.py:639
  47.9 3.3 %collective-permute-done.12.before_ref = f32[2,2,32,256]{3,2,1,0:T(8,128)S(1)} collective-permute-done((f32[2,2,32,256]{3,2,1,0:T(8,128)S(1)}, f32[2,2,32,256]{3,2,1,0:T(8,128)S(1)}, u32[]{:S(2)}, u32[]{:S(2)}) %collective-permute-start.12) | collective-permute-done | bytes 131104 | tf_op jit(solution)/shard_map/ppermute | solution.py:639
  51.1 3.5 %collective-permute-start.6 = (f32[4,2,16,128]{3,2,1,0:T(8,128)S(1)}, f32[4,2,16,128]{3,2,1,0:T(8,128)S(1)}, u32[]{:S(2)}, u32[]{:S(2)}) collective-permute-start(f32[4,2,16,128]{3,2,1,0:T(8,128)S(1)} %fusion.3.refs_0_), channel_id=1, source_target_pairs={{0,8},{1,9},{2,10},{3,11},{4,12},{5,13},{6,14},{7,15},{8,0},{9,1},... | collective-permute-start | bytes 196616 | tf_op jit(solution)/shard_map/ppermute | solution.py:639
  54.7 0.6 collective-permute-start.5
  55.3 2.7 %shard_map.86 = (f32[2,2,32,256]{3,2,1,0:T(8,128)S(1)}, f32[2,2,32,256]{3,2,1,0:T(8,128)S(1)}) custom-call(f32[4,2,32,256]{3,2,1,0:T(8,128)S(1)} %collective-permute-done.9.even_ref, f32[4,2,32,256]{3,2,1,0:T(8,128)S(1)} %collective-permute-done.10.odd_ref, f32[2,2,32,256]{3,2,1,0:T(8,128)S(1)} %collective-permute-done.11.after_ref, ...), custom_call_target="tpu_custom_call" | custom-call | flops 10000000 | bytes 1048576 | tf_op jit(solution)/shard_map/pallas_call | solution.py:689
  58.0 0.1 collective-permute-start.14
  58.1 0.0 collective-permute-done.7.refs_3_
  58.1 0.9 %collective-permute-done.5.refs_1_ = f32[4,2,16,128]{3,2,1,0:T(8,128)S(1)} collective-permute-done((f32[4,2,16,128]{3,2,1,0:T(8,128)S(1)}, f32[4,2,16,128]{3,2,1,0:T(8,128)S(1)}, u32[]{:S(2)}, u32[]{:S(2)}) %collective-permute-start.5) | collective-permute-done | bytes 65568 | tf_op jit(solution)/shard_map/ppermute | solution.py:639
  58.9 2.9 %shard_map.83 = (f32[5,2,16,128]{3,2,1,0:T(8,128)S(1)}, f32[5,2,16,128]{3,2,1,0:T(8,128)S(1)}) custom-call(f32[4,2,16,128]{3,2,1,0:T(8,128)S(1)} %fusion.3.refs_0_, f32[4,2,16,128]{3,2,1,0:T(8,128)S(1)} %collective-permute-done.5.refs_1_, f32[4,2,16,128]{3,2,1,0:T(8,128)S(1)} %collective-permute-done.6.refs_2_, ...), custom_call_target="tpu_custom_call" | custom-call | flops 100000000 | bytes 1048576 | tf_op jit(solution)/shard_map/pallas_call | solution.py:700
  61.9 0.1 collective-permute-start.13
  61.9 0.9 %shard_map.87.own_ref = f32[2,2,32,256]{3,2,1,0:T(8,128)S(1)} custom-call(f32[5,2,16,128]{3,2,1,0:T(8,128)S(1)} %get-tuple-element.13.w_ref, f32[2,2,32,256]{3,2,1,0:T(8,128)S(1)} %get-tuple-element.14.g_ref), custom_call_target="tpu_custom_call" | custom-call | flops 10000000 | bytes 1048576 | tf_op jit(solution)/shard_map/pallas_call | solution.py:721
  62.9 0.4 collective-permute-done.13.w_ref
  63.2 0.0 collective-permute-done.14.g_ref
  63.2 1.6 %shard_map.88 = f32[2,2,2,32,256]{4,3,2,1,0:T(8,128)} custom-call(f32[2,2,32,256]{3,2,1,0:T(8,128)S(1)} %shard_map.87.own_ref, f32[5,2,16,128]{3,2,1,0:T(8,128)S(1)} %collective-permute-done.13.w_ref, f32[2,2,32,256]{3,2,1,0:T(8,128)S(1)} %collective-permute-done.14.g_ref), custom_call_target="tpu_custom_call" | custom-call | flops 10000000 | bytes 1048576 | tf_op jit(solution)/shard_map/pallas_call | solution.py:722
  (19 shorter events, 0.2 us)
Async XLA Ops:
  0.0 2.8 %copy-start = (f32[64,25,256]{2,0,1:T(8,128)S(1)}, f32[64,25,256]{2,0,1:T(8,128)}, u32[]{:S(2)}) copy-start(f32[64,25,256]{2,0,1:T(8,128)} %param.10) | copy-start | bytes 4915204
  1.8 3.2 %copy-start.2 = (s32[64,1]{0,1:T(1,128)S(1)}, s32[64,1]{0,1:T(1,128)}, u32[]{:S(2)}) copy-start(s32[64,1]{0,1:T(1,128)} %param.12) | copy-start | bytes 772
  1.8 3.2 %copy-start.3 = (s32[64]{0:T(128)S(1)}, s32[64]{0:T(128)}, u32[]{:S(2)}) copy-start(s32[64]{0:T(128)} %param.13) | copy-start | bytes 772
  4.9 9.0 %copy-start.4 = (s32[2,2]{1,0:T(2,128)S(1)}, s32[2,2]{1,0:T(2,128)}, u32[]{:S(2)}) copy-start(s32[2,2]{1,0:T(2,128)} %param.14) | copy-start | bytes 52
  4.9 9.0 %copy-start.5 = (f32[8]{0:T(128)S(1)}, f32[8]{0:T(128)}, u32[]{:S(2)}) copy-start(f32[8]{0:T(128)} %param.15) | copy-start | bytes 100
  4.9 9.4 %copy-start.1 = (f32[2,2,2,32,256]{4,3,2,1,0:T(8,128)S(1)}, f32[2,2,2,32,256]{4,3,2,1,0:T(8,128)}, u32[]{:S(2)}) copy-start(f32[2,2,2,32,256]{4,3,2,1,0:T(8,128)} %pd_ref.3) | copy-start | bytes 786436
  6.5 29.8 %all-to-all-start = ((f32[16,72,128]{2,1,0:T(8,128)}), f32[16,72,128]{2,1,0:T(8,128)S(1)}, u32[]{:S(2)}, u32[]{:S(2)}) async-start(f32[16,72,128]{2,1,0:T(8,128)} %shard_map.84), calls=%async_computation | async-start | bytes 1179648 | tf_op jit(solution)/shard_map/all_to_all | solution.py:661
  18.0 1.6 %collective-permute-start = (f32[16,2,16,128]{3,2,1,0:T(8,128)S(1)}, f32[16,2,16,128]{3,2,1,0:T(8,128)S(1)}, u32[]{:S(2)}, u32[]{:S(2)}) collective-permute-start(f32[16,2,16,128]{3,2,1,0:T(8,128)S(1)} %get-tuple-element.12), channel_id=1, source_target_pairs={{0,1},{1,0},{2,3},{3,2},{4,5},{5,4},{6,7},{7,6},{8,9},{9,8},{10,11... | collective-permute-start | bytes 786440 | tf_op jit(solution)/shard_map/ppermute | solution.py:639
  19.7 11.0 %collective-permute-start.1 = (f32[16,2,16,128]{3,2,1,0:T(8,128)S(1)}, f32[16,2,16,128]{3,2,1,0:T(8,128)S(1)}, u32[]{:S(2)}, u32[]{:S(2)}) collective-permute-start(f32[16,2,16,128]{3,2,1,0:T(8,128)S(1)} %add.63), channel_id=1, source_target_pairs={{0,2},{1,3},{2,0},{3,1},{4,6},{5,7},{6,4},{7,5},{8,10},{9,11},{10,... | collective-permute-start | bytes 786440 | tf_op jit(solution)/shard_map/ppermute | solution.py:639
  21.7 14.6 %collective-permute-start.8 = (f32[2,2,32,256]{3,2,1,0:T(8,128)S(1)}, f32[2,2,32,256]{3,2,1,0:T(8,128)S(1)}, u32[]{:S(2)}, u32[]{:S(2)}) collective-permute-start(f32[2,2,32,256]{3,2,1,0:T(8,128)S(1)} %dynamic-slice_bitcast_fusion), channel_id=1, source_target_pairs={{0,1},{1,0},{2,3},{3,2},{4,5},{5,4},{6,7},{7,6},{8,9},{9,8},{10,11... | collective-permute-start | bytes 393224 | tf_op jit(solution)/shard_map/ppermute | solution.py:639
  31.5 7.6 %collective-permute-start.2 = (f32[4,2,16,128]{3,2,1,0:T(8,128)}, f32[4,2,16,128]{3,2,1,0:T(8,128)S(1)}, u32[]{:S(2)}, u32[]{:S(2)}) collective-permute-start(f32[4,2,16,128]{3,2,1,0:T(8,128)} %get-tuple-element.21), channel_id=1, source_target_pairs={{0,4},{1,5},{2,6},{3,7},{4,8},{5,9},{6,10},{7,11},{8,12},{9,13},{1... | collective-permute-start | bytes 196616 | tf_op jit(solution)/shard_map/ppermute | solution.py:639
  33.4 11.0 %collective-permute-start.4 = (f32[4,2,16,128]{3,2,1,0:T(8,128)}, f32[4,2,16,128]{3,2,1,0:T(8,128)S(1)}, u32[]{:S(2)}, u32[]{:S(2)}) collective-permute-start(f32[4,2,16,128]{3,2,1,0:T(8,128)} %get-tuple-element.22), channel_id=1, source_target_pairs={{0,12},{1,13},{2,14},{3,15},{4,0},{5,1},{6,2},{7,3},{8,4},{9,5},{1... | collective-permute-start | bytes 196616 | tf_op jit(solution)/shard_map/ppermute | solution.py:639
  35.3 9.1 %collective-permute-start.3 = (f32[4,2,16,128]{3,2,1,0:T(8,128)S(1)}, f32[4,2,16,128]{3,2,1,0:T(8,128)S(1)}, u32[]{:S(2)}, u32[]{:S(2)}) collective-permute-start(f32[4,2,16,128]{3,2,1,0:T(8,128)S(1)} %get-tuple-element.23), channel_id=1, source_target_pairs={{0,8},{1,9},{2,10},{3,11},{4,12},{5,13},{6,14},{7,15},{8,0},{9,1},... | collective-permute-start | bytes 196616 | tf_op jit(solution)/shard_map/ppermute | solution.py:639
  36.9 18.4 %collective-permute-start.10 = (f32[4,2,32,256]{3,2,1,0:T(8,128)S(1)}, f32[4,2,32,256]{3,2,1,0:T(8,128)S(1)}, u32[]{:S(2)}, u32[]{:S(2)}) collective-permute-start(f32[4,2,32,256]{3,2,1,0:T(8,128)S(1)} %shard_map.85.f_ref), channel_id=1, source_target_pairs={{0,14},{1,15},{2,4},{3,5},{4,2},{5,3},{6,8},{7,9},{8,6},{9,7},{10,... | collective-permute-start | bytes 786440 | tf_op jit(solution)/shard_map/ppermute | solution.py:639
  38.8 16.4 %collective-permute-start.9 = (f32[4,2,32,256]{3,2,1,0:T(8,128)S(1)}, f32[4,2,32,256]{3,2,1,0:T(8,128)S(1)}, u32[]{:S(2)}, u32[]{:S(2)}) collective-permute-start(f32[4,2,32,256]{3,2,1,0:T(8,128)S(1)} %shard_map.85.f_ref), channel_id=1, source_target_pairs={{0,2},{1,3},{2,0},{3,1},{4,6},{5,7},{6,4},{7,5},{8,10},{9,11},{10,... | collective-permute-start | bytes 786440 | tf_op jit(solution)/shard_map/ppermute | solution.py:639
  39.0 12.1 %collective-permute-start.12 = (f32[2,2,32,256]{3,2,1,0:T(8,128)S(1)}, f32[2,2,32,256]{3,2,1,0:T(8,128)S(1)}, u32[]{:S(2)}, u32[]{:S(2)}) collective-permute-start(f32[2,2,32,256]{3,2,1,0:T(8,128)S(1)} %get-tuple-element.19), channel_id=1, source_target_pairs={{0,4},{1,5},{2,6},{3,7},{4,8},{5,9},{6,10},{7,11},{8,12},{9,13},{1... | collective-permute-start | bytes 393224 | tf_op jit(solution)/shard_map/ppermute | solution.py:639
  44.3 10.3 %collective-permute-start.11 = (f32[2,2,32,256]{3,2,1,0:T(8,128)S(1)}, f32[2,2,32,256]{3,2,1,0:T(8,128)S(1)}, u32[]{:S(2)}, u32[]{:S(2)}) collective-permute-start(f32[2,2,32,256]{3,2,1,0:T(8,128)S(1)} %get-tuple-element.20), channel_id=1, source_target_pairs={{0,12},{1,13},{2,14},{3,15},{4,0},{5,1},{6,2},{7,3},{8,4},{9,5},{1... | collective-permute-start | bytes 393224 | tf_op jit(solution)/shard_map/ppermute | solution.py:639
  44.4 13.7 %collective-permute-start.7 = (f32[4,2,16,128]{3,2,1,0:T(8,128)S(1)}, f32[4,2,16,128]{3,2,1,0:T(8,128)S(1)}, u32[]{:S(2)}, u32[]{:S(2)}) collective-permute-start(f32[4,2,16,128]{3,2,1,0:T(8,128)S(1)} %fusion.3.refs_0_), channel_id=1, source_target_pairs={{0,4},{1,5},{2,6},{3,7},{4,8},{5,9},{6,10},{7,11},{8,12},{9,13},{1... | collective-permute-start | bytes 196616 | tf_op jit(solution)/shard_map/ppermute | solution.py:639
  51.1 6.9 %collective-permute-start.6 = (f32[4,2,16,128]{3,2,1,0:T(8,128)S(1)}, f32[4,2,16,128]{3,2,1,0:T(8,128)S(1)}, u32[]{:S(2)}, u32[]{:S(2)}) collective-permute-start(f32[4,2,16,128]{3,2,1,0:T(8,128)S(1)} %fusion.3.refs_0_), channel_id=1, source_target_pairs={{0,8},{1,9},{2,10},{3,11},{4,12},{5,13},{6,14},{7,15},{8,0},{9,1},... | collective-permute-start | bytes 196616 | tf_op jit(solution)/shard_map/ppermute | solution.py:639
  54.7 4.3 %collective-permute-start.5 = (f32[4,2,16,128]{3,2,1,0:T(8,128)S(1)}, f32[4,2,16,128]{3,2,1,0:T(8,128)S(1)}, u32[]{:S(2)}, u32[]{:S(2)}) collective-permute-start(f32[4,2,16,128]{3,2,1,0:T(8,128)S(1)} %fusion.3.refs_0_), channel_id=1, source_target_pairs={{0,12},{1,13},{2,14},{3,15},{4,0},{5,1},{6,2},{7,3},{8,4},{9,5},{1... | collective-permute-start | bytes 196616 | tf_op jit(solution)/shard_map/ppermute | solution.py:639
  58.0 5.2 %collective-permute-start.14 = (f32[2,2,32,256]{3,2,1,0:T(8,128)S(1)}, f32[2,2,32,256]{3,2,1,0:T(8,128)S(1)}, u32[]{:S(2)}, u32[]{:S(2)}) collective-permute-start(f32[2,2,32,256]{3,2,1,0:T(8,128)S(1)} %get-tuple-element.16), channel_id=1, source_target_pairs={{0,1},{1,0},{2,3},{3,2},{4,5},{5,4},{6,7},{7,6},{8,9},{9,8},{10,11... | collective-permute-start | bytes 393224 | tf_op jit(solution)/shard_map/ppermute | solution.py:639
  61.9 1.3 %collective-permute-start.13 = (f32[5,2,16,128]{3,2,1,0:T(8,128)S(1)}, f32[5,2,16,128]{3,2,1,0:T(8,128)S(1)}, u32[]{:S(2)}, u32[]{:S(2)}) collective-permute-start(f32[5,2,16,128]{3,2,1,0:T(8,128)S(1)} %get-tuple-element.15), channel_id=1, source_target_pairs={{0,1},{1,0},{2,3},{3,2},{4,5},{5,4},{6,7},{7,6},{8,9},{9,8},{10,11... | collective-permute-start | bytes 245768 | tf_op jit(solution)/shard_map/ppermute | solution.py:639

commit v5 on v3

--- a/solution.py
+++ b/solution.py
@@ -99,71 +99,117 @@
         place_planes(ext, middle + planes, odd_ref, *high)
 
 
-def pack_kernel(rows_ref, column_ref, row_ref, line_ref, out_ref):
-    slots = rows_ref.shape[0]
-    tiles, height, _ = out_ref.shape
+def as_column(row):
+    n = row.shape[1]
+    i = lax.broadcasted_iota(jnp.int32, (n, n), 0)
+    j = lax.broadcasted_iota(jnp.int32, (n, n), 1)
+    return jnp.sum(jnp.where(i == j, row, 0.0), axis=1, keepdims=True)
+
+
+def rows_kernel(moments_ref, shapes_ref, atom_ref, tile_ref, line_ref, keep_ref, send_ref, rows):
+    core = lax.rem(lax.axis_index("grid"), 2)
+    slots, channels, depth = shapes_ref.shape
+    atoms = moments_ref.shape[0]
+    atom = as_column(atom_ref[...].astype(jnp.float32))
+    picks = [jnp.where(atom == float(a), 1.0, 0.0) for a in range(atoms)]
+    chosen = []
+    for f in range(4):
+        total = None
+        for a in range(atoms):
+            value = picks[a] * moments_ref[a, f // 2, f % 2 : f % 2 + 1]
+            total = value if total is None else total + value
+        chosen.append(total)
+    for i in range(slots // 8):
+        near = slice(8 * i, 8 * i + 8)
+        totals = [None] * 4
+        for channel in range(channels):
+            shape = shapes_ref[near, channel]
+            for f in range(4):
+                value = chosen[f][near, channel : channel + 1] * shape
+                totals[f] = value if totals[f] is None else totals[f] + value
+        for f in range(4):
+            rows[f // 2, near, f % 2 * depth : (f % 2 + 1) * depth] = totals[f]
+    keep_ref[...] = rows[core]
+    send_ref[0:slots] = rows[1 - core]
+    send_ref[slots:] = jnp.zeros((8, 2 * depth), jnp.float32)
+    number = (tile_ref[...] * 64 + line_ref[...]).astype(jnp.float32)
+    send_ref[slots : slots + 1, 0:slots] = number
+
+
+def pack_kernel(own_ref, got_ref, tile_ref, line_ref, *out_refs):
+    slots = own_ref.shape[0]
+    apart = len(out_refs) > 1
+    height = out_refs[0].shape[-2]
     ranks = (height - 8) // 4
-    capacity = ranks // 2
-    buckets = tiles * capacity
-    chips = tiles // 2
-    position = lax.axis_index("grid")
-    i = lax.broadcasted_iota(jnp.int32, (slots, slots), 0)
-    j = lax.broadcasted_iota(jnp.int32, (slots, slots), 1)
-    ahead = jnp.where((column_ref[...] == row_ref[...]) & (i < j), 1.0, 0.0)
+    capacity = ranks // 4
+    chips = lax.axis_size("grid") // 2
+    chip = lax.div(lax.axis_index("grid"), 2)
+    number = (tile_ref[...] * 64 + line_ref[...]).astype(jnp.float32)
+    number = jnp.concatenate([number, got_ref[slots : slots + 1, 0:slots]], axis=1).astype(jnp.int32)
+    tile, line = number // 64, number % 128 + 1
+    column = as_column(tile.astype(jnp.float32)).astype(jnp.int32)
+    i = lax.broadcasted_iota(jnp.int32, (2 * slots, 2 * slots), 0)
+    j = lax.broadcasted_iota(jnp.int32, (2 * slots, 2 * slots), 1)
+    ahead = jnp.where((column == tile) & (i < j) & (i // slots == j // slots), 1.0, 0.0)
     rank = jnp.sum(ahead, axis=0, keepdims=True).astype(jnp.int32)
-    place = row_ref[...] * capacity + rank
-    bucket = lax.broadcasted_iota(jnp.int32, (buckets, slots), 0)
-    pick = bucket == place
-    packed = dot(pick.astype(jnp.float32), rows_ref[...])
-    for chip in range(chips):
-        for p in range(2):
-            for q in range(4):
-                out_ref[2 * chip + p, q * ranks : (q + 1) * ranks] = packed[
-                    chip * ranks : (chip + 1) * ranks, (4 * p + q) * 128 : (4 * p + q + 1) * 128
-                ]
-    thick_lines = 64
-    line = jnp.sum(jnp.where(pick, line_ref[...] + 1, 0).astype(jnp.float32), axis=1, keepdims=True)
-    own = lax.broadcasted_iota(jnp.int32, (buckets, 1), 0) // capacity % 2
-    line = jnp.where(line > 0, line + (own * thick_lines).astype(jnp.float32), 0.0)
-    bucket = lax.broadcasted_iota(jnp.int32, (buckets, 128), 0)
-    lane = lax.broadcasted_iota(jnp.int32, (buckets, 128), 1)
-    start = lax.rem(position, 128 // ranks) * ranks
-    spots = jnp.where(lane - start == bucket % ranks, line, 0.0)
-    i = lax.broadcasted_iota(jnp.int32, (chips, buckets), 0)
-    j = lax.broadcasted_iota(jnp.int32, (chips, buckets), 1)
+    device = lax.broadcasted_iota(jnp.int32, (1, 2 * slots), 1) // slots
+    place = tile // 2 * ranks + (2 * device + tile % 2) * capacity + rank
+    r = lax.broadcasted_iota(jnp.int32, (ranks, 2 * slots), 0)
+    targets = [lax.bitwise_xor(chip, k) if apart else k for k in range(chips)]
+    pick = jnp.concatenate([jnp.where(place == r + target * ranks, 1.0, 0.0) for target in targets])
+    rows = jnp.concatenate([own_ref[...], got_ref[0:slots]], axis=0)
+    packed = dot(pick, rows)
+    lines = jnp.sum(pick * line.astype(jnp.float32), axis=1, keepdims=True)
+    bucket = lax.broadcasted_iota(jnp.int32, (chips * ranks, 128), 0)
+    lane = lax.broadcasted_iota(jnp.int32, (chips * ranks, 128), 1)
+    spot = bucket // ranks if apart else chip
+    spots = jnp.where(lane == spot % (128 // ranks) * ranks + bucket % ranks, lines, 0.0)
+    i = lax.broadcasted_iota(jnp.int32, (chips, chips * ranks), 0)
+    j = lax.broadcasted_iota(jnp.int32, (chips, chips * ranks), 1)
     numbers = dot(jnp.where(i == j // ranks, 1.0, 0.0), spots)
-    for chip in range(chips):
-        value = jnp.broadcast_to(numbers[chip : chip + 1], (8, 128))
-        for p in range(2):
-            out_ref[2 * chip + p, 4 * ranks :] = value
-
-
-def density_kernel(pd_ref, other_ref, received_ref, f_ref, straight_ref, across_ref, b1, half):
+    for k in range(chips):
+        out = out_refs[k] if apart else out_refs[0].at[k]
+        for q in range(4):
+            out[q * ranks : (q + 1) * ranks] = packed[
+                k * ranks : (k + 1) * ranks, q * 128 : (q + 1) * 128
+            ]
+        out[4 * ranks :] = jnp.broadcast_to(numbers[k : k + 1], (8, 128))
+
+
+def density_kernel(*refs):
+    pd_ref, other_ref = refs[:2]
+    f_ref, straight_ref, across_ref, b1, half = refs[-5:]
+    pieces = refs[2:-5]
     position = lax.axis_index("grid")
     core, side = lax.rem(position, 2), lax.rem(lax.div(position, 2), 2)
     planes, _, lines, depth = f_ref.shape
-    sources, height, _ = received_ref.shape
+    sources = lax.axis_size("grid") // 2
+    height = pieces[0].shape[-2]
     ranks = (height - 8) // 4
     group = 128 // ranks
+
+    def received(source, start, stop):
+        if len(pieces) > 1:
+            return pieces[source][start:stop]
+        return pieces[0][source, start:stop]
+
     added = [None, None]
     for first in range(0, sources, group):
-        count = min(group, sources - first)
-        numbers = received_ref[first, 4 * ranks : 4 * ranks + 1]
-        for k in range(1, count):
-            numbers = numbers + received_ref[first + k, 4 * ranks : 4 * ranks + 1]
+        members = range(first, min(first + group, sources))
+        numbers = sum(received(k, 4 * ranks, 4 * ranks + 1) for k in members)
         line = lax.broadcasted_iota(jnp.int32, (planes * lines, 128), 0)
         spread = jnp.where(line == numbers.astype(jnp.int32) - 1, 1.0, 0.0)
         for part in range(2):
             values = jnp.concatenate(
                 [
-                    received_ref[first : first + count, q * ranks : (q + 1) * ranks].reshape(
-                        count * ranks, 128
+                    jnp.concatenate(
+                        [received(k, q * ranks, (q + 1) * ranks) for k in members], axis=0
                     )
                     for q in (2 * part, 2 * part + 1)
                 ],
                 axis=1,
             )
-            value = dot(spread[:, : count * ranks], values)
+            value = dot(spread[:, : len(members) * ranks], values)
             added[part] = value if added[part] is None else added[part] + value
     for x in range(planes):
         for part in range(2):
@@ -379,7 +425,7 @@
     length = count // radix
     digit = lax.div(block, length // 4)
     for k, piece in enumerate(pieces):
-        s[pl.ds(lax.rem(digit + k, radix) * length, length)] = piece[...]
+        s[pl.ds(lax.bitwise_xor(lax.rem(digit, radix), k) * length, length)] = piece[...]
 
     def sweep(values, target, residual=False):
         values[0, 0], values[0, 1] = rotated(values[count, 0], values[count, 1], cosine, -sine)
@@ -535,35 +581,18 @@
     return jnp.concatenate([jnp.cos(angle), jnp.sin(angle)])
 
 
-def make_rows(moments, shapes, slot_atom):
-    slot_count = shapes.shape[0]
-    atom_count = moments.shape[0]
-    atom_pick = (slot_atom[:, None] == jnp.arange(atom_count, dtype=jnp.int32)[None, :]).astype(
-        jnp.float32
-    )
-    chosen = jnp.dot(atom_pick, moments.reshape(atom_count, -1), precision=highest)
-    chosen = chosen.reshape(slot_count, moments.shape[1] * moments.shape[2], moments.shape[3])
-    return jnp.einsum("sfl,slz->sfz", chosen, shapes, precision=highest).reshape(slot_count, -1)
-
-
 def gather_blocks(value, blocks, block, permute_block):
     stride = 1
     while True:
         radix = min(4, blocks // stride)
         digit = block // stride % radix
-
-        def towards(k):
-            def target(b):
-                own = b // stride % radix
-                return b + ((own - k) % radix - own) * stride
-
-            return target
-
-        pieces = [value] + [permute_block(value, towards(k)) for k in range(1, radix)]
+        pieces = [value] + [
+            permute_block(value, lambda b, k=k: b ^ k * stride) for k in range(1, radix)
+        ]
         stride *= radix
         if stride == blocks:
             return pieces
-        stacked = jnp.roll(jnp.stack(pieces), digit, axis=0)
+        stacked = jnp.stack(pieces)[jnp.arange(radix) ^ digit]
         value = stacked.reshape(-1, *value.shape[1:])
 
 
@@ -625,21 +654,47 @@
     cs = pair_phases(pair_table, k_fraction)
 
     other = permute(lax.dynamic_index_in_dim(pair_density, 1 - core, 0, False), partner)
-    rows = make_rows(moments, shapes, slot_atom)
-    packed = call(pack_kernel, shaped(tile_count, 8 * capacity + 8, 128), vmem(4), [], 10**8)(
-        rows, slot_tile, slot_tile.reshape(1, -1), slot_row.reshape(1, -1)
-    )
-    received = lax.all_to_all(packed, "grid", split_axis=0, concat_axis=0, tiled=True)
+    tile_row, line_row = slot_tile.reshape(1, -1), slot_row.reshape(1, -1)
+    row = 2 * depth
+    kept, sent = call(
+        rows_kernel,
+        [shaped(slot_count, row), shaped(slot_count + 8, row)],
+        vmem(5),
+        [(2, slot_count, row)],
+        10**7,
+    )(moments, shapes, slot_atom.reshape(1, -1), tile_row, line_row)
+    got = permute(sent, partner)
+    apart = chips <= 8
+    height = 16 * capacity + 8
+    packed = call(
+        pack_kernel,
+        [shaped(height, 128)] * chips if apart else [shaped(chips, height, 128)],
+        vmem(4),
+        [],
+        10**8,
+    )(kept, got, tile_row, line_row)
+    if apart:
+        received = {0: packed[0]}
+        for k in sorted(range(1, chips), reverse=True):
+            received[k] = permute(packed[k], lambda i, k=k: i ^ (2 * k))
+        received = [received[k] for k in range(chips)]
+    else:
+        groups = [[2 * k + c for k in range(chips)] for c in range(2)]
+        received = [
+            lax.all_to_all(
+                packed[0], "grid", split_axis=0, concat_axis=0, axis_index_groups=groups, tiled=True
+            )
+        ]
 
     full = (2, lines, depth)
     small = (2, lines // 2, depth // 2)
     f, straight, across = call(
         density_kernel,
         [shaped(planes, *full), shaped(10, lines, 128), shaped(2, *full)],
-        vmem(3),
+        vmem(2 + len(received)),
         [(planes + 4, *full), (8, lines, 128)],
         10**8,
-    )(pair_density, other, received)
+    )(pair_density, other, *received)
     even = permute(f, even_side)
     odd = permute(f, odd_side)
     straight = permute(straight, next_block)

time: 64.1 us -> 60.8 us (0.949)
  waiting for transfers between devices: 26.4 us -> 18.7 us
  starting transfers between devices: 19.1 us -> 24.3 us
  matrix products: 2.92 us -> 0 us
  local copies, waits for them, and re-layouts: 1.34 us -> 2.5 us
  Pallas kernels: 13.4 us -> 14.5 us
    all_to_all x1 -> x0, waiting for transfers between devices: 14.1 us -> none  [per_device(): lax.all_to_all(packed, 'grid', split_axis=0, concat_axis=0, tiled=True)]
    ppermute x10 -> x18, starting transfers between devices: 11.7 us -> 24.3 us  [permute(): return lax.ppermute(value, 'grid', [(i, target(i)) for i in devices])]
    all_to_all x1 -> x0, starting transfers between devices: 7.35 us -> none  [per_device(): lax.all_to_all(packed, 'grid', split_axis=0, concat_axis=0, tiled=True)]
    ppermute x10 -> x18, waiting for transfers between devices: 12.4 us -> 18.7 us  [permute(): return lax.ppermute(value, 'grid', [(i, target(i)) for i in devices])]
    dot_general x2 -> x0, matrix products: 2.92 us -> none  [the longest x1 2.01 us: make_rows(): jnp.einsum('sfl,slz->sfz', chosen, shapes, precision=highest)]
    unnamed x14 -> x15, local copies, waits for them, and re-layouts: 0.18 us -> 2.49 us
    pallas_call x1 -> x2, Pallas kernels: 1.49 us -> 2.54 us  [the longest x1 1.75 us: per_device(): call(rows_kernel, [shaped(slot_count, row), shaped(slot_count + 8, row)],...]
    reshape x1 -> x0, local copies, waits for them, and re-layouts: 0.94 us -> none  [make_rows(): moments.reshape(atom_count, -1)]
  transfers between devices with their start and end apart: 11 -> 18, of which waited for: 7 -> 7; matrix products, arithmetic and copies ran while one was open for 1% -> 1% of each run, Pallas kernels for 14% -> 16%
where the time goes in v5:
time: 60.8 us; the launch traced here: 60.6 us
  starting transfers between devices  24.3 us (40%)
  waiting for transfers between devices  18.7 us (31%)
  Pallas kernels  14.5 us (24%)
  local copies, waits for them, and re-layouts  2.5 us (4%)
    ppermute x18, starting transfers between devices, permute(): return lax.ppermute(value, 'grid', [(i, target(i)) for i in devices])  24.3 us
    ppermute x18, waiting for transfers between devices, permute(): return lax.ppermute(value, 'grid', [(i, target(i)) for i in devices])  18.7 us
    pallas_call x1, Pallas kernels, per_device(): call(cycle_kernel, [shaped(5, *small)] * 2, vmem(len(pieces)) + smem, [(n...  2.93 us
    pallas_call x1, Pallas kernels, per_device(): call(fine_kernel, [shaped(thick, *full)] * 2, vmem(5) + smem, [(3 * plane...  2.73 us
    pallas_call x1, Pallas kernels, per_device(): call(source_kernel, shaped(planes, *small), vmem(4) + smem, [(4 * planes,...  2.51 us
    unnamed x15, local copies, waits for them, and re-layouts  2.49 us
    pallas_call x1, Pallas kernels, per_device(): call(rows_kernel, [shaped(slot_count, row), shaped(slot_count + 8, row)],...  1.75 us
    pallas_call x1, Pallas kernels, per_device(): call(output_kernel, shaped(*pair_density.shape), vmem(3), scratch, 10 ** 7)  1.61 us
  transfers between devices with their start and end apart: 18, of which 7 were waited for; matrix products, arithmetic and copies ran while one was open for 1% of the time, Pallas kernels for 16%

profile of v5, /device:TPU:0, one launch (start us, length us, event | category | flops | bytes accessed | tf_op | source)
XLA Modules:
  0.0 60.6 jit_solution(3930297859423398401)
XLA Ops:
  0.0 2.5 %copy.11.shapes_ref = f32[64,25,256]{2,1,0:T(8,128)S(1)} copy(f32[64,25,256]{2,0,1:T(8,128)} %param.10) | data formatting | bytes 3276800 | tf_op args[2]
  2.5 0.0 copy-start.5
  2.5 0.0 copy-start.6
  2.5 1.7 %shard_map.82 = (f32[64,512]{1,0:T(8,128)S(1)}, f32[72,512]{1,0:T(8,128)S(1)}) custom-call(f32[12,2,2,25]{3,2,1,0:T(2,128)S(1)} %copy-done.1, f32[64,25,256]{2,1,0:T(8,128)S(1)} %copy.11.shapes_ref, s32[1,64]{1,0:T(1,128)S(1)} %bitcast.5, s32[1,64]{1,0:T(1,128)S(1)} %bitcast.6, s32[1,64]{1,0:T(1,128)S(1)} %bitcast.8), custom_call_target="tpu_custom_call" | custom-call | flops 10000000 | bytes 1048576 | tf_op jit(solution)/shard_map/pallas_call | solution.py:659
  4.3 0.5 collective-permute-start.1
  4.8 0.1 collective-permute-start
  5.0 0.9 %collective-permute-done.1.got_ref = f32[72,512]{1,0:T(8,128)S(1)} collective-permute-done((f32[72,512]{1,0:T(8,128)S(1)}, f32[72,512]{1,0:T(8,128)S(1)}, u32[]{:S(2)}, u32[]{:S(2)}) %collective-permute-start.1) | collective-permute-done | bytes 147488 | tf_op jit(solution)/shard_map/ppermute | solution.py:637
  5.8 0.8 %shard_map.83 = (f32[136,128]{1,0:T(8,128)S(1)}, f32[136,128]{1,0:T(8,128)S(1)}, f32[136,128]{1,0:T(8,128)S(1)}, f32[136,128]{1,0:T(8,128)S(1)}, f32[136,128]{1,...) custom-call(f32[64,512]{1,0:T(8,128)S(1)} %get-tuple-element.22.own_ref, ...), custom_call_target="tpu_custom_call" | custom-call | flops 100000000 | bytes 1048576 | tf_op jit(solution)/shard_map/pallas_call | solution.py:669
  6.6 2.9 %collective-permute-start.2 = (f32[136,128]{1,0:T(8,128)S(1)}, f32[136,128]{1,0:T(8,128)S(1)}, u32[]{:S(2)}, u32[]{:S(2)}) collective-permute-start(f32[136,128]{1,0:T(8,128)S(1)} %get-tuple-element.25), channel_id=1, source_target_pairs={{0,2},{1,3},{2,0},{3,1},{4,6},{5,7},{6,4},{7,5},{8,10},{9,11},{10,... | collective-permute-start | bytes 208904 | tf_op jit(solution)/shard_map/ppermute | solution.py:637
  9.5 1.6 %collective-permute-start.3 = (f32[136,128]{1,0:T(8,128)S(1)}, f32[136,128]{1,0:T(8,128)S(1)}, u32[]{:S(2)}, u32[]{:S(2)}) collective-permute-start(f32[136,128]{1,0:T(8,128)S(1)} %get-tuple-element.26), channel_id=1, source_target_pairs={{0,4},{1,5},{2,6},{3,7},{4,0},{5,1},{6,2},{7,3},{8,12},{9,13},{10,... | collective-permute-start | bytes 208904 | tf_op jit(solution)/shard_map/ppermute | solution.py:637
  11.1 0.0 collective-permute-start.4
  11.1 3.0 %collective-permute-start.5 = (f32[136,128]{1,0:T(8,128)S(1)}, f32[136,128]{1,0:T(8,128)S(1)}, u32[]{:S(2)}, u32[]{:S(2)}) collective-permute-start(f32[136,128]{1,0:T(8,128)S(1)} %get-tuple-element.28), channel_id=1, source_target_pairs={{0,8},{1,9},{2,10},{3,11},{4,12},{5,13},{6,14},{7,15},{8,0},{9,1},... | collective-permute-start | bytes 208904 | tf_op jit(solution)/shard_map/ppermute | solution.py:637
  14.1 1.3 %collective-permute-start.6 = (f32[136,128]{1,0:T(8,128)S(1)}, f32[136,128]{1,0:T(8,128)S(1)}, u32[]{:S(2)}, u32[]{:S(2)}) collective-permute-start(f32[136,128]{1,0:T(8,128)S(1)} %get-tuple-element.29), channel_id=1, source_target_pairs={{0,10},{1,11},{2,8},{3,9},{4,14},{5,15},{6,12},{7,13},{8,2},{9,3},... | collective-permute-start | bytes 208904 | tf_op jit(solution)/shard_map/ppermute | solution.py:637
  15.4 3.6 %collective-permute-start.7 = (f32[136,128]{1,0:T(8,128)S(1)}, f32[136,128]{1,0:T(8,128)S(1)}, u32[]{:S(2)}, u32[]{:S(2)}) collective-permute-start(f32[136,128]{1,0:T(8,128)S(1)} %get-tuple-element.30), channel_id=1, source_target_pairs={{0,12},{1,13},{2,14},{3,15},{4,8},{5,9},{6,10},{7,11},{8,4},{9,5},... | collective-permute-start | bytes 208904 | tf_op jit(solution)/shard_map/ppermute | solution.py:637
  19.0 0.0 collective-permute-done.3.refs_4_
  19.0 0.0 collective-permute-start.8
  19.0 0.0 collective-permute-done.4.refs_5_
  19.0 0.0 collective-permute-done.5.refs_6_
  19.0 6.0 %collective-permute-done.6.refs_7_ = f32[136,128]{1,0:T(8,128)S(1)} collective-permute-done((f32[136,128]{1,0:T(8,128)S(1)}, f32[136,128]{1,0:T(8,128)S(1)}, u32[]{:S(2)}, u32[]{:S(2)}) %collective-permute-start.6) | collective-permute-done | bytes 69664 | tf_op jit(solution)/shard_map/ppermute | solution.py:637
  25.0 0.0 collective-permute-done.7.refs_8_
  25.0 1.1 %collective-permute-done.8.refs_9_ = f32[136,128]{1,0:T(8,128)S(1)} collective-permute-done((f32[136,128]{1,0:T(8,128)S(1)}, f32[136,128]{1,0:T(8,128)S(1)}, u32[]{:S(2)}, u32[]{:S(2)}) %collective-permute-start.8) | collective-permute-done | bytes 69664 | tf_op jit(solution)/shard_map/ppermute | solution.py:637
  26.1 1.2 %shard_map.84 = (f32[4,2,32,256]{3,2,1,0:T(8,128)S(1)}, f32[10,32,128]{2,1,0:T(8,128)S(1)}, f32[2,2,32,256]{3,2,1,0:T(8,128)S(1)}) custom-call(f32[2,2,2,32,256]{4,3,2,1,0:T(8,128)S(1)} %copy-done, f32[2,2,32,256]{3,2,1,0:T(8,128)S(1)} %collective-permute-done.refs_1_, f32[136,128]{1,0:T(8,128)S(1)} %get-tuple-element.24.refs_2_, ...), custom_call_target="tpu_custom_call" | custom-call | flops 100000000 | bytes 1048576 | tf_op jit(solution)/shard_map/pallas_call | solution.py:691
  27.3 2.4 %collective-permute-start.10 = (f32[4,2,32,256]{3,2,1,0:T(8,128)S(1)}, f32[4,2,32,256]{3,2,1,0:T(8,128)S(1)}, u32[]{:S(2)}, u32[]{:S(2)}) collective-permute-start(f32[4,2,32,256]{3,2,1,0:T(8,128)S(1)} %get-tuple-element.32.f_ref), channel_id=1, source_target_pairs={{0,14},{1,15},{2,4},{3,5},{4,2},{5,3},{6,8},{7,9},{8,6},{9,7},{10,... | collective-permute-start | bytes 786440 | tf_op jit(solution)/shard_map/ppermute | solution.py:637
  29.7 1.8 %collective-permute-start.9 = (f32[4,2,32,256]{3,2,1,0:T(8,128)S(1)}, f32[4,2,32,256]{3,2,1,0:T(8,128)S(1)}, u32[]{:S(2)}, u32[]{:S(2)}) collective-permute-start(f32[4,2,32,256]{3,2,1,0:T(8,128)S(1)} %get-tuple-element.32.f_ref), channel_id=1, source_target_pairs={{0,2},{1,3},{2,0},{3,1},{4,6},{5,7},{6,4},{7,5},{8,10},{9,11},{10,... | collective-permute-start | bytes 786440 | tf_op jit(solution)/shard_map/ppermute | solution.py:637
  31.4 0.2 fusion
  31.6 1.2 %collective-permute-start.11 = (f32[10,32,128]{2,1,0:T(8,128)S(1)}, f32[10,32,128]{2,1,0:T(8,128)S(1)}, u32[]{:S(2)}, u32[]{:S(2)}) collective-permute-start(f32[10,32,128]{2,1,0:T(8,128)S(1)} %get-tuple-element.33), channel_id=1, source_target_pairs={{0,12},{1,13},{2,6},{3,7},{4,0},{5,1},{6,10},{7,11},{8,4},{9,5},{1... | collective-permute-start | bytes 491528 | tf_op jit(solution)/shard_map/ppermute | solution.py:637
  32.8 0.2 cosine_reduce_fusion
  33.1 0.8 %collective-permute-start.15 = (f32[2,2,32,256]{3,2,1,0:T(8,128)S(1)}, f32[2,2,32,256]{3,2,1,0:T(8,128)S(1)}, u32[]{:S(2)}, u32[]{:S(2)}) collective-permute-start(f32[2,2,32,256]{3,2,1,0:T(8,128)S(1)} %get-tuple-element.35), channel_id=1, source_target_pairs={{0,4},{1,5},{2,14},{3,15},{4,8},{5,9},{6,2},{7,3},{8,12},{9,13},{1... | collective-permute-start | bytes 393224 | tf_op jit(solution)/shard_map/ppermute | solution.py:637
  33.9 0.1 pad_maximum_fusion.cs_ref.refs_4_
  34.0 5.5 %collective-permute-done.11.straight_ref = f32[10,32,128]{2,1,0:T(8,128)S(1)} collective-permute-done((f32[10,32,128]{2,1,0:T(8,128)S(1)}, f32[10,32,128]{2,1,0:T(8,128)S(1)}, u32[]{:S(2)}, u32[]{:S(2)}) %collective-permute-start.11) | collective-permute-done | bytes 163872 | tf_op jit(solution)/shard_map/ppermute | solution.py:637
  39.5 0.0 collective-permute-done.10.odd_ref
  39.5 2.2 %collective-permute-done.9.even_ref = f32[4,2,32,256]{3,2,1,0:T(8,128)S(1)} collective-permute-done((f32[4,2,32,256]{3,2,1,0:T(8,128)S(1)}, f32[4,2,32,256]{3,2,1,0:T(8,128)S(1)}, u32[]{:S(2)}, u32[]{:S(2)}) %collective-permute-start.9) | collective-permute-done | bytes 262176 | tf_op jit(solution)/shard_map/ppermute | solution.py:637
  41.7 2.5 %shard_map.85.refs_0_ = f32[4,2,16,128]{3,2,1,0:T(8,128)S(1)} custom-call(f32[4,2,32,256]{3,2,1,0:T(8,128)S(1)} %collective-permute-done.9.even_ref, f32[4,2,32,256]{3,2,1,0:T(8,128)S(1)} %collective-permute-done.10.odd_ref, f32[10,32,128]{2,1,0:T(8,128)S(1)} %collective-permute-done.11.straight_ref, f32[4,2,32,256]{3,2,1,0:T(8,128)S(1)} %get-tuple-element.32.f_ref, ...), custom_call_target="tpu_custom_call" | custom-call | flops 10000000 | bytes 1048576 | tf_op jit(solution)/shard_map/pallas_call | solution.py:702
  44.2 2.6 %collective-permute-start.12 = (f32[4,2,16,128]{3,2,1,0:T(8,128)S(1)}, f32[4,2,16,128]{3,2,1,0:T(8,128)S(1)}, u32[]{:S(2)}, u32[]{:S(2)}) collective-permute-start(f32[4,2,16,128]{3,2,1,0:T(8,128)S(1)} %shard_map.85.refs_0_), channel_id=1, source_target_pairs={{0,4},{1,5},{2,6},{3,7},{4,0},{5,1},{6,2},{7,3},{8,12},{9,13},{10,... | collective-permute-start | bytes 196616 | tf_op jit(solution)/shard_map/ppermute | solution.py:637
  46.8 0.8 %collective-permute-start.13 = (f32[4,2,16,128]{3,2,1,0:T(8,128)S(1)}, f32[4,2,16,128]{3,2,1,0:T(8,128)S(1)}, u32[]{:S(2)}, u32[]{:S(2)}) collective-permute-start(f32[4,2,16,128]{3,2,1,0:T(8,128)S(1)} %shard_map.85.refs_0_), channel_id=1, source_target_pairs={{0,8},{1,9},{2,10},{3,11},{4,12},{5,13},{6,14},{7,15},{8,0},{9,1},... | collective-permute-start | bytes 196616 | tf_op jit(solution)/shard_map/ppermute | solution.py:637
  47.6 1.6 %collective-permute-start.14 = (f32[4,2,16,128]{3,2,1,0:T(8,128)S(1)}, f32[4,2,16,128]{3,2,1,0:T(8,128)S(1)}, u32[]{:S(2)}, u32[]{:S(2)}) collective-permute-start(f32[4,2,16,128]{3,2,1,0:T(8,128)S(1)} %shard_map.85.refs_0_), channel_id=1, source_target_pairs={{0,12},{1,13},{2,14},{3,15},{4,8},{5,9},{6,10},{7,11},{8,4},{9,5},... | collective-permute-start | bytes 196616 | tf_op jit(solution)/shard_map/ppermute | solution.py:637
  49.2 0.0 collective-permute-done.15.across_ref
  49.2 2.7 %shard_map.87 = (f32[2,2,32,256]{3,2,1,0:T(8,128)S(1)}, f32[2,2,32,256]{3,2,1,0:T(8,128)S(1)}) custom-call(f32[4,2,32,256]{3,2,1,0:T(8,128)S(1)} %collective-permute-done.9.even_ref, f32[4,2,32,256]{3,2,1,0:T(8,128)S(1)} %collective-permute-done.10.odd_ref, f32[10,32,128]{2,1,0:T(8,128)S(1)} %collective-permute-done.11.straight_ref, ...), custom_call_target="tpu_custom_call" | custom-call | flops 10000000 | bytes 1048576 | tf_op jit(solution)/shard_map/pallas_call | solution.py:710
  52.0 0.1 collective-permute-start.17
  52.0 0.0 collective-permute-done.12.refs_1_
  52.0 2.7 %collective-permute-done.13.refs_2_ = f32[4,2,16,128]{3,2,1,0:T(8,128)S(1)} collective-permute-done((f32[4,2,16,128]{3,2,1,0:T(8,128)S(1)}, f32[4,2,16,128]{3,2,1,0:T(8,128)S(1)}, u32[]{:S(2)}, u32[]{:S(2)}) %collective-permute-start.13) | collective-permute-done | bytes 65568 | tf_op jit(solution)/shard_map/ppermute | solution.py:637
  54.7 0.0 collective-permute-done.14.refs_3_
  54.7 2.9 %shard_map.86 = (f32[5,2,16,128]{3,2,1,0:T(8,128)S(1)}, f32[5,2,16,128]{3,2,1,0:T(8,128)S(1)}) custom-call(f32[4,2,16,128]{3,2,1,0:T(8,128)S(1)} %shard_map.85.refs_0_, f32[4,2,16,128]{3,2,1,0:T(8,128)S(1)} %collective-permute-done.12.refs_1_, f32[4,2,16,128]{3,2,1,0:T(8,128)S(1)} %collective-permute-done.13.refs_2_, ...), custom_call_target="tpu_custom_call" | custom-call | flops 100000000 | bytes 1048576 | tf_op jit(solution)/shard_map/pallas_call | solution.py:721
  57.7 0.1 collective-permute-start.16
  57.7 0.9 %shard_map.88.own_ref = f32[2,2,32,256]{3,2,1,0:T(8,128)S(1)} custom-call(f32[5,2,16,128]{3,2,1,0:T(8,128)S(1)} %get-tuple-element.34.w_ref, f32[2,2,32,256]{3,2,1,0:T(8,128)S(1)} %get-tuple-element.36.g_ref), custom_call_target="tpu_custom_call" | custom-call | flops 10000000 | bytes 1048576 | tf_op jit(solution)/shard_map/pallas_call | solution.py:742
  58.6 0.0 collective-permute-done.17.g_ref
  58.7 0.3 collective-permute-done.16.w_ref
  59.0 1.6 %shard_map.89 = f32[2,2,2,32,256]{4,3,2,1,0:T(8,128)} custom-call(f32[2,2,32,256]{3,2,1,0:T(8,128)S(1)} %shard_map.88.own_ref, f32[5,2,16,128]{3,2,1,0:T(8,128)S(1)} %collective-permute-done.16.w_ref, f32[2,2,32,256]{3,2,1,0:T(8,128)S(1)} %collective-permute-done.17.g_ref), custom_call_target="tpu_custom_call" | custom-call | flops 10000000 | bytes 1048576 | tf_op jit(solution)/shard_map/pallas_call | solution.py:743
  (15 shorter events, 0.0 us)
Async XLA Ops:
  0.0 2.5 %copy-start.3 = (s32[64,1]{0,1:T(1,128)S(1)}, s32[64,1]{0,1:T(1,128)}, u32[]{:S(2)}) copy-start(s32[64,1]{0,1:T(1,128)} %param.12) | copy-start | bytes 772
  0.0 2.5 %copy-start.4 = (s32[64]{0:T(128)S(1)}, s32[64]{0:T(128)}, u32[]{:S(2)}) copy-start(s32[64]{0:T(128)} %param.13) | copy-start | bytes 772
  0.0 2.5 %copy-start.2 = (s32[64]{0:T(128)S(1)}, s32[64]{0:T(128)}, u32[]{:S(2)}) copy-start(s32[64]{0:T(128)} %param.11) | copy-start | bytes 772
  0.0 2.5 %copy-start.1 = (f32[12,2,2,25]{3,2,1,0:T(2,128)S(1)}, f32[12,2,2,25]{3,2,1,0:T(2,128)}, u32[]{:S(2)}) copy-start(f32[12,2,2,25]{3,2,1,0:T(2,128)} %moments_ref.1) | copy-start | bytes 14404
  0.0 4.8 %copy-start = (f32[2,2,2,32,256]{4,3,2,1,0:T(8,128)S(1)}, f32[2,2,2,32,256]{4,3,2,1,0:T(8,128)}, u32[]{:S(2)}) copy-start(f32[2,2,2,32,256]{4,3,2,1,0:T(8,128)} %refs_0_.1) | copy-start | bytes 786436
  2.5 29.0 %copy-start.5 = (s32[2,2]{1,0:T(2,128)S(1)}, s32[2,2]{1,0:T(2,128)}, u32[]{:S(2)}) copy-start(s32[2,2]{1,0:T(2,128)} %param.14) | copy-start | bytes 52
  2.5 28.9 %copy-start.6 = (f32[8]{0:T(128)S(1)}, f32[8]{0:T(128)}, u32[]{:S(2)}) copy-start(f32[8]{0:T(128)} %param.15) | copy-start | bytes 100
  4.3 1.5 %collective-permute-start.1 = (f32[72,512]{1,0:T(8,128)S(1)}, f32[72,512]{1,0:T(8,128)S(1)}, u32[]{:S(2)}, u32[]{:S(2)}) collective-permute-start(f32[72,512]{1,0:T(8,128)S(1)} %get-tuple-element.23), channel_id=1, source_target_pairs={{0,1},{1,0},{2,3},{3,2},{4,5},{5,4},{6,7},{7,6},{8,9},{9,8},{10,11... | collective-permute-start | bytes 442376 | tf_op jit(solution)/shard_map/ppermute | solution.py:637
  4.8 9.3 %collective-permute-start = (f32[2,2,32,256]{3,2,1,0:T(8,128)S(1)}, f32[2,2,32,256]{3,2,1,0:T(8,128)S(1)}, u32[]{:S(2)}, u32[]{:S(2)}) collective-permute-start(f32[2,2,32,256]{3,2,1,0:T(8,128)S(1)} %dynamic-slice_bitcast_fusion), channel_id=1, source_target_pairs={{0,1},{1,0},{2,3},{3,2},{4,5},{5,4},{6,7},{7,6},{8,9},{9,8},{10,11... | collective-permute-start | bytes 393224 | tf_op jit(solution)/shard_map/ppermute | solution.py:637
  6.6 8.8 %collective-permute-start.2 = (f32[136,128]{1,0:T(8,128)S(1)}, f32[136,128]{1,0:T(8,128)S(1)}, u32[]{:S(2)}, u32[]{:S(2)}) collective-permute-start(f32[136,128]{1,0:T(8,128)S(1)} %get-tuple-element.25), channel_id=1, source_target_pairs={{0,2},{1,3},{2,0},{3,1},{4,6},{5,7},{6,4},{7,5},{8,10},{9,11},{10,... | collective-permute-start | bytes 208904 | tf_op jit(solution)/shard_map/ppermute | solution.py:637
  9.5 9.5 %collective-permute-start.3 = (f32[136,128]{1,0:T(8,128)S(1)}, f32[136,128]{1,0:T(8,128)S(1)}, u32[]{:S(2)}, u32[]{:S(2)}) collective-permute-start(f32[136,128]{1,0:T(8,128)S(1)} %get-tuple-element.26), channel_id=1, source_target_pairs={{0,4},{1,5},{2,6},{3,7},{4,0},{5,1},{6,2},{7,3},{8,12},{9,13},{10,... | collective-permute-start | bytes 208904 | tf_op jit(solution)/shard_map/ppermute | solution.py:637
  11.1 7.9 %collective-permute-start.4 = (f32[136,128]{1,0:T(8,128)S(1)}, f32[136,128]{1,0:T(8,128)S(1)}, u32[]{:S(2)}, u32[]{:S(2)}) collective-permute-start(f32[136,128]{1,0:T(8,128)S(1)} %get-tuple-element.27), channel_id=1, source_target_pairs={{0,6},{1,7},{2,4},{3,5},{4,2},{5,3},{6,0},{7,1},{8,14},{9,15},{10,... | collective-permute-start | bytes 208904 | tf_op jit(solution)/shard_map/ppermute | solution.py:637
  11.1 7.9 %collective-permute-start.5 = (f32[136,128]{1,0:T(8,128)S(1)}, f32[136,128]{1,0:T(8,128)S(1)}, u32[]{:S(2)}, u32[]{:S(2)}) collective-permute-start(f32[136,128]{1,0:T(8,128)S(1)} %get-tuple-element.28), channel_id=1, source_target_pairs={{0,8},{1,9},{2,10},{3,11},{4,12},{5,13},{6,14},{7,15},{8,0},{9,1},... | collective-permute-start | bytes 208904 | tf_op jit(solution)/shard_map/ppermute | solution.py:637
  14.1 10.9 %collective-permute-start.6 = (f32[136,128]{1,0:T(8,128)S(1)}, f32[136,128]{1,0:T(8,128)S(1)}, u32[]{:S(2)}, u32[]{:S(2)}) collective-permute-start(f32[136,128]{1,0:T(8,128)S(1)} %get-tuple-element.29), channel_id=1, source_target_pairs={{0,10},{1,11},{2,8},{3,9},{4,14},{5,15},{6,12},{7,13},{8,2},{9,3},... | collective-permute-start | bytes 208904 | tf_op jit(solution)/shard_map/ppermute | solution.py:637
  15.4 9.6 %collective-permute-start.7 = (f32[136,128]{1,0:T(8,128)S(1)}, f32[136,128]{1,0:T(8,128)S(1)}, u32[]{:S(2)}, u32[]{:S(2)}) collective-permute-start(f32[136,128]{1,0:T(8,128)S(1)} %get-tuple-element.30), channel_id=1, source_target_pairs={{0,12},{1,13},{2,14},{3,15},{4,8},{5,9},{6,10},{7,11},{8,4},{9,5},... | collective-permute-start | bytes 208904 | tf_op jit(solution)/shard_map/ppermute | solution.py:637
  19.0 7.1 %collective-permute-start.8 = (f32[136,128]{1,0:T(8,128)S(1)}, f32[136,128]{1,0:T(8,128)S(1)}, u32[]{:S(2)}, u32[]{:S(2)}) collective-permute-start(f32[136,128]{1,0:T(8,128)S(1)} %get-tuple-element.31), channel_id=1, source_target_pairs={{0,14},{1,15},{2,12},{3,13},{4,10},{5,11},{6,8},{7,9},{8,6},{9,7},... | collective-permute-start | bytes 208904 | tf_op jit(solution)/shard_map/ppermute | solution.py:637
  27.3 12.2 %collective-permute-start.10 = (f32[4,2,32,256]{3,2,1,0:T(8,128)S(1)}, f32[4,2,32,256]{3,2,1,0:T(8,128)S(1)}, u32[]{:S(2)}, u32[]{:S(2)}) collective-permute-start(f32[4,2,32,256]{3,2,1,0:T(8,128)S(1)} %get-tuple-element.32.f_ref), channel_id=1, source_target_pairs={{0,14},{1,15},{2,4},{3,5},{4,2},{5,3},{6,8},{7,9},{8,6},{9,7},{10,... | collective-permute-start | bytes 786440 | tf_op jit(solution)/shard_map/ppermute | solution.py:637
  29.7 12.0 %collective-permute-start.9 = (f32[4,2,32,256]{3,2,1,0:T(8,128)S(1)}, f32[4,2,32,256]{3,2,1,0:T(8,128)S(1)}, u32[]{:S(2)}, u32[]{:S(2)}) collective-permute-start(f32[4,2,32,256]{3,2,1,0:T(8,128)S(1)} %get-tuple-element.32.f_ref), channel_id=1, source_target_pairs={{0,2},{1,3},{2,0},{3,1},{4,6},{5,7},{6,4},{7,5},{8,10},{9,11},{10,... | collective-permute-start | bytes 786440 | tf_op jit(solution)/shard_map/ppermute | solution.py:637
  31.6 7.9 %collective-permute-start.11 = (f32[10,32,128]{2,1,0:T(8,128)S(1)}, f32[10,32,128]{2,1,0:T(8,128)S(1)}, u32[]{:S(2)}, u32[]{:S(2)}) collective-permute-start(f32[10,32,128]{2,1,0:T(8,128)S(1)} %get-tuple-element.33), channel_id=1, source_target_pairs={{0,12},{1,13},{2,6},{3,7},{4,0},{5,1},{6,10},{7,11},{8,4},{9,5},{1... | collective-permute-start | bytes 491528 | tf_op jit(solution)/shard_map/ppermute | solution.py:637
  33.1 16.2 %collective-permute-start.15 = (f32[2,2,32,256]{3,2,1,0:T(8,128)S(1)}, f32[2,2,32,256]{3,2,1,0:T(8,128)S(1)}, u32[]{:S(2)}, u32[]{:S(2)}) collective-permute-start(f32[2,2,32,256]{3,2,1,0:T(8,128)S(1)} %get-tuple-element.35), channel_id=1, source_target_pairs={{0,4},{1,5},{2,14},{3,15},{4,8},{5,9},{6,2},{7,3},{8,12},{9,13},{1... | collective-permute-start | bytes 393224 | tf_op jit(solution)/shard_map/ppermute | solution.py:637
  44.2 7.8 %collective-permute-start.12 = (f32[4,2,16,128]{3,2,1,0:T(8,128)S(1)}, f32[4,2,16,128]{3,2,1,0:T(8,128)S(1)}, u32[]{:S(2)}, u32[]{:S(2)}) collective-permute-start(f32[4,2,16,128]{3,2,1,0:T(8,128)S(1)} %shard_map.85.refs_0_), channel_id=1, source_target_pairs={{0,4},{1,5},{2,6},{3,7},{4,0},{5,1},{6,2},{7,3},{8,12},{9,13},{10,... | collective-permute-start | bytes 196616 | tf_op jit(solution)/shard_map/ppermute | solution.py:637
  46.8 7.9 %collective-permute-start.13 = (f32[4,2,16,128]{3,2,1,0:T(8,128)S(1)}, f32[4,2,16,128]{3,2,1,0:T(8,128)S(1)}, u32[]{:S(2)}, u32[]{:S(2)}) collective-permute-start(f32[4,2,16,128]{3,2,1,0:T(8,128)S(1)} %shard_map.85.refs_0_), channel_id=1, source_target_pairs={{0,8},{1,9},{2,10},{3,11},{4,12},{5,13},{6,14},{7,15},{8,0},{9,1},... | collective-permute-start | bytes 196616 | tf_op jit(solution)/shard_map/ppermute | solution.py:637
  47.6 7.1 %collective-permute-start.14 = (f32[4,2,16,128]{3,2,1,0:T(8,128)S(1)}, f32[4,2,16,128]{3,2,1,0:T(8,128)S(1)}, u32[]{:S(2)}, u32[]{:S(2)}) collective-permute-start(f32[4,2,16,128]{3,2,1,0:T(8,128)S(1)} %shard_map.85.refs_0_), channel_id=1, source_target_pairs={{0,12},{1,13},{2,14},{3,15},{4,8},{5,9},{6,10},{7,11},{8,4},{9,5},... | collective-permute-start | bytes 196616 | tf_op jit(solution)/shard_map/ppermute | solution.py:637
  52.0 6.7 %collective-permute-start.17 = (f32[2,2,32,256]{3,2,1,0:T(8,128)S(1)}, f32[2,2,32,256]{3,2,1,0:T(8,128)S(1)}, u32[]{:S(2)}, u32[]{:S(2)}) collective-permute-start(f32[2,2,32,256]{3,2,1,0:T(8,128)S(1)} %get-tuple-element.38), channel_id=1, source_target_pairs={{0,1},{1,0},{2,3},{3,2},{4,5},{5,4},{6,7},{7,6},{8,9},{9,8},{10,11... | collective-permute-start | bytes 393224 | tf_op jit(solution)/shard_map/ppermute | solution.py:637
  57.7 1.3 %collective-permute-start.16 = (f32[5,2,16,128]{3,2,1,0:T(8,128)S(1)}, f32[5,2,16,128]{3,2,1,0:T(8,128)S(1)}, u32[]{:S(2)}, u32[]{:S(2)}) collective-permute-start(f32[5,2,16,128]{3,2,1,0:T(8,128)S(1)} %get-tuple-element.37), channel_id=1, source_target_pairs={{0,1},{1,0},{2,3},{3,2},{4,5},{5,4},{6,7},{7,6},{8,9},{9,8},{10,11... | collective-permute-start | bytes 245768 | tf_op jit(solution)/shard_map/ppermute | solution.py:637

commit v6 on v5

--- a/solution.py
+++ b/solution.py
@@ -108,7 +108,7 @@
 
 def rows_kernel(moments_ref, shapes_ref, atom_ref, tile_ref, line_ref, keep_ref, send_ref, rows):
     core = lax.rem(lax.axis_index("grid"), 2)
-    slots, channels, depth = shapes_ref.shape
+    channels, slots, depth = shapes_ref.shape
     atoms = moments_ref.shape[0]
     atom = as_column(atom_ref[...].astype(jnp.float32))
     picks = [jnp.where(atom == float(a), 1.0, 0.0) for a in range(atoms)]
@@ -123,7 +123,7 @@
         near = slice(8 * i, 8 * i + 8)
         totals = [None] * 4
         for channel in range(channels):
-            shape = shapes_ref[near, channel]
+            shape = shapes_ref[channel, near]
             for f in range(4):
                 value = chosen[f][near, channel : channel + 1] * shape
                 totals[f] = value if totals[f] is None else totals[f] + value
@@ -136,7 +136,7 @@
     send_ref[slots : slots + 1, 0:slots] = number
 
 
-def pack_kernel(own_ref, got_ref, tile_ref, line_ref, *out_refs):
+def pack_kernel(own_ref, got_ref, tile_ref, line_ref, _, *out_refs):
     slots = own_ref.shape[0]
     apart = len(out_refs) > 1
     height = out_refs[0].shape[-2]
@@ -176,6 +176,11 @@
         out[4 * ranks :] = jnp.broadcast_to(numbers[k : k + 1], (8, 128))
 
 
+def message_order(chips):
+    half = chips // 2
+    return [0, 1, *range(half + 2, chips), half, half + 1, *range(2, half)]
+
+
 def density_kernel(*refs):
     pd_ref, other_ref = refs[:2]
     f_ref, straight_ref, across_ref, b1, half = refs[-5:]
@@ -190,7 +195,7 @@
 
     def received(source, start, stop):
         if len(pieces) > 1:
-            return pieces[source][start:stop]
+            return pieces[message_order(sources).index(source)][start:stop]
         return pieces[0][source, start:stop]
 
     added = [None, None]
@@ -662,22 +667,22 @@
         vmem(5),
         [(2, slot_count, row)],
         10**7,
-    )(moments, shapes, slot_atom.reshape(1, -1), tile_row, line_row)
+    )(moments, shapes.transpose(1, 0, 2), slot_atom.reshape(1, -1), tile_row, line_row)
     got = permute(sent, partner)
     apart = chips <= 8
     height = 16 * capacity + 8
     packed = call(
         pack_kernel,
         [shaped(height, 128)] * chips if apart else [shaped(chips, height, 128)],
-        vmem(4),
+        vmem(4) + [pl.BlockSpec(memory_space=pl.ANY)],
         [],
         10**8,
-    )(kept, got, tile_row, line_row)
+    )(kept, got, tile_row, line_row, other)
     if apart:
-        received = {0: packed[0]}
-        for k in sorted(range(1, chips), reverse=True):
-            received[k] = permute(packed[k], lambda i, k=k: i ^ (2 * k))
-        received = [received[k] for k in range(chips)]
+        received = [
+            permute(packed[k], lambda i, k=k: i ^ (2 * k)) if k else packed[k]
+            for k in message_order(chips)
+        ]
     else:
         groups = [[2 * k + c for k in range(chips)] for c in range(2)]
         received = [

time: 60.8 us -> 61 us (level)
  local copies, waits for them, and re-layouts: 2.5 us -> 4.19 us
  starting transfers between devices: 24.3 us -> 23.4 us
    unnamed x15 -> x20, local copies, waits for them, and re-layouts: 2.49 us -> 4.18 us
    ppermute x18, starting transfers between devices: 24.3 us -> 23.4 us  [permute(): return lax.ppermute(value, 'grid', [(i, target(i)) for i in devices])]
  transfers between devices with their start and end apart: 18 -> 18, of which waited for: 7 -> 10; matrix products, arithmetic and copies ran while one was open for 1% -> 1% of each run, Pallas kernels for 16% -> 15%
where the time goes in v6:
time: 61 us; the launch traced here: 60.8 us
  starting transfers between devices  23.4 us (38%)
  waiting for transfers between devices  18.4 us (30%)
  Pallas kernels  14.2 us (23%)
  local copies, waits for them, and re-layouts  4.19 us (7%)
    ppermute x18, starting transfers between devices, permute(): return lax.ppermute(value, 'grid', [(i, target(i)) for i in devices])  23.4 us
    ppermute x18, waiting for transfers between devices, permute(): return lax.ppermute(value, 'grid', [(i, target(i)) for i in devices])  18.4 us
    unnamed x20, local copies, waits for them, and re-layouts  4.18 us
    pallas_call x1, Pallas kernels, per_device(): call(cycle_kernel, [shaped(5, *small)] * 2, vmem(len(pieces)) + smem, [(n...  2.93 us
    pallas_call x1, Pallas kernels, per_device(): call(fine_kernel, [shaped(thick, *full)] * 2, vmem(5) + smem, [(3 * plane...  2.73 us
    pallas_call x1, Pallas kernels, per_device(): call(source_kernel, shaped(planes, *small), vmem(4) + smem, [(4 * planes,...  2.51 us
    pallas_call x1, Pallas kernels, per_device(): call(output_kernel, shaped(*pair_density.shape), vmem(3), scratch, 10 ** 7)  1.61 us
    pallas_call x1, Pallas kernels, per_device(): call(rows_kernel, [shaped(slot_count, row), shaped(slot_count + 8, row)],...  1.49 us
  transfers between devices with their start and end apart: 18, of which 10 were waited for; matrix products, arithmetic and copies ran while one was open for 1% of the time, Pallas kernels for 15%

profile of v6, /device:TPU:0, one launch (start us, length us, event | category | flops | bytes accessed | tf_op | source)
XLA Modules:
  0.0 60.8 jit_solution(10822039277484971834)
XLA Ops:
  0.0 1.5 %copy-done = f32[64,25,256]{2,0,1:T(8,128)S(1)} copy-done((f32[64,25,256]{2,0,1:T(8,128)S(1)}, f32[64,25,256]{2,0,1:T(8,128)}, u32[]{:S(2)}) %copy-start) | copy-done | bytes 1638424
  1.5 0.7 %copy-done.2 = f32[12,2,2,25]{3,2,1,0:T(2,128)S(1)} copy-done((f32[12,2,2,25]{3,2,1,0:T(2,128)S(1)}, f32[12,2,2,25]{3,2,1,0:T(2,128)}, u32[]{:S(2)}) %copy-start.2) | copy-done | bytes 4824
  2.2 0.7 %copy-done.3 = s32[64,1]{0,1:T(1,128)S(1)} copy-done((s32[64,1]{0,1:T(1,128)S(1)}, s32[64,1]{0,1:T(1,128)}, u32[]{:S(2)}) %copy-start.3) | copy-done | bytes 280
  2.9 0.7 %copy-done.5 = s32[64]{0:T(128)S(1)} copy-done((s32[64]{0:T(128)S(1)}, s32[64]{0:T(128)}, u32[]{:S(2)}) %copy-start.5) | copy-done | bytes 280
  3.5 0.7 %copy-done.7 = s32[64]{0:T(128)S(1)} copy-done((s32[64]{0:T(128)S(1)}, s32[64]{0:T(128)}, u32[]{:S(2)}) %copy-start.7) | copy-done | bytes 280
  4.2 1.5 %shard_map.82 = (f32[64,512]{1,0:T(8,128)S(1)}, f32[72,512]{1,0:T(8,128)S(1)}) custom-call(f32[12,2,2,25]{3,2,1,0:T(2,128)S(1)} %copy-done.2, f32[25,64,256]{2,1,0:T(8,128)S(1)} %bitcast.6, s32[1,64]{1,0:T(1,128)S(1)} %bitcast.11, s32[1,64]{1,0:T(1,128)S(1)} %bitcast.7, s32[1,64]{1,0:T(1,128)S(1)} %bitcast.9), custom_call_target="tpu_custom_call" | custom-call | flops 10000000 | bytes 1048576 | tf_op jit(solution)/shard_map/pallas_call | solution.py:664
  5.7 0.5 collective-permute-start.1
  6.2 0.1 collective-permute-start
  6.3 1.3 %collective-permute-done._.refs_1_ = f32[2,2,32,256]{3,2,1,0:T(8,128)S(1)} collective-permute-done((f32[2,2,32,256]{3,2,1,0:T(8,128)S(1)}, f32[2,2,32,256]{3,2,1,0:T(8,128)S(1)}, u32[]{:S(2)}, u32[]{:S(2)}) %collective-permute-start) | collective-permute-done | bytes 131104 | tf_op jit(solution)/shard_map/ppermute | solution.py:642
  7.6 0.0 collective-permute-done.1.got_ref
  7.6 0.8 %shard_map.83 = (f32[136,128]{1,0:T(8,128)S(1)}, f32[136,128]{1,0:T(8,128)S(1)}, f32[136,128]{1,0:T(8,128)S(1)}, f32[136,128]{1,0:T(8,128)S(1)}, f32[136,128]{1,...) custom-call(f32[64,512]{1,0:T(8,128)S(1)} %get-tuple-element.22.own_ref, ...), custom_call_target="tpu_custom_call" | custom-call | flops 100000000 | bytes 1048576 | tf_op jit(solution)/shard_map/pallas_call | solution.py:674
  8.4 2.7 %collective-permute-start.2 = (f32[136,128]{1,0:T(8,128)S(1)}, f32[136,128]{1,0:T(8,128)S(1)}, u32[]{:S(2)}, u32[]{:S(2)}) collective-permute-start(f32[136,128]{1,0:T(8,128)S(1)} %get-tuple-element.25), channel_id=1, source_target_pairs={{0,2},{1,3},{2,0},{3,1},{4,6},{5,7},{6,4},{7,5},{8,10},{9,11},{10,... | collective-permute-start | bytes 208904 | tf_op jit(solution)/shard_map/ppermute | solution.py:642
  11.1 3.6 %collective-permute-start.3 = (f32[136,128]{1,0:T(8,128)S(1)}, f32[136,128]{1,0:T(8,128)S(1)}, u32[]{:S(2)}, u32[]{:S(2)}) collective-permute-start(f32[136,128]{1,0:T(8,128)S(1)} %get-tuple-element.26), channel_id=1, source_target_pairs={{0,12},{1,13},{2,14},{3,15},{4,8},{5,9},{6,10},{7,11},{8,4},{9,5},... | collective-permute-start | bytes 208904 | tf_op jit(solution)/shard_map/ppermute | solution.py:642
  14.7 1.0 %collective-permute-start.5 = (f32[136,128]{1,0:T(8,128)S(1)}, f32[136,128]{1,0:T(8,128)S(1)}, u32[]{:S(2)}, u32[]{:S(2)}) collective-permute-start(f32[136,128]{1,0:T(8,128)S(1)} %get-tuple-element.28), channel_id=1, source_target_pairs={{0,8},{1,9},{2,10},{3,11},{4,12},{5,13},{6,14},{7,15},{8,0},{9,1},... | collective-permute-start | bytes 208904 | tf_op jit(solution)/shard_map/ppermute | solution.py:642
  15.7 3.1 %collective-permute-start.6 = (f32[136,128]{1,0:T(8,128)S(1)}, f32[136,128]{1,0:T(8,128)S(1)}, u32[]{:S(2)}, u32[]{:S(2)}) collective-permute-start(f32[136,128]{1,0:T(8,128)S(1)} %get-tuple-element.29), channel_id=1, source_target_pairs={{0,10},{1,11},{2,8},{3,9},{4,14},{5,15},{6,12},{7,13},{8,2},{9,3},... | collective-permute-start | bytes 208904 | tf_op jit(solution)/shard_map/ppermute | solution.py:642
  18.8 0.0 collective-permute-done.2.refs_3_
  18.8 1.3 %collective-permute-start.7 = (f32[136,128]{1,0:T(8,128)S(1)}, f32[136,128]{1,0:T(8,128)S(1)}, u32[]{:S(2)}, u32[]{:S(2)}) collective-permute-start(f32[136,128]{1,0:T(8,128)S(1)} %get-tuple-element.30), channel_id=1, source_target_pairs={{0,4},{1,5},{2,6},{3,7},{4,0},{5,1},{6,2},{7,3},{8,12},{9,13},{10,... | collective-permute-start | bytes 208904 | tf_op jit(solution)/shard_map/ppermute | solution.py:642
  20.0 0.0 collective-permute-done.3.refs_4_
  20.0 0.6 collective-permute-start.8
  20.6 1.6 %collective-permute-done.4.refs_5_ = f32[136,128]{1,0:T(8,128)S(1)} collective-permute-done((f32[136,128]{1,0:T(8,128)S(1)}, f32[136,128]{1,0:T(8,128)S(1)}, u32[]{:S(2)}, u32[]{:S(2)}) %collective-permute-start.4) | collective-permute-done | bytes 69664 | tf_op jit(solution)/shard_map/ppermute | solution.py:642
  22.1 3.9 %collective-permute-done.5.refs_6_ = f32[136,128]{1,0:T(8,128)S(1)} collective-permute-done((f32[136,128]{1,0:T(8,128)S(1)}, f32[136,128]{1,0:T(8,128)S(1)}, u32[]{:S(2)}, u32[]{:S(2)}) %collective-permute-start.5) | collective-permute-done | bytes 69664 | tf_op jit(solution)/shard_map/ppermute | solution.py:642
  26.1 0.8 %collective-permute-done.6.refs_7_ = f32[136,128]{1,0:T(8,128)S(1)} collective-permute-done((f32[136,128]{1,0:T(8,128)S(1)}, f32[136,128]{1,0:T(8,128)S(1)}, u32[]{:S(2)}, u32[]{:S(2)}) %collective-permute-start.6) | collective-permute-done | bytes 69664 | tf_op jit(solution)/shard_map/ppermute | solution.py:642
  26.9 0.0 collective-permute-done.7.refs_8_
  26.9 0.2 collective-permute-done.8.refs_9_
  27.1 1.2 %shard_map.84 = (f32[4,2,32,256]{3,2,1,0:T(8,128)S(1)}, f32[10,32,128]{2,1,0:T(8,128)S(1)}, f32[2,2,32,256]{3,2,1,0:T(8,128)S(1)}) custom-call(f32[2,2,2,32,256]{4,3,2,1,0:T(8,128)S(1)} %copy-done.1, f32[2,2,32,256]{3,2,1,0:T(8,128)S(1)} %collective-permute-done._.refs_1_, f32[136,128]{1,0:T(8,128)S(1)} %get-tuple-element.24.refs_2_, ...), custom_call_target="tpu_custom_call" | custom-call | flops 100000000 | bytes 1048576 | tf_op jit(solution)/shard_map/pallas_call | solution.py:696
  28.3 4.0 %collective-permute-start.10 = (f32[4,2,32,256]{3,2,1,0:T(8,128)S(1)}, f32[4,2,32,256]{3,2,1,0:T(8,128)S(1)}, u32[]{:S(2)}, u32[]{:S(2)}) collective-permute-start(f32[4,2,32,256]{3,2,1,0:T(8,128)S(1)} %get-tuple-element.32.f_ref), channel_id=1, source_target_pairs={{0,14},{1,15},{2,4},{3,5},{4,2},{5,3},{6,8},{7,9},{8,6},{9,7},{10,... | collective-permute-start | bytes 786440 | tf_op jit(solution)/shard_map/ppermute | solution.py:642
  32.3 0.2 fusion
  32.5 1.4 %collective-permute-start.11 = (f32[10,32,128]{2,1,0:T(8,128)S(1)}, f32[10,32,128]{2,1,0:T(8,128)S(1)}, u32[]{:S(2)}, u32[]{:S(2)}) collective-permute-start(f32[10,32,128]{2,1,0:T(8,128)S(1)} %get-tuple-element.33), channel_id=1, source_target_pairs={{0,12},{1,13},{2,6},{3,7},{4,0},{5,1},{6,10},{7,11},{8,4},{9,5},{1... | collective-permute-start | bytes 491528 | tf_op jit(solution)/shard_map/ppermute | solution.py:642
  33.8 0.2 cosine_reduce_fusion
  34.0 0.7 %collective-permute-start.15 = (f32[2,2,32,256]{3,2,1,0:T(8,128)S(1)}, f32[2,2,32,256]{3,2,1,0:T(8,128)S(1)}, u32[]{:S(2)}, u32[]{:S(2)}) collective-permute-start(f32[2,2,32,256]{3,2,1,0:T(8,128)S(1)} %get-tuple-element.35), channel_id=1, source_target_pairs={{0,4},{1,5},{2,14},{3,15},{4,8},{5,9},{6,2},{7,3},{8,12},{9,13},{1... | collective-permute-start | bytes 393224 | tf_op jit(solution)/shard_map/ppermute | solution.py:642
  34.8 0.1 pad_maximum_fusion.cs_ref.refs_4_
  34.8 6.8 %collective-permute-done.11.straight_ref = f32[10,32,128]{2,1,0:T(8,128)S(1)} collective-permute-done((f32[10,32,128]{2,1,0:T(8,128)S(1)}, f32[10,32,128]{2,1,0:T(8,128)S(1)}, u32[]{:S(2)}, u32[]{:S(2)}) %collective-permute-start.11) | collective-permute-done | bytes 163872 | tf_op jit(solution)/shard_map/ppermute | solution.py:642
  41.6 0.0 collective-permute-done.10.odd_ref
  41.6 2.4 %collective-permute-done.9.even_ref = f32[4,2,32,256]{3,2,1,0:T(8,128)S(1)} collective-permute-done((f32[4,2,32,256]{3,2,1,0:T(8,128)S(1)}, f32[4,2,32,256]{3,2,1,0:T(8,128)S(1)}, u32[]{:S(2)}, u32[]{:S(2)}) %collective-permute-start.9) | collective-permute-done | bytes 262176 | tf_op jit(solution)/shard_map/ppermute | solution.py:642
  44.0 2.5 %shard_map.85.refs_0_ = f32[4,2,16,128]{3,2,1,0:T(8,128)S(1)} custom-call(f32[4,2,32,256]{3,2,1,0:T(8,128)S(1)} %collective-permute-done.9.even_ref, f32[4,2,32,256]{3,2,1,0:T(8,128)S(1)} %collective-permute-done.10.odd_ref, f32[10,32,128]{2,1,0:T(8,128)S(1)} %collective-permute-done.11.straight_ref, f32[4,2,32,256]{3,2,1,0:T(8,128)S(1)} %get-tuple-element.32.f_ref, ...), custom_call_target="tpu_custom_call" | custom-call | flops 10000000 | bytes 1048576 | tf_op jit(solution)/shard_map/pallas_call | solution.py:707
  46.5 0.1 collective-permute-start.12
  46.6 2.1 %collective-permute-start.13 = (f32[4,2,16,128]{3,2,1,0:T(8,128)S(1)}, f32[4,2,16,128]{3,2,1,0:T(8,128)S(1)}, u32[]{:S(2)}, u32[]{:S(2)}) collective-permute-start(f32[4,2,16,128]{3,2,1,0:T(8,128)S(1)} %shard_map.85.refs_0_), channel_id=1, source_target_pairs={{0,8},{1,9},{2,10},{3,11},{4,12},{5,13},{6,14},{7,15},{8,0},{9,1},... | collective-permute-start | bytes 196616 | tf_op jit(solution)/shard_map/ppermute | solution.py:642
  48.7 2.3 %collective-permute-start.14 = (f32[4,2,16,128]{3,2,1,0:T(8,128)S(1)}, f32[4,2,16,128]{3,2,1,0:T(8,128)S(1)}, u32[]{:S(2)}, u32[]{:S(2)}) collective-permute-start(f32[4,2,16,128]{3,2,1,0:T(8,128)S(1)} %shard_map.85.refs_0_), channel_id=1, source_target_pairs={{0,12},{1,13},{2,14},{3,15},{4,8},{5,9},{6,10},{7,11},{8,4},{9,5},... | collective-permute-start | bytes 196616 | tf_op jit(solution)/shard_map/ppermute | solution.py:642
  51.0 2.7 %shard_map.87 = (f32[2,2,32,256]{3,2,1,0:T(8,128)S(1)}, f32[2,2,32,256]{3,2,1,0:T(8,128)S(1)}) custom-call(f32[4,2,32,256]{3,2,1,0:T(8,128)S(1)} %collective-permute-done.9.even_ref, f32[4,2,32,256]{3,2,1,0:T(8,128)S(1)} %collective-permute-done.10.odd_ref, f32[10,32,128]{2,1,0:T(8,128)S(1)} %collective-permute-done.11.straight_ref, ...), custom_call_target="tpu_custom_call" | custom-call | flops 10000000 | bytes 1048576 | tf_op jit(solution)/shard_map/pallas_call | solution.py:715
  53.7 0.1 collective-permute-start.17
  53.8 0.4 collective-permute-done.13.refs_2_
  54.2 0.7 %collective-permute-done.14.refs_3_ = f32[4,2,16,128]{3,2,1,0:T(8,128)S(1)} collective-permute-done((f32[4,2,16,128]{3,2,1,0:T(8,128)S(1)}, f32[4,2,16,128]{3,2,1,0:T(8,128)S(1)}, u32[]{:S(2)}, u32[]{:S(2)}) %collective-permute-start.14) | collective-permute-done | bytes 65568 | tf_op jit(solution)/shard_map/ppermute | solution.py:642
  54.9 2.9 %shard_map.86 = (f32[5,2,16,128]{3,2,1,0:T(8,128)S(1)}, f32[5,2,16,128]{3,2,1,0:T(8,128)S(1)}) custom-call(f32[4,2,16,128]{3,2,1,0:T(8,128)S(1)} %shard_map.85.refs_0_, f32[4,2,16,128]{3,2,1,0:T(8,128)S(1)} %collective-permute-done.12.refs_1_, f32[4,2,16,128]{3,2,1,0:T(8,128)S(1)} %collective-permute-done.13.refs_2_, ...), custom_call_target="tpu_custom_call" | custom-call | flops 100000000 | bytes 1048576 | tf_op jit(solution)/shard_map/pallas_call | solution.py:726
  57.8 0.1 collective-permute-start.16
  57.9 0.9 %shard_map.88.own_ref = f32[2,2,32,256]{3,2,1,0:T(8,128)S(1)} custom-call(f32[5,2,16,128]{3,2,1,0:T(8,128)S(1)} %get-tuple-element.34.w_ref, f32[2,2,32,256]{3,2,1,0:T(8,128)S(1)} %get-tuple-element.36.g_ref), custom_call_target="tpu_custom_call" | custom-call | flops 10000000 | bytes 1048576 | tf_op jit(solution)/shard_map/pallas_call | solution.py:747
  58.8 0.0 collective-permute-done.17.g_ref
  58.8 0.3 collective-permute-done.16.w_ref
  59.2 1.6 %shard_map.89 = f32[2,2,2,32,256]{4,3,2,1,0:T(8,128)} custom-call(f32[2,2,32,256]{3,2,1,0:T(8,128)S(1)} %shard_map.88.own_ref, f32[5,2,16,128]{3,2,1,0:T(8,128)S(1)} %collective-permute-done.16.w_ref, f32[2,2,32,256]{3,2,1,0:T(8,128)S(1)} %collective-permute-done.17.g_ref), custom_call_target="tpu_custom_call" | custom-call | flops 10000000 | bytes 1048576 | tf_op jit(solution)/shard_map/pallas_call | solution.py:748
  (20 shorter events, 0.0 us)
Async XLA Ops:
  0.0 7.6 %copy-start.4 = (s32[64,1]{0,1:T(1,128)S(1)}, s32[64,1]{0,1:T(1,128)}, u32[]{:S(2)}) copy-start(s32[64,1]{0,1:T(1,128)} %param.12) | copy-start | bytes 772
  0.0 7.6 %copy-start.6 = (s32[64]{0:T(128)S(1)}, s32[64]{0:T(128)}, u32[]{:S(2)}) copy-start(s32[64]{0:T(128)} %param.13) | copy-start | bytes 772
  0.0 1.5 %copy-start = (f32[64,25,256]{2,0,1:T(8,128)S(1)}, f32[64,25,256]{2,0,1:T(8,128)}, u32[]{:S(2)}) copy-start(f32[64,25,256]{2,0,1:T(8,128)} %param.10) | copy-start | bytes 4915204
  1.5 0.7 %copy-start.2 = (f32[12,2,2,25]{3,2,1,0:T(2,128)S(1)}, f32[12,2,2,25]{3,2,1,0:T(2,128)}, u32[]{:S(2)}) copy-start(f32[12,2,2,25]{3,2,1,0:T(2,128)} %moments_ref.1) | copy-start | bytes 14404
  2.2 0.7 %copy-start.3 = (s32[64,1]{0,1:T(1,128)S(1)}, s32[64,1]{0,1:T(1,128)}, u32[]{:S(2)}) copy-start(s32[64,1]{0,1:T(1,128)} %param.12) | copy-start | bytes 772
  2.9 0.7 %copy-start.5 = (s32[64]{0:T(128)S(1)}, s32[64]{0:T(128)}, u32[]{:S(2)}) copy-start(s32[64]{0:T(128)} %param.13) | copy-start | bytes 772
  3.5 0.7 %copy-start.7 = (s32[64]{0:T(128)S(1)}, s32[64]{0:T(128)}, u32[]{:S(2)}) copy-start(s32[64]{0:T(128)} %param.11) | copy-start | bytes 772
  4.2 2.0 %copy-start.1 = (f32[2,2,2,32,256]{4,3,2,1,0:T(8,128)S(1)}, f32[2,2,2,32,256]{4,3,2,1,0:T(8,128)}, u32[]{:S(2)}) copy-start(f32[2,2,2,32,256]{4,3,2,1,0:T(8,128)} %refs_0_.1) | copy-start | bytes 786436
  4.2 28.1 %copy-start.8 = (s32[2,2]{1,0:T(2,128)S(1)}, s32[2,2]{1,0:T(2,128)}, u32[]{:S(2)}) copy-start(s32[2,2]{1,0:T(2,128)} %param.14) | copy-start | bytes 52
  4.2 28.1 %copy-start.9 = (f32[8]{0:T(128)S(1)}, f32[8]{0:T(128)}, u32[]{:S(2)}) copy-start(f32[8]{0:T(128)} %param.15) | copy-start | bytes 100
  5.7 2.0 %collective-permute-start.1 = (f32[72,512]{1,0:T(8,128)S(1)}, f32[72,512]{1,0:T(8,128)S(1)}, u32[]{:S(2)}, u32[]{:S(2)}) collective-permute-start(f32[72,512]{1,0:T(8,128)S(1)} %get-tuple-element.23), channel_id=1, source_target_pairs={{0,1},{1,0},{2,3},{3,2},{4,5},{5,4},{6,7},{7,6},{8,9},{9,8},{10,11... | collective-permute-start | bytes 442376 | tf_op jit(solution)/shard_map/ppermute | solution.py:642
  6.2 1.4 %collective-permute-start = (f32[2,2,32,256]{3,2,1,0:T(8,128)S(1)}, f32[2,2,32,256]{3,2,1,0:T(8,128)S(1)}, u32[]{:S(2)}, u32[]{:S(2)}) collective-permute-start(f32[2,2,32,256]{3,2,1,0:T(8,128)S(1)} %dynamic-slice_bitcast_fusion), channel_id=1, source_target_pairs={{0,1},{1,0},{2,3},{3,2},{4,5},{5,4},{6,7},{7,6},{8,9},{9,8},{10,11... | collective-permute-start | bytes 393224 | tf_op jit(solution)/shard_map/ppermute | solution.py:642
  8.4 10.3 %collective-permute-start.2 = (f32[136,128]{1,0:T(8,128)S(1)}, f32[136,128]{1,0:T(8,128)S(1)}, u32[]{:S(2)}, u32[]{:S(2)}) collective-permute-start(f32[136,128]{1,0:T(8,128)S(1)} %get-tuple-element.25), channel_id=1, source_target_pairs={{0,2},{1,3},{2,0},{3,1},{4,6},{5,7},{6,4},{7,5},{8,10},{9,11},{10,... | collective-permute-start | bytes 208904 | tf_op jit(solution)/shard_map/ppermute | solution.py:642
  11.1 8.9 %collective-permute-start.3 = (f32[136,128]{1,0:T(8,128)S(1)}, f32[136,128]{1,0:T(8,128)S(1)}, u32[]{:S(2)}, u32[]{:S(2)}) collective-permute-start(f32[136,128]{1,0:T(8,128)S(1)} %get-tuple-element.26), channel_id=1, source_target_pairs={{0,12},{1,13},{2,14},{3,15},{4,8},{5,9},{6,10},{7,11},{8,4},{9,5},... | collective-permute-start | bytes 208904 | tf_op jit(solution)/shard_map/ppermute | solution.py:642
  14.7 7.4 %collective-permute-start.4 = (f32[136,128]{1,0:T(8,128)S(1)}, f32[136,128]{1,0:T(8,128)S(1)}, u32[]{:S(2)}, u32[]{:S(2)}) collective-permute-start(f32[136,128]{1,0:T(8,128)S(1)} %get-tuple-element.27), channel_id=1, source_target_pairs={{0,14},{1,15},{2,12},{3,13},{4,10},{5,11},{6,8},{7,9},{8,6},{9,7},... | collective-permute-start | bytes 208904 | tf_op jit(solution)/shard_map/ppermute | solution.py:642
  14.7 11.3 %collective-permute-start.5 = (f32[136,128]{1,0:T(8,128)S(1)}, f32[136,128]{1,0:T(8,128)S(1)}, u32[]{:S(2)}, u32[]{:S(2)}) collective-permute-start(f32[136,128]{1,0:T(8,128)S(1)} %get-tuple-element.28), channel_id=1, source_target_pairs={{0,8},{1,9},{2,10},{3,11},{4,12},{5,13},{6,14},{7,15},{8,0},{9,1},... | collective-permute-start | bytes 208904 | tf_op jit(solution)/shard_map/ppermute | solution.py:642
  15.7 11.2 %collective-permute-start.6 = (f32[136,128]{1,0:T(8,128)S(1)}, f32[136,128]{1,0:T(8,128)S(1)}, u32[]{:S(2)}, u32[]{:S(2)}) collective-permute-start(f32[136,128]{1,0:T(8,128)S(1)} %get-tuple-element.29), channel_id=1, source_target_pairs={{0,10},{1,11},{2,8},{3,9},{4,14},{5,15},{6,12},{7,13},{8,2},{9,3},... | collective-permute-start | bytes 208904 | tf_op jit(solution)/shard_map/ppermute | solution.py:642
  18.8 8.1 %collective-permute-start.7 = (f32[136,128]{1,0:T(8,128)S(1)}, f32[136,128]{1,0:T(8,128)S(1)}, u32[]{:S(2)}, u32[]{:S(2)}) collective-permute-start(f32[136,128]{1,0:T(8,128)S(1)} %get-tuple-element.30), channel_id=1, source_target_pairs={{0,4},{1,5},{2,6},{3,7},{4,0},{5,1},{6,2},{7,3},{8,12},{9,13},{10,... | collective-permute-start | bytes 208904 | tf_op jit(solution)/shard_map/ppermute | solution.py:642
  20.0 7.1 %collective-permute-start.8 = (f32[136,128]{1,0:T(8,128)S(1)}, f32[136,128]{1,0:T(8,128)S(1)}, u32[]{:S(2)}, u32[]{:S(2)}) collective-permute-start(f32[136,128]{1,0:T(8,128)S(1)} %get-tuple-element.31), channel_id=1, source_target_pairs={{0,6},{1,7},{2,4},{3,5},{4,2},{5,3},{6,0},{7,1},{8,14},{9,15},{10,... | collective-permute-start | bytes 208904 | tf_op jit(solution)/shard_map/ppermute | solution.py:642
  28.3 13.3 %collective-permute-start.10 = (f32[4,2,32,256]{3,2,1,0:T(8,128)S(1)}, f32[4,2,32,256]{3,2,1,0:T(8,128)S(1)}, u32[]{:S(2)}, u32[]{:S(2)}) collective-permute-start(f32[4,2,32,256]{3,2,1,0:T(8,128)S(1)} %get-tuple-element.32.f_ref), channel_id=1, source_target_pairs={{0,14},{1,15},{2,4},{3,5},{4,2},{5,3},{6,8},{7,9},{8,6},{9,7},{10,... | collective-permute-start | bytes 786440 | tf_op jit(solution)/shard_map/ppermute | solution.py:642
  32.3 11.7 %collective-permute-start.9 = (f32[4,2,32,256]{3,2,1,0:T(8,128)S(1)}, f32[4,2,32,256]{3,2,1,0:T(8,128)S(1)}, u32[]{:S(2)}, u32[]{:S(2)}) collective-permute-start(f32[4,2,32,256]{3,2,1,0:T(8,128)S(1)} %get-tuple-element.32.f_ref), channel_id=1, source_target_pairs={{0,2},{1,3},{2,0},{3,1},{4,6},{5,7},{6,4},{7,5},{8,10},{9,11},{10,... | collective-permute-start | bytes 786440 | tf_op jit(solution)/shard_map/ppermute | solution.py:642
  32.5 9.2 %collective-permute-start.11 = (f32[10,32,128]{2,1,0:T(8,128)S(1)}, f32[10,32,128]{2,1,0:T(8,128)S(1)}, u32[]{:S(2)}, u32[]{:S(2)}) collective-permute-start(f32[10,32,128]{2,1,0:T(8,128)S(1)} %get-tuple-element.33), channel_id=1, source_target_pairs={{0,12},{1,13},{2,6},{3,7},{4,0},{5,1},{6,10},{7,11},{8,4},{9,5},{1... | collective-permute-start | bytes 491528 | tf_op jit(solution)/shard_map/ppermute | solution.py:642
  34.0 16.9 %collective-permute-start.15 = (f32[2,2,32,256]{3,2,1,0:T(8,128)S(1)}, f32[2,2,32,256]{3,2,1,0:T(8,128)S(1)}, u32[]{:S(2)}, u32[]{:S(2)}) collective-permute-start(f32[2,2,32,256]{3,2,1,0:T(8,128)S(1)} %get-tuple-element.35), channel_id=1, source_target_pairs={{0,4},{1,5},{2,14},{3,15},{4,8},{5,9},{6,2},{7,3},{8,12},{9,13},{1... | collective-permute-start | bytes 393224 | tf_op jit(solution)/shard_map/ppermute | solution.py:642
  46.5 7.3 %collective-permute-start.12 = (f32[4,2,16,128]{3,2,1,0:T(8,128)S(1)}, f32[4,2,16,128]{3,2,1,0:T(8,128)S(1)}, u32[]{:S(2)}, u32[]{:S(2)}) collective-permute-start(f32[4,2,16,128]{3,2,1,0:T(8,128)S(1)} %shard_map.85.refs_0_), channel_id=1, source_target_pairs={{0,4},{1,5},{2,6},{3,7},{4,0},{5,1},{6,2},{7,3},{8,12},{9,13},{10,... | collective-permute-start | bytes 196616 | tf_op jit(solution)/shard_map/ppermute | solution.py:642
  46.6 7.6 %collective-permute-start.13 = (f32[4,2,16,128]{3,2,1,0:T(8,128)S(1)}, f32[4,2,16,128]{3,2,1,0:T(8,128)S(1)}, u32[]{:S(2)}, u32[]{:S(2)}) collective-permute-start(f32[4,2,16,128]{3,2,1,0:T(8,128)S(1)} %shard_map.85.refs_0_), channel_id=1, source_target_pairs={{0,8},{1,9},{2,10},{3,11},{4,12},{5,13},{6,14},{7,15},{8,0},{9,1},... | collective-permute-start | bytes 196616 | tf_op jit(solution)/shard_map/ppermute | solution.py:642
  48.7 6.2 %collective-permute-start.14 = (f32[4,2,16,128]{3,2,1,0:T(8,128)S(1)}, f32[4,2,16,128]{3,2,1,0:T(8,128)S(1)}, u32[]{:S(2)}, u32[]{:S(2)}) collective-permute-start(f32[4,2,16,128]{3,2,1,0:T(8,128)S(1)} %shard_map.85.refs_0_), channel_id=1, source_target_pairs={{0,12},{1,13},{2,14},{3,15},{4,8},{5,9},{6,10},{7,11},{8,4},{9,5},... | collective-permute-start | bytes 196616 | tf_op jit(solution)/shard_map/ppermute | solution.py:642
  53.7 5.1 %collective-permute-start.17 = (f32[2,2,32,256]{3,2,1,0:T(8,128)S(1)}, f32[2,2,32,256]{3,2,1,0:T(8,128)S(1)}, u32[]{:S(2)}, u32[]{:S(2)}) collective-permute-start(f32[2,2,32,256]{3,2,1,0:T(8,128)S(1)} %get-tuple-element.38), channel_id=1, source_target_pairs={{0,1},{1,0},{2,3},{3,2},{4,5},{5,4},{6,7},{7,6},{8,9},{9,8},{10,11... | collective-permute-start | bytes 393224 | tf_op jit(solution)/shard_map/ppermute | solution.py:642
  57.8 1.3 %collective-permute-start.16 = (f32[5,2,16,128]{3,2,1,0:T(8,128)S(1)}, f32[5,2,16,128]{3,2,1,0:T(8,128)S(1)}, u32[]{:S(2)}, u32[]{:S(2)}) collective-permute-start(f32[5,2,16,128]{3,2,1,0:T(8,128)S(1)} %get-tuple-element.37), channel_id=1, source_target_pairs={{0,1},{1,0},{2,3},{3,2},{4,5},{5,4},{6,7},{7,6},{8,9},{9,8},{10,11... | collective-permute-start | bytes 245768 | tf_op jit(solution)/shard_map/ppermute | solution.py:642

commit v7 on v6

--- a/solution.py
+++ b/solution.py
@@ -77,16 +77,19 @@
         target[base + x, 1] = imag
 
 
+def place_in_grid():
+    position = lax.axis_index("grid")
+    return lax.rem(lax.div(position, 2), 2), lax.rem(position, 2), lax.div(position, 4)
+
+
 def place_halo(ext, middle, even_ref, odd_ref, cs_ref):
-    position = lax.axis_index("grid")
-    chips = lax.axis_size("grid") // 2
-    core, chip = lax.rem(position, 2), lax.div(position, 2)
-    cosine, sine = cs_ref[core], cs_ref[2 + core]
-    first, last = chip == 0, chip == chips - 1
+    blocks = lax.axis_size("grid") // 4
+    pair, parity, block = place_in_grid()
+    cosine, sine = cs_ref[pair], cs_ref[2 + pair]
+    first, last = (block == 0) & (parity == 0), (block == blocks - 1) & (parity == 1)
     low = (jnp.where(first, cosine, 1.0), jnp.where(first, -sine, 0.0))
     high = (jnp.where(last, cosine, 1.0), jnp.where(last, sine, 0.0))
     planes = even_ref.shape[0]
-    parity = lax.rem(chip, 2)
 
     @pl.when(parity == 0)
     def _():
@@ -106,9 +109,21 @@
     return jnp.sum(jnp.where(i == j, row, 0.0), axis=1, keepdims=True)
 
 
-def rows_kernel(moments_ref, shapes_ref, atom_ref, tile_ref, line_ref, keep_ref, send_ref, rows):
-    core = lax.rem(lax.axis_index("grid"), 2)
-    channels, slots, depth = shapes_ref.shape
+def rows_kernel(moments_ref, shapes_ref, atom_ref, tile_ref, line_ref, out_ref, shapes, arrived):
+    channels, slots, depth = shapes.shape
+    steps = arrived.shape[0]
+    cuts = [channels * k // steps for k in range(steps + 1)]
+    copies = [
+        pltpu.make_async_copy(
+            shapes_ref.at[cuts[k] : cuts[k + 1]], shapes.at[cuts[k] : cuts[k + 1]], arrived.at[k]
+        )
+        for k in range(steps)
+    ]
+    for copy in copies:
+        copy.start()
+    out_ref[slots:] = jnp.zeros((8, 4 * depth), jnp.float32)
+    number = (tile_ref[...] * 64 + line_ref[...]).astype(jnp.float32)
+    out_ref[slots : slots + 1, 0:slots] = number
     atoms = moments_ref.shape[0]
     atom = as_column(atom_ref[...].astype(jnp.float32))
     picks = [jnp.where(atom == float(a), 1.0, 0.0) for a in range(atoms)]
@@ -119,33 +134,34 @@
             value = picks[a] * moments_ref[a, f // 2, f % 2 : f % 2 + 1]
             total = value if total is None else total + value
         chosen.append(total)
-    for i in range(slots // 8):
-        near = slice(8 * i, 8 * i + 8)
-        totals = [None] * 4
-        for channel in range(channels):
-            shape = shapes_ref[channel, near]
+    for k in range(steps):
+        copies[k].wait()
+        for i in range(slots // 8):
+            near = slice(8 * i, 8 * i + 8)
+            totals = [out_ref[near, f * depth : (f + 1) * depth] if k else None for f in range(4)]
+            for channel in range(cuts[k], cuts[k + 1]):
+                shape = shapes[channel, near]
+                for f in range(4):
+                    value = chosen[f][near, channel : channel + 1] * shape
+                    totals[f] = value if totals[f] is None else totals[f] + value
             for f in range(4):
-                value = chosen[f][near, channel : channel + 1] * shape
-                totals[f] = value if totals[f] is None else totals[f] + value
-        for f in range(4):
-            rows[f // 2, near, f % 2 * depth : (f % 2 + 1) * depth] = totals[f]
-    keep_ref[...] = rows[core]
-    send_ref[0:slots] = rows[1 - core]
-    send_ref[slots:] = jnp.zeros((8, 2 * depth), jnp.float32)
-    number = (tile_ref[...] * 64 + line_ref[...]).astype(jnp.float32)
-    send_ref[slots : slots + 1, 0:slots] = number
-
-
-def pack_kernel(own_ref, got_ref, tile_ref, line_ref, _, *out_refs):
-    slots = own_ref.shape[0]
+                out_ref[near, f * depth : (f + 1) * depth] = totals[f]
+
+
+def pack_kernel(own_ref, got_ref, *refs):
+    out_refs, scratch = refs[:-1], refs[-1]
+    slots = own_ref.shape[0] - 8
     apart = len(out_refs) > 1
     height = out_refs[0].shape[-2]
     ranks = (height - 8) // 4
     capacity = ranks // 4
     chips = lax.axis_size("grid") // 2
-    chip = lax.div(lax.axis_index("grid"), 2)
-    number = (tile_ref[...] * 64 + line_ref[...]).astype(jnp.float32)
-    number = jnp.concatenate([number, got_ref[slots : slots + 1, 0:slots]], axis=1).astype(jnp.int32)
+    blocks = chips // 2
+    position = lax.axis_index("grid")
+    side, chip = lax.rem(position, 2), lax.div(position, 2)
+    number = jnp.concatenate(
+        [ref[slots : slots + 1, 0:slots] for ref in (own_ref, got_ref)], axis=1
+    ).astype(jnp.int32)
     tile, line = number // 64, number % 128 + 1
     column = as_column(tile.astype(jnp.float32)).astype(jnp.int32)
     i = lax.broadcasted_iota(jnp.int32, (2 * slots, 2 * slots), 0)
@@ -153,26 +169,33 @@
     ahead = jnp.where((column == tile) & (i < j) & (i // slots == j // slots), 1.0, 0.0)
     rank = jnp.sum(ahead, axis=0, keepdims=True).astype(jnp.int32)
     device = lax.broadcasted_iota(jnp.int32, (1, 2 * slots), 1) // slots
-    place = tile // 2 * ranks + (2 * device + tile % 2) * capacity + rank
-    r = lax.broadcasted_iota(jnp.int32, (ranks, 2 * slots), 0)
-    targets = [lax.bitwise_xor(chip, k) if apart else k for k in range(chips)]
-    pick = jnp.concatenate([jnp.where(place == r + target * ranks, 1.0, 0.0) for target in targets])
-    rows = jnp.concatenate([own_ref[...], got_ref[0:slots]], axis=0)
+    place = tile // 4 * ranks + (2 * device + tile % 2) * capacity + rank
+    place = jnp.where(tile % 4 // 2 == side, place, -1)
+    buckets = blocks * ranks
+    pick = jnp.where(place == lax.broadcasted_iota(jnp.int32, (buckets, 2 * slots), 0), 1.0, 0.0)
+    rows = jnp.concatenate([own_ref[0:slots], got_ref[0:slots]], axis=0)
     packed = dot(pick, rows)
+    for q in range(8):
+        scratch[q] = packed[:, q * 128 : (q + 1) * 128]
     lines = jnp.sum(pick * line.astype(jnp.float32), axis=1, keepdims=True)
-    bucket = lax.broadcasted_iota(jnp.int32, (chips * ranks, 128), 0)
-    lane = lax.broadcasted_iota(jnp.int32, (chips * ranks, 128), 1)
-    spot = bucket // ranks if apart else chip
-    spots = jnp.where(lane == spot % (128 // ranks) * ranks + bucket % ranks, lines, 0.0)
-    i = lax.broadcasted_iota(jnp.int32, (chips, chips * ranks), 0)
-    j = lax.broadcasted_iota(jnp.int32, (chips, chips * ranks), 1)
-    numbers = dot(jnp.where(i == j // ranks, 1.0, 0.0), spots)
+    bucket = lax.broadcasted_iota(jnp.int32, (buckets, 128), 0)
+    lane = lax.broadcasted_iota(jnp.int32, (buckets, 128), 1)
+    spots = jnp.where(lane % ranks == bucket % ranks, lines, 0.0)
+    i = lax.broadcasted_iota(jnp.int32, (chips, buckets), 0)
+    j = lax.broadcasted_iota(jnp.int32, (chips, buckets), 1)
+    target = lax.bitwise_xor(i, jnp.full(i.shape, chip, jnp.int32)) if apart else i
+    numbers = dot(jnp.where(target // 2 == j // ranks, 1.0, 0.0), spots)
+    spot = lax.broadcasted_iota(jnp.int32, (chips, 128), 0) if apart else chip
+    lane = lax.broadcasted_iota(jnp.int32, (chips, 128), 1)
+    numbers = jnp.where(lane // ranks == spot % (128 // ranks), numbers, 0.0)
     for k in range(chips):
         out = out_refs[k] if apart else out_refs[0].at[k]
+        target = lax.bitwise_xor(chip, k) if apart else k
+        block, pair = (lax.div(target, 2), lax.rem(target, 2)) if apart else (k // 2, k % 2)
         for q in range(4):
-            out[q * ranks : (q + 1) * ranks] = packed[
-                k * ranks : (k + 1) * ranks, q * 128 : (q + 1) * 128
-            ]
+            start = block * ranks
+            start = pl.multiple_of(start, ranks) if apart else start
+            out[q * ranks : (q + 1) * ranks] = scratch[4 * pair + q, pl.ds(start, ranks)]
         out[4 * ranks :] = jnp.broadcast_to(numbers[k : k + 1], (8, 128))
 
 
@@ -182,11 +205,10 @@
 
 
 def density_kernel(*refs):
-    pd_ref, other_ref = refs[:2]
+    first_ref, second_ref = refs[:2]
     f_ref, straight_ref, across_ref, b1, half = refs[-5:]
     pieces = refs[2:-5]
-    position = lax.axis_index("grid")
-    core, side = lax.rem(position, 2), lax.rem(lax.div(position, 2), 2)
+    pair, side, _ = place_in_grid()
     planes, _, lines, depth = f_ref.shape
     sources = lax.axis_size("grid") // 2
     height = pieces[0].shape[-2]
@@ -222,8 +244,8 @@
     thick = planes // 2
     for x in range(thick):
         for part in range(2):
-            f_ref[core * thick + x, part] += pd_ref[core, part, x]
-            f_ref[(1 - core) * thick + x, part] += other_ref[part, x]
+            f_ref[pair * thick + x, part] += first_ref[part, x]
+            f_ref[(1 - pair) * thick + x, part] += second_ref[part, x]
 
     def density(x, part):
         return f_ref[x, part] if 0 <= x < planes else None
@@ -279,10 +301,9 @@
 
 
 def source_kernel(even_ref, odd_ref, straight_ref, f_ref, cs_ref, s_ref, ext, b1, half):
-    position = lax.axis_index("grid")
     blocks = lax.axis_size("grid") // 4
-    core, side, block = lax.rem(position, 2), lax.rem(lax.div(position, 2), 2), lax.div(position, 4)
-    cosine, sine = cs_ref[core], cs_ref[2 + core]
+    pair, side, block = place_in_grid()
+    cosine, sine = cs_ref[pair], cs_ref[2 + pair]
     planes = f_ref.shape[0]
     lines, depth = f_ref.shape[2:]
     first, last = block == 0, block == blocks - 1
@@ -332,16 +353,15 @@
 
 
 def fine_kernel(
-    even_ref, odd_ref, straight_ref, across_ref, f_ref, cs_ref, own_ref, send_ref, ext, b1, b2, g
+    even_ref, odd_ref, straight_ref, across_ref, f_ref, cs_ref, first_ref, second_ref, ext, b1, b2, g
 ):
-    position = lax.axis_index("grid")
-    chips = lax.axis_size("grid") // 2
-    core, chip = lax.rem(position, 2), lax.div(position, 2)
-    cosine, sine = cs_ref[core], cs_ref[2 + core]
+    blocks = lax.axis_size("grid") // 4
+    pair, side, block = place_in_grid()
+    cosine, sine = cs_ref[pair], cs_ref[2 + pair]
     planes = f_ref.shape[0]
     place_halo(ext, planes + 2, even_ref, odd_ref, cs_ref)
     ext[planes + 2 : 2 * planes + 2] = f_ref[...]
-    first, last = chip < 2, chip >= chips - 2
+    first, last = block == 0, block == blocks - 1
     low = (jnp.where(first, cosine, 1.0), jnp.where(first, -sine, 0.0))
     high = (jnp.where(last, cosine, 1.0), jnp.where(last, sine, 0.0))
 
@@ -353,12 +373,12 @@
             ]
             ext[base + x, 0], ext[base + x, 1] = rotated(real, imag, c, t)
 
-    @pl.when(lax.rem(chip, 2) == 0)
+    @pl.when(side == 0)
     def _():
         place_planes(ext, 0, across_ref, *low)
         place_straight(3 * planes + 2, *high)
 
-    @pl.when(lax.rem(chip, 2) == 1)
+    @pl.when(side == 1)
     def _():
         place_straight(0, *low)
         place_planes(ext, 3 * planes + 2, across_ref, *high)
@@ -375,8 +395,8 @@
             g[x, part] = fine_scale * (f_ref[x, part] + b1[x + 4, part] + b2[x + 2, part] + b3)
     half = planes // 2
     for x in range(half):
-        own_ref[x] = g[core * half + x]
-        send_ref[x] = g[(1 - core) * half + x]
+        first_ref[x] = g[pair * half + x]
+        second_ref[x] = g[(1 - pair) * half + x]
 
 
 def shift_z(v, step):
@@ -420,10 +440,10 @@
     pieces, refs = refs[:radix], refs[radix:]
     cs_ref, own_ref, send_ref, s, u, v, r1, s2, u2, v2, r2, s3, u3, v3 = refs
     position = lax.axis_index("grid")
-    core, block = lax.rem(position, 2), lax.div(position, 4)
+    pair, _, block = place_in_grid()
     count = s.shape[0]
     rate, near_rate = level_numbers(1)
-    cosine, sine = cs_ref[core], cs_ref[2 + core]
+    cosine, sine = cs_ref[pair], cs_ref[2 + pair]
     lane = lax.broadcasted_iota(jnp.int32, (8, 128), 1)
     lane_sine = jnp.where(lane < 64, -sine, sine)
 
@@ -530,7 +550,7 @@
     sweep(v, u)
     sweep(u, v)
 
-    for target, tile in ((own_ref, position), (send_ref, position + 1 - 2 * core)):
+    for target, tile in ((own_ref, position), (send_ref, position + 2 - 4 * pair)):
         for k in range(5):
             q = tile + k - 2
             low, high = q < 0, q >= count
@@ -540,7 +560,8 @@
             target[k, 0], target[k, 1] = rotated(v[q + 1, 0], v[q + 1, 1], c, t)
 
 
-def correct(w_ref, g_ref, e, b1, store):
+def correct(w_ref, pair, first_ref, second_ref, e, b1, store):
+    own = place_in_grid()[1] == pair
     lines = w_ref.shape[2]
     wide = dot(w_ref[...].reshape(10 * lines, 128), spread_matrix(128, 256))
     for r in range(10):
@@ -558,24 +579,25 @@
             b1[x, f] = smooth_fine(expanded, x + 2, f)
     for x in range(2):
         for f in range(2):
-            store(f, x, g_ref[x, f] + smooth_fine(lambda i, g: b1[i, g], x + 2, f))
-
-
-def own_kernel(w_ref, g_ref, out_ref, e, b1):
+            g = jnp.where(own, first_ref[x, f], second_ref[x, f])
+            store(f, x, g + smooth_fine(lambda i, g: b1[i, g], x + 2, f))
+
+
+def own_kernel(w_ref, first_ref, second_ref, out_ref, e, b1):
     def store(part, x, value):
         out_ref[part, x] = value
 
-    correct(w_ref, g_ref, e, b1, store)
-
-
-def output_kernel(own_ref, w_ref, g_ref, out_ref, e, b1):
-    core = lax.rem(lax.axis_index("grid"), 2)
-    out_ref[core] = own_ref[...]
+    correct(w_ref, place_in_grid()[0], first_ref, second_ref, e, b1, store)
+
+
+def output_kernel(own_ref, w_ref, first_ref, second_ref, out_ref, e, b1):
+    pair = place_in_grid()[0]
+    out_ref[pair] = own_ref[...]
 
     def store(part, x, value):
-        out_ref[1 - core, part, x] = value
-
-    correct(w_ref, g_ref, e, b1, store)
+        out_ref[1 - pair, part, x] = value
+
+    correct(w_ref, 1 - pair, first_ref, second_ref, e, b1, store)
 
 
 def pair_phases(pair_table, k_fraction):
@@ -615,7 +637,10 @@
         out_shape=out_shape,
         in_specs=in_specs,
         out_specs=vmem(1)[0] if single else vmem(len(out_shape)),
-        scratch_shapes=[pltpu.VMEM(shape, jnp.float32) for shape in scratch],
+        scratch_shapes=[
+            pltpu.VMEM(shape, jnp.float32) if isinstance(shape, tuple) else shape
+            for shape in scratch
+        ],
         compiler_params=pltpu.CompilerParams(vmem_limit_bytes=48 * 2**20),
         cost_estimate=pl.CostEstimate(flops=flops, bytes_accessed=2**20, transcendentals=0),
     )
@@ -644,40 +669,53 @@
     def permute_block(value, target):
         return permute(value, lambda i: target(i // 4) * 4 + i % 4)
 
-    def partner(i):
+    def within_block(move):
+        return lambda i: i // 4 * 4 + 2 * move(i // 2 % 2, i % 2)[0] + move(i // 2 % 2, i % 2)[1]
+
+    def other_half(i):
         return i ^ 1
 
-    def even_side(i):
-        return i ^ 2
-
-    def odd_side(i):
-        return (i // 2 + (1 if i // 2 % 2 else -1)) % chips * 2 + i % 2
+    def next_half(i):
+        return (i + (3 if i % 2 else -3)) % tile_count
 
     def next_block(i):
-        return (i + (4 if i // 2 % 2 else -4)) % tile_count
+        return (i + (4 if i % 2 else -4)) % tile_count
+
+    def block_behind(i):
+        return (i + (-4 if i % 2 else 4)) % tile_count
 
     cs = pair_phases(pair_table, k_fraction)
 
-    other = permute(lax.dynamic_index_in_dim(pair_density, 1 - core, 0, False), partner)
-    tile_row, line_row = slot_tile.reshape(1, -1), slot_row.reshape(1, -1)
-    row = 2 * depth
-    kept, sent = call(
+    first = permute(
+        lax.dynamic_index_in_dim(pair_density, core, 0, False), within_block(lambda h, c: (c, h))
+    )
+    second = permute(
+        lax.dynamic_index_in_dim(pair_density, 1 - core, 0, False),
+        within_block(lambda h, c: (1 - c, h)),
+    )
+    rows = call(
         rows_kernel,
-        [shaped(slot_count, row), shaped(slot_count + 8, row)],
-        vmem(5),
-        [(2, slot_count, row)],
+        shaped(slot_count + 8, 4 * depth),
+        vmem(1) + [pl.BlockSpec(memory_space=pltpu.HBM)] + vmem(3),
+        [(shapes.shape[1], slot_count, depth), pltpu.SemaphoreType.DMA((5,))],
         10**7,
-    )(moments, shapes.transpose(1, 0, 2), slot_atom.reshape(1, -1), tile_row, line_row)
-    got = permute(sent, partner)
+    )(
+        moments,
+        shapes.transpose(1, 0, 2),
+        slot_atom.reshape(1, -1),
+        slot_tile.reshape(1, -1),
+        slot_row.reshape(1, -1),
+    )
+    got = permute(rows, other_half)
     apart = chips <= 8
     height = 16 * capacity + 8
     packed = call(
         pack_kernel,
         [shaped(height, 128)] * chips if apart else [shaped(chips, height, 128)],
-        vmem(4) + [pl.BlockSpec(memory_space=pl.ANY)],
-        [],
+        vmem(2),
+        [(8, 4 * capacity * blocks, 128)],
         10**8,
-    )(kept, got, tile_row, line_row, other)
+    )(rows, got)
     if apart:
         received = [
             permute(packed[k], lambda i, k=k: i ^ (2 * k)) if k else packed[k]
@@ -699,11 +737,11 @@
         vmem(2 + len(received)),
         [(planes + 4, *full), (8, lines, 128)],
         10**8,
-    )(pair_density, other, *received)
-    even = permute(f, even_side)
-    odd = permute(f, odd_side)
+    )(first, second, *received)
+    even = permute(f, other_half)
+    odd = permute(f, next_half)
     straight = permute(straight, next_block)
-    across = permute(across, lambda i: (i + (-4 if i // 2 % 2 else 4)) % tile_count)
+    across = permute(across, block_behind)
     source = call(
         source_kernel,
         shaped(planes, *small),
@@ -712,14 +750,15 @@
         10**7,
     )(even, odd, straight, f, cs)
     pieces = gather_blocks(source, blocks, block, permute_block)
-    own, send = call(
+    first, second = call(
         fine_kernel,
         [shaped(thick, *full)] * 2,
         vmem(5) + smem,
         [(3 * planes + 4, *full), (planes + 8, *full), (planes + 4, *full), (planes, *full)],
         10**7,
     )(even, odd, straight, across, f, cs)
-    got = permute(send, partner)
+    first = permute(first, within_block(lambda h, c: (c, h)))
+    second = permute(second, within_block(lambda h, c: (c, 1 - h)))
 
     n1, n2, n3 = tile_count, tile_count // 2, tile_count // 4
     tile = (8, 128)
@@ -742,11 +781,13 @@
         ],
         10**8,
     )(*pieces, cs)
-    w_got = permute(w_send, partner)
+    w_got = permute(w_send, lambda i: i ^ 2)
     scratch = [(20, lines, 128), (6, *full)]
-    result = call(own_kernel, shaped(2, thick, lines, depth), vmem(2), scratch, 10**7)(w_own, own)
-    return call(output_kernel, shaped(*pair_density.shape), vmem(3), scratch, 10**7)(
-        result, w_got, got
+    result = call(own_kernel, shaped(2, thick, lines, depth), vmem(3), scratch, 10**7)(
+        w_own, first, second
+    )
+    return call(output_kernel, shaped(*pair_density.shape), vmem(4), scratch, 10**7)(
+        result, w_got, first, second
     )
 
 

time: 61 us -> 68.3 us (1.12)
  starting transfers between devices: 23.4 us -> 32 us
  waiting for transfers between devices: 18.4 us -> 16.5 us
    ppermute x18 -> x20, starting transfers between devices: 23.4 us -> 32 us  [permute(): return lax.ppermute(value, 'grid', [(i, target(i)) for i in devices])]
    ppermute x18 -> x20, waiting for transfers between devices: 18.4 us -> 16.5 us  [permute(): return lax.ppermute(value, 'grid', [(i, target(i)) for i in devices])]
    pallas_call x3, Pallas kernels: 4.01 us -> 4.77 us  [the longest x1 2.25 us: per_device(): call(rows_kernel, shaped(slot_count + 8, 4 * depth), vmem(1) + [pl.BlockS...]
    unnamed x20 -> x16, local copies, waits for them, and re-layouts: 4.18 us -> 4.14 us
  transfers between devices with their start and end apart: 18 -> 20, of which waited for: 10 -> 6; matrix products, arithmetic and copies ran while one was open for 1% -> 1% of each run, Pallas kernels for 15% -> 14%
where the time goes in v7:
time: 68.3 us; the launch traced here: 68.1 us
  starting transfers between devices  32 us (47%)
  waiting for transfers between devices  16.5 us (24%)
  Pallas kernels  14.8 us (22%)
  local copies, waits for them, and re-layouts  4.16 us (6%)
    ppermute x20, starting transfers between devices, permute(): return lax.ppermute(value, 'grid', [(i, target(i)) for i in devices])  32 us
    ppermute x20, waiting for transfers between devices, permute(): return lax.ppermute(value, 'grid', [(i, target(i)) for i in devices])  16.5 us
    unnamed x16, local copies, waits for them, and re-layouts  4.14 us
    pallas_call x1, Pallas kernels, per_device(): call(cycle_kernel, [shaped(5, *small)] * 2, vmem(len(pieces)) + smem, [(n...  2.93 us
    pallas_call x1, Pallas kernels, per_device(): call(fine_kernel, [shaped(thick, *full)] * 2, vmem(5) + smem, [(3 * plane...  2.55 us
    pallas_call x1, Pallas kernels, per_device(): call(source_kernel, shaped(planes, *small), vmem(4) + smem, [(4 * planes,...  2.52 us
    pallas_call x1, Pallas kernels, per_device(): call(rows_kernel, shaped(slot_count + 8, 4 * depth), vmem(1) + [pl.BlockS...  2.25 us
    pallas_call x1, Pallas kernels, per_device(): call(output_kernel, shaped(*pair_density.shape), vmem(4), scratch, 10 ** 7)  1.62 us
  transfers between devices with their start and end apart: 20, of which 6 were waited for; matrix products, arithmetic and copies ran while one was open for 1% of the time, Pallas kernels for 14%

profile of v7, /device:TPU:0, one launch (start us, length us, event | category | flops | bytes accessed | tf_op | source)
XLA Modules:
  0.0 68.1 jit_solution(5708625146520674904)
XLA Ops:
  0.0 1.4 %copy-done = f32[64,25,256]{2,0,1:T(8,128)S(1)} copy-done((f32[64,25,256]{2,0,1:T(8,128)S(1)}, f32[64,25,256]{2,0,1:T(8,128)}, u32[]{:S(2)}) %copy-start) | copy-done | bytes 1638424
  1.4 0.7 %copy-done.1 = f32[12,2,2,25]{3,2,1,0:T(2,128)S(1)} copy-done((f32[12,2,2,25]{3,2,1,0:T(2,128)S(1)}, f32[12,2,2,25]{3,2,1,0:T(2,128)}, u32[]{:S(2)}) %copy-start.1) | copy-done | bytes 4824
  2.2 0.7 copy-done.2
  2.8 0.7 copy-done.3
  3.5 0.7 copy-done.4
  4.1 2.2 %shard_map.82.own_ref = f32[72,1024]{1,0:T(8,128)S(1)} custom-call(f32[12,2,2,25]{3,2,1,0:T(2,128)S(1)} %copy-done.1, f32[25,64,256]{2,1,0:T(8,128)S(1)} %bitcast.8, s32[1,64]{1,0:T(1,128)S(1)} %bitcast.9, s32[1,64]{1,0:T(1,128)S(1)} %bitcast.10, s32[1,64]{1,0:T(1,128)S(1)} %bitcast.11), custom_call_target="tpu_custom_call" | custom-call | flops 10000000 | bytes 1048576 | tf_op jit(solution)/shard_map/pallas_call | solution.py:696
  6.4 0.5 collective-permute-start.2
  6.9 0.7 collective-permute-start
  7.6 3.8 %collective-permute-start.1 = (f32[2,2,32,256]{3,2,1,0:T(8,128)S(1)}, f32[2,2,32,256]{3,2,1,0:T(8,128)S(1)}, u32[]{:S(2)}, u32[]{:S(2)}) collective-permute-start(f32[2,2,32,256]{3,2,1,0:T(8,128)S(1)} %get-tuple-element.37), channel_id=1, source_target_pairs={{0,2},{1,0},{2,3},{3,1},{4,6},{5,4},{6,7},{7,5},{8,10},{9,8},{10,1... | collective-permute-start | bytes 393224 | tf_op jit(solution)/shard_map/ppermute | solution.py:667
  11.4 0.8 %shard_map.83 = (f32[136,128]{1,0:T(8,128)S(1)}, f32[136,128]{1,0:T(8,128)S(1)}, f32[136,128]{1,0:T(8,128)S(1)}, f32[136,128]{1,0:T(8,128)S(1)}, f32[136,128]{1,...) custom-call(f32[72,1024]{1,0:T(8,128)S(1)} %shard_map.82.own_ref, ...), custom_call_target="tpu_custom_call" | custom-call | flops 100000000 | bytes 1048576 | tf_op jit(solution)/shard_map/pallas_call | solution.py:712
  12.3 0.1 collective-permute-start.3
  12.3 4.2 %collective-permute-start.4 = (f32[136,128]{1,0:T(8,128)S(1)}, f32[136,128]{1,0:T(8,128)S(1)}, u32[]{:S(2)}, u32[]{:S(2)}) collective-permute-start(f32[136,128]{1,0:T(8,128)S(1)} %get-tuple-element.22), channel_id=1, source_target_pairs={{0,12},{1,13},{2,14},{3,15},{4,8},{5,9},{6,10},{7,11},{8,4},{9,5},... | collective-permute-start | bytes 208904 | tf_op jit(solution)/shard_map/ppermute | solution.py:667
  16.6 1.4 %collective-permute-start.5 = (f32[136,128]{1,0:T(8,128)S(1)}, f32[136,128]{1,0:T(8,128)S(1)}, u32[]{:S(2)}, u32[]{:S(2)}) collective-permute-start(f32[136,128]{1,0:T(8,128)S(1)} %get-tuple-element.23), channel_id=1, source_target_pairs={{0,14},{1,15},{2,12},{3,13},{4,10},{5,11},{6,8},{7,9},{8,6},{9,7},... | collective-permute-start | bytes 208904 | tf_op jit(solution)/shard_map/ppermute | solution.py:667
  18.0 1.0 %collective-permute-start.6 = (f32[136,128]{1,0:T(8,128)S(1)}, f32[136,128]{1,0:T(8,128)S(1)}, u32[]{:S(2)}, u32[]{:S(2)}) collective-permute-start(f32[136,128]{1,0:T(8,128)S(1)} %get-tuple-element.24), channel_id=1, source_target_pairs={{0,8},{1,9},{2,10},{3,11},{4,12},{5,13},{6,14},{7,15},{8,0},{9,1},... | collective-permute-start | bytes 208904 | tf_op jit(solution)/shard_map/ppermute | solution.py:667
  19.0 0.0 collective-permute-done.1.refs_1_
  19.0 1.9 %collective-permute-start.7 = (f32[136,128]{1,0:T(8,128)S(1)}, f32[136,128]{1,0:T(8,128)S(1)}, u32[]{:S(2)}, u32[]{:S(2)}) collective-permute-start(f32[136,128]{1,0:T(8,128)S(1)} %get-tuple-element.25), channel_id=1, source_target_pairs={{0,10},{1,11},{2,8},{3,9},{4,14},{5,15},{6,12},{7,13},{8,2},{9,3},... | collective-permute-start | bytes 208904 | tf_op jit(solution)/shard_map/ppermute | solution.py:667
  20.9 0.0 collective-permute-done.3.refs_3_
  20.9 1.5 %collective-permute-start.8 = (f32[136,128]{1,0:T(8,128)S(1)}, f32[136,128]{1,0:T(8,128)S(1)}, u32[]{:S(2)}, u32[]{:S(2)}) collective-permute-start(f32[136,128]{1,0:T(8,128)S(1)} %get-tuple-element.26), channel_id=1, source_target_pairs={{0,4},{1,5},{2,6},{3,7},{4,0},{5,1},{6,2},{7,3},{8,12},{9,13},{10,... | collective-permute-start | bytes 208904 | tf_op jit(solution)/shard_map/ppermute | solution.py:667
  22.4 0.0 collective-permute-done.4.refs_4_
  22.4 2.6 %collective-permute-start.9 = (f32[136,128]{1,0:T(8,128)S(1)}, f32[136,128]{1,0:T(8,128)S(1)}, u32[]{:S(2)}, u32[]{:S(2)}) collective-permute-start(f32[136,128]{1,0:T(8,128)S(1)} %get-tuple-element.27), channel_id=1, source_target_pairs={{0,6},{1,7},{2,4},{3,5},{4,2},{5,3},{6,0},{7,1},{8,14},{9,15},{10,... | collective-permute-start | bytes 208904 | tf_op jit(solution)/shard_map/ppermute | solution.py:667
  25.0 3.0 %collective-permute-done.6.refs_6_ = f32[136,128]{1,0:T(8,128)S(1)} collective-permute-done((f32[136,128]{1,0:T(8,128)S(1)}, f32[136,128]{1,0:T(8,128)S(1)}, u32[]{:S(2)}, u32[]{:S(2)}) %collective-permute-start.6) | collective-permute-done | bytes 69664 | tf_op jit(solution)/shard_map/ppermute | solution.py:667
  28.0 1.4 %collective-permute-done.7.refs_7_ = f32[136,128]{1,0:T(8,128)S(1)} collective-permute-done((f32[136,128]{1,0:T(8,128)S(1)}, f32[136,128]{1,0:T(8,128)S(1)}, u32[]{:S(2)}, u32[]{:S(2)}) %collective-permute-start.7) | collective-permute-done | bytes 69664 | tf_op jit(solution)/shard_map/ppermute | solution.py:667
  29.4 0.0 collective-permute-done.8.refs_8_
  29.4 0.4 collective-permute-done.9.refs_9_
  29.8 1.2 %shard_map.84 = (f32[4,2,32,256]{3,2,1,0:T(8,128)S(1)}, f32[10,32,128]{2,1,0:T(8,128)S(1)}, f32[2,2,32,256]{3,2,1,0:T(8,128)S(1)}) custom-call(f32[2,2,32,256]{3,2,1,0:T(8,128)S(1)} %collective-permute-done.refs_0_, f32[2,2,32,256]{3,2,1,0:T(8,128)S(1)} %collective-permute-done.1.refs_1_, f32[136,128]{1,0:T(8,128)S(1)} %get-tuple-element.20.refs_2_, ...), custom_call_target="tpu_custom_call" | custom-call | flops 100000000 | bytes 1048576 | tf_op jit(solution)/shard_map/pallas_call | solution.py:734
  31.0 0.1 collective-permute-start.10
  31.1 3.5 %collective-permute-start.11 = (f32[4,2,32,256]{3,2,1,0:T(8,128)S(1)}, f32[4,2,32,256]{3,2,1,0:T(8,128)S(1)}, u32[]{:S(2)}, u32[]{:S(2)}) collective-permute-start(f32[4,2,32,256]{3,2,1,0:T(8,128)S(1)} %get-tuple-element.28.f_ref), channel_id=1, source_target_pairs={{0,13},{1,4},{2,15},{3,6},{4,1},{5,8},{6,3},{7,10},{8,5},{9,12},{1... | collective-permute-start | bytes 786440 | tf_op jit(solution)/shard_map/ppermute | solution.py:667
  34.6 0.2 fusion
  34.7 0.0 collective-permute-start.12
  34.7 0.2 cosine_reduce_fusion
  35.0 2.1 %collective-permute-start.16 = (f32[2,2,32,256]{3,2,1,0:T(8,128)S(1)}, f32[2,2,32,256]{3,2,1,0:T(8,128)S(1)}, u32[]{:S(2)}, u32[]{:S(2)}) collective-permute-start(f32[2,2,32,256]{3,2,1,0:T(8,128)S(1)} %get-tuple-element.31), channel_id=1, source_target_pairs={{0,4},{1,13},{2,6},{3,15},{4,8},{5,1},{6,10},{7,3},{8,12},{9,5},{1... | collective-permute-start | bytes 393224 | tf_op jit(solution)/shard_map/ppermute | solution.py:667
  37.0 0.1 pad_maximum_fusion.cs_ref.refs_4_
  37.1 8.2 %collective-permute-done.12.straight_ref = f32[10,32,128]{2,1,0:T(8,128)S(1)} collective-permute-done((f32[10,32,128]{2,1,0:T(8,128)S(1)}, f32[10,32,128]{2,1,0:T(8,128)S(1)}, u32[]{:S(2)}, u32[]{:S(2)}) %collective-permute-start.12) | collective-permute-done | bytes 163872 | tf_op jit(solution)/shard_map/ppermute | solution.py:667
  45.4 0.0 collective-permute-done.10.even_ref
  45.4 0.0 collective-permute-done.11.odd_ref
  45.4 2.5 %shard_map.85.refs_0_ = f32[4,2,16,128]{3,2,1,0:T(8,128)S(1)} custom-call(f32[4,2,32,256]{3,2,1,0:T(8,128)S(1)} %collective-permute-done.10.even_ref, f32[4,2,32,256]{3,2,1,0:T(8,128)S(1)} %collective-permute-done.11.odd_ref, f32[10,32,128]{2,1,0:T(8,128)S(1)} %collective-permute-done.12.straight_ref, f32[4,2,32,256]{3,2,1,0:T(8,128)S(1)} %get-tuple-element.28.f_ref, ...), custom_call_target="tpu_custom_call" | custom-call | flops 10000000 | bytes 1048576 | tf_op jit(solution)/shard_map/pallas_call | solution.py:745
  47.9 0.1 collective-permute-start.13
  48.0 2.9 %collective-permute-start.14 = (f32[4,2,16,128]{3,2,1,0:T(8,128)S(1)}, f32[4,2,16,128]{3,2,1,0:T(8,128)S(1)}, u32[]{:S(2)}, u32[]{:S(2)}) collective-permute-start(f32[4,2,16,128]{3,2,1,0:T(8,128)S(1)} %shard_map.85.refs_0_), channel_id=1, source_target_pairs={{0,8},{1,9},{2,10},{3,11},{4,12},{5,13},{6,14},{7,15},{8,0},{9,1},... | collective-permute-start | bytes 196616 | tf_op jit(solution)/shard_map/ppermute | solution.py:667
  50.9 1.5 %collective-permute-start.15 = (f32[4,2,16,128]{3,2,1,0:T(8,128)S(1)}, f32[4,2,16,128]{3,2,1,0:T(8,128)S(1)}, u32[]{:S(2)}, u32[]{:S(2)}) collective-permute-start(f32[4,2,16,128]{3,2,1,0:T(8,128)S(1)} %shard_map.85.refs_0_), channel_id=1, source_target_pairs={{0,12},{1,13},{2,14},{3,15},{4,8},{5,9},{6,10},{7,11},{8,4},{9,5},... | collective-permute-start | bytes 196616 | tf_op jit(solution)/shard_map/ppermute | solution.py:667
  52.4 2.6 %shard_map.87 = (f32[2,2,32,256]{3,2,1,0:T(8,128)S(1)}, f32[2,2,32,256]{3,2,1,0:T(8,128)S(1)}) custom-call(f32[4,2,32,256]{3,2,1,0:T(8,128)S(1)} %collective-permute-done.10.even_ref, f32[4,2,32,256]{3,2,1,0:T(8,128)S(1)} %collective-permute-done.11.odd_ref, f32[10,32,128]{2,1,0:T(8,128)S(1)} %collective-permute-done.12.straight_ref, ...), custom_call_target="tpu_custom_call" | custom-call | flops 10000000 | bytes 1048576 | tf_op jit(solution)/shard_map/pallas_call | solution.py:753
  54.9 0.8 %collective-permute-start.17 = (f32[2,2,32,256]{3,2,1,0:T(8,128)S(1)}, f32[2,2,32,256]{3,2,1,0:T(8,128)S(1)}, u32[]{:S(2)}, u32[]{:S(2)}) collective-permute-start(f32[2,2,32,256]{3,2,1,0:T(8,128)S(1)} %get-tuple-element.32), channel_id=1, source_target_pairs={{0,0},{1,2},{2,1},{3,3},{4,4},{5,6},{6,5},{7,7},{8,8},{9,10},{10,9... | collective-permute-start | bytes 393224 | tf_op jit(solution)/shard_map/ppermute | solution.py:667
  55.8 3.2 %collective-permute-start.18 = (f32[2,2,32,256]{3,2,1,0:T(8,128)S(1)}, f32[2,2,32,256]{3,2,1,0:T(8,128)S(1)}, u32[]{:S(2)}, u32[]{:S(2)}) collective-permute-start(f32[2,2,32,256]{3,2,1,0:T(8,128)S(1)} %get-tuple-element.33), channel_id=1, source_target_pairs={{0,1},{1,3},{2,0},{3,2},{4,5},{5,7},{6,4},{7,6},{8,9},{9,11},{10,8... | collective-permute-start | bytes 393224 | tf_op jit(solution)/shard_map/ppermute | solution.py:667
  59.0 2.9 %shard_map.86 = (f32[5,2,16,128]{3,2,1,0:T(8,128)S(1)}, f32[5,2,16,128]{3,2,1,0:T(8,128)S(1)}) custom-call(f32[4,2,16,128]{3,2,1,0:T(8,128)S(1)} %shard_map.85.refs_0_, f32[4,2,16,128]{3,2,1,0:T(8,128)S(1)} %collective-permute-done.13.refs_1_, f32[4,2,16,128]{3,2,1,0:T(8,128)S(1)} %collective-permute-done.14.refs_2_, ...), custom_call_target="tpu_custom_call" | custom-call | flops 100000000 | bytes 1048576 | tf_op jit(solution)/shard_map/pallas_call | solution.py:765
  61.9 0.1 collective-permute-start.19
  62.0 1.0 %collective-permute-done.18.second_ref = f32[2,2,32,256]{3,2,1,0:T(8,128)S(1)} collective-permute-done((f32[2,2,32,256]{3,2,1,0:T(8,128)S(1)}, f32[2,2,32,256]{3,2,1,0:T(8,128)S(1)}, u32[]{:S(2)}, u32[]{:S(2)}) %collective-permute-start.18) | collective-permute-done | bytes 131104 | tf_op jit(solution)/shard_map/ppermute | solution.py:667
  63.0 0.9 %shard_map.88.own_ref = f32[2,2,32,256]{3,2,1,0:T(8,128)S(1)} custom-call(f32[5,2,16,128]{3,2,1,0:T(8,128)S(1)} %get-tuple-element.30.w_ref, f32[2,2,32,256]{3,2,1,0:T(8,128)S(1)} %collective-permute-done.17.first_ref, f32[2,2,32,256]{3,2,1,0:T(8,128)S(1)} %collective-permute-done.18.second_ref), custom_call_target="tpu_custom_call" | custom-call | flops 10000000 | bytes 1048576 | tf_op jit(solution)/shard_map/pallas_call | solution.py:786
  63.9 2.5 %collective-permute-done.19.w_ref = f32[5,2,16,128]{3,2,1,0:T(8,128)S(1)} collective-permute-done((f32[5,2,16,128]{3,2,1,0:T(8,128)S(1)}, f32[5,2,16,128]{3,2,1,0:T(8,128)S(1)}, u32[]{:S(2)}, u32[]{:S(2)}) %collective-permute-start.19) | collective-permute-done | bytes 81952 | tf_op jit(solution)/shard_map/ppermute | solution.py:667
  66.5 1.6 %shard_map.89 = f32[2,2,2,32,256]{4,3,2,1,0:T(8,128)} custom-call(f32[2,2,32,256]{3,2,1,0:T(8,128)S(1)} %shard_map.88.own_ref, f32[5,2,16,128]{3,2,1,0:T(8,128)S(1)} %collective-permute-done.19.w_ref, f32[2,2,32,256]{3,2,1,0:T(8,128)S(1)} %collective-permute-done.17.first_ref, f32[2,2,32,256]{3,2,1,0:T(8,128)S(1)} %collective-permute-done.18.second_ref), custom_call_target="tpu_custom_call" | custom-call | flops 10000000 | bytes 1048576 | tf_op jit(solution)/shard_map/pallas_call | solution.py:789
  (20 shorter events, 0.1 us)
Async XLA Ops:
  0.0 1.4 %copy-start = (f32[64,25,256]{2,0,1:T(8,128)S(1)}, f32[64,25,256]{2,0,1:T(8,128)}, u32[]{:S(2)}) copy-start(f32[64,25,256]{2,0,1:T(8,128)} %param.10) | copy-start | bytes 4915204
  1.4 0.7 %copy-start.1 = (f32[12,2,2,25]{3,2,1,0:T(2,128)S(1)}, f32[12,2,2,25]{3,2,1,0:T(2,128)}, u32[]{:S(2)}) copy-start(f32[12,2,2,25]{3,2,1,0:T(2,128)} %moments_ref.1) | copy-start | bytes 14404
  2.2 0.7 copy-start.2
  2.8 0.7 copy-start.3
  3.5 0.7 copy-start.4
  4.1 2.8 %copy-start.5 = (f32[2,2,2,32,256]{4,3,2,1,0:T(8,128)S(1)}, f32[2,2,2,32,256]{4,3,2,1,0:T(8,128)}, u32[]{:S(2)}) copy-start(f32[2,2,2,32,256]{4,3,2,1,0:T(8,128)} %param.8) | copy-start | bytes 786436
  4.1 30.4 %copy-start.6 = (s32[2,2]{1,0:T(2,128)S(1)}, s32[2,2]{1,0:T(2,128)}, u32[]{:S(2)}) copy-start(s32[2,2]{1,0:T(2,128)} %param.14) | copy-start | bytes 52
  4.1 30.4 %copy-start.7 = (f32[8]{0:T(128)S(1)}, f32[8]{0:T(128)}, u32[]{:S(2)}) copy-start(f32[8]{0:T(128)} %param.15) | copy-start | bytes 100
  6.4 5.0 %collective-permute-start.2 = (f32[72,1024]{1,0:T(8,128)S(1)}, f32[72,1024]{1,0:T(8,128)S(1)}, u32[]{:S(2)}, u32[]{:S(2)}) collective-permute-start(f32[72,1024]{1,0:T(8,128)S(1)} %shard_map.82.own_ref), channel_id=1, source_target_pairs={{0,1},{1,0},{2,3},{3,2},{4,5},{5,4},{6,7},{7,6},{8,9},{9,8},{10,11... | collective-permute-start | bytes 884744 | tf_op jit(solution)/shard_map/ppermute | solution.py:667
  6.9 11.0 %collective-permute-start = (f32[2,2,32,256]{3,2,1,0:T(8,128)S(1)}, f32[2,2,32,256]{3,2,1,0:T(8,128)S(1)}, u32[]{:S(2)}, u32[]{:S(2)}) collective-permute-start(f32[2,2,32,256]{3,2,1,0:T(8,128)S(1)} %get-tuple-element.38), channel_id=1, source_target_pairs={{0,0},{1,2},{2,1},{3,3},{4,4},{5,6},{6,5},{7,7},{8,8},{9,10},{10,9... | collective-permute-start | bytes 393224 | tf_op jit(solution)/shard_map/ppermute | solution.py:667
  7.6 11.4 %collective-permute-start.1 = (f32[2,2,32,256]{3,2,1,0:T(8,128)S(1)}, f32[2,2,32,256]{3,2,1,0:T(8,128)S(1)}, u32[]{:S(2)}, u32[]{:S(2)}) collective-permute-start(f32[2,2,32,256]{3,2,1,0:T(8,128)S(1)} %get-tuple-element.37), channel_id=1, source_target_pairs={{0,2},{1,0},{2,3},{3,1},{4,6},{5,4},{6,7},{7,5},{8,10},{9,8},{10,1... | collective-permute-start | bytes 393224 | tf_op jit(solution)/shard_map/ppermute | solution.py:667
  12.3 8.7 %collective-permute-start.3 = (f32[136,128]{1,0:T(8,128)S(1)}, f32[136,128]{1,0:T(8,128)S(1)}, u32[]{:S(2)}, u32[]{:S(2)}) collective-permute-start(f32[136,128]{1,0:T(8,128)S(1)} %get-tuple-element.21), channel_id=1, source_target_pairs={{0,2},{1,3},{2,0},{3,1},{4,6},{5,7},{6,4},{7,5},{8,10},{9,11},{10,... | collective-permute-start | bytes 208904 | tf_op jit(solution)/shard_map/ppermute | solution.py:667
  12.3 10.1 %collective-permute-start.4 = (f32[136,128]{1,0:T(8,128)S(1)}, f32[136,128]{1,0:T(8,128)S(1)}, u32[]{:S(2)}, u32[]{:S(2)}) collective-permute-start(f32[136,128]{1,0:T(8,128)S(1)} %get-tuple-element.22), channel_id=1, source_target_pairs={{0,12},{1,13},{2,14},{3,15},{4,8},{5,9},{6,10},{7,11},{8,4},{9,5},... | collective-permute-start | bytes 208904 | tf_op jit(solution)/shard_map/ppermute | solution.py:667
  16.6 8.4 %collective-permute-start.5 = (f32[136,128]{1,0:T(8,128)S(1)}, f32[136,128]{1,0:T(8,128)S(1)}, u32[]{:S(2)}, u32[]{:S(2)}) collective-permute-start(f32[136,128]{1,0:T(8,128)S(1)} %get-tuple-element.23), channel_id=1, source_target_pairs={{0,14},{1,15},{2,12},{3,13},{4,10},{5,11},{6,8},{7,9},{8,6},{9,7},... | collective-permute-start | bytes 208904 | tf_op jit(solution)/shard_map/ppermute | solution.py:667
  18.0 10.0 %collective-permute-start.6 = (f32[136,128]{1,0:T(8,128)S(1)}, f32[136,128]{1,0:T(8,128)S(1)}, u32[]{:S(2)}, u32[]{:S(2)}) collective-permute-start(f32[136,128]{1,0:T(8,128)S(1)} %get-tuple-element.24), channel_id=1, source_target_pairs={{0,8},{1,9},{2,10},{3,11},{4,12},{5,13},{6,14},{7,15},{8,0},{9,1},... | collective-permute-start | bytes 208904 | tf_op jit(solution)/shard_map/ppermute | solution.py:667
  19.0 10.4 %collective-permute-start.7 = (f32[136,128]{1,0:T(8,128)S(1)}, f32[136,128]{1,0:T(8,128)S(1)}, u32[]{:S(2)}, u32[]{:S(2)}) collective-permute-start(f32[136,128]{1,0:T(8,128)S(1)} %get-tuple-element.25), channel_id=1, source_target_pairs={{0,10},{1,11},{2,8},{3,9},{4,14},{5,15},{6,12},{7,13},{8,2},{9,3},... | collective-permute-start | bytes 208904 | tf_op jit(solution)/shard_map/ppermute | solution.py:667
  20.9 8.5 %collective-permute-start.8 = (f32[136,128]{1,0:T(8,128)S(1)}, f32[136,128]{1,0:T(8,128)S(1)}, u32[]{:S(2)}, u32[]{:S(2)}) collective-permute-start(f32[136,128]{1,0:T(8,128)S(1)} %get-tuple-element.26), channel_id=1, source_target_pairs={{0,4},{1,5},{2,6},{3,7},{4,0},{5,1},{6,2},{7,3},{8,12},{9,13},{10,... | collective-permute-start | bytes 208904 | tf_op jit(solution)/shard_map/ppermute | solution.py:667
  22.4 7.3 %collective-permute-start.9 = (f32[136,128]{1,0:T(8,128)S(1)}, f32[136,128]{1,0:T(8,128)S(1)}, u32[]{:S(2)}, u32[]{:S(2)}) collective-permute-start(f32[136,128]{1,0:T(8,128)S(1)} %get-tuple-element.27), channel_id=1, source_target_pairs={{0,6},{1,7},{2,4},{3,5},{4,2},{5,3},{6,0},{7,1},{8,14},{9,15},{10,... | collective-permute-start | bytes 208904 | tf_op jit(solution)/shard_map/ppermute | solution.py:667
  31.0 14.4 %collective-permute-start.10 = (f32[4,2,32,256]{3,2,1,0:T(8,128)S(1)}, f32[4,2,32,256]{3,2,1,0:T(8,128)S(1)}, u32[]{:S(2)}, u32[]{:S(2)}) collective-permute-start(f32[4,2,32,256]{3,2,1,0:T(8,128)S(1)} %get-tuple-element.28.f_ref), channel_id=1, source_target_pairs={{0,1},{1,0},{2,3},{3,2},{4,5},{5,4},{6,7},{7,6},{8,9},{9,8},{10,11... | collective-permute-start | bytes 786440 | tf_op jit(solution)/shard_map/ppermute | solution.py:667
  31.1 14.3 %collective-permute-start.11 = (f32[4,2,32,256]{3,2,1,0:T(8,128)S(1)}, f32[4,2,32,256]{3,2,1,0:T(8,128)S(1)}, u32[]{:S(2)}, u32[]{:S(2)}) collective-permute-start(f32[4,2,32,256]{3,2,1,0:T(8,128)S(1)} %get-tuple-element.28.f_ref), channel_id=1, source_target_pairs={{0,13},{1,4},{2,15},{3,6},{4,1},{5,8},{6,3},{7,10},{8,5},{9,12},{1... | collective-permute-start | bytes 786440 | tf_op jit(solution)/shard_map/ppermute | solution.py:667
  34.7 10.6 %collective-permute-start.12 = (f32[10,32,128]{2,1,0:T(8,128)S(1)}, f32[10,32,128]{2,1,0:T(8,128)S(1)}, u32[]{:S(2)}, u32[]{:S(2)}) collective-permute-start(f32[10,32,128]{2,1,0:T(8,128)S(1)} %get-tuple-element.29), channel_id=1, source_target_pairs={{0,12},{1,5},{2,14},{3,7},{4,0},{5,9},{6,2},{7,11},{8,4},{9,13},{1... | collective-permute-start | bytes 491528 | tf_op jit(solution)/shard_map/ppermute | solution.py:667
  35.0 17.4 %collective-permute-start.16 = (f32[2,2,32,256]{3,2,1,0:T(8,128)S(1)}, f32[2,2,32,256]{3,2,1,0:T(8,128)S(1)}, u32[]{:S(2)}, u32[]{:S(2)}) collective-permute-start(f32[2,2,32,256]{3,2,1,0:T(8,128)S(1)} %get-tuple-element.31), channel_id=1, source_target_pairs={{0,4},{1,13},{2,6},{3,15},{4,8},{5,1},{6,10},{7,3},{8,12},{9,5},{1... | collective-permute-start | bytes 393224 | tf_op jit(solution)/shard_map/ppermute | solution.py:667
  47.9 11.1 %collective-permute-start.13 = (f32[4,2,16,128]{3,2,1,0:T(8,128)S(1)}, f32[4,2,16,128]{3,2,1,0:T(8,128)S(1)}, u32[]{:S(2)}, u32[]{:S(2)}) collective-permute-start(f32[4,2,16,128]{3,2,1,0:T(8,128)S(1)} %shard_map.85.refs_0_), channel_id=1, source_target_pairs={{0,4},{1,5},{2,6},{3,7},{4,0},{5,1},{6,2},{7,3},{8,12},{9,13},{10,... | collective-permute-start | bytes 196616 | tf_op jit(solution)/shard_map/ppermute | solution.py:667
  48.0 11.0 %collective-permute-start.14 = (f32[4,2,16,128]{3,2,1,0:T(8,128)S(1)}, f32[4,2,16,128]{3,2,1,0:T(8,128)S(1)}, u32[]{:S(2)}, u32[]{:S(2)}) collective-permute-start(f32[4,2,16,128]{3,2,1,0:T(8,128)S(1)} %shard_map.85.refs_0_), channel_id=1, source_target_pairs={{0,8},{1,9},{2,10},{3,11},{4,12},{5,13},{6,14},{7,15},{8,0},{9,1},... | collective-permute-start | bytes 196616 | tf_op jit(solution)/shard_map/ppermute | solution.py:667
  50.9 8.1 %collective-permute-start.15 = (f32[4,2,16,128]{3,2,1,0:T(8,128)S(1)}, f32[4,2,16,128]{3,2,1,0:T(8,128)S(1)}, u32[]{:S(2)}, u32[]{:S(2)}) collective-permute-start(f32[4,2,16,128]{3,2,1,0:T(8,128)S(1)} %shard_map.85.refs_0_), channel_id=1, source_target_pairs={{0,12},{1,13},{2,14},{3,15},{4,8},{5,9},{6,10},{7,11},{8,4},{9,5},... | collective-permute-start | bytes 196616 | tf_op jit(solution)/shard_map/ppermute | solution.py:667
  54.9 7.1 %collective-permute-start.17 = (f32[2,2,32,256]{3,2,1,0:T(8,128)S(1)}, f32[2,2,32,256]{3,2,1,0:T(8,128)S(1)}, u32[]{:S(2)}, u32[]{:S(2)}) collective-permute-start(f32[2,2,32,256]{3,2,1,0:T(8,128)S(1)} %get-tuple-element.32), channel_id=1, source_target_pairs={{0,0},{1,2},{2,1},{3,3},{4,4},{5,6},{6,5},{7,7},{8,8},{9,10},{10,9... | collective-permute-start | bytes 393224 | tf_op jit(solution)/shard_map/ppermute | solution.py:667
  55.8 7.2 %collective-permute-start.18 = (f32[2,2,32,256]{3,2,1,0:T(8,128)S(1)}, f32[2,2,32,256]{3,2,1,0:T(8,128)S(1)}, u32[]{:S(2)}, u32[]{:S(2)}) collective-permute-start(f32[2,2,32,256]{3,2,1,0:T(8,128)S(1)} %get-tuple-element.33), channel_id=1, source_target_pairs={{0,1},{1,3},{2,0},{3,2},{4,5},{5,7},{6,4},{7,6},{8,9},{9,11},{10,8... | collective-permute-start | bytes 393224 | tf_op jit(solution)/shard_map/ppermute | solution.py:667
  61.9 4.5 %collective-permute-start.19 = (f32[5,2,16,128]{3,2,1,0:T(8,128)S(1)}, f32[5,2,16,128]{3,2,1,0:T(8,128)S(1)}, u32[]{:S(2)}, u32[]{:S(2)}) collective-permute-start(f32[5,2,16,128]{3,2,1,0:T(8,128)S(1)} %get-tuple-element.34), channel_id=1, source_target_pairs={{0,2},{1,3},{2,0},{3,1},{4,6},{5,7},{6,4},{7,5},{8,10},{9,11},{10,... | collective-permute-start | bytes 245768 | tf_op jit(solution)/shard_map/ppermute | solution.py:667

commit v8 on v6

--- a/solution.py
+++ b/solution.py
@@ -106,11 +106,11 @@
     return jnp.sum(jnp.where(i == j, row, 0.0), axis=1, keepdims=True)
 
 
-def rows_kernel(moments_ref, shapes_ref, atom_ref, tile_ref, line_ref, keep_ref, send_ref, rows):
+def rows_kernel(moments_ref, shapes_ref, slots_ref, keep_ref, send_ref, rows):
     core = lax.rem(lax.axis_index("grid"), 2)
     channels, slots, depth = shapes_ref.shape
     atoms = moments_ref.shape[0]
-    atom = as_column(atom_ref[...].astype(jnp.float32))
+    atom = as_column(slots_ref[0:1].astype(jnp.float32))
     picks = [jnp.where(atom == float(a), 1.0, 0.0) for a in range(atoms)]
     chosen = []
     for f in range(4):
@@ -132,11 +132,11 @@
     keep_ref[...] = rows[core]
     send_ref[0:slots] = rows[1 - core]
     send_ref[slots:] = jnp.zeros((8, 2 * depth), jnp.float32)
-    number = (tile_ref[...] * 64 + line_ref[...]).astype(jnp.float32)
+    number = (slots_ref[1:2] * 64 + slots_ref[2:3]).astype(jnp.float32)
     send_ref[slots : slots + 1, 0:slots] = number
 
 
-def pack_kernel(own_ref, got_ref, tile_ref, line_ref, _, *out_refs):
+def pack_kernel(own_ref, got_ref, slots_ref, _, *out_refs):
     slots = own_ref.shape[0]
     apart = len(out_refs) > 1
     height = out_refs[0].shape[-2]
@@ -144,7 +144,7 @@
     capacity = ranks // 4
     chips = lax.axis_size("grid") // 2
     chip = lax.div(lax.axis_index("grid"), 2)
-    number = (tile_ref[...] * 64 + line_ref[...]).astype(jnp.float32)
+    number = (slots_ref[1:2] * 64 + slots_ref[2:3]).astype(jnp.float32)
     number = jnp.concatenate([number, got_ref[slots : slots + 1, 0:slots]], axis=1).astype(jnp.int32)
     tile, line = number // 64, number % 128 + 1
     column = as_column(tile.astype(jnp.float32)).astype(jnp.int32)
@@ -183,7 +183,7 @@
 
 def density_kernel(*refs):
     pd_ref, other_ref = refs[:2]
-    f_ref, straight_ref, across_ref, b1, half = refs[-5:]
+    f_ref, inner_ref, outer_ref, b1, half = refs[-5:]
     pieces = refs[2:-5]
     position = lax.axis_index("grid")
     core, side = lax.rem(position, 2), lax.rem(lax.div(position, 2), 2)
@@ -231,35 +231,30 @@
     def once(x, part):
         return b1[x + 2, part] if -2 <= x < planes + 2 else None
 
-    def outer(base, first_plane, one):
-        for x in range(one, one + 4):
-            for part in range(2):
-                b1[x + 2, part] = smooth_fine(density, x, part)
-        for i in range(2):
-            for part in range(2):
-                x = base + 2 * i
-                total = smooth_fine(once, x, part) + smooth_fine(once, x + 1, part)
-                for h in range(2):
-                    half[(2 * i + part) * 2 + h] = total[:, h * 128 : (h + 1) * 128]
-        for r, value in enumerate(lowered(half, 4, lines, depth)):
-            straight_ref[8 + r // 2, r % 2 * 16 : r % 2 * 16 + 16] = value
-        for x in range(2):
-            for part in range(2):
-                for h in range(2):
-                    straight_ref[(2 * x + part) * 2 + h] = f_ref[
-                        first_plane + x, part, :, h * 128 : (h + 1) * 128
-                    ]
-        other = planes - 2 - first_plane
-        for x in range(2):
-            across_ref[x] = f_ref[other + x]
+    for x in range(-2, planes + 2):
+        for part in range(2):
+            b1[x + 2, part] = smooth_fine(density, x, part)
+    rows = (planes + 8) // 2 * 2
+    for i in range(rows // 2):
+        for part in range(2):
+            total = smooth_fine(once, 2 * i - 4, part) + smooth_fine(once, 2 * i - 3, part)
+            for h in range(2):
+                half[(2 * i + part) * 2 + h] = total[:, h * 128 : (h + 1) * 128]
+    coarse = lowered(half, rows, lines, depth)
 
     @pl.when(side == 0)
     def _():
-        outer(-4, 0, -2)
+        for r in range(8):
+            inner_ref[r // 2, r % 2] = coarse[4 + r]
+        for r in range(4):
+            outer_ref[r // 2, r % 2] = coarse[r]
 
     @pl.when(side == 1)
     def _():
-        outer(planes, planes - 2, planes - 2)
+        for r in range(8):
+            inner_ref[r // 2, r % 2] = coarse[r]
+        for r in range(4):
+            outer_ref[r // 2, r % 2] = coarse[8 + r]
 
 
 def lowered(half, rows, lines, depth):
@@ -278,61 +273,33 @@
     return [total[r * lines // 2 : (r + 1) * lines // 2] for r in range(rows)]
 
 
-def source_kernel(even_ref, odd_ref, straight_ref, f_ref, cs_ref, s_ref, ext, b1, half):
+def source_kernel(own_ref, partner_ref, straight_ref, across_ref, cs_ref, _, s_ref, __):
     position = lax.axis_index("grid")
     blocks = lax.axis_size("grid") // 4
     core, side, block = lax.rem(position, 2), lax.rem(lax.div(position, 2), 2), lax.div(position, 4)
     cosine, sine = cs_ref[core], cs_ref[2 + core]
-    planes = f_ref.shape[0]
-    lines, depth = f_ref.shape[2:]
     first, last = block == 0, block == blocks - 1
     low = (jnp.where(first, cosine, 1.0), jnp.where(first, -sine, 0.0))
     high = (jnp.where(last, cosine, 1.0), jnp.where(last, sine, 0.0))
 
+    def total(low_ref, high_ref):
+        for x in range(4):
+            source, (c, s) = (low_ref, low) if x < 2 else (high_ref, high)
+            real, imag = rotated(source[x % 2, 0], source[x % 2, 1], c, s)
+            s_ref[x, 0] = own_ref[x, 0] + partner_ref[x, 0] + real
+            s_ref[x, 1] = own_ref[x, 1] + partner_ref[x, 1] + imag
+
     @pl.when(side == 0)
     def _():
-        place_planes(ext, 0, odd_ref, *low)
-        ext[planes : 2 * planes] = f_ref[...]
-        ext[2 * planes : 3 * planes] = even_ref[...]
-        ext[3 * planes :] = jnp.zeros((planes, 2, lines, depth), jnp.float32)
+        total(across_ref, straight_ref)
 
     @pl.when(side == 1)
     def _():
-        ext[:planes] = jnp.zeros((planes, 2, lines, depth), jnp.float32)
-        ext[planes : 2 * planes] = even_ref[...]
-        ext[2 * planes : 3 * planes] = f_ref[...]
-        place_planes(ext, 3 * planes, odd_ref, *high)
-
-    for x in range(2 * planes + 4):
-        for part in range(2):
-            b1[x, part] = smooth_fine(lambda i, p: ext[i, p], x + planes - 2, part)
-    for i in range(planes):
-        for part in range(2):
-            total = smooth_fine(lambda i, p: b1[i, p], 2 * i + 2, part) + smooth_fine(
-                lambda i, p: b1[i, p], 2 * i + 3, part
-            )
-            for h in range(2):
-                half[(2 * i + part) * 2 + h] = total[:, h * 128 : (h + 1) * 128]
-    for r, value in enumerate(lowered(half, 2 * planes, lines, depth)):
-        s_ref[r // 2, r % 2] = value
-
-    def add(base, c, t):
-        for x in range(2):
-            real, imag = rotated(straight_ref[8 + x, 0:16], straight_ref[8 + x, 16:32], c, t)
-            s_ref[base + x, 0] += real
-            s_ref[base + x, 1] += imag
-
-    @pl.when(side == 0)
-    def _():
-        add(2, *high)
-
-    @pl.when(side == 1)
-    def _():
-        add(0, *low)
+        total(straight_ref, across_ref)
 
 
 def fine_kernel(
-    even_ref, odd_ref, straight_ref, across_ref, f_ref, cs_ref, own_ref, send_ref, ext, b1, b2, g
+    even_ref, odd_ref, after_ref, before_ref, f_ref, cs_ref, _, own_ref, send_ref, ext, b1, b2, g
 ):
     position = lax.axis_index("grid")
     chips = lax.axis_size("grid") // 2
@@ -342,27 +309,16 @@
     place_halo(ext, planes + 2, even_ref, odd_ref, cs_ref)
     ext[planes + 2 : 2 * planes + 2] = f_ref[...]
     first, last = chip < 2, chip >= chips - 2
-    low = (jnp.where(first, cosine, 1.0), jnp.where(first, -sine, 0.0))
-    high = (jnp.where(last, cosine, 1.0), jnp.where(last, sine, 0.0))
-
-    def place_straight(base, c, t):
-        for x in range(2):
-            real, imag = [
-                jnp.concatenate([straight_ref[4 * x + 2 * p], straight_ref[4 * x + 2 * p + 1]], axis=1)
-                for p in range(2)
-            ]
-            ext[base + x, 0], ext[base + x, 1] = rotated(real, imag, c, t)
-
-    @pl.when(lax.rem(chip, 2) == 0)
-    def _():
-        place_planes(ext, 0, across_ref, *low)
-        place_straight(3 * planes + 2, *high)
-
-    @pl.when(lax.rem(chip, 2) == 1)
-    def _():
-        place_straight(0, *low)
-        place_planes(ext, 3 * planes + 2, across_ref, *high)
-
+    place_planes(
+        ext, 0, before_ref, jnp.where(first, cosine, 1.0), jnp.where(first, -sine, 0.0)
+    )
+    place_planes(
+        ext,
+        3 * planes + 2,
+        after_ref,
+        jnp.where(last, cosine, 1.0),
+        jnp.where(last, sine, 0.0),
+    )
     for x in range(planes + 8):
         for part in range(2):
             b1[x, part] = smooth_fine(lambda i, p: ext[i, p], x + 2, part)
@@ -379,6 +335,10 @@
         send_ref[x] = g[(1 - core) * half + x]
 
 
+def gate_kernel(*_):
+    pass
+
+
 def shift_z(v, step):
     width = v.shape[-1] // 2
     lane = lax.broadcasted_iota(jnp.int32, v.shape, len(v.shape) - 1)
@@ -608,13 +568,19 @@
 smem = [pl.BlockSpec(memory_space=pltpu.SMEM)]
 
 
-def call(kernel, out_shape, in_specs, scratch, flops):
+def call(kernel, out_shape, in_specs, scratch, flops, aliases={}):
     single = not isinstance(out_shape, (list, tuple))
     return pl.pallas_call(
         kernel,
         out_shape=out_shape,
         in_specs=in_specs,
-        out_specs=vmem(1)[0] if single else vmem(len(out_shape)),
+        out_specs=vmem(1)[0]
+        if single
+        else [
+            pl.BlockSpec(memory_space=pl.ANY if i in aliases.values() else pltpu.VMEM)
+            for i in range(len(out_shape))
+        ],
+        input_output_aliases=aliases,
         scratch_shapes=[pltpu.VMEM(shape, jnp.float32) for shape in scratch],
         compiler_params=pltpu.CompilerParams(vmem_limit_bytes=48 * 2**20),
         cost_estimate=pl.CostEstimate(flops=flops, bytes_accessed=2**20, transcendentals=0),
@@ -659,25 +625,25 @@
     cs = pair_phases(pair_table, k_fraction)
 
     other = permute(lax.dynamic_index_in_dim(pair_density, 1 - core, 0, False), partner)
-    tile_row, line_row = slot_tile.reshape(1, -1), slot_row.reshape(1, -1)
+    slots = jnp.stack([slot_atom, slot_tile[:, 0], slot_row])
     row = 2 * depth
     kept, sent = call(
         rows_kernel,
         [shaped(slot_count, row), shaped(slot_count + 8, row)],
-        vmem(5),
+        vmem(3),
         [(2, slot_count, row)],
         10**7,
-    )(moments, shapes.transpose(1, 0, 2), slot_atom.reshape(1, -1), tile_row, line_row)
+    )(moments, shapes.transpose(1, 0, 2), slots)
     got = permute(sent, partner)
     apart = chips <= 8
     height = 16 * capacity + 8
     packed = call(
         pack_kernel,
         [shaped(height, 128)] * chips if apart else [shaped(chips, height, 128)],
-        vmem(4) + [pl.BlockSpec(memory_space=pl.ANY)],
+        vmem(3) + [pl.BlockSpec(memory_space=pl.ANY)],
         [],
         10**8,
-    )(kept, got, tile_row, line_row, other)
+    )(kept, got, slots, other)
     if apart:
         received = [
             permute(packed[k], lambda i, k=k: i ^ (2 * k)) if k else packed[k]
@@ -693,34 +659,41 @@
 
     full = (2, lines, depth)
     small = (2, lines // 2, depth // 2)
-    f, straight, across = call(
+    f, inner, outer = call(
         density_kernel,
-        [shaped(planes, *full), shaped(10, lines, 128), shaped(2, *full)],
+        [shaped(planes, *full), shaped(4, *small), shaped(2, *small)],
         vmem(2 + len(received)),
-        [(planes + 4, *full), (8, lines, 128)],
+        [(planes + 4, *full), (2 * (planes + 8), lines, 128)],
         10**8,
     )(pair_density, other, *received)
+    source, f = call(
+        source_kernel,
+        [shaped(4, *small), shaped(planes, *full)],
+        vmem(4) + smem + [pl.BlockSpec(memory_space=pl.ANY)],
+        [],
+        10**6,
+        {5: 1},
+    )(
+        inner,
+        permute(inner, even_side),
+        permute(outer, next_block),
+        permute(outer, odd_side),
+        cs,
+        f,
+    )
+    pieces = gather_blocks(source, blocks, block, permute_block)
     even = permute(f, even_side)
     odd = permute(f, odd_side)
-    straight = permute(straight, next_block)
-    across = permute(across, lambda i: (i + (-4 if i // 2 % 2 else 4)) % tile_count)
-    source = call(
-        source_kernel,
-        shaped(planes, *small),
-        vmem(4) + smem,
-        [(4 * planes, *full), (2 * planes + 4, *full), (4 * planes, lines, 128)],
-        10**7,
-    )(even, odd, straight, f, cs)
-    pieces = gather_blocks(source, blocks, block, permute_block)
-    own, send = call(
-        fine_kernel,
+    low, high = call(
+        gate_kernel,
         [shaped(thick, *full)] * 2,
-        vmem(5) + smem,
-        [(3 * planes + 4, *full), (planes + 8, *full), (planes + 4, *full), (planes, *full)],
-        10**7,
-    )(even, odd, straight, across, f, cs)
-    got = permute(send, partner)
-
+        [pl.BlockSpec(memory_space=pl.ANY)] * (len(pieces) + 1),
+        [],
+        10**4,
+        {0: 0, 1: 1},
+    )(f[:thick], f[thick:], *pieces[1:])
+    after = permute(low, lambda i: (i - 4) % tile_count)
+    before = permute(high, lambda i: (i + 4) % tile_count)
     n1, n2, n3 = tile_count, tile_count // 2, tile_count // 4
     tile = (8, 128)
     w_own, w_send = call(
@@ -742,6 +715,15 @@
         ],
         10**8,
     )(*pieces, cs)
+    own, send = call(
+        fine_kernel,
+        [shaped(thick, *full)] * 2,
+        vmem(5) + smem + [pl.BlockSpec(memory_space=pl.ANY)],
+        [(3 * planes + 4, *full), (planes + 8, *full), (planes + 4, *full), (planes, *full)],
+        10**7,
+    )(even, odd, after, before, f, cs, w_own)
+    got = permute(send, partner)
+
     w_got = permute(w_send, partner)
     scratch = [(20, lines, 128), (6, *full)]
     result = call(own_kernel, shaped(2, thick, lines, depth), vmem(2), scratch, 10**7)(w_own, own)

time: 61 us -> 65.7 us (1.077)
  starting transfers between devices: 23.4 us -> 31.8 us
  local copies, waits for them, and re-layouts: 4.19 us -> 2.2 us
  Pallas kernels: 14.2 us -> 12.8 us
  waiting for transfers between devices: 18.4 us -> 17.4 us
  other arithmetic: 0.45 us -> 1.17 us
    ppermute x18 -> x21, starting transfers between devices: 23.4 us -> 31.8 us  [permute(): return lax.ppermute(value, 'grid', [(i, target(i)) for i in devices])]
    unnamed x20 -> x10, local copies, waits for them, and re-layouts: 4.18 us -> 2.18 us
    pallas_call x3 -> x4, Pallas kernels: 6.47 us -> 5.11 us  [the longest x1 2.52 us: per_device(): call(fine_kernel, [shaped(thick, *full)] * 2, vmem(5) + smem + [pl.BlockS...]
    ppermute x18 -> x21, waiting for transfers between devices: 18.4 us -> 17.4 us  [permute(): return lax.ppermute(value, 'grid', [(i, target(i)) for i in devices])]
    another operation x0 -> x1, other arithmetic: none -> 0.72 us  [per_device(): slots = jnp.stack([slot_atom, slot_tile[:, 0], slot_row])]
  transfers between devices with their start and end apart: 18 -> 21, of which waited for: 10 -> 10; matrix products, arithmetic and copies ran while one was open for 1% -> 1% of each run, Pallas kernels for 15% -> 6%
where the time goes in v8:
time: 65.7 us; the launch traced here: 65.5 us
  starting transfers between devices  31.8 us (48%)
  waiting for transfers between devices  17.4 us (26%)
  Pallas kernels  12.8 us (19%)
  local copies, waits for them, and re-layouts  2.2 us (3%)
  other arithmetic  1.17 us (2%)
    ppermute x21, starting transfers between devices, permute(): return lax.ppermute(value, 'grid', [(i, target(i)) for i in devices])  31.8 us
    ppermute x21, waiting for transfers between devices, permute(): return lax.ppermute(value, 'grid', [(i, target(i)) for i in devices])  17.4 us
    pallas_call x1, Pallas kernels, per_device(): call(cycle_kernel, [shaped(5, *small)] * 2, vmem(len(pieces)) + smem, [(n...  2.93 us
    pallas_call x1, Pallas kernels, per_device(): call(fine_kernel, [shaped(thick, *full)] * 2, vmem(5) + smem + [pl.BlockS...  2.52 us
    unnamed x10, local copies, waits for them, and re-layouts  2.18 us
    pallas_call x1, Pallas kernels, per_device(): call(density_kernel, [shaped(planes, *full), shaped(4, *small), shaped(2,...  2.02 us
    pallas_call x1, Pallas kernels, per_device(): call(output_kernel, shaped(*pair_density.shape), vmem(3), scratch, 10 ** 7)  1.61 us
    pallas_call x1, Pallas kernels, per_device(): call(rows_kernel, [shaped(slot_count, row), shaped(slot_count + 8, row)],...  1.49 us
  transfers between devices with their start and end apart: 21, of which 10 were waited for; matrix products, arithmetic and copies ran while one was open for 1% of the time, Pallas kernels for 6%

profile of v8, /device:TPU:0, one launch (start us, length us, event | category | flops | bytes accessed | tf_op | source)
XLA Modules:
  0.0 65.5 jit_solution(30598875312916743)
XLA Ops:
  0.0 0.7 %pad_add_fusion.slots_ref = s32[3,64]{1,0:T(4,128)S(1)} fusion(s32[1,64]{1,0:T(1,128)} %bitcast.7, s32[1,64]{1,0:T(1,128)} %bitcast.8, s32[1,64]{1,0:T(1,128)} %bitcast.9), kind=kLoop, calls=%fused_computation.3 | loop fusion | flops 384 | bytes 1536 | tf_op jit(solution)/shard_map/stack | solution.py:628
  0.7 1.4 %copy-done = f32[64,25,256]{2,0,1:T(8,128)S(1)} copy-done((f32[64,25,256]{2,0,1:T(8,128)S(1)}, f32[64,25,256]{2,0,1:T(8,128)}, u32[]{:S(2)}) %copy-start) | copy-done | bytes 1638424
  2.2 0.7 %copy-done.2 = f32[12,2,2,25]{3,2,1,0:T(2,128)S(1)} copy-done((f32[12,2,2,25]{3,2,1,0:T(2,128)S(1)}, f32[12,2,2,25]{3,2,1,0:T(2,128)}, u32[]{:S(2)}) %copy-start.2) | copy-done | bytes 4824
  2.9 1.5 %shard_map.82 = (f32[64,512]{1,0:T(8,128)S(1)}, f32[72,512]{1,0:T(8,128)S(1)}) custom-call(f32[12,2,2,25]{3,2,1,0:T(2,128)S(1)} %copy-done.2, f32[25,64,256]{2,1,0:T(8,128)S(1)} %bitcast.6, s32[3,64]{1,0:T(4,128)S(1)} %pad_add_fusion.slots_ref), custom_call_target="tpu_custom_call" | custom-call | flops 10000000 | bytes 1048576 | tf_op jit(solution)/shard_map/pallas_call | solution.py:630
  4.4 0.5 collective-permute-start.1
  4.9 0.1 collective-permute-start
  5.1 1.3 %collective-permute-done._.refs_1_ = f32[2,2,32,256]{3,2,1,0:T(8,128)S(1)} collective-permute-done((f32[2,2,32,256]{3,2,1,0:T(8,128)S(1)}, f32[2,2,32,256]{3,2,1,0:T(8,128)S(1)}, u32[]{:S(2)}, u32[]{:S(2)}) %collective-permute-start) | collective-permute-done | bytes 131104 | tf_op jit(solution)/shard_map/ppermute | solution.py:608
  6.3 0.0 collective-permute-done.1.got_ref
  6.4 0.8 %shard_map.83 = (f32[136,128]{1,0:T(8,128)S(1)}, f32[136,128]{1,0:T(8,128)S(1)}, f32[136,128]{1,0:T(8,128)S(1)}, f32[136,128]{1,0:T(8,128)S(1)}, f32[136,128]{1,...) custom-call(f32[64,512]{1,0:T(8,128)S(1)} %get-tuple-element.26.own_ref, ...), custom_call_target="tpu_custom_call" | custom-call | flops 100000000 | bytes 1048576 | tf_op jit(solution)/shard_map/pallas_call | solution.py:640
  7.1 2.7 %collective-permute-start.2 = (f32[136,128]{1,0:T(8,128)S(1)}, f32[136,128]{1,0:T(8,128)S(1)}, u32[]{:S(2)}, u32[]{:S(2)}) collective-permute-start(f32[136,128]{1,0:T(8,128)S(1)} %get-tuple-element.29), channel_id=1, source_target_pairs={{0,2},{1,3},{2,0},{3,1},{4,6},{5,7},{6,4},{7,5},{8,10},{9,11},{10,... | collective-permute-start | bytes 208904 | tf_op jit(solution)/shard_map/ppermute | solution.py:608
  9.8 3.6 %collective-permute-start.3 = (f32[136,128]{1,0:T(8,128)S(1)}, f32[136,128]{1,0:T(8,128)S(1)}, u32[]{:S(2)}, u32[]{:S(2)}) collective-permute-start(f32[136,128]{1,0:T(8,128)S(1)} %get-tuple-element.30), channel_id=1, source_target_pairs={{0,12},{1,13},{2,14},{3,15},{4,8},{5,9},{6,10},{7,11},{8,4},{9,5},... | collective-permute-start | bytes 208904 | tf_op jit(solution)/shard_map/ppermute | solution.py:608
  13.5 0.2 fusion
  13.6 0.0 collective-permute-start.4
  13.6 1.0 %collective-permute-start.5 = (f32[136,128]{1,0:T(8,128)S(1)}, f32[136,128]{1,0:T(8,128)S(1)}, u32[]{:S(2)}, u32[]{:S(2)}) collective-permute-start(f32[136,128]{1,0:T(8,128)S(1)} %get-tuple-element.32), channel_id=1, source_target_pairs={{0,8},{1,9},{2,10},{3,11},{4,12},{5,13},{6,14},{7,15},{8,0},{9,1},... | collective-permute-start | bytes 208904 | tf_op jit(solution)/shard_map/ppermute | solution.py:608
  14.6 3.1 %collective-permute-start.6 = (f32[136,128]{1,0:T(8,128)S(1)}, f32[136,128]{1,0:T(8,128)S(1)}, u32[]{:S(2)}, u32[]{:S(2)}) collective-permute-start(f32[136,128]{1,0:T(8,128)S(1)} %get-tuple-element.33), channel_id=1, source_target_pairs={{0,10},{1,11},{2,8},{3,9},{4,14},{5,15},{6,12},{7,13},{8,2},{9,3},... | collective-permute-start | bytes 208904 | tf_op jit(solution)/shard_map/ppermute | solution.py:608
  17.6 1.3 %collective-permute-start.7 = (f32[136,128]{1,0:T(8,128)S(1)}, f32[136,128]{1,0:T(8,128)S(1)}, u32[]{:S(2)}, u32[]{:S(2)}) collective-permute-start(f32[136,128]{1,0:T(8,128)S(1)} %get-tuple-element.34), channel_id=1, source_target_pairs={{0,4},{1,5},{2,6},{3,7},{4,0},{5,1},{6,2},{7,3},{8,12},{9,13},{10,... | collective-permute-start | bytes 208904 | tf_op jit(solution)/shard_map/ppermute | solution.py:608
  18.9 0.6 collective-permute-start.8
  19.5 0.2 cosine_reduce_fusion
  19.8 1.3 %collective-permute-done.4.refs_5_ = f32[136,128]{1,0:T(8,128)S(1)} collective-permute-done((f32[136,128]{1,0:T(8,128)S(1)}, f32[136,128]{1,0:T(8,128)S(1)}, u32[]{:S(2)}, u32[]{:S(2)}) %collective-permute-start.4) | collective-permute-done | bytes 69664 | tf_op jit(solution)/shard_map/ppermute | solution.py:608
  21.0 3.7 %collective-permute-done.5.refs_6_ = f32[136,128]{1,0:T(8,128)S(1)} collective-permute-done((f32[136,128]{1,0:T(8,128)S(1)}, f32[136,128]{1,0:T(8,128)S(1)}, u32[]{:S(2)}, u32[]{:S(2)}) %collective-permute-start.5) | collective-permute-done | bytes 69664 | tf_op jit(solution)/shard_map/ppermute | solution.py:608
  24.8 0.8 %collective-permute-done.6.refs_7_ = f32[136,128]{1,0:T(8,128)S(1)} collective-permute-done((f32[136,128]{1,0:T(8,128)S(1)}, f32[136,128]{1,0:T(8,128)S(1)}, u32[]{:S(2)}, u32[]{:S(2)}) %collective-permute-start.6) | collective-permute-done | bytes 69664 | tf_op jit(solution)/shard_map/ppermute | solution.py:608
  25.5 0.3 collective-permute-done.8.refs_9_
  25.8 2.0 %shard_map.84 = (f32[4,2,32,256]{3,2,1,0:T(8,128)S(1)}, f32[4,2,16,128]{3,2,1,0:T(8,128)S(1)}, f32[2,2,16,128]{3,2,1,0:T(8,128)S(1)}) custom-call(f32[2,2,2,32,256]{4,3,2,1,0:T(8,128)S(1)} %copy-done.1, f32[2,2,32,256]{3,2,1,0:T(8,128)S(1)} %collective-permute-done._.refs_1_, f32[136,128]{1,0:T(8,128)S(1)} %get-tuple-element.28.refs_2_, ...), custom_call_target="tpu_custom_call" | custom-call | flops 100000000 | bytes 1048576 | tf_op jit(solution)/shard_map/pallas_call | solution.py:662
  27.8 4.1 %collective-permute-start.11 = (f32[2,2,16,128]{3,2,1,0:T(8,128)S(1)}, f32[2,2,16,128]{3,2,1,0:T(8,128)S(1)}, u32[]{:S(2)}, u32[]{:S(2)}) collective-permute-start(f32[2,2,16,128]{3,2,1,0:T(8,128)S(1)} %get-tuple-element.37), channel_id=1, source_target_pairs={{0,14},{1,15},{2,4},{3,5},{4,2},{5,3},{6,8},{7,9},{8,6},{9,7},{10,... | collective-permute-start | bytes 98312 | tf_op jit(solution)/shard_map/ppermute | solution.py:608
  31.9 0.0 collective-permute-start.10
  31.9 0.4 collective-permute-start.9
  32.3 0.1 pad_maximum_fusion.cs_ref.refs_4_
  32.3 2.2 %collective-permute-done.11.across_ref = f32[2,2,16,128]{3,2,1,0:T(8,128)S(1)} collective-permute-done((f32[2,2,16,128]{3,2,1,0:T(8,128)S(1)}, f32[2,2,16,128]{3,2,1,0:T(8,128)S(1)}, u32[]{:S(2)}, u32[]{:S(2)}) %collective-permute-start.11) | collective-permute-done | bytes 32800 | tf_op jit(solution)/shard_map/ppermute | solution.py:608
  34.5 1.3 %collective-permute-done.10.straight_ref = f32[2,2,16,128]{3,2,1,0:T(8,128)S(1)} collective-permute-done((f32[2,2,16,128]{3,2,1,0:T(8,128)S(1)}, f32[2,2,16,128]{3,2,1,0:T(8,128)S(1)}, u32[]{:S(2)}, u32[]{:S(2)}) %collective-permute-start.10) | collective-permute-done | bytes 32800 | tf_op jit(solution)/shard_map/ppermute | solution.py:608
  35.8 0.4 collective-permute-done.9.partner_ref
  36.2 0.6 shard_map.85
  36.8 1.9 %collective-permute-start.14 = (f32[4,2,16,128]{3,2,1,0:T(8,128)S(1)}, f32[4,2,16,128]{3,2,1,0:T(8,128)S(1)}, u32[]{:S(2)}, u32[]{:S(2)}) collective-permute-start(f32[4,2,16,128]{3,2,1,0:T(8,128)S(1)} %get-tuple-element.39.refs_0_), channel_id=1, source_target_pairs={{0,12},{1,13},{2,14},{3,15},{4,8},{5,9},{6,10},{7,11},{8,4},{9,5},... | collective-permute-start | bytes 196616 | tf_op jit(solution)/shard_map/ppermute | solution.py:608
  38.6 1.7 %collective-permute-start.13 = (f32[4,2,16,128]{3,2,1,0:T(8,128)S(1)}, f32[4,2,16,128]{3,2,1,0:T(8,128)S(1)}, u32[]{:S(2)}, u32[]{:S(2)}) collective-permute-start(f32[4,2,16,128]{3,2,1,0:T(8,128)S(1)} %get-tuple-element.39.refs_0_), channel_id=1, source_target_pairs={{0,8},{1,9},{2,10},{3,11},{4,12},{5,13},{6,14},{7,15},{8,0},{9,1},... | collective-permute-start | bytes 196616 | tf_op jit(solution)/shard_map/ppermute | solution.py:608
  40.3 0.9 %collective-permute-start.12 = (f32[4,2,16,128]{3,2,1,0:T(8,128)S(1)}, f32[4,2,16,128]{3,2,1,0:T(8,128)S(1)}, u32[]{:S(2)}, u32[]{:S(2)}) collective-permute-start(f32[4,2,16,128]{3,2,1,0:T(8,128)S(1)} %get-tuple-element.39.refs_0_), channel_id=1, source_target_pairs={{0,4},{1,5},{2,6},{3,7},{4,0},{5,1},{6,2},{7,3},{8,12},{9,13},{10,... | collective-permute-start | bytes 196616 | tf_op jit(solution)/shard_map/ppermute | solution.py:608
  41.2 2.3 %collective-permute-start.16 = (f32[4,2,32,256]{3,2,1,0:T(8,128)S(1)}, f32[4,2,32,256]{3,2,1,0:T(8,128)S(1)}, u32[]{:S(2)}, u32[]{:S(2)}) collective-permute-start(f32[4,2,32,256]{3,2,1,0:T(8,128)S(1)} %get-tuple-element.41.f_ref), channel_id=1, source_target_pairs={{0,14},{1,15},{2,4},{3,5},{4,2},{5,3},{6,8},{7,9},{8,6},{9,7},{10,... | collective-permute-start | bytes 786440 | tf_op jit(solution)/shard_map/ppermute | solution.py:608
  43.6 0.2 collective-permute-start.15
  43.8 0.0 collective-permute-done.14.refs_3_.__4_
  43.8 2.3 %collective-permute-done.13.refs_2_.__3_ = f32[4,2,16,128]{3,2,1,0:T(8,128)S(1)} collective-permute-done((f32[4,2,16,128]{3,2,1,0:T(8,128)S(1)}, f32[4,2,16,128]{3,2,1,0:T(8,128)S(1)}, u32[]{:S(2)}, u32[]{:S(2)}) %collective-permute-start.13) | collective-permute-done | bytes 65568 | tf_op jit(solution)/shard_map/ppermute | solution.py:608
  46.1 6.9 %collective-permute-start.17 = (f32[2,2,32,256]{3,2,1,0:T(8,128)S(1)}, f32[2,2,32,256]{3,2,1,0:T(8,128)S(1)}, u32[]{:S(2)}, u32[]{:S(2)}) collective-permute-start(f32[2,2,32,256]{3,2,1,0:T(8,128)S(1)} %get-tuple-element.42), channel_id=1, source_target_pairs={{0,12},{1,13},{2,14},{3,15},{4,0},{5,1},{6,2},{7,3},{8,4},{9,5},{1... | collective-permute-start | bytes 393224 | tf_op jit(solution)/shard_map/ppermute | solution.py:608
  53.0 0.0 collective-permute-start.18
  53.0 2.9 %shard_map.86 = (f32[5,2,16,128]{3,2,1,0:T(8,128)S(1)}, f32[5,2,16,128]{3,2,1,0:T(8,128)S(1)}) custom-call(f32[4,2,16,128]{3,2,1,0:T(8,128)S(1)} %get-tuple-element.39.refs_0_, f32[4,2,16,128]{3,2,1,0:T(8,128)S(1)} %collective-permute-done.12.refs_1_.__2_, f32[4,2,16,128]{3,2,1,0:T(8,128)S(1)} %collective-permute-done.13.refs_2_.__3_, ...), custom_call_target="tpu_custom_call" | custom-call | flops 100000000 | bytes 1048576 | tf_op jit(solution)/shard_map/pallas_call | solution.py:699
  56.0 3.8 %collective-permute-done.18.before_ref = f32[2,2,32,256]{3,2,1,0:T(8,128)S(1)} collective-permute-done((f32[2,2,32,256]{3,2,1,0:T(8,128)S(1)}, f32[2,2,32,256]{3,2,1,0:T(8,128)S(1)}, u32[]{:S(2)}, u32[]{:S(2)}) %collective-permute-start.18) | collective-permute-done | bytes 131104 | tf_op jit(solution)/shard_map/ppermute | solution.py:608
  59.8 2.5 %shard_map.88 = (f32[2,2,32,256]{3,2,1,0:T(8,128)S(1)}, f32[2,2,32,256]{3,2,1,0:T(8,128)S(1)}) custom-call(f32[4,2,32,256]{3,2,1,0:T(8,128)S(1)} %collective-permute-done.15.even_ref, f32[4,2,32,256]{3,2,1,0:T(8,128)S(1)} %collective-permute-done.16.odd_ref, f32[2,2,32,256]{3,2,1,0:T(8,128)S(1)} %collective-permute-done.17.after_ref, ...), custom_call_target="tpu_custom_call" | custom-call | flops 10000000 | bytes 1048576 | tf_op jit(solution)/shard_map/pallas_call | solution.py:718
  62.3 0.1 collective-permute-start.20
  62.4 0.5 collective-permute-start.19
  62.9 0.9 %shard_map.89.own_ref = f32[2,2,32,256]{3,2,1,0:T(8,128)S(1)} custom-call(f32[5,2,16,128]{3,2,1,0:T(8,128)S(1)} %get-tuple-element.40._.w_ref, f32[2,2,32,256]{3,2,1,0:T(8,128)S(1)} %get-tuple-element.44.g_ref), custom_call_target="tpu_custom_call" | custom-call | flops 10000000 | bytes 1048576 | tf_op jit(solution)/shard_map/pallas_call | solution.py:729
  63.8 0.0 collective-permute-done.19.w_ref
  63.9 1.6 %shard_map.90 = f32[2,2,2,32,256]{4,3,2,1,0:T(8,128)} custom-call(f32[2,2,32,256]{3,2,1,0:T(8,128)S(1)} %shard_map.89.own_ref, f32[5,2,16,128]{3,2,1,0:T(8,128)S(1)} %collective-permute-done.19.w_ref, f32[2,2,32,256]{3,2,1,0:T(8,128)S(1)} %collective-permute-done.20.g_ref), custom_call_target="tpu_custom_call" | custom-call | flops 10000000 | bytes 1048576 | tf_op jit(solution)/shard_map/pallas_call | solution.py:730
  (19 shorter events, 0.1 us)
Async XLA Ops:
  0.0 13.4 %copy-start.4 = (f32[8]{0:T(128)S(1)}, f32[8]{0:T(128)}, u32[]{:S(2)}) copy-start(f32[8]{0:T(128)} %param.15) | copy-start | bytes 100
  0.0 13.4 %copy-start.3 = (s32[2,2]{1,0:T(2,128)S(1)}, s32[2,2]{1,0:T(2,128)}, u32[]{:S(2)}) copy-start(s32[2,2]{1,0:T(2,128)} %param.14) | copy-start | bytes 52
  0.7 1.4 %copy-start = (f32[64,25,256]{2,0,1:T(8,128)S(1)}, f32[64,25,256]{2,0,1:T(8,128)}, u32[]{:S(2)}) copy-start(f32[64,25,256]{2,0,1:T(8,128)} %param.10) | copy-start | bytes 4915204
  2.2 0.7 %copy-start.2 = (f32[12,2,2,25]{3,2,1,0:T(2,128)S(1)}, f32[12,2,2,25]{3,2,1,0:T(2,128)}, u32[]{:S(2)}) copy-start(f32[12,2,2,25]{3,2,1,0:T(2,128)} %moments_ref.1) | copy-start | bytes 14404
  2.9 2.0 %copy-start.1 = (f32[2,2,2,32,256]{4,3,2,1,0:T(8,128)S(1)}, f32[2,2,2,32,256]{4,3,2,1,0:T(8,128)}, u32[]{:S(2)}) copy-start(f32[2,2,2,32,256]{4,3,2,1,0:T(8,128)} %refs_0_.1) | copy-start | bytes 786436
  4.4 2.0 %collective-permute-start.1 = (f32[72,512]{1,0:T(8,128)S(1)}, f32[72,512]{1,0:T(8,128)S(1)}, u32[]{:S(2)}, u32[]{:S(2)}) collective-permute-start(f32[72,512]{1,0:T(8,128)S(1)} %get-tuple-element.27), channel_id=1, source_target_pairs={{0,1},{1,0},{2,3},{3,2},{4,5},{5,4},{6,7},{7,6},{8,9},{9,8},{10,11... | collective-permute-start | bytes 442376 | tf_op jit(solution)/shard_map/ppermute | solution.py:608
  4.9 1.4 %collective-permute-start = (f32[2,2,32,256]{3,2,1,0:T(8,128)S(1)}, f32[2,2,32,256]{3,2,1,0:T(8,128)S(1)}, u32[]{:S(2)}, u32[]{:S(2)}) collective-permute-start(f32[2,2,32,256]{3,2,1,0:T(8,128)S(1)} %dynamic-slice_bitcast_fusion), channel_id=1, source_target_pairs={{0,1},{1,0},{2,3},{3,2},{4,5},{5,4},{6,7},{7,6},{8,9},{9,8},{10,11... | collective-permute-start | bytes 393224 | tf_op jit(solution)/shard_map/ppermute | solution.py:608
  7.1 10.5 %collective-permute-start.2 = (f32[136,128]{1,0:T(8,128)S(1)}, f32[136,128]{1,0:T(8,128)S(1)}, u32[]{:S(2)}, u32[]{:S(2)}) collective-permute-start(f32[136,128]{1,0:T(8,128)S(1)} %get-tuple-element.29), channel_id=1, source_target_pairs={{0,2},{1,3},{2,0},{3,1},{4,6},{5,7},{6,4},{7,5},{8,10},{9,11},{10,... | collective-permute-start | bytes 208904 | tf_op jit(solution)/shard_map/ppermute | solution.py:608
  9.8 9.1 %collective-permute-start.3 = (f32[136,128]{1,0:T(8,128)S(1)}, f32[136,128]{1,0:T(8,128)S(1)}, u32[]{:S(2)}, u32[]{:S(2)}) collective-permute-start(f32[136,128]{1,0:T(8,128)S(1)} %get-tuple-element.30), channel_id=1, source_target_pairs={{0,12},{1,13},{2,14},{3,15},{4,8},{5,9},{6,10},{7,11},{8,4},{9,5},... | collective-permute-start | bytes 208904 | tf_op jit(solution)/shard_map/ppermute | solution.py:608
  13.6 7.4 %collective-permute-start.4 = (f32[136,128]{1,0:T(8,128)S(1)}, f32[136,128]{1,0:T(8,128)S(1)}, u32[]{:S(2)}, u32[]{:S(2)}) collective-permute-start(f32[136,128]{1,0:T(8,128)S(1)} %get-tuple-element.31), channel_id=1, source_target_pairs={{0,14},{1,15},{2,12},{3,13},{4,10},{5,11},{6,8},{7,9},{8,6},{9,7},... | collective-permute-start | bytes 208904 | tf_op jit(solution)/shard_map/ppermute | solution.py:608
  13.6 11.2 %collective-permute-start.5 = (f32[136,128]{1,0:T(8,128)S(1)}, f32[136,128]{1,0:T(8,128)S(1)}, u32[]{:S(2)}, u32[]{:S(2)}) collective-permute-start(f32[136,128]{1,0:T(8,128)S(1)} %get-tuple-element.32), channel_id=1, source_target_pairs={{0,8},{1,9},{2,10},{3,11},{4,12},{5,13},{6,14},{7,15},{8,0},{9,1},... | collective-permute-start | bytes 208904 | tf_op jit(solution)/shard_map/ppermute | solution.py:608
  14.6 10.9 %collective-permute-start.6 = (f32[136,128]{1,0:T(8,128)S(1)}, f32[136,128]{1,0:T(8,128)S(1)}, u32[]{:S(2)}, u32[]{:S(2)}) collective-permute-start(f32[136,128]{1,0:T(8,128)S(1)} %get-tuple-element.33), channel_id=1, source_target_pairs={{0,10},{1,11},{2,8},{3,9},{4,14},{5,15},{6,12},{7,13},{8,2},{9,3},... | collective-permute-start | bytes 208904 | tf_op jit(solution)/shard_map/ppermute | solution.py:608
  17.6 7.9 %collective-permute-start.7 = (f32[136,128]{1,0:T(8,128)S(1)}, f32[136,128]{1,0:T(8,128)S(1)}, u32[]{:S(2)}, u32[]{:S(2)}) collective-permute-start(f32[136,128]{1,0:T(8,128)S(1)} %get-tuple-element.34), channel_id=1, source_target_pairs={{0,4},{1,5},{2,6},{3,7},{4,0},{5,1},{6,2},{7,3},{8,12},{9,13},{10,... | collective-permute-start | bytes 208904 | tf_op jit(solution)/shard_map/ppermute | solution.py:608
  18.9 6.9 %collective-permute-start.8 = (f32[136,128]{1,0:T(8,128)S(1)}, f32[136,128]{1,0:T(8,128)S(1)}, u32[]{:S(2)}, u32[]{:S(2)}) collective-permute-start(f32[136,128]{1,0:T(8,128)S(1)} %get-tuple-element.35), channel_id=1, source_target_pairs={{0,6},{1,7},{2,4},{3,5},{4,2},{5,3},{6,0},{7,1},{8,14},{9,15},{10,... | collective-permute-start | bytes 208904 | tf_op jit(solution)/shard_map/ppermute | solution.py:608
  27.8 6.7 %collective-permute-start.11 = (f32[2,2,16,128]{3,2,1,0:T(8,128)S(1)}, f32[2,2,16,128]{3,2,1,0:T(8,128)S(1)}, u32[]{:S(2)}, u32[]{:S(2)}) collective-permute-start(f32[2,2,16,128]{3,2,1,0:T(8,128)S(1)} %get-tuple-element.37), channel_id=1, source_target_pairs={{0,14},{1,15},{2,4},{3,5},{4,2},{5,3},{6,8},{7,9},{8,6},{9,7},{10,... | collective-permute-start | bytes 98312 | tf_op jit(solution)/shard_map/ppermute | solution.py:608
  31.9 3.9 %collective-permute-start.10 = (f32[2,2,16,128]{3,2,1,0:T(8,128)S(1)}, f32[2,2,16,128]{3,2,1,0:T(8,128)S(1)}, u32[]{:S(2)}, u32[]{:S(2)}) collective-permute-start(f32[2,2,16,128]{3,2,1,0:T(8,128)S(1)} %get-tuple-element.37), channel_id=1, source_target_pairs={{0,12},{1,13},{2,6},{3,7},{4,0},{5,1},{6,10},{7,11},{8,4},{9,5},{1... | collective-permute-start | bytes 98312 | tf_op jit(solution)/shard_map/ppermute | solution.py:608
  31.9 4.3 %collective-permute-start.9 = (f32[4,2,16,128]{3,2,1,0:T(8,128)S(1)}, f32[4,2,16,128]{3,2,1,0:T(8,128)S(1)}, u32[]{:S(2)}, u32[]{:S(2)}) collective-permute-start(f32[4,2,16,128]{3,2,1,0:T(8,128)S(1)} %get-tuple-element.36.own_ref), channel_id=1, source_target_pairs={{0,2},{1,3},{2,0},{3,1},{4,6},{5,7},{6,4},{7,5},{8,10},{9,11},{10,... | collective-permute-start | bytes 196616 | tf_op jit(solution)/shard_map/ppermute | solution.py:608
  36.8 7.1 %collective-permute-start.14 = (f32[4,2,16,128]{3,2,1,0:T(8,128)S(1)}, f32[4,2,16,128]{3,2,1,0:T(8,128)S(1)}, u32[]{:S(2)}, u32[]{:S(2)}) collective-permute-start(f32[4,2,16,128]{3,2,1,0:T(8,128)S(1)} %get-tuple-element.39.refs_0_), channel_id=1, source_target_pairs={{0,12},{1,13},{2,14},{3,15},{4,8},{5,9},{6,10},{7,11},{8,4},{9,5},... | collective-permute-start | bytes 196616 | tf_op jit(solution)/shard_map/ppermute | solution.py:608
  38.6 7.5 %collective-permute-start.13 = (f32[4,2,16,128]{3,2,1,0:T(8,128)S(1)}, f32[4,2,16,128]{3,2,1,0:T(8,128)S(1)}, u32[]{:S(2)}, u32[]{:S(2)}) collective-permute-start(f32[4,2,16,128]{3,2,1,0:T(8,128)S(1)} %get-tuple-element.39.refs_0_), channel_id=1, source_target_pairs={{0,8},{1,9},{2,10},{3,11},{4,12},{5,13},{6,14},{7,15},{8,0},{9,1},... | collective-permute-start | bytes 196616 | tf_op jit(solution)/shard_map/ppermute | solution.py:608
  40.3 5.8 %collective-permute-start.12 = (f32[4,2,16,128]{3,2,1,0:T(8,128)S(1)}, f32[4,2,16,128]{3,2,1,0:T(8,128)S(1)}, u32[]{:S(2)}, u32[]{:S(2)}) collective-permute-start(f32[4,2,16,128]{3,2,1,0:T(8,128)S(1)} %get-tuple-element.39.refs_0_), channel_id=1, source_target_pairs={{0,4},{1,5},{2,6},{3,7},{4,0},{5,1},{6,2},{7,3},{8,12},{9,13},{10,... | collective-permute-start | bytes 196616 | tf_op jit(solution)/shard_map/ppermute | solution.py:608
  41.2 18.6 %collective-permute-start.16 = (f32[4,2,32,256]{3,2,1,0:T(8,128)S(1)}, f32[4,2,32,256]{3,2,1,0:T(8,128)S(1)}, u32[]{:S(2)}, u32[]{:S(2)}) collective-permute-start(f32[4,2,32,256]{3,2,1,0:T(8,128)S(1)} %get-tuple-element.41.f_ref), channel_id=1, source_target_pairs={{0,14},{1,15},{2,4},{3,5},{4,2},{5,3},{6,8},{7,9},{8,6},{9,7},{10,... | collective-permute-start | bytes 786440 | tf_op jit(solution)/shard_map/ppermute | solution.py:608
  43.6 16.2 %collective-permute-start.15 = (f32[4,2,32,256]{3,2,1,0:T(8,128)S(1)}, f32[4,2,32,256]{3,2,1,0:T(8,128)S(1)}, u32[]{:S(2)}, u32[]{:S(2)}) collective-permute-start(f32[4,2,32,256]{3,2,1,0:T(8,128)S(1)} %get-tuple-element.41.f_ref), channel_id=1, source_target_pairs={{0,2},{1,3},{2,0},{3,1},{4,6},{5,7},{6,4},{7,5},{8,10},{9,11},{10,... | collective-permute-start | bytes 786440 | tf_op jit(solution)/shard_map/ppermute | solution.py:608
  46.1 9.8 %collective-permute-start.17 = (f32[2,2,32,256]{3,2,1,0:T(8,128)S(1)}, f32[2,2,32,256]{3,2,1,0:T(8,128)S(1)}, u32[]{:S(2)}, u32[]{:S(2)}) collective-permute-start(f32[2,2,32,256]{3,2,1,0:T(8,128)S(1)} %get-tuple-element.42), channel_id=1, source_target_pairs={{0,12},{1,13},{2,14},{3,15},{4,0},{5,1},{6,2},{7,3},{8,4},{9,5},{1... | collective-permute-start | bytes 393224 | tf_op jit(solution)/shard_map/ppermute | solution.py:608
  53.0 6.8 %collective-permute-start.18 = (f32[2,2,32,256]{3,2,1,0:T(8,128)S(1)}, f32[2,2,32,256]{3,2,1,0:T(8,128)S(1)}, u32[]{:S(2)}, u32[]{:S(2)}) collective-permute-start(f32[2,2,32,256]{3,2,1,0:T(8,128)S(1)} %get-tuple-element.43), channel_id=1, source_target_pairs={{0,4},{1,5},{2,6},{3,7},{4,8},{5,9},{6,10},{7,11},{8,12},{9,13},{1... | collective-permute-start | bytes 393224 | tf_op jit(solution)/shard_map/ppermute | solution.py:608
  62.3 1.5 %collective-permute-start.20 = (f32[2,2,32,256]{3,2,1,0:T(8,128)S(1)}, f32[2,2,32,256]{3,2,1,0:T(8,128)S(1)}, u32[]{:S(2)}, u32[]{:S(2)}) collective-permute-start(f32[2,2,32,256]{3,2,1,0:T(8,128)S(1)} %get-tuple-element.46), channel_id=1, source_target_pairs={{0,1},{1,0},{2,3},{3,2},{4,5},{5,4},{6,7},{7,6},{8,9},{9,8},{10,11... | collective-permute-start | bytes 393224 | tf_op jit(solution)/shard_map/ppermute | solution.py:608
  62.4 1.5 %collective-permute-start.19 = (f32[5,2,16,128]{3,2,1,0:T(8,128)S(1)}, f32[5,2,16,128]{3,2,1,0:T(8,128)S(1)}, u32[]{:S(2)}, u32[]{:S(2)}) collective-permute-start(f32[5,2,16,128]{3,2,1,0:T(8,128)S(1)} %get-tuple-element.45), channel_id=1, source_target_pairs={{0,1},{1,0},{2,3},{3,2},{4,5},{5,4},{6,7},{7,6},{8,9},{9,8},{10,11... | collective-permute-start | bytes 245768 | tf_op jit(solution)/shard_map/ppermute | solution.py:608

commit v9 on v8

--- a/solution.py
+++ b/solution.py
@@ -70,33 +70,15 @@
     return cosine * real - sine * imag, sine * real + cosine * imag
 
 
-def place_planes(target, base, source, cosine, sine):
-    for x in range(source.shape[0]):
-        real, imag = rotated(source[x, 0], source[x, 1], cosine, sine)
+def place_planes(target, base, count, at, cosine, sine):
+    for x in range(count):
+        real, imag = rotated(at(x, 0), at(x, 1), cosine, sine)
         target[base + x, 0] = real
         target[base + x, 1] = imag
 
 
-def place_halo(ext, middle, even_ref, odd_ref, cs_ref):
-    position = lax.axis_index("grid")
-    chips = lax.axis_size("grid") // 2
-    core, chip = lax.rem(position, 2), lax.div(position, 2)
-    cosine, sine = cs_ref[core], cs_ref[2 + core]
-    first, last = chip == 0, chip == chips - 1
-    low = (jnp.where(first, cosine, 1.0), jnp.where(first, -sine, 0.0))
-    high = (jnp.where(last, cosine, 1.0), jnp.where(last, sine, 0.0))
-    planes = even_ref.shape[0]
-    parity = lax.rem(chip, 2)
-
-    @pl.when(parity == 0)
-    def _():
-        place_planes(ext, middle - planes, odd_ref, *low)
-        place_planes(ext, middle + planes, even_ref, *high)
-
-    @pl.when(parity == 1)
-    def _():
-        place_planes(ext, middle - planes, even_ref, *low)
-        place_planes(ext, middle + planes, odd_ref, *high)
+def whole_planes(ref):
+    return lambda x, part: ref[x, part]
 
 
 def as_column(row):
@@ -183,8 +165,8 @@
 
 def density_kernel(*refs):
     pd_ref, other_ref = refs[:2]
-    f_ref, inner_ref, outer_ref, b1, half = refs[-5:]
-    pieces = refs[2:-5]
+    f_ref, inner_ref, odd_ref, straight_ref, across_ref, b1, half = refs[-7:]
+    pieces = refs[2:-7]
     position = lax.axis_index("grid")
     core, side = lax.rem(position, 2), lax.rem(lax.div(position, 2), 2)
     planes, _, lines, depth = f_ref.shape
@@ -242,19 +224,37 @@
                 half[(2 * i + part) * 2 + h] = total[:, h * 128 : (h + 1) * 128]
     coarse = lowered(half, rows, lines, depth)
 
+    def send(inner, outer, near):
+        for r in range(8):
+            inner_ref[r // 2, r % 2] = coarse[inner + r]
+        for target in (odd_ref, straight_ref):
+            first = 0 if target is odd_ref else near
+            count = (target.shape[0] - 2) // 4
+            for x in range(count):
+                for part in range(2):
+                    for h in range(2):
+                        target[(2 * x + part) * 2 + h] = f_ref[
+                            first + x, part, :, h * 128 : (h + 1) * 128
+                        ]
+            for r in range(4):
+                target[4 * count + r // 2, r % 2 * 16 : r % 2 * 16 + 16] = coarse[outer + r]
+        for x in range(2):
+            across_ref[x] = f_ref[planes - 2 - near + x]
+
     @pl.when(side == 0)
     def _():
-        for r in range(8):
-            inner_ref[r // 2, r % 2] = coarse[4 + r]
-        for r in range(4):
-            outer_ref[r // 2, r % 2] = coarse[r]
+        send(4, 0, 0)
 
     @pl.when(side == 1)
     def _():
-        for r in range(8):
-            inner_ref[r // 2, r % 2] = coarse[r]
-        for r in range(4):
-            outer_ref[r // 2, r % 2] = coarse[8 + r]
+        send(0, 8, planes - 2)
+
+
+def packed_planes(ref):
+    def at(x, part):
+        return jnp.concatenate([ref[(2 * x + part) * 2], ref[(2 * x + part) * 2 + 1]], axis=1)
+
+    return at
 
 
 def lowered(half, rows, lines, depth):
@@ -273,7 +273,7 @@
     return [total[r * lines // 2 : (r + 1) * lines // 2] for r in range(rows)]
 
 
-def source_kernel(own_ref, partner_ref, straight_ref, across_ref, cs_ref, _, s_ref, __):
+def source_kernel(own_ref, partner_ref, straight_ref, odd_ref, cs_ref, _, s_ref, __):
     position = lax.axis_index("grid")
     blocks = lax.axis_size("grid") // 4
     core, side, block = lax.rem(position, 2), lax.rem(lax.div(position, 2), 2), lax.div(position, 4)
@@ -285,40 +285,47 @@
     def total(low_ref, high_ref):
         for x in range(4):
             source, (c, s) = (low_ref, low) if x < 2 else (high_ref, high)
-            real, imag = rotated(source[x % 2, 0], source[x % 2, 1], c, s)
+            place = source.shape[0] - 2 + x % 2
+            real, imag = rotated(source[place, 0:16], source[place, 16:32], c, s)
             s_ref[x, 0] = own_ref[x, 0] + partner_ref[x, 0] + real
             s_ref[x, 1] = own_ref[x, 1] + partner_ref[x, 1] + imag
 
     @pl.when(side == 0)
     def _():
-        total(across_ref, straight_ref)
+        total(odd_ref, straight_ref)
 
     @pl.when(side == 1)
     def _():
-        total(straight_ref, across_ref)
+        total(straight_ref, odd_ref)
 
 
 def fine_kernel(
-    even_ref, odd_ref, after_ref, before_ref, f_ref, cs_ref, _, own_ref, send_ref, ext, b1, b2, g
+    even_ref, odd_ref, straight_ref, across_ref, f_ref, cs_ref, _, own_ref, send_ref, ext, b1, b2, g
 ):
     position = lax.axis_index("grid")
-    chips = lax.axis_size("grid") // 2
-    core, chip = lax.rem(position, 2), lax.div(position, 2)
+    blocks = lax.axis_size("grid") // 4
+    core, side, block = lax.rem(position, 2), lax.rem(lax.div(position, 2), 2), lax.div(position, 4)
     cosine, sine = cs_ref[core], cs_ref[2 + core]
     planes = f_ref.shape[0]
-    place_halo(ext, planes + 2, even_ref, odd_ref, cs_ref)
+    first, last = block == 0, block == blocks - 1
+    low = (jnp.where(first, cosine, 1.0), jnp.where(first, -sine, 0.0))
+    high = (jnp.where(last, cosine, 1.0), jnp.where(last, sine, 0.0))
     ext[planes + 2 : 2 * planes + 2] = f_ref[...]
-    first, last = chip < 2, chip >= chips - 2
-    place_planes(
-        ext, 0, before_ref, jnp.where(first, cosine, 1.0), jnp.where(first, -sine, 0.0)
-    )
-    place_planes(
-        ext,
-        3 * planes + 2,
-        after_ref,
-        jnp.where(last, cosine, 1.0),
-        jnp.where(last, sine, 0.0),
-    )
+
+    @pl.when(side == 0)
+    def _():
+        place_planes(ext, 0, 2, whole_planes(across_ref), *low)
+        place_planes(ext, 2, planes, packed_planes(odd_ref), *low)
+        ext[2 * planes + 2 : 3 * planes + 2] = even_ref[...]
+        place_planes(ext, 3 * planes + 2, 2, packed_planes(straight_ref), *high)
+
+    @pl.when(side == 1)
+    def _():
+        place_planes(ext, 0, 2, packed_planes(straight_ref), *low)
+        ext[2 : planes + 2] = even_ref[...]
+        place_planes(ext, 2 * planes + 2, planes, packed_planes(odd_ref), *high)
+        place_planes(ext, 3 * planes + 2, 2, whole_planes(across_ref), *high)
+
     for x in range(planes + 8):
         for part in range(2):
             b1[x, part] = smooth_fine(lambda i, p: ext[i, p], x + 2, part)
@@ -333,10 +340,6 @@
     for x in range(half):
         own_ref[x] = g[core * half + x]
         send_ref[x] = g[(1 - core) * half + x]
-
-
-def gate_kernel(*_):
-    pass
 
 
 def shift_z(v, step):
@@ -621,6 +624,9 @@
 
     def next_block(i):
         return (i + (4 if i // 2 % 2 else -4)) % tile_count
+
+    def block_behind(i):
+        return (i + (-4 if i // 2 % 2 else 4)) % tile_count
 
     cs = pair_phases(pair_table, k_fraction)
 
@@ -659,13 +665,22 @@
 
     full = (2, lines, depth)
     small = (2, lines // 2, depth // 2)
-    f, inner, outer = call(
+    f, inner, odd, straight, across = call(
         density_kernel,
-        [shaped(planes, *full), shaped(4, *small), shaped(2, *small)],
+        [
+            shaped(planes, *full),
+            shaped(4, *small),
+            shaped(4 * planes + 2, lines, 128),
+            shaped(10, lines, 128),
+            shaped(2, *full),
+        ],
         vmem(2 + len(received)),
         [(planes + 4, *full), (2 * (planes + 8), lines, 128)],
         10**8,
     )(pair_density, other, *received)
+    odd = permute(odd, odd_side)
+    straight = permute(straight, next_block)
+    across = permute(across, block_behind)
     source, f = call(
         source_kernel,
         [shaped(4, *small), shaped(planes, *full)],
@@ -673,27 +688,10 @@
         [],
         10**6,
         {5: 1},
-    )(
-        inner,
-        permute(inner, even_side),
-        permute(outer, next_block),
-        permute(outer, odd_side),
-        cs,
-        f,
-    )
+    )(inner, permute(inner, even_side), straight, odd, cs, f)
     pieces = gather_blocks(source, blocks, block, permute_block)
     even = permute(f, even_side)
-    odd = permute(f, odd_side)
-    low, high = call(
-        gate_kernel,
-        [shaped(thick, *full)] * 2,
-        [pl.BlockSpec(memory_space=pl.ANY)] * (len(pieces) + 1),
-        [],
-        10**4,
-        {0: 0, 1: 1},
-    )(f[:thick], f[thick:], *pieces[1:])
-    after = permute(low, lambda i: (i - 4) % tile_count)
-    before = permute(high, lambda i: (i + 4) % tile_count)
+
     n1, n2, n3 = tile_count, tile_count // 2, tile_count // 4
     tile = (8, 128)
     w_own, w_send = call(
@@ -721,7 +719,7 @@
         vmem(5) + smem + [pl.BlockSpec(memory_space=pl.ANY)],
         [(3 * planes + 4, *full), (planes + 8, *full), (planes + 4, *full), (planes, *full)],
         10**7,
-    )(even, odd, after, before, f, cs, w_own)
+    )(even, odd, straight, across, f, cs, w_own)
     got = permute(send, partner)
 
     w_got = permute(w_send, partner)

time: 65.7 us -> 62.9 us (0.957)
  starting transfers between devices: 31.8 us -> 24.7 us
  waiting for transfers between devices: 17.4 us -> 21.7 us
    ppermute x21 -> x19, starting transfers between devices: 31.8 us -> 24.7 us  [permute(): return lax.ppermute(value, 'grid', [(i, target(i)) for i in devices])]
    ppermute x21 -> x19, waiting for transfers between devices: 17.4 us -> 21.7 us  [permute(): return lax.ppermute(value, 'grid', [(i, target(i)) for i in devices])]
    pallas_call x2 -> x1, Pallas kernels: 2.02 us -> 2 us  [per_device(): call(density_kernel, [shaped(planes, *full), shaped(4, *small), shaped(4...]
  transfers between devices with their start and end apart: 21 -> 19, of which waited for: 10 -> 12; matrix products, arithmetic and copies ran while one was open for 1% -> 1% of each run, Pallas kernels for 6% -> 6%
where the time goes in v9:
time: 62.9 us; the launch traced here: 62.7 us
  starting transfers between devices  24.7 us (39%)
  waiting for transfers between devices  21.7 us (34%)
  Pallas kernels  12.8 us (20%)
  local copies, waits for them, and re-layouts  2.19 us (3%)
  other arithmetic  1.15 us (2%)
    ppermute x19, starting transfers between devices, permute(): return lax.ppermute(value, 'grid', [(i, target(i)) for i in devices])  24.7 us
    ppermute x19, waiting for transfers between devices, permute(): return lax.ppermute(value, 'grid', [(i, target(i)) for i in devices])  21.7 us
    pallas_call x1, Pallas kernels, per_device(): call(cycle_kernel, [shaped(5, *small)] * 2, vmem(len(pieces)) + smem, [(n...  2.93 us
    pallas_call x1, Pallas kernels, per_device(): call(fine_kernel, [shaped(thick, *full)] * 2, vmem(5) + smem + [pl.BlockS...  2.51 us
    unnamed x10, local copies, waits for them, and re-layouts  2.18 us
    pallas_call x1, Pallas kernels, per_device(): call(density_kernel, [shaped(planes, *full), shaped(4, *small), shaped(4...  2 us
    pallas_call x1, Pallas kernels, per_device(): call(output_kernel, shaped(*pair_density.shape), vmem(3), scratch, 10 ** 7)  1.61 us
    pallas_call x1, Pallas kernels, per_device(): call(rows_kernel, [shaped(slot_count, row), shaped(slot_count + 8, row)],...  1.49 us
  transfers between devices with their start and end apart: 19, of which 12 were waited for; matrix products, arithmetic and copies ran while one was open for 1% of the time, Pallas kernels for 6%

profile of v9, /device:TPU:0, one launch (start us, length us, event | category | flops | bytes accessed | tf_op | source)
XLA Modules:
  0.0 62.7 jit_solution(3413901659840309366)
XLA Ops:
  0.0 0.7 %pad_add_fusion.slots_ref = s32[3,64]{1,0:T(4,128)S(1)} fusion(s32[1,64]{1,0:T(1,128)} %bitcast.7, s32[1,64]{1,0:T(1,128)} %bitcast.8, s32[1,64]{1,0:T(1,128)} %bitcast.9), kind=kLoop, calls=%fused_computation.3 | loop fusion | flops 384 | bytes 1536 | tf_op jit(solution)/shard_map/stack | solution.py:634
  0.7 1.4 %copy-done = f32[64,25,256]{2,0,1:T(8,128)S(1)} copy-done((f32[64,25,256]{2,0,1:T(8,128)S(1)}, f32[64,25,256]{2,0,1:T(8,128)}, u32[]{:S(2)}) %copy-start) | copy-done | bytes 1638424
  2.1 0.7 %copy-done.2 = f32[12,2,2,25]{3,2,1,0:T(2,128)S(1)} copy-done((f32[12,2,2,25]{3,2,1,0:T(2,128)S(1)}, f32[12,2,2,25]{3,2,1,0:T(2,128)}, u32[]{:S(2)}) %copy-start.2) | copy-done | bytes 4824
  2.9 1.5 %shard_map.82 = (f32[64,512]{1,0:T(8,128)S(1)}, f32[72,512]{1,0:T(8,128)S(1)}) custom-call(f32[12,2,2,25]{3,2,1,0:T(2,128)S(1)} %copy-done.2, f32[25,64,256]{2,1,0:T(8,128)S(1)} %bitcast.6, s32[3,64]{1,0:T(4,128)S(1)} %pad_add_fusion.slots_ref), custom_call_target="tpu_custom_call" | custom-call | flops 10000000 | bytes 1048576 | tf_op jit(solution)/shard_map/pallas_call | solution.py:636
  4.4 0.5 collective-permute-start.1
  4.9 0.1 collective-permute-start
  5.0 1.3 %collective-permute-done._.refs_1_ = f32[2,2,32,256]{3,2,1,0:T(8,128)S(1)} collective-permute-done((f32[2,2,32,256]{3,2,1,0:T(8,128)S(1)}, f32[2,2,32,256]{3,2,1,0:T(8,128)S(1)}, u32[]{:S(2)}, u32[]{:S(2)}) %collective-permute-start) | collective-permute-done | bytes 131104 | tf_op jit(solution)/shard_map/ppermute | solution.py:611
  6.3 0.0 collective-permute-done.1.got_ref
  6.3 0.8 %shard_map.83 = (f32[136,128]{1,0:T(8,128)S(1)}, f32[136,128]{1,0:T(8,128)S(1)}, f32[136,128]{1,0:T(8,128)S(1)}, f32[136,128]{1,0:T(8,128)S(1)}, f32[136,128]{1,...) custom-call(f32[64,512]{1,0:T(8,128)S(1)} %get-tuple-element.26.own_ref, ...), custom_call_target="tpu_custom_call" | custom-call | flops 100000000 | bytes 1048576 | tf_op jit(solution)/shard_map/pallas_call | solution.py:646
  7.1 2.7 %collective-permute-start.2 = (f32[136,128]{1,0:T(8,128)S(1)}, f32[136,128]{1,0:T(8,128)S(1)}, u32[]{:S(2)}, u32[]{:S(2)}) collective-permute-start(f32[136,128]{1,0:T(8,128)S(1)} %get-tuple-element.29), channel_id=1, source_target_pairs={{0,2},{1,3},{2,0},{3,1},{4,6},{5,7},{6,4},{7,5},{8,10},{9,11},{10,... | collective-permute-start | bytes 208904 | tf_op jit(solution)/shard_map/ppermute | solution.py:611
  9.8 3.6 %collective-permute-start.3 = (f32[136,128]{1,0:T(8,128)S(1)}, f32[136,128]{1,0:T(8,128)S(1)}, u32[]{:S(2)}, u32[]{:S(2)}) collective-permute-start(f32[136,128]{1,0:T(8,128)S(1)} %get-tuple-element.30), channel_id=1, source_target_pairs={{0,12},{1,13},{2,14},{3,15},{4,8},{5,9},{6,10},{7,11},{8,4},{9,5},... | collective-permute-start | bytes 208904 | tf_op jit(solution)/shard_map/ppermute | solution.py:611
  13.4 0.0 collective-permute-start.4
  13.4 1.0 %collective-permute-start.5 = (f32[136,128]{1,0:T(8,128)S(1)}, f32[136,128]{1,0:T(8,128)S(1)}, u32[]{:S(2)}, u32[]{:S(2)}) collective-permute-start(f32[136,128]{1,0:T(8,128)S(1)} %get-tuple-element.32), channel_id=1, source_target_pairs={{0,8},{1,9},{2,10},{3,11},{4,12},{5,13},{6,14},{7,15},{8,0},{9,1},... | collective-permute-start | bytes 208904 | tf_op jit(solution)/shard_map/ppermute | solution.py:611
  14.4 3.1 %collective-permute-start.6 = (f32[136,128]{1,0:T(8,128)S(1)}, f32[136,128]{1,0:T(8,128)S(1)}, u32[]{:S(2)}, u32[]{:S(2)}) collective-permute-start(f32[136,128]{1,0:T(8,128)S(1)} %get-tuple-element.33), channel_id=1, source_target_pairs={{0,10},{1,11},{2,8},{3,9},{4,14},{5,15},{6,12},{7,13},{8,2},{9,3},... | collective-permute-start | bytes 208904 | tf_op jit(solution)/shard_map/ppermute | solution.py:611
  17.5 0.0 collective-permute-done.2.refs_3_
  17.5 1.2 %collective-permute-start.7 = (f32[136,128]{1,0:T(8,128)S(1)}, f32[136,128]{1,0:T(8,128)S(1)}, u32[]{:S(2)}, u32[]{:S(2)}) collective-permute-start(f32[136,128]{1,0:T(8,128)S(1)} %get-tuple-element.34), channel_id=1, source_target_pairs={{0,4},{1,5},{2,6},{3,7},{4,0},{5,1},{6,2},{7,3},{8,12},{9,13},{10,... | collective-permute-start | bytes 208904 | tf_op jit(solution)/shard_map/ppermute | solution.py:611
  18.7 0.6 collective-permute-start.8
  19.3 1.6 %collective-permute-done.4.refs_5_ = f32[136,128]{1,0:T(8,128)S(1)} collective-permute-done((f32[136,128]{1,0:T(8,128)S(1)}, f32[136,128]{1,0:T(8,128)S(1)}, u32[]{:S(2)}, u32[]{:S(2)}) %collective-permute-start.4) | collective-permute-done | bytes 69664 | tf_op jit(solution)/shard_map/ppermute | solution.py:611
  20.8 3.9 %collective-permute-done.5.refs_6_ = f32[136,128]{1,0:T(8,128)S(1)} collective-permute-done((f32[136,128]{1,0:T(8,128)S(1)}, f32[136,128]{1,0:T(8,128)S(1)}, u32[]{:S(2)}, u32[]{:S(2)}) %collective-permute-start.5) | collective-permute-done | bytes 69664 | tf_op jit(solution)/shard_map/ppermute | solution.py:611
  24.8 0.9 %collective-permute-done.6.refs_7_ = f32[136,128]{1,0:T(8,128)S(1)} collective-permute-done((f32[136,128]{1,0:T(8,128)S(1)}, f32[136,128]{1,0:T(8,128)S(1)}, u32[]{:S(2)}, u32[]{:S(2)}) %collective-permute-start.6) | collective-permute-done | bytes 69664 | tf_op jit(solution)/shard_map/ppermute | solution.py:611
  25.6 0.0 collective-permute-done.7.refs_8_
  25.6 0.2 collective-permute-done.8.refs_9_
  25.8 2.0 %shard_map.84 = (f32[4,2,32,256]{3,2,1,0:T(8,128)S(1)}, f32[4,2,16,128]{3,2,1,0:T(8,128)S(1)}, f32[18,32,128]{2,1,0:T(8,128)S(1)}, f32[10,32,128]{2,1,0:T(8,128)S(1)}, f32[2,2,32,256]{3,2,1,0:T(8,128)S(1)}) custom-call(f32[2,2,2,32,256]{4,3,2,1,0:T(8,128)S(1)} %copy-done.1, f32[2,2,32,256]{3,2,1,0:T(8,128)S(1)} %collective-permute-done._.refs_1_, ...), custom_call_target="tpu_custom_call" | custom-call | flops 100000000 | bytes 1048576 | tf_op jit(solution)/shard_map/pallas_call | solution.py:668
  27.8 4.0 %collective-permute-start.11 = (f32[18,32,128]{2,1,0:T(8,128)S(1)}, f32[18,32,128]{2,1,0:T(8,128)S(1)}, u32[]{:S(2)}, u32[]{:S(2)}) collective-permute-start(f32[18,32,128]{2,1,0:T(8,128)S(1)} %get-tuple-element.38), channel_id=1, source_target_pairs={{0,14},{1,15},{2,4},{3,5},{4,2},{5,3},{6,8},{7,9},{8,6},{9,7},{10,... | collective-permute-start | bytes 884744 | tf_op jit(solution)/shard_map/ppermute | solution.py:611
  31.8 0.2 fusion
  32.0 0.2 cosine_reduce_fusion
  32.2 0.5 collective-permute-start.9
  32.7 0.1 pad_maximum_fusion.cs_ref.refs_4_
  32.8 6.9 %collective-permute-done.9.partner_ref = f32[4,2,16,128]{3,2,1,0:T(8,128)S(1)} collective-permute-done((f32[4,2,16,128]{3,2,1,0:T(8,128)S(1)}, f32[4,2,16,128]{3,2,1,0:T(8,128)S(1)}, u32[]{:S(2)}, u32[]{:S(2)}) %collective-permute-start.9) | collective-permute-done | bytes 65568 | tf_op jit(solution)/shard_map/ppermute | solution.py:611
  39.7 0.7 %collective-permute-done.10.straight_ref = f32[10,32,128]{2,1,0:T(8,128)S(1)} collective-permute-done((f32[10,32,128]{2,1,0:T(8,128)S(1)}, f32[10,32,128]{2,1,0:T(8,128)S(1)}, u32[]{:S(2)}, u32[]{:S(2)}) %collective-permute-start.10) | collective-permute-done | bytes 163872 | tf_op jit(solution)/shard_map/ppermute | solution.py:611
  40.4 0.1 collective-permute-done.11.odd_ref
  40.5 0.6 shard_map.85
  41.1 2.4 %collective-permute-start.15 = (f32[4,2,32,256]{3,2,1,0:T(8,128)S(1)}, f32[4,2,32,256]{3,2,1,0:T(8,128)S(1)}, u32[]{:S(2)}, u32[]{:S(2)}) collective-permute-start(f32[4,2,32,256]{3,2,1,0:T(8,128)S(1)} %get-tuple-element.42.f_ref), channel_id=1, source_target_pairs={{0,2},{1,3},{2,0},{3,1},{4,6},{5,7},{6,4},{7,5},{8,10},{9,11},{10,... | collective-permute-start | bytes 786440 | tf_op jit(solution)/shard_map/ppermute | solution.py:611
  43.5 0.0 collective-permute-start.16
  43.5 0.0 collective-permute-start.12
  43.5 4.4 %collective-permute-start.13 = (f32[4,2,16,128]{3,2,1,0:T(8,128)S(1)}, f32[4,2,16,128]{3,2,1,0:T(8,128)S(1)}, u32[]{:S(2)}, u32[]{:S(2)}) collective-permute-start(f32[4,2,16,128]{3,2,1,0:T(8,128)S(1)} %get-tuple-element.40.refs_0_), channel_id=1, source_target_pairs={{0,8},{1,9},{2,10},{3,11},{4,12},{5,13},{6,14},{7,15},{8,0},{9,1},... | collective-permute-start | bytes 196616 | tf_op jit(solution)/shard_map/ppermute | solution.py:611
  47.9 0.6 collective-permute-done.12.refs_1_
  48.4 4.2 %collective-permute-done.13.refs_2_ = f32[4,2,16,128]{3,2,1,0:T(8,128)S(1)} collective-permute-done((f32[4,2,16,128]{3,2,1,0:T(8,128)S(1)}, f32[4,2,16,128]{3,2,1,0:T(8,128)S(1)}, u32[]{:S(2)}, u32[]{:S(2)}) %collective-permute-start.13) | collective-permute-done | bytes 65568 | tf_op jit(solution)/shard_map/ppermute | solution.py:611
  52.6 1.4 %collective-permute-done.14.refs_3_ = f32[4,2,16,128]{3,2,1,0:T(8,128)S(1)} collective-permute-done((f32[4,2,16,128]{3,2,1,0:T(8,128)S(1)}, f32[4,2,16,128]{3,2,1,0:T(8,128)S(1)}, u32[]{:S(2)}, u32[]{:S(2)}) %collective-permute-start.14) | collective-permute-done | bytes 65568 | tf_op jit(solution)/shard_map/ppermute | solution.py:611
  54.0 2.9 %shard_map.86 = (f32[5,2,16,128]{3,2,1,0:T(8,128)S(1)}, f32[5,2,16,128]{3,2,1,0:T(8,128)S(1)}) custom-call(f32[4,2,16,128]{3,2,1,0:T(8,128)S(1)} %get-tuple-element.40.refs_0_, f32[4,2,16,128]{3,2,1,0:T(8,128)S(1)} %collective-permute-done.12.refs_1_, f32[4,2,16,128]{3,2,1,0:T(8,128)S(1)} %collective-permute-done.13.refs_2_, ...), custom_call_target="tpu_custom_call" | custom-call | flops 100000000 | bytes 1048576 | tf_op jit(solution)/shard_map/pallas_call | solution.py:697
  57.0 0.0 collective-permute-done.15.even_ref
  57.0 2.5 %shard_map.87 = (f32[2,2,32,256]{3,2,1,0:T(8,128)S(1)}, f32[2,2,32,256]{3,2,1,0:T(8,128)S(1)}) custom-call(f32[4,2,32,256]{3,2,1,0:T(8,128)S(1)} %collective-permute-done.15.even_ref, f32[18,32,128]{2,1,0:T(8,128)S(1)} %collective-permute-done.11.odd_ref, f32[10,32,128]{2,1,0:T(8,128)S(1)} %collective-permute-done.10.straight_ref, ...), custom_call_target="tpu_custom_call" | custom-call | flops 10000000 | bytes 1048576 | tf_op jit(solution)/shard_map/pallas_call | solution.py:716
  59.5 0.1 collective-permute-start.18
  59.6 0.5 collective-permute-start.17
  60.1 0.9 %shard_map.88.own_ref = f32[2,2,32,256]{3,2,1,0:T(8,128)S(1)} custom-call(f32[5,2,16,128]{3,2,1,0:T(8,128)S(1)} %get-tuple-element.41._.w_ref, f32[2,2,32,256]{3,2,1,0:T(8,128)S(1)} %get-tuple-element.44.g_ref), custom_call_target="tpu_custom_call" | custom-call | flops 10000000 | bytes 1048576 | tf_op jit(solution)/shard_map/pallas_call | solution.py:727
  61.0 0.1 collective-permute-done.17.w_ref
  61.0 0.0 collective-permute-done.18.g_ref
  61.0 1.6 %shard_map.89 = f32[2,2,2,32,256]{4,3,2,1,0:T(8,128)} custom-call(f32[2,2,32,256]{3,2,1,0:T(8,128)S(1)} %shard_map.88.own_ref, f32[5,2,16,128]{3,2,1,0:T(8,128)S(1)} %collective-permute-done.17.w_ref, f32[2,2,32,256]{3,2,1,0:T(8,128)S(1)} %collective-permute-done.18.g_ref), custom_call_target="tpu_custom_call" | custom-call | flops 10000000 | bytes 1048576 | tf_op jit(solution)/shard_map/pallas_call | solution.py:728
  (13 shorter events, 0.0 us)
Async XLA Ops:
  0.7 1.4 %copy-start = (f32[64,25,256]{2,0,1:T(8,128)S(1)}, f32[64,25,256]{2,0,1:T(8,128)}, u32[]{:S(2)}) copy-start(f32[64,25,256]{2,0,1:T(8,128)} %param.10) | copy-start | bytes 4915204
  2.1 0.7 %copy-start.2 = (f32[12,2,2,25]{3,2,1,0:T(2,128)S(1)}, f32[12,2,2,25]{3,2,1,0:T(2,128)}, u32[]{:S(2)}) copy-start(f32[12,2,2,25]{3,2,1,0:T(2,128)} %moments_ref.1) | copy-start | bytes 14404
  2.9 2.0 %copy-start.1 = (f32[2,2,2,32,256]{4,3,2,1,0:T(8,128)S(1)}, f32[2,2,2,32,256]{4,3,2,1,0:T(8,128)}, u32[]{:S(2)}) copy-start(f32[2,2,2,32,256]{4,3,2,1,0:T(8,128)} %refs_0_.1) | copy-start | bytes 786436
  2.9 28.9 %copy-start.3 = (s32[2,2]{1,0:T(2,128)S(1)}, s32[2,2]{1,0:T(2,128)}, u32[]{:S(2)}) copy-start(s32[2,2]{1,0:T(2,128)} %param.14) | copy-start | bytes 52
  2.9 28.9 %copy-start.4 = (f32[8]{0:T(128)S(1)}, f32[8]{0:T(128)}, u32[]{:S(2)}) copy-start(f32[8]{0:T(128)} %param.15) | copy-start | bytes 100
  4.4 2.0 %collective-permute-start.1 = (f32[72,512]{1,0:T(8,128)S(1)}, f32[72,512]{1,0:T(8,128)S(1)}, u32[]{:S(2)}, u32[]{:S(2)}) collective-permute-start(f32[72,512]{1,0:T(8,128)S(1)} %get-tuple-element.27), channel_id=1, source_target_pairs={{0,1},{1,0},{2,3},{3,2},{4,5},{5,4},{6,7},{7,6},{8,9},{9,8},{10,11... | collective-permute-start | bytes 442376 | tf_op jit(solution)/shard_map/ppermute | solution.py:611
  4.9 1.4 %collective-permute-start = (f32[2,2,32,256]{3,2,1,0:T(8,128)S(1)}, f32[2,2,32,256]{3,2,1,0:T(8,128)S(1)}, u32[]{:S(2)}, u32[]{:S(2)}) collective-permute-start(f32[2,2,32,256]{3,2,1,0:T(8,128)S(1)} %dynamic-slice_bitcast_fusion), channel_id=1, source_target_pairs={{0,1},{1,0},{2,3},{3,2},{4,5},{5,4},{6,7},{7,6},{8,9},{9,8},{10,11... | collective-permute-start | bytes 393224 | tf_op jit(solution)/shard_map/ppermute | solution.py:611
  7.1 10.3 %collective-permute-start.2 = (f32[136,128]{1,0:T(8,128)S(1)}, f32[136,128]{1,0:T(8,128)S(1)}, u32[]{:S(2)}, u32[]{:S(2)}) collective-permute-start(f32[136,128]{1,0:T(8,128)S(1)} %get-tuple-element.29), channel_id=1, source_target_pairs={{0,2},{1,3},{2,0},{3,1},{4,6},{5,7},{6,4},{7,5},{8,10},{9,11},{10,... | collective-permute-start | bytes 208904 | tf_op jit(solution)/shard_map/ppermute | solution.py:611
  9.8 8.9 %collective-permute-start.3 = (f32[136,128]{1,0:T(8,128)S(1)}, f32[136,128]{1,0:T(8,128)S(1)}, u32[]{:S(2)}, u32[]{:S(2)}) collective-permute-start(f32[136,128]{1,0:T(8,128)S(1)} %get-tuple-element.30), channel_id=1, source_target_pairs={{0,12},{1,13},{2,14},{3,15},{4,8},{5,9},{6,10},{7,11},{8,4},{9,5},... | collective-permute-start | bytes 208904 | tf_op jit(solution)/shard_map/ppermute | solution.py:611
  13.4 7.4 %collective-permute-start.4 = (f32[136,128]{1,0:T(8,128)S(1)}, f32[136,128]{1,0:T(8,128)S(1)}, u32[]{:S(2)}, u32[]{:S(2)}) collective-permute-start(f32[136,128]{1,0:T(8,128)S(1)} %get-tuple-element.31), channel_id=1, source_target_pairs={{0,14},{1,15},{2,12},{3,13},{4,10},{5,11},{6,8},{7,9},{8,6},{9,7},... | collective-permute-start | bytes 208904 | tf_op jit(solution)/shard_map/ppermute | solution.py:611
  13.4 11.3 %collective-permute-start.5 = (f32[136,128]{1,0:T(8,128)S(1)}, f32[136,128]{1,0:T(8,128)S(1)}, u32[]{:S(2)}, u32[]{:S(2)}) collective-permute-start(f32[136,128]{1,0:T(8,128)S(1)} %get-tuple-element.32), channel_id=1, source_target_pairs={{0,8},{1,9},{2,10},{3,11},{4,12},{5,13},{6,14},{7,15},{8,0},{9,1},... | collective-permute-start | bytes 208904 | tf_op jit(solution)/shard_map/ppermute | solution.py:611
  14.4 11.2 %collective-permute-start.6 = (f32[136,128]{1,0:T(8,128)S(1)}, f32[136,128]{1,0:T(8,128)S(1)}, u32[]{:S(2)}, u32[]{:S(2)}) collective-permute-start(f32[136,128]{1,0:T(8,128)S(1)} %get-tuple-element.33), channel_id=1, source_target_pairs={{0,10},{1,11},{2,8},{3,9},{4,14},{5,15},{6,12},{7,13},{8,2},{9,3},... | collective-permute-start | bytes 208904 | tf_op jit(solution)/shard_map/ppermute | solution.py:611
  17.5 8.2 %collective-permute-start.7 = (f32[136,128]{1,0:T(8,128)S(1)}, f32[136,128]{1,0:T(8,128)S(1)}, u32[]{:S(2)}, u32[]{:S(2)}) collective-permute-start(f32[136,128]{1,0:T(8,128)S(1)} %get-tuple-element.34), channel_id=1, source_target_pairs={{0,4},{1,5},{2,6},{3,7},{4,0},{5,1},{6,2},{7,3},{8,12},{9,13},{10,... | collective-permute-start | bytes 208904 | tf_op jit(solution)/shard_map/ppermute | solution.py:611
  18.7 7.1 %collective-permute-start.8 = (f32[136,128]{1,0:T(8,128)S(1)}, f32[136,128]{1,0:T(8,128)S(1)}, u32[]{:S(2)}, u32[]{:S(2)}) collective-permute-start(f32[136,128]{1,0:T(8,128)S(1)} %get-tuple-element.35), channel_id=1, source_target_pairs={{0,6},{1,7},{2,4},{3,5},{4,2},{5,3},{6,0},{7,1},{8,14},{9,15},{10,... | collective-permute-start | bytes 208904 | tf_op jit(solution)/shard_map/ppermute | solution.py:611
  27.8 12.7 %collective-permute-start.11 = (f32[18,32,128]{2,1,0:T(8,128)S(1)}, f32[18,32,128]{2,1,0:T(8,128)S(1)}, u32[]{:S(2)}, u32[]{:S(2)}) collective-permute-start(f32[18,32,128]{2,1,0:T(8,128)S(1)} %get-tuple-element.38), channel_id=1, source_target_pairs={{0,14},{1,15},{2,4},{3,5},{4,2},{5,3},{6,8},{7,9},{8,6},{9,7},{10,... | collective-permute-start | bytes 884744 | tf_op jit(solution)/shard_map/ppermute | solution.py:611
  31.9 8.5 %collective-permute-start.10 = (f32[10,32,128]{2,1,0:T(8,128)S(1)}, f32[10,32,128]{2,1,0:T(8,128)S(1)}, u32[]{:S(2)}, u32[]{:S(2)}) collective-permute-start(f32[10,32,128]{2,1,0:T(8,128)S(1)} %get-tuple-element.37), channel_id=1, source_target_pairs={{0,12},{1,13},{2,6},{3,7},{4,0},{5,1},{6,10},{7,11},{8,4},{9,5},{1... | collective-permute-start | bytes 491528 | tf_op jit(solution)/shard_map/ppermute | solution.py:611
  32.2 7.5 %collective-permute-start.9 = (f32[4,2,16,128]{3,2,1,0:T(8,128)S(1)}, f32[4,2,16,128]{3,2,1,0:T(8,128)S(1)}, u32[]{:S(2)}, u32[]{:S(2)}) collective-permute-start(f32[4,2,16,128]{3,2,1,0:T(8,128)S(1)} %get-tuple-element.36.own_ref), channel_id=1, source_target_pairs={{0,2},{1,3},{2,0},{3,1},{4,6},{5,7},{6,4},{7,5},{8,10},{9,11},{10,... | collective-permute-start | bytes 196616 | tf_op jit(solution)/shard_map/ppermute | solution.py:611
  41.1 15.9 %collective-permute-start.15 = (f32[4,2,32,256]{3,2,1,0:T(8,128)S(1)}, f32[4,2,32,256]{3,2,1,0:T(8,128)S(1)}, u32[]{:S(2)}, u32[]{:S(2)}) collective-permute-start(f32[4,2,32,256]{3,2,1,0:T(8,128)S(1)} %get-tuple-element.42.f_ref), channel_id=1, source_target_pairs={{0,2},{1,3},{2,0},{3,1},{4,6},{5,7},{6,4},{7,5},{8,10},{9,11},{10,... | collective-permute-start | bytes 786440 | tf_op jit(solution)/shard_map/ppermute | solution.py:611
  43.5 13.5 %collective-permute-start.16 = (f32[2,2,32,256]{3,2,1,0:T(8,128)S(1)}, f32[2,2,32,256]{3,2,1,0:T(8,128)S(1)}, u32[]{:S(2)}, u32[]{:S(2)}) collective-permute-start(f32[2,2,32,256]{3,2,1,0:T(8,128)S(1)} %get-tuple-element.43), channel_id=1, source_target_pairs={{0,4},{1,5},{2,14},{3,15},{4,8},{5,9},{6,2},{7,3},{8,12},{9,13},{1... | collective-permute-start | bytes 393224 | tf_op jit(solution)/shard_map/ppermute | solution.py:611
  43.5 4.9 %collective-permute-start.12 = (f32[4,2,16,128]{3,2,1,0:T(8,128)S(1)}, f32[4,2,16,128]{3,2,1,0:T(8,128)S(1)}, u32[]{:S(2)}, u32[]{:S(2)}) collective-permute-start(f32[4,2,16,128]{3,2,1,0:T(8,128)S(1)} %get-tuple-element.40.refs_0_), channel_id=1, source_target_pairs={{0,4},{1,5},{2,6},{3,7},{4,0},{5,1},{6,2},{7,3},{8,12},{9,13},{10,... | collective-permute-start | bytes 196616 | tf_op jit(solution)/shard_map/ppermute | solution.py:611
  43.5 9.2 %collective-permute-start.13 = (f32[4,2,16,128]{3,2,1,0:T(8,128)S(1)}, f32[4,2,16,128]{3,2,1,0:T(8,128)S(1)}, u32[]{:S(2)}, u32[]{:S(2)}) collective-permute-start(f32[4,2,16,128]{3,2,1,0:T(8,128)S(1)} %get-tuple-element.40.refs_0_), channel_id=1, source_target_pairs={{0,8},{1,9},{2,10},{3,11},{4,12},{5,13},{6,14},{7,15},{8,0},{9,1},... | collective-permute-start | bytes 196616 | tf_op jit(solution)/shard_map/ppermute | solution.py:611
  47.9 6.2 %collective-permute-start.14 = (f32[4,2,16,128]{3,2,1,0:T(8,128)S(1)}, f32[4,2,16,128]{3,2,1,0:T(8,128)S(1)}, u32[]{:S(2)}, u32[]{:S(2)}) collective-permute-start(f32[4,2,16,128]{3,2,1,0:T(8,128)S(1)} %get-tuple-element.40.refs_0_), channel_id=1, source_target_pairs={{0,12},{1,13},{2,14},{3,15},{4,8},{5,9},{6,10},{7,11},{8,4},{9,5},... | collective-permute-start | bytes 196616 | tf_op jit(solution)/shard_map/ppermute | solution.py:611
  59.5 1.5 %collective-permute-start.18 = (f32[2,2,32,256]{3,2,1,0:T(8,128)S(1)}, f32[2,2,32,256]{3,2,1,0:T(8,128)S(1)}, u32[]{:S(2)}, u32[]{:S(2)}) collective-permute-start(f32[2,2,32,256]{3,2,1,0:T(8,128)S(1)} %get-tuple-element.46), channel_id=1, source_target_pairs={{0,1},{1,0},{2,3},{3,2},{4,5},{5,4},{6,7},{7,6},{8,9},{9,8},{10,11... | collective-permute-start | bytes 393224 | tf_op jit(solution)/shard_map/ppermute | solution.py:611
  59.6 1.5 %collective-permute-start.17 = (f32[5,2,16,128]{3,2,1,0:T(8,128)S(1)}, f32[5,2,16,128]{3,2,1,0:T(8,128)S(1)}, u32[]{:S(2)}, u32[]{:S(2)}) collective-permute-start(f32[5,2,16,128]{3,2,1,0:T(8,128)S(1)} %get-tuple-element.45), channel_id=1, source_target_pairs={{0,1},{1,0},{2,3},{3,2},{4,5},{5,4},{6,7},{7,6},{8,9},{9,8},{10,11... | collective-permute-start | bytes 245768 | tf_op jit(solution)/shard_map/ppermute | solution.py:611

commit v10 on v9

--- a/solution.py
+++ b/solution.py
@@ -273,7 +273,7 @@
     return [total[r * lines // 2 : (r + 1) * lines // 2] for r in range(rows)]
 
 
-def source_kernel(own_ref, partner_ref, straight_ref, odd_ref, cs_ref, _, s_ref, __):
+def source_kernel(own_ref, partner_ref, straight_ref, odd_ref, cs_ref, _, s_ref):
     position = lax.axis_index("grid")
     blocks = lax.axis_size("grid") // 4
     core, side, block = lax.rem(position, 2), lax.rem(lax.div(position, 2), 2), lax.div(position, 4)
@@ -300,7 +300,7 @@
 
 
 def fine_kernel(
-    even_ref, odd_ref, straight_ref, across_ref, f_ref, cs_ref, _, own_ref, send_ref, ext, b1, b2, g
+    even_ref, odd_ref, straight_ref, across_ref, f_ref, cs_ref, own_ref, send_ref, ext, b1, b2, g
 ):
     position = lax.axis_index("grid")
     blocks = lax.axis_size("grid") // 4
@@ -571,7 +571,7 @@
 smem = [pl.BlockSpec(memory_space=pltpu.SMEM)]
 
 
-def call(kernel, out_shape, in_specs, scratch, flops, aliases={}):
+def call(kernel, out_shape, in_specs, scratch, flops):
     single = not isinstance(out_shape, (list, tuple))
     return pl.pallas_call(
         kernel,
@@ -579,15 +579,26 @@
         in_specs=in_specs,
         out_specs=vmem(1)[0]
         if single
-        else [
-            pl.BlockSpec(memory_space=pl.ANY if i in aliases.values() else pltpu.VMEM)
-            for i in range(len(out_shape))
-        ],
-        input_output_aliases=aliases,
+        else vmem(len(out_shape)),
         scratch_shapes=[pltpu.VMEM(shape, jnp.float32) for shape in scratch],
         compiler_params=pltpu.CompilerParams(vmem_limit_bytes=48 * 2**20),
         cost_estimate=pl.CostEstimate(flops=flops, bytes_accessed=2**20, transcendentals=0),
     )
+
+
+def gate_kernel(*_):
+    pass
+
+
+def gate(value, other):
+    return pl.pallas_call(
+        gate_kernel,
+        out_shape=jax.ShapeDtypeStruct(value.shape, value.dtype),
+        in_specs=[pl.BlockSpec(memory_space=pl.ANY)] * 2,
+        out_specs=pl.BlockSpec(memory_space=pl.ANY),
+        input_output_aliases={0: 0},
+        cost_estimate=pl.CostEstimate(flops=0, bytes_accessed=0, transcendentals=0),
+    )(value, other)
 
 
 def shaped(*shape):
@@ -681,16 +692,26 @@
     odd = permute(odd, odd_side)
     straight = permute(straight, next_block)
     across = permute(across, block_behind)
-    source, f = call(
+    theirs = permute(inner, even_side)
+    f = gate(f, theirs)
+    even = permute(f, even_side)
+    source = call(
         source_kernel,
-        [shaped(4, *small), shaped(planes, *full)],
+        shaped(4, *small),
         vmem(4) + smem + [pl.BlockSpec(memory_space=pl.ANY)],
         [],
         10**6,
-        {5: 1},
-    )(inner, permute(inner, even_side), straight, odd, cs, f)
+    )(inner, theirs, straight, odd, cs, across)
     pieces = gather_blocks(source, blocks, block, permute_block)
-    even = permute(f, even_side)
+
+    own, send = call(
+        fine_kernel,
+        [shaped(thick, *full)] * 2,
+        vmem(5) + smem,
+        [(3 * planes + 4, *full), (planes + 8, *full), (planes + 4, *full), (planes, *full)],
+        10**7,
+    )(even, odd, straight, across, f, cs)
+    got = permute(send, partner)
 
     n1, n2, n3 = tile_count, tile_count // 2, tile_count // 4
     tile = (8, 128)
@@ -713,15 +734,6 @@
         ],
         10**8,
     )(*pieces, cs)
-    own, send = call(
-        fine_kernel,
-        [shaped(thick, *full)] * 2,
-        vmem(5) + smem + [pl.BlockSpec(memory_space=pl.ANY)],
-        [(3 * planes + 4, *full), (planes + 8, *full), (planes + 4, *full), (planes, *full)],
-        10**7,
-    )(even, odd, straight, across, f, cs, w_own)
-    got = permute(send, partner)
-
     w_got = permute(w_send, partner)
     scratch = [(20, lines, 128), (6, *full)]
     result = call(own_kernel, shaped(2, thick, lines, depth), vmem(2), scratch, 10**7)(w_own, own)

time: 62.9 us -> 63.9 us (1.016)
  waiting for transfers between devices: 21.7 us -> 16.7 us
  local copies, waits for them, and re-layouts: 2.19 us -> 5.29 us
  starting transfers between devices: 24.7 us -> 27.6 us
    ppermute x19, waiting for transfers between devices: 21.7 us -> 16.7 us  [permute(): return lax.ppermute(value, 'grid', [(i, target(i)) for i in devices])]
    unnamed x10 -> x18, local copies, waits for them, and re-layouts: 2.18 us -> 5.28 us
    ppermute x19, starting transfers between devices: 24.7 us -> 27.6 us  [permute(): return lax.ppermute(value, 'grid', [(i, target(i)) for i in devices])]
    pallas_call x2 -> x3, Pallas kernels: 3.08 us -> 3.08 us  [the longest x1 2.51 us: per_device(): call(fine_kernel, [shaped(thick, *full)] * 2, vmem(5) + smem, [(3 * plane...]
  transfers between devices with their start and end apart: 19 -> 19, of which waited for: 12 -> 7; matrix products, arithmetic and copies ran while one was open for 1% -> 1% of each run, Pallas kernels for 6% -> 11%
where the time goes in v10:
time: 63.9 us; the launch traced here: 63.6 us
  starting transfers between devices  27.6 us (43%)
  waiting for transfers between devices  16.7 us (26%)
  Pallas kernels  12.8 us (20%)
  local copies, waits for them, and re-layouts  5.29 us (8%)
  other arithmetic  1.15 us (2%)
    ppermute x19, starting transfers between devices, permute(): return lax.ppermute(value, 'grid', [(i, target(i)) for i in devices])  27.6 us
    ppermute x19, waiting for transfers between devices, permute(): return lax.ppermute(value, 'grid', [(i, target(i)) for i in devices])  16.7 us
    unnamed x18, local copies, waits for them, and re-layouts  5.28 us
    pallas_call x1, Pallas kernels, per_device(): call(cycle_kernel, [shaped(5, *small)] * 2, vmem(len(pieces)) + smem, [(n...  2.93 us
    pallas_call x1, Pallas kernels, per_device(): call(fine_kernel, [shaped(thick, *full)] * 2, vmem(5) + smem, [(3 * plane...  2.51 us
    pallas_call x1, Pallas kernels, per_device(): call(density_kernel, [shaped(planes, *full), shaped(4, *small), shaped(4...  2 us
    pallas_call x1, Pallas kernels, per_device(): call(output_kernel, shaped(*pair_density.shape), vmem(3), scratch, 10 ** 7)  1.61 us
    pallas_call x1, Pallas kernels, per_device(): call(rows_kernel, [shaped(slot_count, row), shaped(slot_count + 8, row)],...  1.46 us
  transfers between devices with their start and end apart: 19, of which 7 were waited for; matrix products, arithmetic and copies ran while one was open for 1% of the time, Pallas kernels for 11%

profile of v10, /device:TPU:0, one launch (start us, length us, event | category | flops | bytes accessed | tf_op | source)
XLA Modules:
  0.0 63.6 jit_solution(3584202328418304352)
XLA Ops:
  0.0 0.7 %pad_add_fusion.slots_ref = s32[3,64]{1,0:T(4,128)S(1)} fusion(s32[1,64]{1,0:T(1,128)} %bitcast.7, s32[1,64]{1,0:T(1,128)} %bitcast.8, s32[1,64]{1,0:T(1,128)} %bitcast.9), kind=kLoop, calls=%fused_computation.3 | loop fusion | flops 384 | bytes 1536 | tf_op jit(solution)/shard_map/stack | solution.py:645
  0.7 1.4 %copy-done = f32[64,25,256]{2,0,1:T(8,128)S(1)} copy-done((f32[64,25,256]{2,0,1:T(8,128)S(1)}, f32[64,25,256]{2,0,1:T(8,128)}, u32[]{:S(2)}) %copy-start) | copy-done | bytes 1638424
  2.1 0.7 %copy-done.6 = f32[12,2,2,25]{3,2,1,0:T(2,128)S(1)} copy-done((f32[12,2,2,25]{3,2,1,0:T(2,128)S(1)}, f32[12,2,2,25]{3,2,1,0:T(2,128)}, u32[]{:S(2)}) %copy-start.6) | copy-done | bytes 4824
  2.9 1.5 %shard_map.82 = (f32[64,512]{1,0:T(8,128)S(1)}, f32[72,512]{1,0:T(8,128)S(1)}) custom-call(f32[12,2,2,25]{3,2,1,0:T(2,128)S(1)} %copy-done.6, f32[25,64,256]{2,1,0:T(8,128)S(1)} %bitcast.6, s32[3,64]{1,0:T(4,128)S(1)} %pad_add_fusion.slots_ref), custom_call_target="tpu_custom_call" | custom-call | flops 10000000 | bytes 1048576 | tf_op jit(solution)/shard_map/pallas_call | solution.py:647
  4.3 0.5 collective-permute-start.1
  4.9 0.1 collective-permute-start
  5.0 1.3 %collective-permute-done._.refs_1_ = f32[2,2,32,256]{3,2,1,0:T(8,128)S(1)} collective-permute-done((f32[2,2,32,256]{3,2,1,0:T(8,128)S(1)}, f32[2,2,32,256]{3,2,1,0:T(8,128)S(1)}, u32[]{:S(2)}, u32[]{:S(2)}) %collective-permute-start) | collective-permute-done | bytes 131104 | tf_op jit(solution)/shard_map/ppermute | solution.py:622
  6.3 0.0 collective-permute-done.1.got_ref
  6.3 0.8 %shard_map.83 = (f32[136,128]{1,0:T(8,128)S(1)}, f32[136,128]{1,0:T(8,128)S(1)}, f32[136,128]{1,0:T(8,128)S(1)}, f32[136,128]{1,0:T(8,128)S(1)}, f32[136,128]{1,...) custom-call(f32[64,512]{1,0:T(8,128)S(1)} %get-tuple-element.24.own_ref, ...), custom_call_target="tpu_custom_call" | custom-call | flops 100000000 | bytes 1048576 | tf_op jit(solution)/shard_map/pallas_call | solution.py:657
  7.1 2.7 %collective-permute-start.2 = (f32[136,128]{1,0:T(8,128)S(1)}, f32[136,128]{1,0:T(8,128)S(1)}, u32[]{:S(2)}, u32[]{:S(2)}) collective-permute-start(f32[136,128]{1,0:T(8,128)S(1)} %get-tuple-element.27), channel_id=1, source_target_pairs={{0,2},{1,3},{2,0},{3,1},{4,6},{5,7},{6,4},{7,5},{8,10},{9,11},{10,... | collective-permute-start | bytes 208904 | tf_op jit(solution)/shard_map/ppermute | solution.py:622
  9.8 3.6 %collective-permute-start.3 = (f32[136,128]{1,0:T(8,128)S(1)}, f32[136,128]{1,0:T(8,128)S(1)}, u32[]{:S(2)}, u32[]{:S(2)}) collective-permute-start(f32[136,128]{1,0:T(8,128)S(1)} %get-tuple-element.28), channel_id=1, source_target_pairs={{0,12},{1,13},{2,14},{3,15},{4,8},{5,9},{6,10},{7,11},{8,4},{9,5},... | collective-permute-start | bytes 208904 | tf_op jit(solution)/shard_map/ppermute | solution.py:622
  13.4 0.0 collective-permute-start.4
  13.4 1.0 %collective-permute-start.5 = (f32[136,128]{1,0:T(8,128)S(1)}, f32[136,128]{1,0:T(8,128)S(1)}, u32[]{:S(2)}, u32[]{:S(2)}) collective-permute-start(f32[136,128]{1,0:T(8,128)S(1)} %get-tuple-element.30), channel_id=1, source_target_pairs={{0,8},{1,9},{2,10},{3,11},{4,12},{5,13},{6,14},{7,15},{8,0},{9,1},... | collective-permute-start | bytes 208904 | tf_op jit(solution)/shard_map/ppermute | solution.py:622
  14.4 3.1 %collective-permute-start.6 = (f32[136,128]{1,0:T(8,128)S(1)}, f32[136,128]{1,0:T(8,128)S(1)}, u32[]{:S(2)}, u32[]{:S(2)}) collective-permute-start(f32[136,128]{1,0:T(8,128)S(1)} %get-tuple-element.31), channel_id=1, source_target_pairs={{0,10},{1,11},{2,8},{3,9},{4,14},{5,15},{6,12},{7,13},{8,2},{9,3},... | collective-permute-start | bytes 208904 | tf_op jit(solution)/shard_map/ppermute | solution.py:622
  17.4 1.2 %collective-permute-start.7 = (f32[136,128]{1,0:T(8,128)S(1)}, f32[136,128]{1,0:T(8,128)S(1)}, u32[]{:S(2)}, u32[]{:S(2)}) collective-permute-start(f32[136,128]{1,0:T(8,128)S(1)} %get-tuple-element.32), channel_id=1, source_target_pairs={{0,4},{1,5},{2,6},{3,7},{4,0},{5,1},{6,2},{7,3},{8,12},{9,13},{10,... | collective-permute-start | bytes 208904 | tf_op jit(solution)/shard_map/ppermute | solution.py:622
  18.7 0.6 collective-permute-start.8
  19.2 1.6 %collective-permute-done.4.refs_5_ = f32[136,128]{1,0:T(8,128)S(1)} collective-permute-done((f32[136,128]{1,0:T(8,128)S(1)}, f32[136,128]{1,0:T(8,128)S(1)}, u32[]{:S(2)}, u32[]{:S(2)}) %collective-permute-start.4) | collective-permute-done | bytes 69664 | tf_op jit(solution)/shard_map/ppermute | solution.py:622
  20.8 3.9 %collective-permute-done.5.refs_6_ = f32[136,128]{1,0:T(8,128)S(1)} collective-permute-done((f32[136,128]{1,0:T(8,128)S(1)}, f32[136,128]{1,0:T(8,128)S(1)}, u32[]{:S(2)}, u32[]{:S(2)}) %collective-permute-start.5) | collective-permute-done | bytes 69664 | tf_op jit(solution)/shard_map/ppermute | solution.py:622
  24.7 0.8 %collective-permute-done.6.refs_7_ = f32[136,128]{1,0:T(8,128)S(1)} collective-permute-done((f32[136,128]{1,0:T(8,128)S(1)}, f32[136,128]{1,0:T(8,128)S(1)}, u32[]{:S(2)}, u32[]{:S(2)}) %collective-permute-start.6) | collective-permute-done | bytes 69664 | tf_op jit(solution)/shard_map/ppermute | solution.py:622
  25.6 0.0 collective-permute-done.7.refs_8_
  25.6 0.2 collective-permute-done.8.refs_9_
  25.7 2.0 %shard_map.84 = (f32[4,2,32,256]{3,2,1,0:T(8,128)S(1)}, f32[4,2,16,128]{3,2,1,0:T(8,128)S(1)}, f32[18,32,128]{2,1,0:T(8,128)S(1)}, f32[10,32,128]{2,1,0:T(8,128)S(1)}, f32[2,2,32,256]{3,2,1,0:T(8,128)S(1)}) custom-call(f32[2,2,2,32,256]{4,3,2,1,0:T(8,128)S(1)} %copy-done.3, f32[2,2,32,256]{3,2,1,0:T(8,128)S(1)} %collective-permute-done._.refs_1_, ...), custom_call_target="tpu_custom_call" | custom-call | flops 100000000 | bytes 1048576 | tf_op jit(solution)/shard_map/pallas_call | solution.py:679
  27.7 0.0 copy-start.1
  27.7 0.7 %copy-done.1 = f32[4,2,32,256]{3,2,1,0:T(8,128)} copy-done((f32[4,2,32,256]{3,2,1,0:T(8,128)}, f32[4,2,32,256]{3,2,1,0:T(8,128)S(1)}, u32[]{:S(2)}) %copy-start.1) | copy-done | bytes 262168
  28.4 1.3 %collective-permute-start.9 = (f32[4,2,16,128]{3,2,1,0:T(8,128)S(1)}, f32[4,2,16,128]{3,2,1,0:T(8,128)S(1)}, u32[]{:S(2)}, u32[]{:S(2)}) collective-permute-start(f32[4,2,16,128]{3,2,1,0:T(8,128)S(1)} %get-tuple-element.34.own_ref), channel_id=1, source_target_pairs={{0,2},{1,3},{2,0},{3,1},{4,6},{5,7},{6,4},{7,5},{8,10},{9,11},{10,... | collective-permute-start | bytes 196616 | tf_op jit(solution)/shard_map/ppermute | solution.py:622
  29.7 3.4 %collective-permute-start.11 = (f32[18,32,128]{2,1,0:T(8,128)S(1)}, f32[18,32,128]{2,1,0:T(8,128)S(1)}, u32[]{:S(2)}, u32[]{:S(2)}) collective-permute-start(f32[18,32,128]{2,1,0:T(8,128)S(1)} %get-tuple-element.36), channel_id=1, source_target_pairs={{0,14},{1,15},{2,4},{3,5},{4,2},{5,3},{6,8},{7,9},{8,6},{9,7},{10,... | collective-permute-start | bytes 884744 | tf_op jit(solution)/shard_map/ppermute | solution.py:622
  33.1 3.6 %collective-permute-done.9.partner_ref.__1_ = f32[4,2,16,128]{3,2,1,0:T(8,128)S(1)} collective-permute-done((f32[4,2,16,128]{3,2,1,0:T(8,128)S(1)}, f32[4,2,16,128]{3,2,1,0:T(8,128)S(1)}, u32[]{:S(2)}, u32[]{:S(2)}) %collective-permute-start.9) | collective-permute-done | bytes 65568 | tf_op jit(solution)/shard_map/ppermute | solution.py:622
  36.7 0.6 copy-done.4
  37.4 3.0 %collective-permute-start.16 = (f32[4,2,32,256]{3,2,1,0:T(8,128)}, f32[4,2,32,256]{3,2,1,0:T(8,128)S(1)}, u32[]{:S(2)}, u32[]{:S(2)}) collective-permute-start(f32[4,2,32,256]{3,2,1,0:T(8,128)} %shard_map.87.f_ref), channel_id=1, source_target_pairs={{0,2},{1,3},{2,0},{3,1},{4,6},{5,7},{6,4},{7,5},{8,10},{9,11},{10,... | collective-permute-start | bytes 786440 | tf_op jit(solution)/shard_map/ppermute | solution.py:622
  40.3 0.2 fusion
  40.5 0.8 %collective-permute-start.10 = (f32[10,32,128]{2,1,0:T(8,128)S(1)}, f32[10,32,128]{2,1,0:T(8,128)S(1)}, u32[]{:S(2)}, u32[]{:S(2)}) collective-permute-start(f32[10,32,128]{2,1,0:T(8,128)S(1)} %get-tuple-element.35), channel_id=1, source_target_pairs={{0,12},{1,13},{2,6},{3,7},{4,0},{5,1},{6,10},{7,11},{8,4},{9,5},{1... | collective-permute-start | bytes 491528 | tf_op jit(solution)/shard_map/ppermute | solution.py:622
  41.3 1.3 %collective-permute-start.12 = (f32[2,2,32,256]{3,2,1,0:T(8,128)S(1)}, f32[2,2,32,256]{3,2,1,0:T(8,128)S(1)}, u32[]{:S(2)}, u32[]{:S(2)}) collective-permute-start(f32[2,2,32,256]{3,2,1,0:T(8,128)S(1)} %get-tuple-element.37), channel_id=1, source_target_pairs={{0,4},{1,5},{2,14},{3,15},{4,8},{5,9},{6,2},{7,3},{8,12},{9,13},{1... | collective-permute-start | bytes 393224 | tf_op jit(solution)/shard_map/ppermute | solution.py:622
  42.5 0.2 cosine_reduce_fusion
  42.7 0.1 pad_maximum_fusion.cs_ref.refs_4_
  42.8 5.3 %collective-permute-done.12._.across_ref = f32[2,2,32,256]{3,2,1,0:T(8,128)S(1)} collective-permute-done((f32[2,2,32,256]{3,2,1,0:T(8,128)S(1)}, f32[2,2,32,256]{3,2,1,0:T(8,128)S(1)}, u32[]{:S(2)}, u32[]{:S(2)}) %collective-permute-start.12) | collective-permute-done | bytes 131104 | tf_op jit(solution)/shard_map/ppermute | solution.py:622
  48.1 0.8 %copy-done.5 = f32[4,2,16,128]{3,2,1,0:T(8,128)S(1)} copy-done((f32[4,2,16,128]{3,2,1,0:T(8,128)S(1)}, f32[4,2,16,128]{3,2,1,0:T(8,128)}, u32[]{:S(2)}) %copy-start.5) | copy-done | bytes 65560
  49.0 0.6 shard_map.85.refs_0_
  49.6 0.1 collective-permute-start.13
  49.6 1.0 %collective-permute-start.14 = (f32[4,2,16,128]{3,2,1,0:T(8,128)S(1)}, f32[4,2,16,128]{3,2,1,0:T(8,128)S(1)}, u32[]{:S(2)}, u32[]{:S(2)}) collective-permute-start(f32[4,2,16,128]{3,2,1,0:T(8,128)S(1)} %shard_map.85.refs_0_), channel_id=1, source_target_pairs={{0,8},{1,9},{2,10},{3,11},{4,12},{5,13},{6,14},{7,15},{8,0},{9,1},... | collective-permute-start | bytes 196616 | tf_op jit(solution)/shard_map/ppermute | solution.py:622
  50.6 3.4 %collective-permute-start.15 = (f32[4,2,16,128]{3,2,1,0:T(8,128)S(1)}, f32[4,2,16,128]{3,2,1,0:T(8,128)S(1)}, u32[]{:S(2)}, u32[]{:S(2)}) collective-permute-start(f32[4,2,16,128]{3,2,1,0:T(8,128)S(1)} %shard_map.85.refs_0_), channel_id=1, source_target_pairs={{0,12},{1,13},{2,14},{3,15},{4,8},{5,9},{6,10},{7,11},{8,4},{9,5},... | collective-permute-start | bytes 196616 | tf_op jit(solution)/shard_map/ppermute | solution.py:622
  54.0 0.9 %copy-done.2 = f32[4,2,32,256]{3,2,1,0:T(8,128)S(1)} copy-done((f32[4,2,32,256]{3,2,1,0:T(8,128)S(1)}, f32[4,2,32,256]{3,2,1,0:T(8,128)}, u32[]{:S(2)}) %copy-start.2) | copy-done | bytes 262168
  55.0 2.5 %shard_map.88 = (f32[2,2,32,256]{3,2,1,0:T(8,128)S(1)}, f32[2,2,32,256]{3,2,1,0:T(8,128)S(1)}) custom-call(f32[4,2,32,256]{3,2,1,0:T(8,128)S(1)} %collective-permute-done.16.even_ref, f32[18,32,128]{2,1,0:T(8,128)S(1)} %collective-permute-done.11.odd_ref, f32[10,32,128]{2,1,0:T(8,128)S(1)} %collective-permute-done.10.straight_ref, ...), custom_call_target="tpu_custom_call" | custom-call | flops 10000000 | bytes 1048576 | tf_op jit(solution)/shard_map/pallas_call | solution.py:707
  57.5 0.1 collective-permute-start.18
  57.6 2.9 %shard_map.86 = (f32[5,2,16,128]{3,2,1,0:T(8,128)S(1)}, f32[5,2,16,128]{3,2,1,0:T(8,128)S(1)}) custom-call(f32[4,2,16,128]{3,2,1,0:T(8,128)S(1)} %shard_map.85.refs_0_, f32[4,2,16,128]{3,2,1,0:T(8,128)S(1)} %collective-permute-done.13.refs_1_, f32[4,2,16,128]{3,2,1,0:T(8,128)S(1)} %collective-permute-done.14.refs_2_, ...), custom_call_target="tpu_custom_call" | custom-call | flops 100000000 | bytes 1048576 | tf_op jit(solution)/shard_map/pallas_call | solution.py:718
  60.5 0.5 collective-permute-start.17
  61.1 0.9 %shard_map.89.own_ref = f32[2,2,32,256]{3,2,1,0:T(8,128)S(1)} custom-call(f32[5,2,16,128]{3,2,1,0:T(8,128)S(1)} %get-tuple-element.38.w_ref, f32[2,2,32,256]{3,2,1,0:T(8,128)S(1)} %get-tuple-element.40.g_ref), custom_call_target="tpu_custom_call" | custom-call | flops 10000000 | bytes 1048576 | tf_op jit(solution)/shard_map/pallas_call | solution.py:739
  62.0 0.0 collective-permute-done.17.w_ref
  62.0 1.6 %shard_map.90 = f32[2,2,2,32,256]{4,3,2,1,0:T(8,128)} custom-call(f32[2,2,32,256]{3,2,1,0:T(8,128)S(1)} %shard_map.89.own_ref, f32[5,2,16,128]{3,2,1,0:T(8,128)S(1)} %collective-permute-done.17.w_ref, f32[2,2,32,256]{3,2,1,0:T(8,128)S(1)} %collective-permute-done.18.g_ref), custom_call_target="tpu_custom_call" | custom-call | flops 10000000 | bytes 1048576 | tf_op jit(solution)/shard_map/pallas_call | solution.py:740
  (22 shorter events, 0.1 us)
Async XLA Ops:
  0.7 1.4 %copy-start = (f32[64,25,256]{2,0,1:T(8,128)S(1)}, f32[64,25,256]{2,0,1:T(8,128)}, u32[]{:S(2)}) copy-start(f32[64,25,256]{2,0,1:T(8,128)} %param.10) | copy-start | bytes 4915204
  2.1 0.7 %copy-start.6 = (f32[12,2,2,25]{3,2,1,0:T(2,128)S(1)}, f32[12,2,2,25]{3,2,1,0:T(2,128)}, u32[]{:S(2)}) copy-start(f32[12,2,2,25]{3,2,1,0:T(2,128)} %moments_ref.1) | copy-start | bytes 14404
  2.9 2.0 %copy-start.3 = (f32[2,2,2,32,256]{4,3,2,1,0:T(8,128)S(1)}, f32[2,2,2,32,256]{4,3,2,1,0:T(8,128)}, u32[]{:S(2)}) copy-start(f32[2,2,2,32,256]{4,3,2,1,0:T(8,128)} %refs_0_.1) | copy-start | bytes 786436
  2.9 37.5 %copy-start.7 = (s32[2,2]{1,0:T(2,128)S(1)}, s32[2,2]{1,0:T(2,128)}, u32[]{:S(2)}) copy-start(s32[2,2]{1,0:T(2,128)} %param.14) | copy-start | bytes 52
  2.9 37.5 %copy-start.8 = (f32[8]{0:T(128)S(1)}, f32[8]{0:T(128)}, u32[]{:S(2)}) copy-start(f32[8]{0:T(128)} %param.15) | copy-start | bytes 100
  4.3 2.0 %collective-permute-start.1 = (f32[72,512]{1,0:T(8,128)S(1)}, f32[72,512]{1,0:T(8,128)S(1)}, u32[]{:S(2)}, u32[]{:S(2)}) collective-permute-start(f32[72,512]{1,0:T(8,128)S(1)} %get-tuple-element.25), channel_id=1, source_target_pairs={{0,1},{1,0},{2,3},{3,2},{4,5},{5,4},{6,7},{7,6},{8,9},{9,8},{10,11... | collective-permute-start | bytes 442376 | tf_op jit(solution)/shard_map/ppermute | solution.py:622
  4.9 1.4 %collective-permute-start = (f32[2,2,32,256]{3,2,1,0:T(8,128)S(1)}, f32[2,2,32,256]{3,2,1,0:T(8,128)S(1)}, u32[]{:S(2)}, u32[]{:S(2)}) collective-permute-start(f32[2,2,32,256]{3,2,1,0:T(8,128)S(1)} %dynamic-slice_bitcast_fusion), channel_id=1, source_target_pairs={{0,1},{1,0},{2,3},{3,2},{4,5},{5,4},{6,7},{7,6},{8,9},{9,8},{10,11... | collective-permute-start | bytes 393224 | tf_op jit(solution)/shard_map/ppermute | solution.py:622
  7.1 10.4 %collective-permute-start.2 = (f32[136,128]{1,0:T(8,128)S(1)}, f32[136,128]{1,0:T(8,128)S(1)}, u32[]{:S(2)}, u32[]{:S(2)}) collective-permute-start(f32[136,128]{1,0:T(8,128)S(1)} %get-tuple-element.27), channel_id=1, source_target_pairs={{0,2},{1,3},{2,0},{3,1},{4,6},{5,7},{6,4},{7,5},{8,10},{9,11},{10,... | collective-permute-start | bytes 208904 | tf_op jit(solution)/shard_map/ppermute | solution.py:622
  9.8 8.9 %collective-permute-start.3 = (f32[136,128]{1,0:T(8,128)S(1)}, f32[136,128]{1,0:T(8,128)S(1)}, u32[]{:S(2)}, u32[]{:S(2)}) collective-permute-start(f32[136,128]{1,0:T(8,128)S(1)} %get-tuple-element.28), channel_id=1, source_target_pairs={{0,12},{1,13},{2,14},{3,15},{4,8},{5,9},{6,10},{7,11},{8,4},{9,5},... | collective-permute-start | bytes 208904 | tf_op jit(solution)/shard_map/ppermute | solution.py:622
  13.4 7.4 %collective-permute-start.4 = (f32[136,128]{1,0:T(8,128)S(1)}, f32[136,128]{1,0:T(8,128)S(1)}, u32[]{:S(2)}, u32[]{:S(2)}) collective-permute-start(f32[136,128]{1,0:T(8,128)S(1)} %get-tuple-element.29), channel_id=1, source_target_pairs={{0,14},{1,15},{2,12},{3,13},{4,10},{5,11},{6,8},{7,9},{8,6},{9,7},... | collective-permute-start | bytes 208904 | tf_op jit(solution)/shard_map/ppermute | solution.py:622
  13.4 11.3 %collective-permute-start.5 = (f32[136,128]{1,0:T(8,128)S(1)}, f32[136,128]{1,0:T(8,128)S(1)}, u32[]{:S(2)}, u32[]{:S(2)}) collective-permute-start(f32[136,128]{1,0:T(8,128)S(1)} %get-tuple-element.30), channel_id=1, source_target_pairs={{0,8},{1,9},{2,10},{3,11},{4,12},{5,13},{6,14},{7,15},{8,0},{9,1},... | collective-permute-start | bytes 208904 | tf_op jit(solution)/shard_map/ppermute | solution.py:622
  14.4 11.2 %collective-permute-start.6 = (f32[136,128]{1,0:T(8,128)S(1)}, f32[136,128]{1,0:T(8,128)S(1)}, u32[]{:S(2)}, u32[]{:S(2)}) collective-permute-start(f32[136,128]{1,0:T(8,128)S(1)} %get-tuple-element.31), channel_id=1, source_target_pairs={{0,10},{1,11},{2,8},{3,9},{4,14},{5,15},{6,12},{7,13},{8,2},{9,3},... | collective-permute-start | bytes 208904 | tf_op jit(solution)/shard_map/ppermute | solution.py:622
  17.4 8.1 %collective-permute-start.7 = (f32[136,128]{1,0:T(8,128)S(1)}, f32[136,128]{1,0:T(8,128)S(1)}, u32[]{:S(2)}, u32[]{:S(2)}) collective-permute-start(f32[136,128]{1,0:T(8,128)S(1)} %get-tuple-element.32), channel_id=1, source_target_pairs={{0,4},{1,5},{2,6},{3,7},{4,0},{5,1},{6,2},{7,3},{8,12},{9,13},{10,... | collective-permute-start | bytes 208904 | tf_op jit(solution)/shard_map/ppermute | solution.py:622
  18.7 7.0 %collective-permute-start.8 = (f32[136,128]{1,0:T(8,128)S(1)}, f32[136,128]{1,0:T(8,128)S(1)}, u32[]{:S(2)}, u32[]{:S(2)}) collective-permute-start(f32[136,128]{1,0:T(8,128)S(1)} %get-tuple-element.33), channel_id=1, source_target_pairs={{0,6},{1,7},{2,4},{3,5},{4,2},{5,3},{6,0},{7,1},{8,14},{9,15},{10,... | collective-permute-start | bytes 208904 | tf_op jit(solution)/shard_map/ppermute | solution.py:622
  27.7 0.7 %copy-start.1 = (f32[4,2,32,256]{3,2,1,0:T(8,128)}, f32[4,2,32,256]{3,2,1,0:T(8,128)S(1)}, u32[]{:S(2)}) copy-start(f32[4,2,32,256]{3,2,1,0:T(8,128)S(1)} %get-tuple-element.39.__0_) | copy-start | bytes 786436
  28.4 8.3 %collective-permute-start.9 = (f32[4,2,16,128]{3,2,1,0:T(8,128)S(1)}, f32[4,2,16,128]{3,2,1,0:T(8,128)S(1)}, u32[]{:S(2)}, u32[]{:S(2)}) collective-permute-start(f32[4,2,16,128]{3,2,1,0:T(8,128)S(1)} %get-tuple-element.34.own_ref), channel_id=1, source_target_pairs={{0,2},{1,3},{2,0},{3,1},{4,6},{5,7},{6,4},{7,5},{8,10},{9,11},{10,... | collective-permute-start | bytes 196616 | tf_op jit(solution)/shard_map/ppermute | solution.py:622
  29.7 18.4 %collective-permute-start.11 = (f32[18,32,128]{2,1,0:T(8,128)S(1)}, f32[18,32,128]{2,1,0:T(8,128)S(1)}, u32[]{:S(2)}, u32[]{:S(2)}) collective-permute-start(f32[18,32,128]{2,1,0:T(8,128)S(1)} %get-tuple-element.36), channel_id=1, source_target_pairs={{0,14},{1,15},{2,4},{3,5},{4,2},{5,3},{6,8},{7,9},{8,6},{9,7},{10,... | collective-permute-start | bytes 884744 | tf_op jit(solution)/shard_map/ppermute | solution.py:622
  36.7 0.6 copy-start.4
  37.4 16.7 %collective-permute-start.16 = (f32[4,2,32,256]{3,2,1,0:T(8,128)}, f32[4,2,32,256]{3,2,1,0:T(8,128)S(1)}, u32[]{:S(2)}, u32[]{:S(2)}) collective-permute-start(f32[4,2,32,256]{3,2,1,0:T(8,128)} %shard_map.87.f_ref), channel_id=1, source_target_pairs={{0,2},{1,3},{2,0},{3,1},{4,6},{5,7},{6,4},{7,5},{8,10},{9,11},{10,... | collective-permute-start | bytes 786440 | tf_op jit(solution)/shard_map/ppermute | solution.py:622
  40.5 7.6 %collective-permute-start.10 = (f32[10,32,128]{2,1,0:T(8,128)S(1)}, f32[10,32,128]{2,1,0:T(8,128)S(1)}, u32[]{:S(2)}, u32[]{:S(2)}) collective-permute-start(f32[10,32,128]{2,1,0:T(8,128)S(1)} %get-tuple-element.35), channel_id=1, source_target_pairs={{0,12},{1,13},{2,6},{3,7},{4,0},{5,1},{6,10},{7,11},{8,4},{9,5},{1... | collective-permute-start | bytes 491528 | tf_op jit(solution)/shard_map/ppermute | solution.py:622
  41.3 6.9 %collective-permute-start.12 = (f32[2,2,32,256]{3,2,1,0:T(8,128)S(1)}, f32[2,2,32,256]{3,2,1,0:T(8,128)S(1)}, u32[]{:S(2)}, u32[]{:S(2)}) collective-permute-start(f32[2,2,32,256]{3,2,1,0:T(8,128)S(1)} %get-tuple-element.37), channel_id=1, source_target_pairs={{0,4},{1,5},{2,14},{3,15},{4,8},{5,9},{6,2},{7,3},{8,12},{9,13},{1... | collective-permute-start | bytes 393224 | tf_op jit(solution)/shard_map/ppermute | solution.py:622
  48.1 0.8 %copy-start.5 = (f32[4,2,16,128]{3,2,1,0:T(8,128)S(1)}, f32[4,2,16,128]{3,2,1,0:T(8,128)}, u32[]{:S(2)}) copy-start(f32[4,2,16,128]{3,2,1,0:T(8,128)} %copy-done.4) | copy-start | bytes 196612
  49.6 8.0 %collective-permute-start.13 = (f32[4,2,16,128]{3,2,1,0:T(8,128)S(1)}, f32[4,2,16,128]{3,2,1,0:T(8,128)S(1)}, u32[]{:S(2)}, u32[]{:S(2)}) collective-permute-start(f32[4,2,16,128]{3,2,1,0:T(8,128)S(1)} %shard_map.85.refs_0_), channel_id=1, source_target_pairs={{0,4},{1,5},{2,6},{3,7},{4,0},{5,1},{6,2},{7,3},{8,12},{9,13},{10,... | collective-permute-start | bytes 196616 | tf_op jit(solution)/shard_map/ppermute | solution.py:622
  49.6 7.9 %collective-permute-start.14 = (f32[4,2,16,128]{3,2,1,0:T(8,128)S(1)}, f32[4,2,16,128]{3,2,1,0:T(8,128)S(1)}, u32[]{:S(2)}, u32[]{:S(2)}) collective-permute-start(f32[4,2,16,128]{3,2,1,0:T(8,128)S(1)} %shard_map.85.refs_0_), channel_id=1, source_target_pairs={{0,8},{1,9},{2,10},{3,11},{4,12},{5,13},{6,14},{7,15},{8,0},{9,1},... | collective-permute-start | bytes 196616 | tf_op jit(solution)/shard_map/ppermute | solution.py:622
  50.6 7.0 %collective-permute-start.15 = (f32[4,2,16,128]{3,2,1,0:T(8,128)S(1)}, f32[4,2,16,128]{3,2,1,0:T(8,128)S(1)}, u32[]{:S(2)}, u32[]{:S(2)}) collective-permute-start(f32[4,2,16,128]{3,2,1,0:T(8,128)S(1)} %shard_map.85.refs_0_), channel_id=1, source_target_pairs={{0,12},{1,13},{2,14},{3,15},{4,8},{5,9},{6,10},{7,11},{8,4},{9,5},... | collective-permute-start | bytes 196616 | tf_op jit(solution)/shard_map/ppermute | solution.py:622
  54.0 1.0 %copy-start.2 = (f32[4,2,32,256]{3,2,1,0:T(8,128)S(1)}, f32[4,2,32,256]{3,2,1,0:T(8,128)}, u32[]{:S(2)}) copy-start(f32[4,2,32,256]{3,2,1,0:T(8,128)} %shard_map.87.f_ref) | copy-start | bytes 786436
  57.5 4.5 %collective-permute-start.18 = (f32[2,2,32,256]{3,2,1,0:T(8,128)S(1)}, f32[2,2,32,256]{3,2,1,0:T(8,128)S(1)}, u32[]{:S(2)}, u32[]{:S(2)}) collective-permute-start(f32[2,2,32,256]{3,2,1,0:T(8,128)S(1)} %get-tuple-element.42), channel_id=1, source_target_pairs={{0,1},{1,0},{2,3},{3,2},{4,5},{5,4},{6,7},{7,6},{8,9},{9,8},{10,11... | collective-permute-start | bytes 393224 | tf_op jit(solution)/shard_map/ppermute | solution.py:622
  60.5 1.5 %collective-permute-start.17 = (f32[5,2,16,128]{3,2,1,0:T(8,128)S(1)}, f32[5,2,16,128]{3,2,1,0:T(8,128)S(1)}, u32[]{:S(2)}, u32[]{:S(2)}) collective-permute-start(f32[5,2,16,128]{3,2,1,0:T(8,128)S(1)} %get-tuple-element.41), channel_id=1, source_target_pairs={{0,1},{1,0},{2,3},{3,2},{4,5},{5,4},{6,7},{7,6},{8,9},{9,8},{10,11... | collective-permute-start | bytes 245768 | tf_op jit(solution)/shard_map/ppermute | solution.py:622

commit v11 on v6

--- a/solution.py
+++ b/solution.py
@@ -106,17 +106,17 @@
     return jnp.sum(jnp.where(i == j, row, 0.0), axis=1, keepdims=True)
 
 
-def rows_kernel(moments_ref, shapes_ref, atom_ref, tile_ref, line_ref, keep_ref, send_ref, rows):
+def rows_kernel(moments_ref, shapes_ref, slots_ref, keep_ref, send_ref, rows):
     core = lax.rem(lax.axis_index("grid"), 2)
     channels, slots, depth = shapes_ref.shape
-    atoms = moments_ref.shape[0]
-    atom = as_column(atom_ref[...].astype(jnp.float32))
+    atoms = moments_ref.shape[1]
+    atom = as_column(slots_ref[0:1].astype(jnp.float32))
     picks = [jnp.where(atom == float(a), 1.0, 0.0) for a in range(atoms)]
     chosen = []
     for f in range(4):
         total = None
         for a in range(atoms):
-            value = picks[a] * moments_ref[a, f // 2, f % 2 : f % 2 + 1]
+            value = picks[a] * moments_ref[f, a : a + 1]
             total = value if total is None else total + value
         chosen.append(total)
     for i in range(slots // 8):
@@ -132,11 +132,11 @@
     keep_ref[...] = rows[core]
     send_ref[0:slots] = rows[1 - core]
     send_ref[slots:] = jnp.zeros((8, 2 * depth), jnp.float32)
-    number = (tile_ref[...] * 64 + line_ref[...]).astype(jnp.float32)
+    number = (slots_ref[1:2] * 64 + slots_ref[2:3]).astype(jnp.float32)
     send_ref[slots : slots + 1, 0:slots] = number
 
 
-def pack_kernel(own_ref, got_ref, tile_ref, line_ref, _, *out_refs):
+def pack_kernel(own_ref, got_ref, slots_ref, _, *out_refs):
     slots = own_ref.shape[0]
     apart = len(out_refs) > 1
     height = out_refs[0].shape[-2]
@@ -144,7 +144,7 @@
     capacity = ranks // 4
     chips = lax.axis_size("grid") // 2
     chip = lax.div(lax.axis_index("grid"), 2)
-    number = (tile_ref[...] * 64 + line_ref[...]).astype(jnp.float32)
+    number = (slots_ref[1:2] * 64 + slots_ref[2:3]).astype(jnp.float32)
     number = jnp.concatenate([number, got_ref[slots : slots + 1, 0:slots]], axis=1).astype(jnp.int32)
     tile, line = number // 64, number % 128 + 1
     column = as_column(tile.astype(jnp.float32)).astype(jnp.int32)
@@ -659,25 +659,26 @@
     cs = pair_phases(pair_table, k_fraction)
 
     other = permute(lax.dynamic_index_in_dim(pair_density, 1 - core, 0, False), partner)
-    tile_row, line_row = slot_tile.reshape(1, -1), slot_row.reshape(1, -1)
+    slots = jnp.stack([slot_atom, slot_tile[:, 0], slot_row])
+    fields = moments.reshape(moments.shape[0], 4, -1).transpose(1, 0, 2)
     row = 2 * depth
     kept, sent = call(
         rows_kernel,
         [shaped(slot_count, row), shaped(slot_count + 8, row)],
-        vmem(5),
+        vmem(3),
         [(2, slot_count, row)],
         10**7,
-    )(moments, shapes.transpose(1, 0, 2), slot_atom.reshape(1, -1), tile_row, line_row)
+    )(fields, shapes.transpose(1, 0, 2), slots)
     got = permute(sent, partner)
     apart = chips <= 8
     height = 16 * capacity + 8
     packed = call(
         pack_kernel,
         [shaped(height, 128)] * chips if apart else [shaped(chips, height, 128)],
-        vmem(4) + [pl.BlockSpec(memory_space=pl.ANY)],
+        vmem(3) + [pl.BlockSpec(memory_space=pl.ANY)],
         [],
         10**8,
-    )(kept, got, tile_row, line_row, other)
+    )(kept, got, slots, other)
     if apart:
         received = [
             permute(packed[k], lambda i, k=k: i ^ (2 * k)) if k else packed[k]

time: 61 us -> 59.6 us (0.977)
  local copies, waits for them, and re-layouts: 4.19 us -> 2.19 us
  other arithmetic: 0.45 us -> 1.15 us
    unnamed x20 -> x9, local copies, waits for them, and re-layouts: 4.18 us -> 2.18 us
    another operation x0 -> x1, other arithmetic: none -> 0.7 us  [per_device(): slots = jnp.stack([slot_atom, slot_tile[:, 0], slot_row])]
where the time goes in v11:
time: 59.6 us; the launch traced here: 59.4 us
  starting transfers between devices  23.4 us (39%)
  waiting for transfers between devices  18.4 us (31%)
  Pallas kernels  14.2 us (24%)
  local copies, waits for them, and re-layouts  2.19 us (4%)
  other arithmetic  1.15 us (2%)
    ppermute x18, starting transfers between devices, permute(): return lax.ppermute(value, 'grid', [(i, target(i)) for i in devices])  23.4 us
    ppermute x18, waiting for transfers between devices, permute(): return lax.ppermute(value, 'grid', [(i, target(i)) for i in devices])  18.4 us
    pallas_call x1, Pallas kernels, per_device(): call(cycle_kernel, [shaped(5, *small)] * 2, vmem(len(pieces)) + smem, [(n...  2.93 us
    pallas_call x1, Pallas kernels, per_device(): call(fine_kernel, [shaped(thick, *full)] * 2, vmem(5) + smem, [(3 * plane...  2.73 us
    pallas_call x1, Pallas kernels, per_device(): call(source_kernel, shaped(planes, *small), vmem(4) + smem, [(4 * planes,...  2.51 us
    unnamed x9, local copies, waits for them, and re-layouts  2.18 us
    pallas_call x1, Pallas kernels, per_device(): call(output_kernel, shaped(*pair_density.shape), vmem(3), scratch, 10 ** 7)  1.61 us
    pallas_call x1, Pallas kernels, per_device(): call(rows_kernel, [shaped(slot_count, row), shaped(slot_count + 8, row)],...  1.46 us
  transfers between devices with their start and end apart: 18, of which 10 were waited for; matrix products, arithmetic and copies ran while one was open for 1% of the time, Pallas kernels for 15%

profile of v11, /device:TPU:0, one launch (start us, length us, event | category | flops | bytes accessed | tf_op | source)
XLA Modules:
  0.0 59.4 jit_solution(3231491120269450107)
XLA Ops:
  0.0 0.7 %copy.11 = f32[12,2,2,25]{3,0,2,1:T(8,128)S(1)} copy(f32[12,2,2,25]{3,2,1,0:T(2,128)} %param.9) | data formatting | bytes 9600 | tf_op args[1]
  0.7 0.7 %pad_add_fusion.slots_ref = s32[3,64]{1,0:T(4,128)S(1)} fusion(s32[1,64]{1,0:T(1,128)} %bitcast.11, s32[1,64]{1,0:T(1,128)} %bitcast.12, s32[1,64]{1,0:T(1,128)} %bitcast.13), kind=kLoop, calls=%fused_computation.3 | loop fusion | flops 384 | bytes 1536 | tf_op jit(solution)/shard_map/stack | solution.py:662
  1.4 1.4 %copy-done = f32[64,25,256]{2,0,1:T(8,128)S(1)} copy-done((f32[64,25,256]{2,0,1:T(8,128)S(1)}, f32[64,25,256]{2,0,1:T(8,128)}, u32[]{:S(2)}) %copy-start) | copy-done | bytes 1638424
  2.9 1.5 %shard_map.82 = (f32[64,512]{1,0:T(8,128)S(1)}, f32[72,512]{1,0:T(8,128)S(1)}) custom-call(f32[4,12,25]{2,1,0:T(8,128)S(1)} %bitcast.10, f32[25,64,256]{2,1,0:T(8,128)S(1)} %bitcast.9, s32[3,64]{1,0:T(4,128)S(1)} %pad_add_fusion.slots_ref), custom_call_target="tpu_custom_call" | custom-call | flops 10000000 | bytes 1048576 | tf_op jit(solution)/shard_map/pallas_call | solution.py:665
  4.3 0.5 collective-permute-start.1
  4.9 0.1 collective-permute-start
  5.0 1.3 %collective-permute-done._.refs_1_ = f32[2,2,32,256]{3,2,1,0:T(8,128)S(1)} collective-permute-done((f32[2,2,32,256]{3,2,1,0:T(8,128)S(1)}, f32[2,2,32,256]{3,2,1,0:T(8,128)S(1)}, u32[]{:S(2)}, u32[]{:S(2)}) %collective-permute-start) | collective-permute-done | bytes 131104 | tf_op jit(solution)/shard_map/ppermute | solution.py:642
  6.3 0.0 collective-permute-done.1.got_ref
  6.3 0.8 %shard_map.83 = (f32[136,128]{1,0:T(8,128)S(1)}, f32[136,128]{1,0:T(8,128)S(1)}, f32[136,128]{1,0:T(8,128)S(1)}, f32[136,128]{1,0:T(8,128)S(1)}, f32[136,128]{1,...) custom-call(f32[64,512]{1,0:T(8,128)S(1)} %get-tuple-element.22.own_ref, ...), custom_call_target="tpu_custom_call" | custom-call | flops 100000000 | bytes 1048576 | tf_op jit(solution)/shard_map/pallas_call | solution.py:675
  7.1 2.7 %collective-permute-start.2 = (f32[136,128]{1,0:T(8,128)S(1)}, f32[136,128]{1,0:T(8,128)S(1)}, u32[]{:S(2)}, u32[]{:S(2)}) collective-permute-start(f32[136,128]{1,0:T(8,128)S(1)} %get-tuple-element.25), channel_id=1, source_target_pairs={{0,2},{1,3},{2,0},{3,1},{4,6},{5,7},{6,4},{7,5},{8,10},{9,11},{10,... | collective-permute-start | bytes 208904 | tf_op jit(solution)/shard_map/ppermute | solution.py:642
  9.8 3.6 %collective-permute-start.3 = (f32[136,128]{1,0:T(8,128)S(1)}, f32[136,128]{1,0:T(8,128)S(1)}, u32[]{:S(2)}, u32[]{:S(2)}) collective-permute-start(f32[136,128]{1,0:T(8,128)S(1)} %get-tuple-element.26), channel_id=1, source_target_pairs={{0,12},{1,13},{2,14},{3,15},{4,8},{5,9},{6,10},{7,11},{8,4},{9,5},... | collective-permute-start | bytes 208904 | tf_op jit(solution)/shard_map/ppermute | solution.py:642
  13.4 0.0 collective-permute-start.4
  13.4 1.0 %collective-permute-start.5 = (f32[136,128]{1,0:T(8,128)S(1)}, f32[136,128]{1,0:T(8,128)S(1)}, u32[]{:S(2)}, u32[]{:S(2)}) collective-permute-start(f32[136,128]{1,0:T(8,128)S(1)} %get-tuple-element.28), channel_id=1, source_target_pairs={{0,8},{1,9},{2,10},{3,11},{4,12},{5,13},{6,14},{7,15},{8,0},{9,1},... | collective-permute-start | bytes 208904 | tf_op jit(solution)/shard_map/ppermute | solution.py:642
  14.4 3.1 %collective-permute-start.6 = (f32[136,128]{1,0:T(8,128)S(1)}, f32[136,128]{1,0:T(8,128)S(1)}, u32[]{:S(2)}, u32[]{:S(2)}) collective-permute-start(f32[136,128]{1,0:T(8,128)S(1)} %get-tuple-element.29), channel_id=1, source_target_pairs={{0,10},{1,11},{2,8},{3,9},{4,14},{5,15},{6,12},{7,13},{8,2},{9,3},... | collective-permute-start | bytes 208904 | tf_op jit(solution)/shard_map/ppermute | solution.py:642
  17.4 0.0 collective-permute-done.2.refs_3_
  17.4 1.2 %collective-permute-start.7 = (f32[136,128]{1,0:T(8,128)S(1)}, f32[136,128]{1,0:T(8,128)S(1)}, u32[]{:S(2)}, u32[]{:S(2)}) collective-permute-start(f32[136,128]{1,0:T(8,128)S(1)} %get-tuple-element.30), channel_id=1, source_target_pairs={{0,4},{1,5},{2,6},{3,7},{4,0},{5,1},{6,2},{7,3},{8,12},{9,13},{10,... | collective-permute-start | bytes 208904 | tf_op jit(solution)/shard_map/ppermute | solution.py:642
  18.7 0.0 collective-permute-done.3.refs_4_
  18.7 0.6 collective-permute-start.8
  19.2 1.6 %collective-permute-done.4.refs_5_ = f32[136,128]{1,0:T(8,128)S(1)} collective-permute-done((f32[136,128]{1,0:T(8,128)S(1)}, f32[136,128]{1,0:T(8,128)S(1)}, u32[]{:S(2)}, u32[]{:S(2)}) %collective-permute-start.4) | collective-permute-done | bytes 69664 | tf_op jit(solution)/shard_map/ppermute | solution.py:642
  20.8 3.9 %collective-permute-done.5.refs_6_ = f32[136,128]{1,0:T(8,128)S(1)} collective-permute-done((f32[136,128]{1,0:T(8,128)S(1)}, f32[136,128]{1,0:T(8,128)S(1)}, u32[]{:S(2)}, u32[]{:S(2)}) %collective-permute-start.5) | collective-permute-done | bytes 69664 | tf_op jit(solution)/shard_map/ppermute | solution.py:642
  24.7 0.9 %collective-permute-done.6.refs_7_ = f32[136,128]{1,0:T(8,128)S(1)} collective-permute-done((f32[136,128]{1,0:T(8,128)S(1)}, f32[136,128]{1,0:T(8,128)S(1)}, u32[]{:S(2)}, u32[]{:S(2)}) %collective-permute-start.6) | collective-permute-done | bytes 69664 | tf_op jit(solution)/shard_map/ppermute | solution.py:642
  25.6 0.0 collective-permute-done.7.refs_8_
  25.6 0.2 collective-permute-done.8.refs_9_
  25.7 1.2 %shard_map.84 = (f32[4,2,32,256]{3,2,1,0:T(8,128)S(1)}, f32[10,32,128]{2,1,0:T(8,128)S(1)}, f32[2,2,32,256]{3,2,1,0:T(8,128)S(1)}) custom-call(f32[2,2,2,32,256]{4,3,2,1,0:T(8,128)S(1)} %copy-done.1, f32[2,2,32,256]{3,2,1,0:T(8,128)S(1)} %collective-permute-done._.refs_1_, f32[136,128]{1,0:T(8,128)S(1)} %get-tuple-element.24.refs_2_, ...), custom_call_target="tpu_custom_call" | custom-call | flops 100000000 | bytes 1048576 | tf_op jit(solution)/shard_map/pallas_call | solution.py:697
  27.0 4.0 %collective-permute-start.10 = (f32[4,2,32,256]{3,2,1,0:T(8,128)S(1)}, f32[4,2,32,256]{3,2,1,0:T(8,128)S(1)}, u32[]{:S(2)}, u32[]{:S(2)}) collective-permute-start(f32[4,2,32,256]{3,2,1,0:T(8,128)S(1)} %get-tuple-element.32.f_ref), channel_id=1, source_target_pairs={{0,14},{1,15},{2,4},{3,5},{4,2},{5,3},{6,8},{7,9},{8,6},{9,7},{10,... | collective-permute-start | bytes 786440 | tf_op jit(solution)/shard_map/ppermute | solution.py:642
  30.9 0.0 collective-permute-start.9
  31.0 0.2 fusion
  31.1 1.4 %collective-permute-start.11 = (f32[10,32,128]{2,1,0:T(8,128)S(1)}, f32[10,32,128]{2,1,0:T(8,128)S(1)}, u32[]{:S(2)}, u32[]{:S(2)}) collective-permute-start(f32[10,32,128]{2,1,0:T(8,128)S(1)} %get-tuple-element.33), channel_id=1, source_target_pairs={{0,12},{1,13},{2,6},{3,7},{4,0},{5,1},{6,10},{7,11},{8,4},{9,5},{1... | collective-permute-start | bytes 491528 | tf_op jit(solution)/shard_map/ppermute | solution.py:642
  32.5 0.2 cosine_reduce_fusion
  32.7 0.7 %collective-permute-start.15 = (f32[2,2,32,256]{3,2,1,0:T(8,128)S(1)}, f32[2,2,32,256]{3,2,1,0:T(8,128)S(1)}, u32[]{:S(2)}, u32[]{:S(2)}) collective-permute-start(f32[2,2,32,256]{3,2,1,0:T(8,128)S(1)} %get-tuple-element.35), channel_id=1, source_target_pairs={{0,4},{1,5},{2,14},{3,15},{4,8},{5,9},{6,2},{7,3},{8,12},{9,13},{1... | collective-permute-start | bytes 393224 | tf_op jit(solution)/shard_map/ppermute | solution.py:642
  33.4 0.1 pad_maximum_fusion.cs_ref.refs_4_
  33.5 6.8 %collective-permute-done.11.straight_ref = f32[10,32,128]{2,1,0:T(8,128)S(1)} collective-permute-done((f32[10,32,128]{2,1,0:T(8,128)S(1)}, f32[10,32,128]{2,1,0:T(8,128)S(1)}, u32[]{:S(2)}, u32[]{:S(2)}) %collective-permute-start.11) | collective-permute-done | bytes 163872 | tf_op jit(solution)/shard_map/ppermute | solution.py:642
  40.3 0.0 collective-permute-done.10.odd_ref
  40.3 2.4 %collective-permute-done.9.even_ref = f32[4,2,32,256]{3,2,1,0:T(8,128)S(1)} collective-permute-done((f32[4,2,32,256]{3,2,1,0:T(8,128)S(1)}, f32[4,2,32,256]{3,2,1,0:T(8,128)S(1)}, u32[]{:S(2)}, u32[]{:S(2)}) %collective-permute-start.9) | collective-permute-done | bytes 262176 | tf_op jit(solution)/shard_map/ppermute | solution.py:642
  42.7 2.5 %shard_map.85.refs_0_ = f32[4,2,16,128]{3,2,1,0:T(8,128)S(1)} custom-call(f32[4,2,32,256]{3,2,1,0:T(8,128)S(1)} %collective-permute-done.9.even_ref, f32[4,2,32,256]{3,2,1,0:T(8,128)S(1)} %collective-permute-done.10.odd_ref, f32[10,32,128]{2,1,0:T(8,128)S(1)} %collective-permute-done.11.straight_ref, f32[4,2,32,256]{3,2,1,0:T(8,128)S(1)} %get-tuple-element.32.f_ref, ...), custom_call_target="tpu_custom_call" | custom-call | flops 10000000 | bytes 1048576 | tf_op jit(solution)/shard_map/pallas_call | solution.py:708
  45.2 0.1 collective-permute-start.12
  45.3 2.1 %collective-permute-start.13 = (f32[4,2,16,128]{3,2,1,0:T(8,128)S(1)}, f32[4,2,16,128]{3,2,1,0:T(8,128)S(1)}, u32[]{:S(2)}, u32[]{:S(2)}) collective-permute-start(f32[4,2,16,128]{3,2,1,0:T(8,128)S(1)} %shard_map.85.refs_0_), channel_id=1, source_target_pairs={{0,8},{1,9},{2,10},{3,11},{4,12},{5,13},{6,14},{7,15},{8,0},{9,1},... | collective-permute-start | bytes 196616 | tf_op jit(solution)/shard_map/ppermute | solution.py:642
  47.3 2.3 %collective-permute-start.14 = (f32[4,2,16,128]{3,2,1,0:T(8,128)S(1)}, f32[4,2,16,128]{3,2,1,0:T(8,128)S(1)}, u32[]{:S(2)}, u32[]{:S(2)}) collective-permute-start(f32[4,2,16,128]{3,2,1,0:T(8,128)S(1)} %shard_map.85.refs_0_), channel_id=1, source_target_pairs={{0,12},{1,13},{2,14},{3,15},{4,8},{5,9},{6,10},{7,11},{8,4},{9,5},... | collective-permute-start | bytes 196616 | tf_op jit(solution)/shard_map/ppermute | solution.py:642
  49.6 2.7 %shard_map.87 = (f32[2,2,32,256]{3,2,1,0:T(8,128)S(1)}, f32[2,2,32,256]{3,2,1,0:T(8,128)S(1)}) custom-call(f32[4,2,32,256]{3,2,1,0:T(8,128)S(1)} %collective-permute-done.9.even_ref, f32[4,2,32,256]{3,2,1,0:T(8,128)S(1)} %collective-permute-done.10.odd_ref, f32[10,32,128]{2,1,0:T(8,128)S(1)} %collective-permute-done.11.straight_ref, ...), custom_call_target="tpu_custom_call" | custom-call | flops 10000000 | bytes 1048576 | tf_op jit(solution)/shard_map/pallas_call | solution.py:716
  52.4 0.1 collective-permute-start.17
  52.5 0.3 collective-permute-done.13.refs_2_
  52.7 0.8 %collective-permute-done.14.refs_3_ = f32[4,2,16,128]{3,2,1,0:T(8,128)S(1)} collective-permute-done((f32[4,2,16,128]{3,2,1,0:T(8,128)S(1)}, f32[4,2,16,128]{3,2,1,0:T(8,128)S(1)}, u32[]{:S(2)}, u32[]{:S(2)}) %collective-permute-start.14) | collective-permute-done | bytes 65568 | tf_op jit(solution)/shard_map/ppermute | solution.py:642
  53.5 2.9 %shard_map.86 = (f32[5,2,16,128]{3,2,1,0:T(8,128)S(1)}, f32[5,2,16,128]{3,2,1,0:T(8,128)S(1)}) custom-call(f32[4,2,16,128]{3,2,1,0:T(8,128)S(1)} %shard_map.85.refs_0_, f32[4,2,16,128]{3,2,1,0:T(8,128)S(1)} %collective-permute-done.12.refs_1_, f32[4,2,16,128]{3,2,1,0:T(8,128)S(1)} %collective-permute-done.13.refs_2_, ...), custom_call_target="tpu_custom_call" | custom-call | flops 100000000 | bytes 1048576 | tf_op jit(solution)/shard_map/pallas_call | solution.py:727
  56.5 0.1 collective-permute-start.16
  56.5 0.9 %shard_map.88.own_ref = f32[2,2,32,256]{3,2,1,0:T(8,128)S(1)} custom-call(f32[5,2,16,128]{3,2,1,0:T(8,128)S(1)} %get-tuple-element.34.w_ref, f32[2,2,32,256]{3,2,1,0:T(8,128)S(1)} %get-tuple-element.36.g_ref), custom_call_target="tpu_custom_call" | custom-call | flops 10000000 | bytes 1048576 | tf_op jit(solution)/shard_map/pallas_call | solution.py:748
  57.4 0.0 collective-permute-done.17.g_ref
  57.5 0.3 collective-permute-done.16.w_ref
  57.8 1.6 %shard_map.89 = f32[2,2,2,32,256]{4,3,2,1,0:T(8,128)} custom-call(f32[2,2,32,256]{3,2,1,0:T(8,128)S(1)} %shard_map.88.own_ref, f32[5,2,16,128]{3,2,1,0:T(8,128)S(1)} %collective-permute-done.16.w_ref, f32[2,2,32,256]{3,2,1,0:T(8,128)S(1)} %collective-permute-done.17.g_ref), custom_call_target="tpu_custom_call" | custom-call | flops 10000000 | bytes 1048576 | tf_op jit(solution)/shard_map/pallas_call | solution.py:749
  (10 shorter events, 0.0 us)
Async XLA Ops:
  1.4 1.4 %copy-start = (f32[64,25,256]{2,0,1:T(8,128)S(1)}, f32[64,25,256]{2,0,1:T(8,128)}, u32[]{:S(2)}) copy-start(f32[64,25,256]{2,0,1:T(8,128)} %param.10) | copy-start | bytes 4915204
  2.9 2.0 %copy-start.1 = (f32[2,2,2,32,256]{4,3,2,1,0:T(8,128)S(1)}, f32[2,2,2,32,256]{4,3,2,1,0:T(8,128)}, u32[]{:S(2)}) copy-start(f32[2,2,2,32,256]{4,3,2,1,0:T(8,128)} %refs_0_.1) | copy-start | bytes 786436
  2.9 28.1 %copy-start.2 = (s32[2,2]{1,0:T(2,128)S(1)}, s32[2,2]{1,0:T(2,128)}, u32[]{:S(2)}) copy-start(s32[2,2]{1,0:T(2,128)} %param.14) | copy-start | bytes 52
  2.9 28.1 %copy-start.3 = (f32[8]{0:T(128)S(1)}, f32[8]{0:T(128)}, u32[]{:S(2)}) copy-start(f32[8]{0:T(128)} %param.15) | copy-start | bytes 100
  4.3 2.0 %collective-permute-start.1 = (f32[72,512]{1,0:T(8,128)S(1)}, f32[72,512]{1,0:T(8,128)S(1)}, u32[]{:S(2)}, u32[]{:S(2)}) collective-permute-start(f32[72,512]{1,0:T(8,128)S(1)} %get-tuple-element.23), channel_id=1, source_target_pairs={{0,1},{1,0},{2,3},{3,2},{4,5},{5,4},{6,7},{7,6},{8,9},{9,8},{10,11... | collective-permute-start | bytes 442376 | tf_op jit(solution)/shard_map/ppermute | solution.py:642
  4.9 1.4 %collective-permute-start = (f32[2,2,32,256]{3,2,1,0:T(8,128)S(1)}, f32[2,2,32,256]{3,2,1,0:T(8,128)S(1)}, u32[]{:S(2)}, u32[]{:S(2)}) collective-permute-start(f32[2,2,32,256]{3,2,1,0:T(8,128)S(1)} %dynamic-slice_bitcast_fusion), channel_id=1, source_target_pairs={{0,1},{1,0},{2,3},{3,2},{4,5},{5,4},{6,7},{7,6},{8,9},{9,8},{10,11... | collective-permute-start | bytes 393224 | tf_op jit(solution)/shard_map/ppermute | solution.py:642
  7.1 10.3 %collective-permute-start.2 = (f32[136,128]{1,0:T(8,128)S(1)}, f32[136,128]{1,0:T(8,128)S(1)}, u32[]{:S(2)}, u32[]{:S(2)}) collective-permute-start(f32[136,128]{1,0:T(8,128)S(1)} %get-tuple-element.25), channel_id=1, source_target_pairs={{0,2},{1,3},{2,0},{3,1},{4,6},{5,7},{6,4},{7,5},{8,10},{9,11},{10,... | collective-permute-start | bytes 208904 | tf_op jit(solution)/shard_map/ppermute | solution.py:642
  9.8 8.9 %collective-permute-start.3 = (f32[136,128]{1,0:T(8,128)S(1)}, f32[136,128]{1,0:T(8,128)S(1)}, u32[]{:S(2)}, u32[]{:S(2)}) collective-permute-start(f32[136,128]{1,0:T(8,128)S(1)} %get-tuple-element.26), channel_id=1, source_target_pairs={{0,12},{1,13},{2,14},{3,15},{4,8},{5,9},{6,10},{7,11},{8,4},{9,5},... | collective-permute-start | bytes 208904 | tf_op jit(solution)/shard_map/ppermute | solution.py:642
  13.4 7.4 %collective-permute-start.4 = (f32[136,128]{1,0:T(8,128)S(1)}, f32[136,128]{1,0:T(8,128)S(1)}, u32[]{:S(2)}, u32[]{:S(2)}) collective-permute-start(f32[136,128]{1,0:T(8,128)S(1)} %get-tuple-element.27), channel_id=1, source_target_pairs={{0,14},{1,15},{2,12},{3,13},{4,10},{5,11},{6,8},{7,9},{8,6},{9,7},... | collective-permute-start | bytes 208904 | tf_op jit(solution)/shard_map/ppermute | solution.py:642
  13.4 11.3 %collective-permute-start.5 = (f32[136,128]{1,0:T(8,128)S(1)}, f32[136,128]{1,0:T(8,128)S(1)}, u32[]{:S(2)}, u32[]{:S(2)}) collective-permute-start(f32[136,128]{1,0:T(8,128)S(1)} %get-tuple-element.28), channel_id=1, source_target_pairs={{0,8},{1,9},{2,10},{3,11},{4,12},{5,13},{6,14},{7,15},{8,0},{9,1},... | collective-permute-start | bytes 208904 | tf_op jit(solution)/shard_map/ppermute | solution.py:642
  14.4 11.2 %collective-permute-start.6 = (f32[136,128]{1,0:T(8,128)S(1)}, f32[136,128]{1,0:T(8,128)S(1)}, u32[]{:S(2)}, u32[]{:S(2)}) collective-permute-start(f32[136,128]{1,0:T(8,128)S(1)} %get-tuple-element.29), channel_id=1, source_target_pairs={{0,10},{1,11},{2,8},{3,9},{4,14},{5,15},{6,12},{7,13},{8,2},{9,3},... | collective-permute-start | bytes 208904 | tf_op jit(solution)/shard_map/ppermute | solution.py:642
  17.4 8.1 %collective-permute-start.7 = (f32[136,128]{1,0:T(8,128)S(1)}, f32[136,128]{1,0:T(8,128)S(1)}, u32[]{:S(2)}, u32[]{:S(2)}) collective-permute-start(f32[136,128]{1,0:T(8,128)S(1)} %get-tuple-element.30), channel_id=1, source_target_pairs={{0,4},{1,5},{2,6},{3,7},{4,0},{5,1},{6,2},{7,3},{8,12},{9,13},{10,... | collective-permute-start | bytes 208904 | tf_op jit(solution)/shard_map/ppermute | solution.py:642
  18.7 7.1 %collective-permute-start.8 = (f32[136,128]{1,0:T(8,128)S(1)}, f32[136,128]{1,0:T(8,128)S(1)}, u32[]{:S(2)}, u32[]{:S(2)}) collective-permute-start(f32[136,128]{1,0:T(8,128)S(1)} %get-tuple-element.31), channel_id=1, source_target_pairs={{0,6},{1,7},{2,4},{3,5},{4,2},{5,3},{6,0},{7,1},{8,14},{9,15},{10,... | collective-permute-start | bytes 208904 | tf_op jit(solution)/shard_map/ppermute | solution.py:642
  27.0 13.3 %collective-permute-start.10 = (f32[4,2,32,256]{3,2,1,0:T(8,128)S(1)}, f32[4,2,32,256]{3,2,1,0:T(8,128)S(1)}, u32[]{:S(2)}, u32[]{:S(2)}) collective-permute-start(f32[4,2,32,256]{3,2,1,0:T(8,128)S(1)} %get-tuple-element.32.f_ref), channel_id=1, source_target_pairs={{0,14},{1,15},{2,4},{3,5},{4,2},{5,3},{6,8},{7,9},{8,6},{9,7},{10,... | collective-permute-start | bytes 786440 | tf_op jit(solution)/shard_map/ppermute | solution.py:642
  30.9 11.7 %collective-permute-start.9 = (f32[4,2,32,256]{3,2,1,0:T(8,128)S(1)}, f32[4,2,32,256]{3,2,1,0:T(8,128)S(1)}, u32[]{:S(2)}, u32[]{:S(2)}) collective-permute-start(f32[4,2,32,256]{3,2,1,0:T(8,128)S(1)} %get-tuple-element.32.f_ref), channel_id=1, source_target_pairs={{0,2},{1,3},{2,0},{3,1},{4,6},{5,7},{6,4},{7,5},{8,10},{9,11},{10,... | collective-permute-start | bytes 786440 | tf_op jit(solution)/shard_map/ppermute | solution.py:642
  31.1 9.2 %collective-permute-start.11 = (f32[10,32,128]{2,1,0:T(8,128)S(1)}, f32[10,32,128]{2,1,0:T(8,128)S(1)}, u32[]{:S(2)}, u32[]{:S(2)}) collective-permute-start(f32[10,32,128]{2,1,0:T(8,128)S(1)} %get-tuple-element.33), channel_id=1, source_target_pairs={{0,12},{1,13},{2,6},{3,7},{4,0},{5,1},{6,10},{7,11},{8,4},{9,5},{1... | collective-permute-start | bytes 491528 | tf_op jit(solution)/shard_map/ppermute | solution.py:642
  32.7 16.9 %collective-permute-start.15 = (f32[2,2,32,256]{3,2,1,0:T(8,128)S(1)}, f32[2,2,32,256]{3,2,1,0:T(8,128)S(1)}, u32[]{:S(2)}, u32[]{:S(2)}) collective-permute-start(f32[2,2,32,256]{3,2,1,0:T(8,128)S(1)} %get-tuple-element.35), channel_id=1, source_target_pairs={{0,4},{1,5},{2,14},{3,15},{4,8},{5,9},{6,2},{7,3},{8,12},{9,13},{1... | collective-permute-start | bytes 393224 | tf_op jit(solution)/shard_map/ppermute | solution.py:642
  45.2 7.3 %collective-permute-start.12 = (f32[4,2,16,128]{3,2,1,0:T(8,128)S(1)}, f32[4,2,16,128]{3,2,1,0:T(8,128)S(1)}, u32[]{:S(2)}, u32[]{:S(2)}) collective-permute-start(f32[4,2,16,128]{3,2,1,0:T(8,128)S(1)} %shard_map.85.refs_0_), channel_id=1, source_target_pairs={{0,4},{1,5},{2,6},{3,7},{4,0},{5,1},{6,2},{7,3},{8,12},{9,13},{10,... | collective-permute-start | bytes 196616 | tf_op jit(solution)/shard_map/ppermute | solution.py:642
  45.3 7.5 %collective-permute-start.13 = (f32[4,2,16,128]{3,2,1,0:T(8,128)S(1)}, f32[4,2,16,128]{3,2,1,0:T(8,128)S(1)}, u32[]{:S(2)}, u32[]{:S(2)}) collective-permute-start(f32[4,2,16,128]{3,2,1,0:T(8,128)S(1)} %shard_map.85.refs_0_), channel_id=1, source_target_pairs={{0,8},{1,9},{2,10},{3,11},{4,12},{5,13},{6,14},{7,15},{8,0},{9,1},... | collective-permute-start | bytes 196616 | tf_op jit(solution)/shard_map/ppermute | solution.py:642
  47.3 6.2 %collective-permute-start.14 = (f32[4,2,16,128]{3,2,1,0:T(8,128)S(1)}, f32[4,2,16,128]{3,2,1,0:T(8,128)S(1)}, u32[]{:S(2)}, u32[]{:S(2)}) collective-permute-start(f32[4,2,16,128]{3,2,1,0:T(8,128)S(1)} %shard_map.85.refs_0_), channel_id=1, source_target_pairs={{0,12},{1,13},{2,14},{3,15},{4,8},{5,9},{6,10},{7,11},{8,4},{9,5},... | collective-permute-start | bytes 196616 | tf_op jit(solution)/shard_map/ppermute | solution.py:642
  52.4 5.1 %collective-permute-start.17 = (f32[2,2,32,256]{3,2,1,0:T(8,128)S(1)}, f32[2,2,32,256]{3,2,1,0:T(8,128)S(1)}, u32[]{:S(2)}, u32[]{:S(2)}) collective-permute-start(f32[2,2,32,256]{3,2,1,0:T(8,128)S(1)} %get-tuple-element.38), channel_id=1, source_target_pairs={{0,1},{1,0},{2,3},{3,2},{4,5},{5,4},{6,7},{7,6},{8,9},{9,8},{10,11... | collective-permute-start | bytes 393224 | tf_op jit(solution)/shard_map/ppermute | solution.py:642
  56.5 1.3 %collective-permute-start.16 = (f32[5,2,16,128]{3,2,1,0:T(8,128)S(1)}, f32[5,2,16,128]{3,2,1,0:T(8,128)S(1)}, u32[]{:S(2)}, u32[]{:S(2)}) collective-permute-start(f32[5,2,16,128]{3,2,1,0:T(8,128)S(1)} %get-tuple-element.37), channel_id=1, source_target_pairs={{0,1},{1,0},{2,3},{3,2},{4,5},{5,4},{6,7},{7,6},{8,9},{9,8},{10,11... | collective-permute-start | bytes 245768 | tf_op jit(solution)/shard_map/ppermute | solution.py:642

commit v12 on v11

--- a/solution.py
+++ b/solution.py
@@ -7,7 +7,6 @@
 
 omega = 0.8
 screen = 0.05
-highest = lax.Precision.HIGHEST
 
 fine_diagonal = 7.5 + screen
 fine_scale = omega / fine_diagonal
@@ -30,8 +29,24 @@
         pl.loop(0, count, unroll=4)(body)
 
 
-def dot(a, b):
-    return jnp.dot(a, b, precision=highest, preferred_element_type=jnp.float32)
+def parts_of(values):
+    parts = []
+    for _ in range(3):
+        parts.append(values.astype(jnp.bfloat16))
+        values = values - parts[-1].astype(jnp.float32)
+    return parts
+
+
+def dot(values, exact):
+    exact = exact.astype(jnp.bfloat16)
+    products = [jnp.dot(p, exact, preferred_element_type=jnp.float32) for p in parts_of(values)]
+    return products[0] + (products[1] + products[2])
+
+
+def pick_dot(exact, values):
+    exact = exact.astype(jnp.bfloat16)
+    products = [jnp.dot(exact, p, preferred_element_type=jnp.float32) for p in parts_of(values)]
+    return products[0] + (products[1] + products[2])
 
 
 def pair_matrix(rows, columns, value):
@@ -136,7 +151,7 @@
     send_ref[slots : slots + 1, 0:slots] = number
 
 
-def pack_kernel(own_ref, got_ref, slots_ref, _, *out_refs):
+def pack_kernel(own_ref, got_ref, slots_ref, *out_refs):
     slots = own_ref.shape[0]
     apart = len(out_refs) > 1
     height = out_refs[0].shape[-2]
@@ -158,7 +173,7 @@
     targets = [lax.bitwise_xor(chip, k) if apart else k for k in range(chips)]
     pick = jnp.concatenate([jnp.where(place == r + target * ranks, 1.0, 0.0) for target in targets])
     rows = jnp.concatenate([own_ref[...], got_ref[0:slots]], axis=0)
-    packed = dot(pick, rows)
+    packed = pick_dot(pick, rows)
     lines = jnp.sum(pick * line.astype(jnp.float32), axis=1, keepdims=True)
     bucket = lax.broadcasted_iota(jnp.int32, (chips * ranks, 128), 0)
     lane = lax.broadcasted_iota(jnp.int32, (chips * ranks, 128), 1)
@@ -166,7 +181,7 @@
     spots = jnp.where(lane == spot % (128 // ranks) * ranks + bucket % ranks, lines, 0.0)
     i = lax.broadcasted_iota(jnp.int32, (chips, chips * ranks), 0)
     j = lax.broadcasted_iota(jnp.int32, (chips, chips * ranks), 1)
-    numbers = dot(jnp.where(i == j // ranks, 1.0, 0.0), spots)
+    numbers = pick_dot(jnp.where(i == j // ranks, 1.0, 0.0), spots)
     for k in range(chips):
         out = out_refs[k] if apart else out_refs[0].at[k]
         for q in range(4):
@@ -214,7 +229,7 @@
                 ],
                 axis=1,
             )
-            value = dot(spread[:, : len(members) * ranks], values)
+            value = pick_dot(spread[:, : len(members) * ranks], values)
             added[part] = value if added[part] is None else added[part] + value
     for x in range(planes):
         for part in range(2):
@@ -675,10 +690,10 @@
     packed = call(
         pack_kernel,
         [shaped(height, 128)] * chips if apart else [shaped(chips, height, 128)],
-        vmem(3) + [pl.BlockSpec(memory_space=pl.ANY)],
+        vmem(3),
         [],
         10**8,
-    )(kept, got, slots, other)
+    )(kept, got, slots)
     if apart:
         received = [
             permute(packed[k], lambda i, k=k: i ^ (2 * k)) if k else packed[k]

time: 59.6 us -> 58.4 us (0.980)
  waiting for transfers between devices: 18.4 us -> 16.2 us
  starting transfers between devices: 23.4 us -> 25.3 us
  Pallas kernels: 14.2 us -> 13.1 us
    ppermute x18, waiting for transfers between devices: 18.4 us -> 16.2 us  [permute(): return lax.ppermute(value, 'grid', [(i, target(i)) for i in devices])]
    ppermute x18, starting transfers between devices: 23.4 us -> 25.3 us  [permute(): return lax.ppermute(value, 'grid', [(i, target(i)) for i in devices])]
  transfers between devices with their start and end apart: 18 -> 18, of which waited for: 10 -> 9; matrix products, arithmetic and copies ran while one was open for 1% -> 1% of each run, Pallas kernels for 15% -> 16%
where the time goes in v12:
time: 58.4 us; the launch traced here: 58.2 us
  starting transfers between devices  25.3 us (43%)
  waiting for transfers between devices  16.2 us (28%)
  Pallas kernels  13.1 us (22%)
  local copies, waits for them, and re-layouts  2.19 us (4%)
  other arithmetic  1.15 us (2%)
    ppermute x18, starting transfers between devices, permute(): return lax.ppermute(value, 'grid', [(i, target(i)) for i in devices])  25.3 us
    ppermute x18, waiting for transfers between devices, permute(): return lax.ppermute(value, 'grid', [(i, target(i)) for i in devices])  16.2 us
    pallas_call x1, Pallas kernels, per_device(): call(cycle_kernel, [shaped(5, *small)] * 2, vmem(len(pieces)) + smem, [(n...  2.79 us
    pallas_call x1, Pallas kernels, per_device(): call(fine_kernel, [shaped(thick, *full)] * 2, vmem(5) + smem, [(3 * plane...  2.55 us
    pallas_call x1, Pallas kernels, per_device(): call(source_kernel, shaped(planes, *small), vmem(4) + smem, [(4 * planes,...  2.45 us
    unnamed x9, local copies, waits for them, and re-layouts  2.18 us
    pallas_call x1, Pallas kernels, per_device(): call(output_kernel, shaped(*pair_density.shape), vmem(3), scratch, 10 ** 7)  1.54 us
    pallas_call x1, Pallas kernels, per_device(): call(rows_kernel, [shaped(slot_count, row), shaped(slot_count + 8, row)],...  1.46 us
  transfers between devices with their start and end apart: 18, of which 9 were waited for; matrix products, arithmetic and copies ran while one was open for 1% of the time, Pallas kernels for 16%

profile of v12, /device:TPU:0, one launch (start us, length us, event | category | flops | bytes accessed | tf_op | source)
XLA Modules:
  0.0 58.2 jit_solution(14573775774500822269)
XLA Ops:
  0.0 0.7 %copy.11 = f32[12,2,2,25]{3,0,2,1:T(8,128)S(1)} copy(f32[12,2,2,25]{3,2,1,0:T(2,128)} %param.9) | data formatting | bytes 9600 | tf_op args[1]
  0.7 0.7 %pad_add_fusion.slots_ref = s32[3,64]{1,0:T(4,128)S(1)} fusion(s32[1,64]{1,0:T(1,128)} %bitcast.11, s32[1,64]{1,0:T(1,128)} %bitcast.12, s32[1,64]{1,0:T(1,128)} %bitcast.13), kind=kLoop, calls=%fused_computation.3 | loop fusion | flops 384 | bytes 1536 | tf_op jit(solution)/shard_map/stack | solution.py:677
  1.4 1.4 %copy-done = f32[64,25,256]{2,0,1:T(8,128)S(1)} copy-done((f32[64,25,256]{2,0,1:T(8,128)S(1)}, f32[64,25,256]{2,0,1:T(8,128)}, u32[]{:S(2)}) %copy-start) | copy-done | bytes 1638424
  2.9 1.5 %shard_map.82 = (f32[64,512]{1,0:T(8,128)S(1)}, f32[72,512]{1,0:T(8,128)S(1)}) custom-call(f32[4,12,25]{2,1,0:T(8,128)S(1)} %bitcast.10, f32[25,64,256]{2,1,0:T(8,128)S(1)} %bitcast.9, s32[3,64]{1,0:T(4,128)S(1)} %pad_add_fusion.slots_ref), custom_call_target="tpu_custom_call" | custom-call | flops 10000000 | bytes 1048576 | tf_op jit(solution)/shard_map/pallas_call | solution.py:680
  4.3 0.5 collective-permute-start.1
  4.9 0.1 collective-permute-start
  5.0 0.9 %collective-permute-done.1.got_ref = f32[72,512]{1,0:T(8,128)S(1)} collective-permute-done((f32[72,512]{1,0:T(8,128)S(1)}, f32[72,512]{1,0:T(8,128)S(1)}, u32[]{:S(2)}, u32[]{:S(2)}) %collective-permute-start.1) | collective-permute-done | bytes 147488 | tf_op jit(solution)/shard_map/ppermute | solution.py:657
  5.9 0.5 shard_map.83
  6.4 2.9 %collective-permute-start.2 = (f32[136,128]{1,0:T(8,128)S(1)}, f32[136,128]{1,0:T(8,128)S(1)}, u32[]{:S(2)}, u32[]{:S(2)}) collective-permute-start(f32[136,128]{1,0:T(8,128)S(1)} %get-tuple-element.25), channel_id=1, source_target_pairs={{0,2},{1,3},{2,0},{3,1},{4,6},{5,7},{6,4},{7,5},{8,10},{9,11},{10,... | collective-permute-start | bytes 208904 | tf_op jit(solution)/shard_map/ppermute | solution.py:657
  9.3 3.6 %collective-permute-start.3 = (f32[136,128]{1,0:T(8,128)S(1)}, f32[136,128]{1,0:T(8,128)S(1)}, u32[]{:S(2)}, u32[]{:S(2)}) collective-permute-start(f32[136,128]{1,0:T(8,128)S(1)} %get-tuple-element.26), channel_id=1, source_target_pairs={{0,12},{1,13},{2,14},{3,15},{4,8},{5,9},{6,10},{7,11},{8,4},{9,5},... | collective-permute-start | bytes 208904 | tf_op jit(solution)/shard_map/ppermute | solution.py:657
  12.9 0.0 collective-permute-start.4
  12.9 1.0 %collective-permute-start.5 = (f32[136,128]{1,0:T(8,128)S(1)}, f32[136,128]{1,0:T(8,128)S(1)}, u32[]{:S(2)}, u32[]{:S(2)}) collective-permute-start(f32[136,128]{1,0:T(8,128)S(1)} %get-tuple-element.28), channel_id=1, source_target_pairs={{0,8},{1,9},{2,10},{3,11},{4,12},{5,13},{6,14},{7,15},{8,0},{9,1},... | collective-permute-start | bytes 208904 | tf_op jit(solution)/shard_map/ppermute | solution.py:657
  13.9 0.0 collective-permute-done.refs_1_
  13.9 3.1 %collective-permute-start.6 = (f32[136,128]{1,0:T(8,128)S(1)}, f32[136,128]{1,0:T(8,128)S(1)}, u32[]{:S(2)}, u32[]{:S(2)}) collective-permute-start(f32[136,128]{1,0:T(8,128)S(1)} %get-tuple-element.29), channel_id=1, source_target_pairs={{0,10},{1,11},{2,8},{3,9},{4,14},{5,15},{6,12},{7,13},{8,2},{9,3},... | collective-permute-start | bytes 208904 | tf_op jit(solution)/shard_map/ppermute | solution.py:657
  17.0 0.0 collective-permute-done.2.refs_3_
  17.0 1.2 %collective-permute-start.7 = (f32[136,128]{1,0:T(8,128)S(1)}, f32[136,128]{1,0:T(8,128)S(1)}, u32[]{:S(2)}, u32[]{:S(2)}) collective-permute-start(f32[136,128]{1,0:T(8,128)S(1)} %get-tuple-element.30), channel_id=1, source_target_pairs={{0,4},{1,5},{2,6},{3,7},{4,0},{5,1},{6,2},{7,3},{8,12},{9,13},{10,... | collective-permute-start | bytes 208904 | tf_op jit(solution)/shard_map/ppermute | solution.py:657
  18.2 0.0 collective-permute-done.3.refs_4_
  18.2 2.2 %collective-permute-start.8 = (f32[136,128]{1,0:T(8,128)S(1)}, f32[136,128]{1,0:T(8,128)S(1)}, u32[]{:S(2)}, u32[]{:S(2)}) collective-permute-start(f32[136,128]{1,0:T(8,128)S(1)} %get-tuple-element.31), channel_id=1, source_target_pairs={{0,6},{1,7},{2,4},{3,5},{4,2},{5,3},{6,0},{7,1},{8,14},{9,15},{10,... | collective-permute-start | bytes 208904 | tf_op jit(solution)/shard_map/ppermute | solution.py:657
  20.4 0.0 collective-permute-done.4.refs_5_
  20.4 3.7 %collective-permute-done.5.refs_6_ = f32[136,128]{1,0:T(8,128)S(1)} collective-permute-done((f32[136,128]{1,0:T(8,128)S(1)}, f32[136,128]{1,0:T(8,128)S(1)}, u32[]{:S(2)}, u32[]{:S(2)}) %collective-permute-start.5) | collective-permute-done | bytes 69664 | tf_op jit(solution)/shard_map/ppermute | solution.py:657
  24.2 0.7 %collective-permute-done.6.refs_7_ = f32[136,128]{1,0:T(8,128)S(1)} collective-permute-done((f32[136,128]{1,0:T(8,128)S(1)}, f32[136,128]{1,0:T(8,128)S(1)}, u32[]{:S(2)}, u32[]{:S(2)}) %collective-permute-start.6) | collective-permute-done | bytes 69664 | tf_op jit(solution)/shard_map/ppermute | solution.py:657
  24.8 0.0 collective-permute-done.7.refs_8_
  24.8 0.3 collective-permute-done.8.refs_9_
  25.1 1.0 %shard_map.84 = (f32[4,2,32,256]{3,2,1,0:T(8,128)S(1)}, f32[10,32,128]{2,1,0:T(8,128)S(1)}, f32[2,2,32,256]{3,2,1,0:T(8,128)S(1)}) custom-call(f32[2,2,2,32,256]{4,3,2,1,0:T(8,128)S(1)} %copy-done.1, f32[2,2,32,256]{3,2,1,0:T(8,128)S(1)} %collective-permute-done.refs_1_, f32[136,128]{1,0:T(8,128)S(1)} %get-tuple-element.24.refs_2_, ...), custom_call_target="tpu_custom_call" | custom-call | flops 100000000 | bytes 1048576 | tf_op jit(solution)/shard_map/pallas_call | solution.py:712
  26.0 4.0 %collective-permute-start.10 = (f32[4,2,32,256]{3,2,1,0:T(8,128)S(1)}, f32[4,2,32,256]{3,2,1,0:T(8,128)S(1)}, u32[]{:S(2)}, u32[]{:S(2)}) collective-permute-start(f32[4,2,32,256]{3,2,1,0:T(8,128)S(1)} %get-tuple-element.32.f_ref), channel_id=1, source_target_pairs={{0,14},{1,15},{2,4},{3,5},{4,2},{5,3},{6,8},{7,9},{8,6},{9,7},{10,... | collective-permute-start | bytes 786440 | tf_op jit(solution)/shard_map/ppermute | solution.py:657
  30.1 0.0 collective-permute-start.9
  30.1 0.2 fusion
  30.3 1.3 %collective-permute-start.11 = (f32[10,32,128]{2,1,0:T(8,128)S(1)}, f32[10,32,128]{2,1,0:T(8,128)S(1)}, u32[]{:S(2)}, u32[]{:S(2)}) collective-permute-start(f32[10,32,128]{2,1,0:T(8,128)S(1)} %get-tuple-element.33), channel_id=1, source_target_pairs={{0,12},{1,13},{2,6},{3,7},{4,0},{5,1},{6,10},{7,11},{8,4},{9,5},{1... | collective-permute-start | bytes 491528 | tf_op jit(solution)/shard_map/ppermute | solution.py:657
  31.5 0.2 cosine_reduce_fusion
  31.7 0.8 %collective-permute-start.15 = (f32[2,2,32,256]{3,2,1,0:T(8,128)S(1)}, f32[2,2,32,256]{3,2,1,0:T(8,128)S(1)}, u32[]{:S(2)}, u32[]{:S(2)}) collective-permute-start(f32[2,2,32,256]{3,2,1,0:T(8,128)S(1)} %get-tuple-element.35), channel_id=1, source_target_pairs={{0,4},{1,5},{2,14},{3,15},{4,8},{5,9},{6,2},{7,3},{8,12},{9,13},{1... | collective-permute-start | bytes 393224 | tf_op jit(solution)/shard_map/ppermute | solution.py:657
  32.5 0.1 pad_maximum_fusion.cs_ref.refs_4_
  32.6 8.1 %collective-permute-done.11.straight_ref = f32[10,32,128]{2,1,0:T(8,128)S(1)} collective-permute-done((f32[10,32,128]{2,1,0:T(8,128)S(1)}, f32[10,32,128]{2,1,0:T(8,128)S(1)}, u32[]{:S(2)}, u32[]{:S(2)}) %collective-permute-start.11) | collective-permute-done | bytes 163872 | tf_op jit(solution)/shard_map/ppermute | solution.py:657
  40.7 0.0 collective-permute-done.10.odd_ref
  40.7 1.0 %collective-permute-done.9.even_ref = f32[4,2,32,256]{3,2,1,0:T(8,128)S(1)} collective-permute-done((f32[4,2,32,256]{3,2,1,0:T(8,128)S(1)}, f32[4,2,32,256]{3,2,1,0:T(8,128)S(1)}, u32[]{:S(2)}, u32[]{:S(2)}) %collective-permute-start.9) | collective-permute-done | bytes 262176 | tf_op jit(solution)/shard_map/ppermute | solution.py:657
  41.7 2.4 %shard_map.85.refs_0_ = f32[4,2,16,128]{3,2,1,0:T(8,128)S(1)} custom-call(f32[4,2,32,256]{3,2,1,0:T(8,128)S(1)} %collective-permute-done.9.even_ref, f32[4,2,32,256]{3,2,1,0:T(8,128)S(1)} %collective-permute-done.10.odd_ref, f32[10,32,128]{2,1,0:T(8,128)S(1)} %collective-permute-done.11.straight_ref, f32[4,2,32,256]{3,2,1,0:T(8,128)S(1)} %get-tuple-element.32.f_ref, ...), custom_call_target="tpu_custom_call" | custom-call | flops 10000000 | bytes 1048576 | tf_op jit(solution)/shard_map/pallas_call | solution.py:723
  44.1 0.1 collective-permute-start.12
  44.2 2.1 %collective-permute-start.13 = (f32[4,2,16,128]{3,2,1,0:T(8,128)S(1)}, f32[4,2,16,128]{3,2,1,0:T(8,128)S(1)}, u32[]{:S(2)}, u32[]{:S(2)}) collective-permute-start(f32[4,2,16,128]{3,2,1,0:T(8,128)S(1)} %shard_map.85.refs_0_), channel_id=1, source_target_pairs={{0,8},{1,9},{2,10},{3,11},{4,12},{5,13},{6,14},{7,15},{8,0},{9,1},... | collective-permute-start | bytes 196616 | tf_op jit(solution)/shard_map/ppermute | solution.py:657
  46.3 2.3 %collective-permute-start.14 = (f32[4,2,16,128]{3,2,1,0:T(8,128)S(1)}, f32[4,2,16,128]{3,2,1,0:T(8,128)S(1)}, u32[]{:S(2)}, u32[]{:S(2)}) collective-permute-start(f32[4,2,16,128]{3,2,1,0:T(8,128)S(1)} %shard_map.85.refs_0_), channel_id=1, source_target_pairs={{0,12},{1,13},{2,14},{3,15},{4,8},{5,9},{6,10},{7,11},{8,4},{9,5},... | collective-permute-start | bytes 196616 | tf_op jit(solution)/shard_map/ppermute | solution.py:657
  48.6 0.0 collective-permute-done.15.across_ref
  48.6 2.5 %shard_map.87 = (f32[2,2,32,256]{3,2,1,0:T(8,128)S(1)}, f32[2,2,32,256]{3,2,1,0:T(8,128)S(1)}) custom-call(f32[4,2,32,256]{3,2,1,0:T(8,128)S(1)} %collective-permute-done.9.even_ref, f32[4,2,32,256]{3,2,1,0:T(8,128)S(1)} %collective-permute-done.10.odd_ref, f32[10,32,128]{2,1,0:T(8,128)S(1)} %collective-permute-done.11.straight_ref, ...), custom_call_target="tpu_custom_call" | custom-call | flops 10000000 | bytes 1048576 | tf_op jit(solution)/shard_map/pallas_call | solution.py:731
  51.2 0.1 collective-permute-start.17
  51.2 0.5 collective-permute-done.13.refs_2_
  51.8 0.7 %collective-permute-done.14.refs_3_ = f32[4,2,16,128]{3,2,1,0:T(8,128)S(1)} collective-permute-done((f32[4,2,16,128]{3,2,1,0:T(8,128)S(1)}, f32[4,2,16,128]{3,2,1,0:T(8,128)S(1)}, u32[]{:S(2)}, u32[]{:S(2)}) %collective-permute-start.14) | collective-permute-done | bytes 65568 | tf_op jit(solution)/shard_map/ppermute | solution.py:657
  52.5 2.8 %shard_map.86 = (f32[5,2,16,128]{3,2,1,0:T(8,128)S(1)}, f32[5,2,16,128]{3,2,1,0:T(8,128)S(1)}) custom-call(f32[4,2,16,128]{3,2,1,0:T(8,128)S(1)} %shard_map.85.refs_0_, f32[4,2,16,128]{3,2,1,0:T(8,128)S(1)} %collective-permute-done.12.refs_1_, f32[4,2,16,128]{3,2,1,0:T(8,128)S(1)} %collective-permute-done.13.refs_2_, ...), custom_call_target="tpu_custom_call" | custom-call | flops 100000000 | bytes 1048576 | tf_op jit(solution)/shard_map/pallas_call | solution.py:742
  55.3 0.1 collective-permute-start.16
  55.4 0.8 %shard_map.88.own_ref = f32[2,2,32,256]{3,2,1,0:T(8,128)S(1)} custom-call(f32[5,2,16,128]{3,2,1,0:T(8,128)S(1)} %get-tuple-element.34.w_ref, f32[2,2,32,256]{3,2,1,0:T(8,128)S(1)} %get-tuple-element.36.g_ref), custom_call_target="tpu_custom_call" | custom-call | flops 10000000 | bytes 1048576 | tf_op jit(solution)/shard_map/pallas_call | solution.py:763
  56.2 0.4 collective-permute-done.16.w_ref
  56.6 1.5 %shard_map.89 = f32[2,2,2,32,256]{4,3,2,1,0:T(8,128)} custom-call(f32[2,2,32,256]{3,2,1,0:T(8,128)S(1)} %shard_map.88.own_ref, f32[5,2,16,128]{3,2,1,0:T(8,128)S(1)} %collective-permute-done.16.w_ref, f32[2,2,32,256]{3,2,1,0:T(8,128)S(1)} %collective-permute-done.17.g_ref), custom_call_target="tpu_custom_call" | custom-call | flops 10000000 | bytes 1048576 | tf_op jit(solution)/shard_map/pallas_call | solution.py:764
  (10 shorter events, 0.0 us)
Async XLA Ops:
  1.4 1.4 %copy-start = (f32[64,25,256]{2,0,1:T(8,128)S(1)}, f32[64,25,256]{2,0,1:T(8,128)}, u32[]{:S(2)}) copy-start(f32[64,25,256]{2,0,1:T(8,128)} %param.10) | copy-start | bytes 4915204
  2.9 2.0 %copy-start.1 = (f32[2,2,2,32,256]{4,3,2,1,0:T(8,128)S(1)}, f32[2,2,2,32,256]{4,3,2,1,0:T(8,128)}, u32[]{:S(2)}) copy-start(f32[2,2,2,32,256]{4,3,2,1,0:T(8,128)} %refs_0_.1) | copy-start | bytes 786436
  2.9 27.2 %copy-start.2 = (s32[2,2]{1,0:T(2,128)S(1)}, s32[2,2]{1,0:T(2,128)}, u32[]{:S(2)}) copy-start(s32[2,2]{1,0:T(2,128)} %param.14) | copy-start | bytes 52
  2.9 27.2 %copy-start.3 = (f32[8]{0:T(128)S(1)}, f32[8]{0:T(128)}, u32[]{:S(2)}) copy-start(f32[8]{0:T(128)} %param.15) | copy-start | bytes 100
  4.3 1.5 %collective-permute-start.1 = (f32[72,512]{1,0:T(8,128)S(1)}, f32[72,512]{1,0:T(8,128)S(1)}, u32[]{:S(2)}, u32[]{:S(2)}) collective-permute-start(f32[72,512]{1,0:T(8,128)S(1)} %get-tuple-element.23), channel_id=1, source_target_pairs={{0,1},{1,0},{2,3},{3,2},{4,5},{5,4},{6,7},{7,6},{8,9},{9,8},{10,11... | collective-permute-start | bytes 442376 | tf_op jit(solution)/shard_map/ppermute | solution.py:657
  4.9 9.0 %collective-permute-start = (f32[2,2,32,256]{3,2,1,0:T(8,128)S(1)}, f32[2,2,32,256]{3,2,1,0:T(8,128)S(1)}, u32[]{:S(2)}, u32[]{:S(2)}) collective-permute-start(f32[2,2,32,256]{3,2,1,0:T(8,128)S(1)} %dynamic-slice_bitcast_fusion), channel_id=1, source_target_pairs={{0,1},{1,0},{2,3},{3,2},{4,5},{5,4},{6,7},{7,6},{8,9},{9,8},{10,11... | collective-permute-start | bytes 393224 | tf_op jit(solution)/shard_map/ppermute | solution.py:657
  6.4 10.6 %collective-permute-start.2 = (f32[136,128]{1,0:T(8,128)S(1)}, f32[136,128]{1,0:T(8,128)S(1)}, u32[]{:S(2)}, u32[]{:S(2)}) collective-permute-start(f32[136,128]{1,0:T(8,128)S(1)} %get-tuple-element.25), channel_id=1, source_target_pairs={{0,2},{1,3},{2,0},{3,1},{4,6},{5,7},{6,4},{7,5},{8,10},{9,11},{10,... | collective-permute-start | bytes 208904 | tf_op jit(solution)/shard_map/ppermute | solution.py:657
  9.3 8.9 %collective-permute-start.3 = (f32[136,128]{1,0:T(8,128)S(1)}, f32[136,128]{1,0:T(8,128)S(1)}, u32[]{:S(2)}, u32[]{:S(2)}) collective-permute-start(f32[136,128]{1,0:T(8,128)S(1)} %get-tuple-element.26), channel_id=1, source_target_pairs={{0,12},{1,13},{2,14},{3,15},{4,8},{5,9},{6,10},{7,11},{8,4},{9,5},... | collective-permute-start | bytes 208904 | tf_op jit(solution)/shard_map/ppermute | solution.py:657
  12.9 7.5 %collective-permute-start.4 = (f32[136,128]{1,0:T(8,128)S(1)}, f32[136,128]{1,0:T(8,128)S(1)}, u32[]{:S(2)}, u32[]{:S(2)}) collective-permute-start(f32[136,128]{1,0:T(8,128)S(1)} %get-tuple-element.27), channel_id=1, source_target_pairs={{0,14},{1,15},{2,12},{3,13},{4,10},{5,11},{6,8},{7,9},{8,6},{9,7},... | collective-permute-start | bytes 208904 | tf_op jit(solution)/shard_map/ppermute | solution.py:657
  12.9 11.2 %collective-permute-start.5 = (f32[136,128]{1,0:T(8,128)S(1)}, f32[136,128]{1,0:T(8,128)S(1)}, u32[]{:S(2)}, u32[]{:S(2)}) collective-permute-start(f32[136,128]{1,0:T(8,128)S(1)} %get-tuple-element.28), channel_id=1, source_target_pairs={{0,8},{1,9},{2,10},{3,11},{4,12},{5,13},{6,14},{7,15},{8,0},{9,1},... | collective-permute-start | bytes 208904 | tf_op jit(solution)/shard_map/ppermute | solution.py:657
  13.9 10.9 %collective-permute-start.6 = (f32[136,128]{1,0:T(8,128)S(1)}, f32[136,128]{1,0:T(8,128)S(1)}, u32[]{:S(2)}, u32[]{:S(2)}) collective-permute-start(f32[136,128]{1,0:T(8,128)S(1)} %get-tuple-element.29), channel_id=1, source_target_pairs={{0,10},{1,11},{2,8},{3,9},{4,14},{5,15},{6,12},{7,13},{8,2},{9,3},... | collective-permute-start | bytes 208904 | tf_op jit(solution)/shard_map/ppermute | solution.py:657
  17.0 7.8 %collective-permute-start.7 = (f32[136,128]{1,0:T(8,128)S(1)}, f32[136,128]{1,0:T(8,128)S(1)}, u32[]{:S(2)}, u32[]{:S(2)}) collective-permute-start(f32[136,128]{1,0:T(8,128)S(1)} %get-tuple-element.30), channel_id=1, source_target_pairs={{0,4},{1,5},{2,6},{3,7},{4,0},{5,1},{6,2},{7,3},{8,12},{9,13},{10,... | collective-permute-start | bytes 208904 | tf_op jit(solution)/shard_map/ppermute | solution.py:657
  18.2 6.8 %collective-permute-start.8 = (f32[136,128]{1,0:T(8,128)S(1)}, f32[136,128]{1,0:T(8,128)S(1)}, u32[]{:S(2)}, u32[]{:S(2)}) collective-permute-start(f32[136,128]{1,0:T(8,128)S(1)} %get-tuple-element.31), channel_id=1, source_target_pairs={{0,6},{1,7},{2,4},{3,5},{4,2},{5,3},{6,0},{7,1},{8,14},{9,15},{10,... | collective-permute-start | bytes 208904 | tf_op jit(solution)/shard_map/ppermute | solution.py:657
  26.0 14.7 %collective-permute-start.10 = (f32[4,2,32,256]{3,2,1,0:T(8,128)S(1)}, f32[4,2,32,256]{3,2,1,0:T(8,128)S(1)}, u32[]{:S(2)}, u32[]{:S(2)}) collective-permute-start(f32[4,2,32,256]{3,2,1,0:T(8,128)S(1)} %get-tuple-element.32.f_ref), channel_id=1, source_target_pairs={{0,14},{1,15},{2,4},{3,5},{4,2},{5,3},{6,8},{7,9},{8,6},{9,7},{10,... | collective-permute-start | bytes 786440 | tf_op jit(solution)/shard_map/ppermute | solution.py:657
  30.1 11.6 %collective-permute-start.9 = (f32[4,2,32,256]{3,2,1,0:T(8,128)S(1)}, f32[4,2,32,256]{3,2,1,0:T(8,128)S(1)}, u32[]{:S(2)}, u32[]{:S(2)}) collective-permute-start(f32[4,2,32,256]{3,2,1,0:T(8,128)S(1)} %get-tuple-element.32.f_ref), channel_id=1, source_target_pairs={{0,2},{1,3},{2,0},{3,1},{4,6},{5,7},{6,4},{7,5},{8,10},{9,11},{10,... | collective-permute-start | bytes 786440 | tf_op jit(solution)/shard_map/ppermute | solution.py:657
  30.3 10.4 %collective-permute-start.11 = (f32[10,32,128]{2,1,0:T(8,128)S(1)}, f32[10,32,128]{2,1,0:T(8,128)S(1)}, u32[]{:S(2)}, u32[]{:S(2)}) collective-permute-start(f32[10,32,128]{2,1,0:T(8,128)S(1)} %get-tuple-element.33), channel_id=1, source_target_pairs={{0,12},{1,13},{2,6},{3,7},{4,0},{5,1},{6,10},{7,11},{8,4},{9,5},{1... | collective-permute-start | bytes 491528 | tf_op jit(solution)/shard_map/ppermute | solution.py:657
  31.7 16.9 %collective-permute-start.15 = (f32[2,2,32,256]{3,2,1,0:T(8,128)S(1)}, f32[2,2,32,256]{3,2,1,0:T(8,128)S(1)}, u32[]{:S(2)}, u32[]{:S(2)}) collective-permute-start(f32[2,2,32,256]{3,2,1,0:T(8,128)S(1)} %get-tuple-element.35), channel_id=1, source_target_pairs={{0,4},{1,5},{2,14},{3,15},{4,8},{5,9},{6,2},{7,3},{8,12},{9,13},{1... | collective-permute-start | bytes 393224 | tf_op jit(solution)/shard_map/ppermute | solution.py:657
  44.1 7.1 %collective-permute-start.12 = (f32[4,2,16,128]{3,2,1,0:T(8,128)S(1)}, f32[4,2,16,128]{3,2,1,0:T(8,128)S(1)}, u32[]{:S(2)}, u32[]{:S(2)}) collective-permute-start(f32[4,2,16,128]{3,2,1,0:T(8,128)S(1)} %shard_map.85.refs_0_), channel_id=1, source_target_pairs={{0,4},{1,5},{2,6},{3,7},{4,0},{5,1},{6,2},{7,3},{8,12},{9,13},{10,... | collective-permute-start | bytes 196616 | tf_op jit(solution)/shard_map/ppermute | solution.py:657
  44.2 7.6 %collective-permute-start.13 = (f32[4,2,16,128]{3,2,1,0:T(8,128)S(1)}, f32[4,2,16,128]{3,2,1,0:T(8,128)S(1)}, u32[]{:S(2)}, u32[]{:S(2)}) collective-permute-start(f32[4,2,16,128]{3,2,1,0:T(8,128)S(1)} %shard_map.85.refs_0_), channel_id=1, source_target_pairs={{0,8},{1,9},{2,10},{3,11},{4,12},{5,13},{6,14},{7,15},{8,0},{9,1},... | collective-permute-start | bytes 196616 | tf_op jit(solution)/shard_map/ppermute | solution.py:657
  46.3 6.2 %collective-permute-start.14 = (f32[4,2,16,128]{3,2,1,0:T(8,128)S(1)}, f32[4,2,16,128]{3,2,1,0:T(8,128)S(1)}, u32[]{:S(2)}, u32[]{:S(2)}) collective-permute-start(f32[4,2,16,128]{3,2,1,0:T(8,128)S(1)} %shard_map.85.refs_0_), channel_id=1, source_target_pairs={{0,12},{1,13},{2,14},{3,15},{4,8},{5,9},{6,10},{7,11},{8,4},{9,5},... | collective-permute-start | bytes 196616 | tf_op jit(solution)/shard_map/ppermute | solution.py:657
  51.2 5.0 %collective-permute-start.17 = (f32[2,2,32,256]{3,2,1,0:T(8,128)S(1)}, f32[2,2,32,256]{3,2,1,0:T(8,128)S(1)}, u32[]{:S(2)}, u32[]{:S(2)}) collective-permute-start(f32[2,2,32,256]{3,2,1,0:T(8,128)S(1)} %get-tuple-element.38), channel_id=1, source_target_pairs={{0,1},{1,0},{2,3},{3,2},{4,5},{5,4},{6,7},{7,6},{8,9},{9,8},{10,11... | collective-permute-start | bytes 393224 | tf_op jit(solution)/shard_map/ppermute | solution.py:657
  55.3 1.3 %collective-permute-start.16 = (f32[5,2,16,128]{3,2,1,0:T(8,128)S(1)}, f32[5,2,16,128]{3,2,1,0:T(8,128)S(1)}, u32[]{:S(2)}, u32[]{:S(2)}) collective-permute-start(f32[5,2,16,128]{3,2,1,0:T(8,128)S(1)} %get-tuple-element.37), channel_id=1, source_target_pairs={{0,1},{1,0},{2,3},{3,2},{4,5},{5,4},{6,7},{7,6},{8,9},{9,8},{10,11... | collective-permute-start | bytes 245768 | tf_op jit(solution)/shard_map/ppermute | solution.py:657
